TPU v7x, 32 devices: a whole 2x2x4 slice. The times are simulated.
32 devices in a mesh: section: 4 (over y, core), dp: 8 (over z, x).
Axes of the slice: x: 2, y: 2, z: 4, core: 2. Of those that a mesh axis runs over, the one named last changes fastest.
Arguments:
- tokens: bfloat16 [1024, 8192], P('dp'), may hold values from -6 to 6
- cotangent: bfloat16 [1024, 8192], P('dp'), may hold values from -9 to 9
- down_weight: bfloat16 [4, 8192, 256], P('section', 'dp'), may hold values from -0.0625 to 0.0625
- up_weight: bfloat16 [4, 8192, 256], P('section', 'dp'), may hold values from -0.0625 to 0.0625
- norm_gain: float32 [4, 8192], P('section'), may hold values from 0.5 to 1.5
- lengths: int32 [8, 4], P('dp'), may hold values from 1 to 96, 128 in all within a row
Outputs:
- fisher: float32 [4, 8192, 256], P('section', 'dp')
Inputs may be any that keep to these rules, and one draw needn't show every extreme that they name: Each replica's 4 lengths sum to 128, and the longest in each replica is exactly 96.
All inputs are finite; a program needn't handle non-finite values.
Results may differ from a plain program's by a relative error of at most 0.0039.
Values may be sent and summed in bfloat16 or wider, within the bound.
No kernel may reach another device: no remote copies, remote signals or barrier semaphores. Data moves between devices by JAX's collectives and lax.ppermute only.
A program may use at most 64 MiB of HBM per device.

v0:
```python
import jax
import jax.numpy as jnp
from jax import lax
from jax.sharding import PartitionSpec as P

MICRO = 8


epsilon = 1e-05


def from_behind(array, axis, by):
    peers = lax.axis_size(axis)
    pairs = [(i, i + by) for i in range(peers) if 0 <= i + by < peers]
    return lax.ppermute(array, axis, pairs)


def layer_forward(inputs, gain_row, w_down, w_up):
    wide_rows = inputs.astype(jnp.float32)
    inverse_rms = lax.rsqrt(jnp.mean(wide_rows * wide_rows, axis=-1, keepdims=True) + epsilon)
    normed = (wide_rows * inverse_rms * gain_row).astype(jnp.bfloat16)
    pre_act = jnp.dot(normed, w_down, preferred_element_type=jnp.float32)
    activated = jax.nn.silu(pre_act).astype(jnp.bfloat16)
    branch = lax.dot_general(
        activated, w_up, (((1,), (1,)), ((), ())), preferred_element_type=jnp.float32
    )
    return (wide_rows + branch).astype(jnp.bfloat16)


def layer_backward(inputs, upstream, gain_row, w_down, w_up):
    wide_rows = inputs.astype(jnp.float32)
    inverse_rms = lax.rsqrt(jnp.mean(wide_rows * wide_rows, axis=-1, keepdims=True) + epsilon)
    normed = (wide_rows * inverse_rms * gain_row).astype(jnp.bfloat16)
    pre_act = jnp.dot(normed, w_down, preferred_element_type=jnp.float32)
    act_grad = jnp.dot(upstream, w_up, preferred_element_type=jnp.float32)
    sigmoid_z = jax.nn.sigmoid(pre_act)
    pre_grad = (act_grad * sigmoid_z * (1.0 + pre_act * (1.0 - sigmoid_z))).astype(jnp.bfloat16)
    norm_grad = lax.dot_general(
        pre_grad, w_down, (((1,), (1,)), ((), ())), preferred_element_type=jnp.float32
    )
    gained = norm_grad * gain_row
    inner = jnp.mean(wide_rows * gained, axis=-1, keepdims=True)
    input_grad = upstream.astype(jnp.float32) + inverse_rms * (
        gained - wide_rows * inverse_rms * inverse_rms * inner
    )
    return (input_grad.astype(jnp.bfloat16), normed, pre_grad)


def replica_squares(norm_rows, grad_rows, seq_lengths):
    row_ids = jnp.arange(norm_rows.shape[0], dtype=jnp.int32)
    ends = jnp.cumsum(seq_lengths)
    starts = ends - seq_lengths
    fisher_sum = jnp.zeros((norm_rows.shape[1], grad_rows.shape[1]), jnp.float32)
    for seq_index in range(seq_lengths.shape[0]):
        inside = (row_ids >= starts[seq_index]) & (row_ids < ends[seq_index])
        masked = jnp.where(inside[:, None], grad_rows, jnp.zeros_like(grad_rows))
        seq_grad = lax.dot_general(
            norm_rows, masked, (((0,), (0,)), ((), ())), preferred_element_type=jnp.float32
        )
        fisher_sum = fisher_sum + seq_grad * seq_grad
    return fisher_sum


def per_device(tokens, cotangent, down_weight, up_weight, norm_gain, lengths):
    gathered = (
        lax.all_gather(down_weight, "dp", axis=1, tiled=True),
        lax.all_gather(up_weight, "dp", axis=1, tiled=True),
    )
    w_down = gathered[0][0]
    w_up = gathered[1][0]
    gain_row = norm_gain[0]
    section_count = lax.axis_size("section")
    section_index = lax.axis_index("section")
    row_count = tokens.shape[0]
    width = tokens.shape[1]
    hidden_width = w_down.shape[1]
    micro_rows = row_count // MICRO
    tick_count = MICRO + section_count - 1

    def forward_tick(moment, state_now):
        incoming, stored_inputs = state_now
        micro_index = moment - section_index
        active = (micro_index >= 0) & (micro_index < MICRO)
        begin_row = jnp.clip(micro_index, 0, MICRO - 1) * micro_rows
        first_rows = lax.dynamic_slice_in_dim(tokens, begin_row, micro_rows, 0)
        entering = jnp.where(section_index == 0, first_rows, incoming)

        def forward_compute_tick(operands):
            updated = lax.dynamic_update_slice_in_dim(operands[1], operands[0], begin_row, 0)
            return (layer_forward(operands[0], gain_row, w_down, w_up), updated)

        def forward_no_work(operands):
            return (jnp.zeros_like(operands[0]), operands[1])

        leaving, stored_inputs = lax.cond(
            active, forward_compute_tick, forward_no_work, (entering, stored_inputs)
        )
        return (from_behind(leaving, "section", 1), stored_inputs)

    start_state = (
        jnp.zeros((micro_rows, width), jnp.bfloat16),
        jnp.zeros((row_count, width), jnp.bfloat16),
    )
    stored_inputs = lax.fori_loop(0, tick_count, forward_tick, start_state)[1]

    def backward_tick(moment, state_now):
        incoming, norm_rows, grad_rows = state_now
        micro_index = moment - (section_count - 1 - section_index)
        active = (micro_index >= 0) & (micro_index < MICRO)
        begin_row = jnp.clip(micro_index, 0, MICRO - 1) * micro_rows
        last_rows = lax.dynamic_slice_in_dim(cotangent, begin_row, micro_rows, 0)
        entering = jnp.where(section_index == section_count - 1, last_rows, incoming)

        def backward_compute_tick(operands):
            layer_input = lax.dynamic_slice_in_dim(stored_inputs, begin_row, micro_rows, 0)
            input_grad, normed, pre_grad = layer_backward(
                layer_input, operands[0], gain_row, w_down, w_up
            )
            norm_new = lax.dynamic_update_slice_in_dim(operands[1], normed, begin_row, 0)
            grad_new = lax.dynamic_update_slice_in_dim(operands[2], pre_grad, begin_row, 0)
            return (input_grad, norm_new, grad_new)

        def backward_no_work(operands):
            return (jnp.zeros_like(operands[0]), operands[1], operands[2])

        leaving, norm_rows, grad_rows = lax.cond(
            active, backward_compute_tick, backward_no_work, (entering, norm_rows, grad_rows)
        )
        return (from_behind(leaving, "section", -1), norm_rows, grad_rows)

    start_back = (
        jnp.zeros((micro_rows, width), jnp.bfloat16),
        jnp.zeros((row_count, width), jnp.bfloat16),
        jnp.zeros((row_count, hidden_width), jnp.bfloat16),
    )
    finished = lax.fori_loop(0, tick_count, backward_tick, start_back)
    norm_rows = finished[1]
    grad_rows = finished[2]
    dp_count = lax.axis_size("dp")
    fisher_sum = replica_squares(norm_rows, grad_rows, lengths[0])
    owned = lax.psum_scatter(fisher_sum, "dp", scatter_dimension=0, tiled=True)
    fisher = owned / (row_count * dp_count)
    return fisher[None]


def solution(mesh):
    in_specs = (
        P("dp", None),
        P("dp", None),
        P("section", "dp", None),
        P("section", "dp", None),
        P("section", None),
        P("dp", None),
    )
    out_specs = P("section", "dp", None)
    return jax.shard_map(
        per_device, mesh=mesh, in_specs=in_specs, out_specs=out_specs, check_vma=False
    )
```

profile of v0, /device:TPU:0, one launch (start us, length us, event | category | flops | bytes accessed | tf_op | source)
XLA Modules:
  0.0 676.4 jit_solution(471935585091786515)
XLA Ops:
  15.7 69.9 %all-gather.3.cloned.1.call-done = bf16[1,8192,256]{2,1,0:T(8,128)(2,1)} async-done(((bf16[1,1024,256]{2,1,0:T(8,128)(2,1)}), bf16[1,8192,256]{2,1,0:T(8,128)(2,1)}) %all-gather.3.cloned.1.call-update) | async-done | bytes 4194320 | tf_op jit(solution)/shard_map/all_gather | solution.py:66
  85.6 73.8 %all-gather.5.cloned.1.call-done = bf16[1,8192,256]{2,1,0:T(8,128)(2,1)} async-done(((bf16[1,1024,256]{2,1,0:T(8,128)(2,1)}), bf16[1,8192,256]{2,1,0:T(8,128)(2,1)}) %all-gather.5.cloned.1.call-update) | async-done | bytes 4194320 | tf_op jit(solution)/shard_map/all_gather | solution.py:67
  159.7 148.8 %while.38 = (s32[]{:T(128)}, bf16[16,8192]{1,0:T(8,128)(2,1)S(1)}, bf16[128,8192]{1,0:T(8,128)(2,1)S(1)}, s32[]{:T(128)}, pred[]{:T(512)}, /*index=5*/bf16[128,8...) while((s32[]{:T(128)}, bf16[16,8192]{1,0:T(8,128)(2,1)S(1)}, ...), condition=%wide.region_4.5_spmd, body=%wide.region_0.4_spmd.sunk | while | flops 135680016 | bytes 11305566 | solution.py:104
  159.7 7.6 %conditional.4 = (bf16[16,8192]{1,0:T(8,128)(2,1)S(1)}, bf16[128,8192]{1,0:T(8,128)(2,1)S(1)}) conditional(s32[]{:T(128)} %convert_element_type.121, bf16[128,8192]{1,0:T(8,128)(2,1)S(1)} %get-tuple-element.842, (pred[]{:T(512)}, s32[]{:T(128)}, bf16[128,8192]{1,0:T(8,128)(2,1)}, bf16[16,8192]{1,0:T(8,128)(2,1)S(1)}, f32[1,8192]{1,0:T(1,128)S(1)}, ...), branch_computations={%region_1.1_spmd, %region_2.3_spmd} | conditional | flops 135680016 | bytes 10256731 | solution.py:95
  160.9 6.4 fusion
  169.8 7.6 %conditional.4 = (bf16[16,8192]{1,0:T(8,128)(2,1)S(1)}, bf16[128,8192]{1,0:T(8,128)(2,1)S(1)}) conditional(s32[]{:T(128)} %convert_element_type.121, bf16[128,8192]{1,0:T(8,128)(2,1)S(1)} %get-tuple-element.842, (pred[]{:T(512)}, s32[]{:T(128)}, bf16[128,8192]{1,0:T(8,128)(2,1)}, bf16[16,8192]{1,0:T(8,128)(2,1)S(1)}, f32[1,8192]{1,0:T(1,128)S(1)}, ...), branch_computations={%region_1.1_spmd, %region_2.3_spmd} | conditional | flops 135680016 | bytes 10256731 | solution.py:95
  171.0 6.4 fusion
  180.8 7.6 %conditional.4 = (bf16[16,8192]{1,0:T(8,128)(2,1)S(1)}, bf16[128,8192]{1,0:T(8,128)(2,1)S(1)}) conditional(s32[]{:T(128)} %convert_element_type.121, bf16[128,8192]{1,0:T(8,128)(2,1)S(1)} %get-tuple-element.842, (pred[]{:T(512)}, s32[]{:T(128)}, bf16[128,8192]{1,0:T(8,128)(2,1)}, bf16[16,8192]{1,0:T(8,128)(2,1)S(1)}, f32[1,8192]{1,0:T(1,128)S(1)}, ...), branch_computations={%region_1.1_spmd, %region_2.3_spmd} | conditional | flops 135680016 | bytes 10256731 | solution.py:95
  182.0 6.4 fusion
  193.7 7.6 %conditional.4 = (bf16[16,8192]{1,0:T(8,128)(2,1)S(1)}, bf16[128,8192]{1,0:T(8,128)(2,1)S(1)}) conditional(s32[]{:T(128)} %convert_element_type.121, bf16[128,8192]{1,0:T(8,128)(2,1)S(1)} %get-tuple-element.842, (pred[]{:T(512)}, s32[]{:T(128)}, bf16[128,8192]{1,0:T(8,128)(2,1)}, bf16[16,8192]{1,0:T(8,128)(2,1)S(1)}, f32[1,8192]{1,0:T(1,128)S(1)}, ...), branch_computations={%region_1.1_spmd, %region_2.3_spmd} | conditional | flops 135680016 | bytes 10256731 | solution.py:95
  194.9 6.4 fusion
  201.3 6.6 collective-permute-start
  209.0 7.6 %conditional.4 = (bf16[16,8192]{1,0:T(8,128)(2,1)S(1)}, bf16[128,8192]{1,0:T(8,128)(2,1)S(1)}) conditional(s32[]{:T(128)} %convert_element_type.121, bf16[128,8192]{1,0:T(8,128)(2,1)S(1)} %get-tuple-element.842, (pred[]{:T(512)}, s32[]{:T(128)}, bf16[128,8192]{1,0:T(8,128)(2,1)}, bf16[16,8192]{1,0:T(8,128)(2,1)S(1)}, f32[1,8192]{1,0:T(1,128)S(1)}, ...), branch_computations={%region_1.1_spmd, %region_2.3_spmd} | conditional | flops 135680016 | bytes 10256731 | solution.py:95
  210.2 6.4 fusion
  216.6 6.6 collective-permute-start
  224.3 7.6 %conditional.4 = (bf16[16,8192]{1,0:T(8,128)(2,1)S(1)}, bf16[128,8192]{1,0:T(8,128)(2,1)S(1)}) conditional(s32[]{:T(128)} %convert_element_type.121, bf16[128,8192]{1,0:T(8,128)(2,1)S(1)} %get-tuple-element.842, (pred[]{:T(512)}, s32[]{:T(128)}, bf16[128,8192]{1,0:T(8,128)(2,1)}, bf16[16,8192]{1,0:T(8,128)(2,1)S(1)}, f32[1,8192]{1,0:T(1,128)S(1)}, ...), branch_computations={%region_1.1_spmd, %region_2.3_spmd} | conditional | flops 135680016 | bytes 10256731 | solution.py:95
  225.5 6.4 fusion
  231.9 6.6 collective-permute-start
  239.6 7.6 %conditional.4 = (bf16[16,8192]{1,0:T(8,128)(2,1)S(1)}, bf16[128,8192]{1,0:T(8,128)(2,1)S(1)}) conditional(s32[]{:T(128)} %convert_element_type.121, bf16[128,8192]{1,0:T(8,128)(2,1)S(1)} %get-tuple-element.842, (pred[]{:T(512)}, s32[]{:T(128)}, bf16[128,8192]{1,0:T(8,128)(2,1)}, bf16[16,8192]{1,0:T(8,128)(2,1)S(1)}, f32[1,8192]{1,0:T(1,128)S(1)}, ...), branch_computations={%region_1.1_spmd, %region_2.3_spmd} | conditional | flops 135680016 | bytes 10256731 | solution.py:95
  240.8 6.4 fusion
  247.2 6.6 collective-permute-start
  254.9 7.6 %conditional.4 = (bf16[16,8192]{1,0:T(8,128)(2,1)S(1)}, bf16[128,8192]{1,0:T(8,128)(2,1)S(1)}) conditional(s32[]{:T(128)} %convert_element_type.121, bf16[128,8192]{1,0:T(8,128)(2,1)S(1)} %get-tuple-element.842, (pred[]{:T(512)}, s32[]{:T(128)}, bf16[128,8192]{1,0:T(8,128)(2,1)}, bf16[16,8192]{1,0:T(8,128)(2,1)S(1)}, f32[1,8192]{1,0:T(1,128)S(1)}, ...), branch_computations={%region_1.1_spmd, %region_2.3_spmd} | conditional | flops 135680016 | bytes 10256731 | solution.py:95
  256.1 6.4 fusion
  262.5 6.6 collective-permute-start
  270.2 14.1 %collective-permute-start = (bf16[16,8192]{1,0:T(8,128)(2,1)S(1)}, bf16[16,8192]{1,0:T(8,128)(2,1)S(1)}, u32[]{:S(2)}, u32[]{:S(2)}) collective-permute-start(bf16[16,8192]{1,0:T(8,128)(2,1)S(1)} %get-tuple-element.802), channel_id=1, source_target_pairs={{0,8},{8,16},{16,24},{1,9},{9,17},{17,25},{2,10},{10,18},{18,26},{... | collective-permute-start | bytes 786440 | tf_op jit(solution)/shard_map/while/body/eval_jaxpr/ppermute | solution.py:15
  285.5 6.6 collective-permute-start
  293.2 14.1 %collective-permute-start = (bf16[16,8192]{1,0:T(8,128)(2,1)S(1)}, bf16[16,8192]{1,0:T(8,128)(2,1)S(1)}, u32[]{:S(2)}, u32[]{:S(2)}) collective-permute-start(bf16[16,8192]{1,0:T(8,128)(2,1)S(1)} %get-tuple-element.802), channel_id=1, source_target_pairs={{0,8},{8,16},{16,24},{1,9},{9,17},{17,25},{2,10},{10,18},{18,26},{... | collective-permute-start | bytes 786440 | tf_op jit(solution)/shard_map/while/body/eval_jaxpr/ppermute | solution.py:15
  310.1 202.2 %while.39 = (s32[]{:T(128)}, bf16[16,8192]{1,0:T(8,128)(2,1)S(1)}, bf16[128,8192]{1,0:T(8,128)(2,1)S(1)}, bf16[128,256]{1,0:T(8,128)(2,1)S(1)}, s32[]{:T(128)}, ...) while((s32[]{:T(128)}, bf16[16,8192]{1,0:T(8,128)(2,1)S(1)}, ...), condition=%wide.region_10.11_spmd, body=%wide.region_5.10_spmd.sunk | while | flops 204771360 | bytes 51276832 | solution.py:136
  311.5 6.3 collective-permute-done.1
  319.1 7.1 %collective-permute-done.1 = bf16[16,8192]{1,0:T(8,128)(2,1)S(1)} collective-permute-done((bf16[16,8192]{1,0:T(8,128)(2,1)S(1)}, bf16[16,8192]{1,0:T(8,128)(2,1)S(1)}, u32[]{:S(2)}, u32[]{:S(2)}) %collective-permute-start.1) | collective-permute-done | bytes 262176 | tf_op jit(solution)/shard_map/while/body/eval_jaxpr/ppermute | solution.py:15
  327.6 34.7 %collective-permute-done.1 = bf16[16,8192]{1,0:T(8,128)(2,1)S(1)} collective-permute-done((bf16[16,8192]{1,0:T(8,128)(2,1)S(1)}, bf16[16,8192]{1,0:T(8,128)(2,1)S(1)}, u32[]{:S(2)}, u32[]{:S(2)}) %collective-permute-start.1) | collective-permute-done | bytes 262176 | tf_op jit(solution)/shard_map/while/body/eval_jaxpr/ppermute | solution.py:15
  362.3 11.6 %conditional.5 = (bf16[16,8192]{1,0:T(8,128)(2,1)S(1)}, bf16[128,8192]{1,0:T(8,128)(2,1)S(1)}, bf16[128,256]{1,0:T(8,128)(2,1)S(1)}) conditional(s32[]{:T(128)} %convert_element_type.122, (bf16[128,8192]{1,0:T(8,128)(2,1)S(1)}, bf16[128,256]{1,0:T(8,128)(2,1)S(1)}) %tuple.119, (pred[]{:T(512)}, s32[]{:T(128)}, bf16[128,8192]{1,0:T(8,128)(2,1)}, ...), branch_computations={%region_6.6_spmd, %region_7.9_spmd} | conditional | flops 204771360 | bytes 50227948 | solution.py:126
  375.2 6.4 collective-permute-done.1
  381.6 11.6 %conditional.5 = (bf16[16,8192]{1,0:T(8,128)(2,1)S(1)}, bf16[128,8192]{1,0:T(8,128)(2,1)S(1)}, bf16[128,256]{1,0:T(8,128)(2,1)S(1)}) conditional(s32[]{:T(128)} %convert_element_type.122, (bf16[128,8192]{1,0:T(8,128)(2,1)S(1)}, bf16[128,256]{1,0:T(8,128)(2,1)S(1)}) %tuple.119, (pred[]{:T(512)}, s32[]{:T(128)}, bf16[128,8192]{1,0:T(8,128)(2,1)}, ...), branch_computations={%region_6.6_spmd, %region_7.9_spmd} | conditional | flops 204771360 | bytes 50227948 | solution.py:126
  394.5 6.4 collective-permute-done.1
  400.9 11.6 %conditional.5 = (bf16[16,8192]{1,0:T(8,128)(2,1)S(1)}, bf16[128,8192]{1,0:T(8,128)(2,1)S(1)}, bf16[128,256]{1,0:T(8,128)(2,1)S(1)}) conditional(s32[]{:T(128)} %convert_element_type.122, (bf16[128,8192]{1,0:T(8,128)(2,1)S(1)}, bf16[128,256]{1,0:T(8,128)(2,1)S(1)}) %tuple.119, (pred[]{:T(512)}, s32[]{:T(128)}, bf16[128,8192]{1,0:T(8,128)(2,1)}, ...), branch_computations={%region_6.6_spmd, %region_7.9_spmd} | conditional | flops 204771360 | bytes 50227948 | solution.py:126
  413.7 6.4 collective-permute-done.1
  420.1 11.6 %conditional.5 = (bf16[16,8192]{1,0:T(8,128)(2,1)S(1)}, bf16[128,8192]{1,0:T(8,128)(2,1)S(1)}, bf16[128,256]{1,0:T(8,128)(2,1)S(1)}) conditional(s32[]{:T(128)} %convert_element_type.122, (bf16[128,8192]{1,0:T(8,128)(2,1)S(1)}, bf16[128,256]{1,0:T(8,128)(2,1)S(1)}) %tuple.119, (pred[]{:T(512)}, s32[]{:T(128)}, bf16[128,8192]{1,0:T(8,128)(2,1)}, ...), branch_computations={%region_6.6_spmd, %region_7.9_spmd} | conditional | flops 204771360 | bytes 50227948 | solution.py:126
  433.0 6.4 collective-permute-done.1
  439.4 11.6 %conditional.5 = (bf16[16,8192]{1,0:T(8,128)(2,1)S(1)}, bf16[128,8192]{1,0:T(8,128)(2,1)S(1)}, bf16[128,256]{1,0:T(8,128)(2,1)S(1)}) conditional(s32[]{:T(128)} %convert_element_type.122, (bf16[128,8192]{1,0:T(8,128)(2,1)S(1)}, bf16[128,256]{1,0:T(8,128)(2,1)S(1)}) %tuple.119, (pred[]{:T(512)}, s32[]{:T(128)}, bf16[128,8192]{1,0:T(8,128)(2,1)}, ...), branch_computations={%region_6.6_spmd, %region_7.9_spmd} | conditional | flops 204771360 | bytes 50227948 | solution.py:126
  452.3 6.4 collective-permute-done.1
  458.7 11.6 %conditional.5 = (bf16[16,8192]{1,0:T(8,128)(2,1)S(1)}, bf16[128,8192]{1,0:T(8,128)(2,1)S(1)}, bf16[128,256]{1,0:T(8,128)(2,1)S(1)}) conditional(s32[]{:T(128)} %convert_element_type.122, (bf16[128,8192]{1,0:T(8,128)(2,1)S(1)}, bf16[128,256]{1,0:T(8,128)(2,1)S(1)}) %tuple.119, (pred[]{:T(512)}, s32[]{:T(128)}, bf16[128,8192]{1,0:T(8,128)(2,1)}, ...), branch_computations={%region_6.6_spmd, %region_7.9_spmd} | conditional | flops 204771360 | bytes 50227948 | solution.py:126
  471.6 6.4 collective-permute-done.1
  478.0 11.6 %conditional.5 = (bf16[16,8192]{1,0:T(8,128)(2,1)S(1)}, bf16[128,8192]{1,0:T(8,128)(2,1)S(1)}, bf16[128,256]{1,0:T(8,128)(2,1)S(1)}) conditional(s32[]{:T(128)} %convert_element_type.122, (bf16[128,8192]{1,0:T(8,128)(2,1)S(1)}, bf16[128,256]{1,0:T(8,128)(2,1)S(1)}) %tuple.119, (pred[]{:T(512)}, s32[]{:T(128)}, bf16[128,8192]{1,0:T(8,128)(2,1)}, ...), branch_computations={%region_6.6_spmd, %region_7.9_spmd} | conditional | flops 204771360 | bytes 50227948 | solution.py:126
  490.9 6.4 collective-permute-done.1
  497.3 11.6 %conditional.5 = (bf16[16,8192]{1,0:T(8,128)(2,1)S(1)}, bf16[128,8192]{1,0:T(8,128)(2,1)S(1)}, bf16[128,256]{1,0:T(8,128)(2,1)S(1)}) conditional(s32[]{:T(128)} %convert_element_type.122, (bf16[128,8192]{1,0:T(8,128)(2,1)S(1)}, bf16[128,256]{1,0:T(8,128)(2,1)S(1)}) %tuple.119, (pred[]{:T(512)}, s32[]{:T(128)}, bf16[128,8192]{1,0:T(8,128)(2,1)}, ...), branch_computations={%region_6.6_spmd, %region_7.9_spmd} | conditional | flops 204771360 | bytes 50227948 | solution.py:126
  516.4 4.6 fusion.33
  521.1 146.5 %reduce-scatter.2.cloned.1.call-done = f32[1024,256]{1,0:T(8,128)} async-done(((f32[8192,256]{1,0:T(8,128)}), f32[1024,256]{1,0:T(8,128)}) %reduce-scatter.2.cloned.1.call-update) | async-done | bytes 1048592 | tf_op jit(solution)/shard_map/reduce_scatter | solution.py:141
  (185 shorter events, 156.1 us)
Async XLA Ops:
  6.5 153.1 %copy-start.3 = (f32[1,8192]{1,0:T(1,128)S(1)}, f32[1,8192]{1,0:T(1,128)}, u32[]{:S(2)}) copy-start(f32[1,8192]{1,0:T(1,128)} %param.18) | copy-start | bytes 98308
  6.5 79.1 %all-gather.3.cloned.1.call-start = ((), (), s32[]{:S(2)}) async-start(), calls=%async_computation.1 | async-start | bytes 4718592 | tf_op jit(solution)/shard_map/all_gather | solution.py:66
  7.3 152.2 %all-gather.5.cloned.1.call-start = ((), (), s32[]{:S(2)}) async-start(), calls=%async_computation.2 | async-start | bytes 4718592 | tf_op jit(solution)/shard_map/all_gather | solution.py:67
  8.0 659.6 %reduce-scatter.2.cloned.1.call-start = ((), (), s32[]{:S(2)}) async-start(), calls=%async_computation.3 | async-start | bytes 9437184 | tf_op jit(solution)/shard_map/reduce_scatter | solution.py:141
  167.3 2.5 collective-permute-start
  177.4 3.4 collective-permute-start
  188.4 5.2 collective-permute-start
  201.3 7.7 %collective-permute-start = (bf16[16,8192]{1,0:T(8,128)(2,1)S(1)}, bf16[16,8192]{1,0:T(8,128)(2,1)S(1)}, u32[]{:S(2)}, u32[]{:S(2)}) collective-permute-start(bf16[16,8192]{1,0:T(8,128)(2,1)S(1)} %get-tuple-element.802), channel_id=1, source_target_pairs={{0,8},{8,16},{16,24},{1,9},{9,17},{17,25},{2,10},{10,18},{18,26},{... | collective-permute-start | bytes 786440 | tf_op jit(solution)/shard_map/while/body/eval_jaxpr/ppermute | solution.py:15
  216.6 7.7 %collective-permute-start = (bf16[16,8192]{1,0:T(8,128)(2,1)S(1)}, bf16[16,8192]{1,0:T(8,128)(2,1)S(1)}, u32[]{:S(2)}, u32[]{:S(2)}) collective-permute-start(bf16[16,8192]{1,0:T(8,128)(2,1)S(1)} %get-tuple-element.802), channel_id=1, source_target_pairs={{0,8},{8,16},{16,24},{1,9},{9,17},{17,25},{2,10},{10,18},{18,26},{... | collective-permute-start | bytes 786440 | tf_op jit(solution)/shard_map/while/body/eval_jaxpr/ppermute | solution.py:15
  231.9 7.7 %collective-permute-start = (bf16[16,8192]{1,0:T(8,128)(2,1)S(1)}, bf16[16,8192]{1,0:T(8,128)(2,1)S(1)}, u32[]{:S(2)}, u32[]{:S(2)}) collective-permute-start(bf16[16,8192]{1,0:T(8,128)(2,1)S(1)} %get-tuple-element.802), channel_id=1, source_target_pairs={{0,8},{8,16},{16,24},{1,9},{9,17},{17,25},{2,10},{10,18},{18,26},{... | collective-permute-start | bytes 786440 | tf_op jit(solution)/shard_map/while/body/eval_jaxpr/ppermute | solution.py:15
  247.2 7.7 %collective-permute-start = (bf16[16,8192]{1,0:T(8,128)(2,1)S(1)}, bf16[16,8192]{1,0:T(8,128)(2,1)S(1)}, u32[]{:S(2)}, u32[]{:S(2)}) collective-permute-start(bf16[16,8192]{1,0:T(8,128)(2,1)S(1)} %get-tuple-element.802), channel_id=1, source_target_pairs={{0,8},{8,16},{16,24},{1,9},{9,17},{17,25},{2,10},{10,18},{18,26},{... | collective-permute-start | bytes 786440 | tf_op jit(solution)/shard_map/while/body/eval_jaxpr/ppermute | solution.py:15
  262.5 7.7 %collective-permute-start = (bf16[16,8192]{1,0:T(8,128)(2,1)S(1)}, bf16[16,8192]{1,0:T(8,128)(2,1)S(1)}, u32[]{:S(2)}, u32[]{:S(2)}) collective-permute-start(bf16[16,8192]{1,0:T(8,128)(2,1)S(1)} %get-tuple-element.802), channel_id=1, source_target_pairs={{0,8},{8,16},{16,24},{1,9},{9,17},{17,25},{2,10},{10,18},{18,26},{... | collective-permute-start | bytes 786440 | tf_op jit(solution)/shard_map/while/body/eval_jaxpr/ppermute | solution.py:15
  270.2 15.3 %collective-permute-start = (bf16[16,8192]{1,0:T(8,128)(2,1)S(1)}, bf16[16,8192]{1,0:T(8,128)(2,1)S(1)}, u32[]{:S(2)}, u32[]{:S(2)}) collective-permute-start(bf16[16,8192]{1,0:T(8,128)(2,1)S(1)} %get-tuple-element.802), channel_id=1, source_target_pairs={{0,8},{8,16},{16,24},{1,9},{9,17},{17,25},{2,10},{10,18},{18,26},{... | collective-permute-start | bytes 786440 | tf_op jit(solution)/shard_map/while/body/eval_jaxpr/ppermute | solution.py:15
  285.5 7.7 %collective-permute-start = (bf16[16,8192]{1,0:T(8,128)(2,1)S(1)}, bf16[16,8192]{1,0:T(8,128)(2,1)S(1)}, u32[]{:S(2)}, u32[]{:S(2)}) collective-permute-start(bf16[16,8192]{1,0:T(8,128)(2,1)S(1)} %get-tuple-element.802), channel_id=1, source_target_pairs={{0,8},{8,16},{16,24},{1,9},{9,17},{17,25},{2,10},{10,18},{18,26},{... | collective-permute-start | bytes 786440 | tf_op jit(solution)/shard_map/while/body/eval_jaxpr/ppermute | solution.py:15
  293.2 15.3 %collective-permute-start = (bf16[16,8192]{1,0:T(8,128)(2,1)S(1)}, bf16[16,8192]{1,0:T(8,128)(2,1)S(1)}, u32[]{:S(2)}, u32[]{:S(2)}) collective-permute-start(bf16[16,8192]{1,0:T(8,128)(2,1)S(1)} %get-tuple-element.802), channel_id=1, source_target_pairs={{0,8},{8,16},{16,24},{1,9},{9,17},{17,25},{2,10},{10,18},{18,26},{... | collective-permute-start | bytes 786440 | tf_op jit(solution)/shard_map/while/body/eval_jaxpr/ppermute | solution.py:15
  308.5 1.4 copy-start.2
  310.2 7.6 %collective-permute-start.1 = (bf16[16,8192]{1,0:T(8,128)(2,1)S(1)}, bf16[16,8192]{1,0:T(8,128)(2,1)S(1)}, u32[]{:S(2)}, u32[]{:S(2)}) collective-permute-start(bf16[16,8192]{1,0:T(8,128)(2,1)S(1)} %get-tuple-element.815), channel_id=1, source_target_pairs={{8,0},{16,8},{24,16},{9,1},{17,9},{25,17},{10,2},{18,10},{26,18},{... | collective-permute-start | bytes 786440 | tf_op jit(solution)/shard_map/while/body/eval_jaxpr/ppermute | solution.py:15
  317.8 8.4 %collective-permute-start.1 = (bf16[16,8192]{1,0:T(8,128)(2,1)S(1)}, bf16[16,8192]{1,0:T(8,128)(2,1)S(1)}, u32[]{:S(2)}, u32[]{:S(2)}) collective-permute-start(bf16[16,8192]{1,0:T(8,128)(2,1)S(1)} %get-tuple-element.815), channel_id=1, source_target_pairs={{8,0},{16,8},{24,16},{9,1},{17,9},{25,17},{10,2},{18,10},{26,18},{... | collective-permute-start | bytes 786440 | tf_op jit(solution)/shard_map/while/body/eval_jaxpr/ppermute | solution.py:15
  326.3 36.0 %collective-permute-start.1 = (bf16[16,8192]{1,0:T(8,128)(2,1)S(1)}, bf16[16,8192]{1,0:T(8,128)(2,1)S(1)}, u32[]{:S(2)}, u32[]{:S(2)}) collective-permute-start(bf16[16,8192]{1,0:T(8,128)(2,1)S(1)} %get-tuple-element.815), channel_id=1, source_target_pairs={{8,0},{16,8},{24,16},{9,1},{17,9},{25,17},{10,2},{18,10},{26,18},{... | collective-permute-start | bytes 786440 | tf_op jit(solution)/shard_map/while/body/eval_jaxpr/ppermute | solution.py:15
  363.4 3.5 copy-start.1
  367.0 2.3 copy-start
  373.9 7.7 %collective-permute-start.1 = (bf16[16,8192]{1,0:T(8,128)(2,1)S(1)}, bf16[16,8192]{1,0:T(8,128)(2,1)S(1)}, u32[]{:S(2)}, u32[]{:S(2)}) collective-permute-start(bf16[16,8192]{1,0:T(8,128)(2,1)S(1)} %get-tuple-element.815), channel_id=1, source_target_pairs={{8,0},{16,8},{24,16},{9,1},{17,9},{25,17},{10,2},{18,10},{26,18},{... | collective-permute-start | bytes 786440 | tf_op jit(solution)/shard_map/while/body/eval_jaxpr/ppermute | solution.py:15
  382.7 3.5 copy-start.1
  386.2 2.3 copy-start
  393.2 7.7 %collective-permute-start.1 = (bf16[16,8192]{1,0:T(8,128)(2,1)S(1)}, bf16[16,8192]{1,0:T(8,128)(2,1)S(1)}, u32[]{:S(2)}, u32[]{:S(2)}) collective-permute-start(bf16[16,8192]{1,0:T(8,128)(2,1)S(1)} %get-tuple-element.815), channel_id=1, source_target_pairs={{8,0},{16,8},{24,16},{9,1},{17,9},{25,17},{10,2},{18,10},{26,18},{... | collective-permute-start | bytes 786440 | tf_op jit(solution)/shard_map/while/body/eval_jaxpr/ppermute | solution.py:15
  402.0 3.5 copy-start.1
  405.5 2.3 copy-start
  412.4 7.7 %collective-permute-start.1 = (bf16[16,8192]{1,0:T(8,128)(2,1)S(1)}, bf16[16,8192]{1,0:T(8,128)(2,1)S(1)}, u32[]{:S(2)}, u32[]{:S(2)}) collective-permute-start(bf16[16,8192]{1,0:T(8,128)(2,1)S(1)} %get-tuple-element.815), channel_id=1, source_target_pairs={{8,0},{16,8},{24,16},{9,1},{17,9},{25,17},{10,2},{18,10},{26,18},{... | collective-permute-start | bytes 786440 | tf_op jit(solution)/shard_map/while/body/eval_jaxpr/ppermute | solution.py:15
  421.3 3.5 copy-start.1
  424.8 2.3 copy-start
  431.7 7.7 %collective-permute-start.1 = (bf16[16,8192]{1,0:T(8,128)(2,1)S(1)}, bf16[16,8192]{1,0:T(8,128)(2,1)S(1)}, u32[]{:S(2)}, u32[]{:S(2)}) collective-permute-start(bf16[16,8192]{1,0:T(8,128)(2,1)S(1)} %get-tuple-element.815), channel_id=1, source_target_pairs={{8,0},{16,8},{24,16},{9,1},{17,9},{25,17},{10,2},{18,10},{26,18},{... | collective-permute-start | bytes 786440 | tf_op jit(solution)/shard_map/while/body/eval_jaxpr/ppermute | solution.py:15
  440.6 3.5 copy-start.1
  444.1 2.3 copy-start
  451.0 7.7 %collective-permute-start.1 = (bf16[16,8192]{1,0:T(8,128)(2,1)S(1)}, bf16[16,8192]{1,0:T(8,128)(2,1)S(1)}, u32[]{:S(2)}, u32[]{:S(2)}) collective-permute-start(bf16[16,8192]{1,0:T(8,128)(2,1)S(1)} %get-tuple-element.815), channel_id=1, source_target_pairs={{8,0},{16,8},{24,16},{9,1},{17,9},{25,17},{10,2},{18,10},{26,18},{... | collective-permute-start | bytes 786440 | tf_op jit(solution)/shard_map/while/body/eval_jaxpr/ppermute | solution.py:15
  459.8 3.5 copy-start.1
  463.4 2.3 copy-start
  470.3 7.7 %collective-permute-start.1 = (bf16[16,8192]{1,0:T(8,128)(2,1)S(1)}, bf16[16,8192]{1,0:T(8,128)(2,1)S(1)}, u32[]{:S(2)}, u32[]{:S(2)}) collective-permute-start(bf16[16,8192]{1,0:T(8,128)(2,1)S(1)} %get-tuple-element.815), channel_id=1, source_target_pairs={{8,0},{16,8},{24,16},{9,1},{17,9},{25,17},{10,2},{18,10},{26,18},{... | collective-permute-start | bytes 786440 | tf_op jit(solution)/shard_map/while/body/eval_jaxpr/ppermute | solution.py:15
  479.1 3.5 copy-start.1
  482.6 2.3 copy-start
  489.6 7.7 %collective-permute-start.1 = (bf16[16,8192]{1,0:T(8,128)(2,1)S(1)}, bf16[16,8192]{1,0:T(8,128)(2,1)S(1)}, u32[]{:S(2)}, u32[]{:S(2)}) collective-permute-start(bf16[16,8192]{1,0:T(8,128)(2,1)S(1)} %get-tuple-element.815), channel_id=1, source_target_pairs={{8,0},{16,8},{24,16},{9,1},{17,9},{25,17},{10,2},{18,10},{26,18},{... | collective-permute-start | bytes 786440 | tf_op jit(solution)/shard_map/while/body/eval_jaxpr/ppermute | solution.py:15
  498.4 3.5 copy-start.1
  501.9 2.3 copy-start
  508.8 3.4 collective-permute-start.1
Sparse Core Ops, SparseCore 0:
  9.5 76.0 all-gather.2
  87.7 71.6 all-gather.4
  521.2 146.3 reduce-scatter.1
where the time goes:
time: 678 us; the launch traced here: 676 us
  waiting for transfers between devices  399 us (59%)
  matrix products  117 us (17%)
  starting transfers between devices  89.7 us (13%)
  other arithmetic  46.2 us (7%)
  between operations  13.2 us (2%)
  local copies, waits for them, and re-layouts  10.6 us (2%)
    reduce_scatter x1, waiting for transfers between devices, per_device(): owned = lax.psum_scatter(fisher_sum, 'dp', scatter_dimension=0, tiled=True)  147 us
    ppermute x22, waiting for transfers between devices, from_behind(): return lax.ppermute(array, axis, pairs)  107 us
    ppermute x22, starting transfers between devices, from_behind(): return lax.ppermute(array, axis, pairs)  89.6 us
    all_gather x1, waiting for transfers between devices, per_device(): lax.all_gather(up_weight, 'dp', axis=1, tiled=True)  73.8 us
    all_gather x1, waiting for transfers between devices, per_device(): lax.all_gather(down_weight, 'dp', axis=1, tiled=True)  69.9 us
    dot_general x8, matrix products, layer_forward(): lax.dot_general(activated, w_up, (((1,), (1,)), ((), ())), preferred_elem...  51.1 us
    dot_general x8, matrix products, layer_backward(): pre_act = jnp.dot(normed, w_down, preferred_element_type=jnp.float32)  24.9 us
    dot_general x8, matrix products, layer_backward(): lax.dot_general(pre_grad, w_down, (((1,), (1,)), ((), ())), preferred_ele...  18.1 us
  transfers between devices with their start and end apart: 25, of which 25 were waited for; matrix products, arithmetic and copies ran while one was open for 1% of the time, Pallas kernels for 0%

commit v1 on v0

v1 whole, which is shorter than its diff:
```python
import functools

import jax
import jax.numpy as jnp
from jax import lax
from jax.experimental import pallas as pl
from jax.experimental.pallas import tpu as pltpu
from jax.sharding import PartitionSpec as P

epsilon = 1e-05
bf16 = jnp.bfloat16
f32 = jnp.float32
VMEM_BYTES = 56 * 1024 * 1024


def dot(a, b, ca, cb):
    return lax.dot_general(a, b, (((ca,), (cb,)), ((), ())), preferred_element_type=f32)


def core_swap(x):
    count = lax.axis_size("section")
    return lax.ppermute(x, "section", [(i, i ^ 1) for i in range(count)])


def chip_shift(x, by):
    count = lax.axis_size("section")
    return lax.ppermute(x, "section", [(i, (i - 2 * by) % count) for i in range(count)])


def section_order():
    count = lax.axis_size("section")
    me = lax.axis_index("section")
    same = [(me + 2 * j) % count for j in range(count // 2)]
    other = [((me ^ 1) + 2 * j) % count for j in range(count // 2)]
    return jnp.stack(same + other).astype(jnp.int32)


def gather_section(x):
    count = lax.axis_size("section")
    same = [x] + [chip_shift(x, j) for j in range(1, count // 2)]
    return same + [core_swap(b) for b in same]


def spread(x):
    peers = lax.axis_size("dp")
    return lax.all_to_all(jnp.broadcast_to(x[None], (peers,) + x.shape), "dp", 0, 0, tiled=True)


def gram_pairs(count):
    mixed = [(k, l) for l in range(count) for k in range(l)]
    ups = [(k, count + j) for j in range(count - 1) for k in range(j + 1)]
    return mixed + ups


def project_kernel(count, order, left, right, rows_ref, *refs):
    weights = refs[:count]
    part_ref, gram_ref, table = refs[count:]
    peers, _, t, width = rows_ref.shape
    r = table.shape[2]
    for i in range(count):
        table[order[i]] = weights[i][:, :r]
        table[count + order[i]] = weights[i][:, r:]
    x = rows_ref[:, 0].reshape(peers * t, width)
    c = rows_ref[:, 1].reshape(peers * t, width)
    for m in range(3 * count - 1):
        if m < 2 * count - 1:
            out = dot(x, table[m], 1, 0)
        else:
            out = dot(c, table[m - count + 1], 1, 0)
        part_ref[:, m] = out.astype(bf16).reshape(peers, t, r)
    for p in range(count - 1):
        gram_ref[p] = dot(table[count + left[p]], table[right[p]], 0, 0).astype(bf16)


def recur_kernel(count, width, order, sums_ref, sq_ref, *refs):
    grams = refs[:count]
    out_ref, table = refs[count:]
    per = count - 1
    for i in range(count):
        for p in range(per):
            table[order[i] * per + p] = grams[i][p]
    place = {pair: n for n, pair in enumerate(gram_pairs(count))}

    def mixed(k, l):
        return table[place[(k, l)]]

    def ups(k, j, a):
        if k <= j:
            return dot(a, table[place[(k, count + j)]], 1, 0)
        return dot(a, table[place[(j, count + k)]], 1, 1)

    total = jnp.sum(sums_ref[...].astype(f32), axis=0)
    proj = [total[l] for l in range(count)]
    hu = [total[count + k] for k in range(count - 1)]
    back = [total[2 * count - 1 + l] for l in range(count)]
    norm = sq_ref[...]
    invs, pres, hus = [], [], []
    for l in range(count):
        inv = lax.rsqrt(norm / width + epsilon)
        pre = inv * proj[l]
        invs.append(inv)
        pres.append(pre)
        hus.append(list(hu))
        if l < count - 1:
            act = (pre * jax.nn.sigmoid(pre)).astype(bf16)
            out_ref[count + l] = act
            wide = act.astype(f32)
            for j in range(l + 1, count):
                proj[j] = proj[j] + dot(act, mixed(l, j), 1, 0)
            step = [ups(l, j, act) for j in range(count - 1)]
            norm = norm + jnp.sum(wide * (2.0 * hu[l] + step[l]), axis=-1, keepdims=True)
            hu = [hu[j] + step[j] for j in range(count - 1)]
    for l in reversed(range(count)):
        s = jax.nn.sigmoid(pres[l])
        grad = (back[l] * s * (1.0 + pres[l] * (1.0 - s))).astype(bf16)
        wide = grad.astype(f32)
        out_ref[l] = (wide * invs[l]).astype(bf16)
        inner = jnp.sum(wide * proj[l], axis=-1, keepdims=True) / width
        for j in range(l):
            back[j] = back[j] + invs[l] * (
                dot(grad, mixed(j, l), 1, 1) - invs[l] * invs[l] * inner * hus[l][j]
            )


def fisher_kernel(count, seqs, scale, order, me, *refs):
    rows = refs[:count]
    weights = refs[count : 2 * count]
    same_ref, other_ref, seg_ref, gain_ref, out_ref, acc = refs[2 * count :]
    n = pl.program_id(0)
    half = count // 2
    t = rows[0].shape[1]
    r = out_ref.shape[1]
    width = out_ref.shape[0]

    def column(m):
        parts = [same_ref[0, j, m] for j in range(half)] + [other_ref[0, j, m] for j in range(half)]
        return jnp.concatenate(parts, axis=0)

    h = jnp.concatenate([rows[i][0] for i in range(count)], axis=0).astype(f32)
    for i in range(count):
        act = column(2 + jnp.minimum(order[i], count - 2))
        act = jnp.where(order[i] < me[0], act, jnp.zeros_like(act))
        h = h + dot(act, weights[i][:, r:], 1, 1)
    h = h.astype(bf16)
    grad = column(lax.rem(me[0], 2)).astype(f32).T
    seg = seg_ref[0]
    total = jnp.zeros((r, width), f32)
    for q in range(seqs):
        masked = jnp.where(seg == q, grad, 0.0).astype(bf16)
        g = dot(masked, h, 1, 0)
        total = total + g * g

    @pl.when(n == 0)
    def _():
        acc[...] = total

    @pl.when(n > 0)
    def _():
        acc[...] = acc[...] + total

    @pl.when(n == pl.num_programs(0) - 1)
    def _():
        gain = gain_ref[...]
        out_ref[...] = (acc[...] * (gain * gain * scale)).T


def per_device(tokens, cotangent, down_weight, up_weight, norm_gain, lengths):
    count = lax.axis_size("section")
    peers = lax.axis_size("dp")
    me = lax.axis_index("section")
    spot = lax.axis_index("dp")
    row_count, width = tokens.shape
    block = width // peers
    t = row_count // count
    r = down_weight.shape[2]
    order = section_order()
    params = pltpu.CompilerParams(vmem_limit_bytes=VMEM_BYTES)
    smem = pl.BlockSpec(memory_space=pltpu.SMEM)
    vmem = pl.BlockSpec(memory_space=pltpu.VMEM)

    gain = lax.dynamic_slice_in_dim(norm_gain[0], spot * block, block, 0)
    gained = (down_weight[0].astype(f32) * gain[:, None]).astype(bf16)
    weights = gather_section(jnp.concatenate([gained, up_weight[0]], axis=1))

    mine = lax.dynamic_slice_in_dim(tokens, me * t, t, 0)
    mine_cot = lax.dynamic_slice_in_dim(cotangent, me * t, t, 0)
    wide = mine.astype(f32)
    square = jnp.sum(wide * wide, axis=-1, keepdims=True)
    both = jnp.stack([mine.reshape(t, peers, block), mine_cot.reshape(t, peers, block)])
    rows = lax.all_to_all(both.transpose(2, 0, 1, 3), "dp", 0, 0, tiled=True)

    pairs = gram_pairs(count)
    left = lax.dynamic_slice_in_dim(jnp.array([a for a, _ in pairs], jnp.int32), me * (count - 1), count - 1)
    right = lax.dynamic_slice_in_dim(jnp.array([b for _, b in pairs], jnp.int32), me * (count - 1), count - 1)
    part, gram = pl.pallas_call(
        functools.partial(project_kernel, count),
        out_shape=(
            jax.ShapeDtypeStruct((peers, 3 * count - 1, t, r), bf16),
            jax.ShapeDtypeStruct((count - 1, r, r), bf16),
        ),
        in_specs=[smem] * 3 + [vmem] * (1 + count),
        out_specs=(vmem, vmem),
        scratch_shapes=[pltpu.VMEM((2 * count, block, r), bf16)],
        compiler_params=params,
        name="project",
    )(order, left, right, rows, *weights)

    line = jnp.zeros((peers, 16, r), bf16).at[:, 0, : lengths.shape[1]].set(lengths.astype(bf16))
    gram_rows = (count - 1) * r // peers
    packed = jnp.concatenate([gram.reshape(peers, gram_rows, r), line], axis=1)
    packed = lax.all_to_all(packed, "dp", 0, 0, tiled=True)
    gram_sum = jnp.sum(packed[:, :gram_rows].astype(f32), axis=0).astype(bf16)
    all_lengths = packed[:, gram_rows, : lengths.shape[1]].astype(jnp.int32)
    sums = lax.all_to_all(part, "dp", 0, 0, tiled=True)
    grams = gather_section(spread(gram_sum).reshape(count - 1, r, r))

    states = pl.pallas_call(
        functools.partial(recur_kernel, count, width),
        out_shape=jax.ShapeDtypeStruct((2 * count - 1, t, r), bf16),
        in_specs=[smem] + [vmem] * (2 + count),
        out_specs=vmem,
        scratch_shapes=[pltpu.VMEM((count * (count - 1), r, r), bf16)],
        compiler_params=params,
        name="recur",
    )(order, sums, square, *grams)

    def wanted_by(other):
        first = lax.dynamic_slice_in_dim(states, other - lax.rem(other, 2), 2, 0)
        return jnp.concatenate([first, states[count:]], axis=0)

    held = [wanted_by(me)]
    for j in range(1, count // 2):
        held.append(chip_shift(wanted_by(lax.rem(me + count - 2 * j, count)), j))
    same = spread(jnp.stack(held))
    other = core_swap(same)
    all_rows = gather_section(rows[:, 0])

    ends = jnp.cumsum(all_lengths, axis=1)
    position = (order[:, None] * t + jnp.arange(t, dtype=jnp.int32)[None]).reshape(-1)
    seg = jnp.sum(position[None, None, :] >= ends[:, :, None], axis=1).astype(jnp.int32)
    seg = seg.reshape(peers, 1, row_count)

    def whole(shape):
        return pl.BlockSpec(shape, lambda n: (0,) * len(shape))

    def step(shape):
        return pl.BlockSpec(shape, lambda n: (n,) + (0,) * (len(shape) - 1))

    fisher = pl.pallas_call(
        functools.partial(fisher_kernel, count, lengths.shape[1], 1.0 / (row_count * peers)),
        grid=(peers,),
        out_shape=jax.ShapeDtypeStruct((block, r), f32),
        in_specs=[smem, smem]
        + [step((1, t, block))] * count
        + [whole((block, 2 * r))] * count
        + [step((1,) + same.shape[1:])] * 2
        + [step((1, 1, row_count)), whole((1, block))],
        out_specs=whole((block, r)),
        scratch_shapes=[pltpu.VMEM((r, block), f32)],
        compiler_params=params,
        name="squares",
    )(order, me.astype(jnp.int32)[None], *all_rows, *weights, same, other, seg, gain[None])
    return fisher[None]


def solution(mesh):
    in_specs = (
        P("dp", None),
        P("dp", None),
        P("section", "dp", None),
        P("section", "dp", None),
        P("section", None),
        P("dp", None),
    )
    out_specs = P("section", "dp", None)
    return jax.shard_map(
        per_device, mesh=mesh, in_specs=in_specs, out_specs=out_specs, check_vma=False
    )
```

time: 678 us -> 200 us (0.29)
  waiting for transfers between devices: 399 us -> 74.3 us
  matrix products: 117 us -> 0 us
  starting transfers between devices: 89.7 us -> 14.2 us
  blocking collectives: 0 us -> 65.6 us
  other arithmetic: 46.2 us -> 6.23 us
  Pallas kernels: 0 us -> 26.6 us
  between operations: 13.2 us -> 0.16 us
    reduce_scatter x1 -> x0, waiting for transfers between devices: 147 us -> none  [per_device(): owned = lax.psum_scatter(fisher_sum, 'dp', scatter_dimension=0, tiled=True)]
    all_gather x2 -> x0, waiting for transfers between devices: 144 us -> none  [the longest x1 73.8 us: per_device(): lax.all_gather(up_weight, 'dp', axis=1, tiled=True)]
    dot_general x36 -> x0, matrix products: 117 us -> none  [the longest x8 51.1 us: layer_forward(): lax.dot_general(activated, w_up, (((1,), (1,)), ((), ())), preferred_elem...]
    ppermute x22 -> x11, starting transfers between devices: 89.6 us -> 4.77 us  [the longest x4 4.68 us: chip_shift(): lax.ppermute(x, 'section', [(i, (i - 2 * by) % count) for i in range(coun...]
    all_to_all x0 -> x3, blocking collectives: none -> 65.6 us  [the longest x2 49 us: spread(): lax.all_to_all(jnp.broadcast_to(x[None], (peers,) + x.shape), 'dp', 0, 0,...]
    ppermute x22 -> x11, waiting for transfers between devices: 107 us -> 42.9 us  [the longest x4 41 us: chip_shift(): lax.ppermute(x, 'section', [(i, (i - 2 * by) % count) for i in range(coun...]
    all_to_all x0 -> x2, waiting for transfers between devices: none -> 31.4 us  [the longest x1 21.4 us: per_device(): sums = lax.all_to_all(part, 'dp', 0, 0, tiled=True)]
    pallas_call x0 -> x3, Pallas kernels: none -> 26.6 us  [the longest x1 16.6 us: per_device(): pl.pallas_call(functools.partial(fisher_kernel, count, lengths.shape[1],...]
  transfers between devices with their start and end apart: 25 -> 13, of which waited for: 25 -> 8; matrix products, arithmetic and copies ran while one was open for 1% -> 5% of each run, Pallas kernels for 0% -> 0%
where the time goes in v1:
time: 200 us; the launch traced here: 199 us
  waiting for transfers between devices  74.3 us (37%)
  blocking collectives  65.6 us (33%)
  Pallas kernels  26.6 us (13%)
  starting transfers between devices  14.2 us (7%)
  local copies, waits for them, and re-layouts  11.8 us (6%)
  other arithmetic  6.23 us (3%)
    all_to_all x2, blocking collectives, spread(): lax.all_to_all(jnp.broadcast_to(x[None], (peers,) + x.shape), 'dp', 0, 0,...  49 us
    ppermute x4, waiting for transfers between devices, chip_shift(): lax.ppermute(x, 'section', [(i, (i - 2 * by) % count) for i in range(coun...  41 us
    all_to_all x1, waiting for transfers between devices, per_device(): sums = lax.all_to_all(part, 'dp', 0, 0, tiled=True)  21.4 us
    all_to_all x1, blocking collectives, per_device(): packed = lax.all_to_all(packed, 'dp', 0, 0, tiled=True)  16.6 us
    pallas_call x1, Pallas kernels, per_device(): pl.pallas_call(functools.partial(fisher_kernel, count, lengths.shape[1],...  16.6 us
    all_to_all x1, waiting for transfers between devices, per_device(): rows = lax.all_to_all(both.transpose(2, 0, 1, 3), 'dp', 0, 0, tiled=True)  10 us
    all_to_all x1, starting transfers between devices, per_device(): rows = lax.all_to_all(both.transpose(2, 0, 1, 3), 'dp', 0, 0, tiled=True)  5.81 us
    pallas_call x1, Pallas kernels, per_device(): pl.pallas_call(functools.partial(project_kernel, count), out_shape=(jax.S...  5.79 us
  transfers between devices with their start and end apart: 13, of which 8 were waited for; matrix products, arithmetic and copies ran while one was open for 5% of the time, Pallas kernels for 0%

profile of v1, /device:TPU:0, one launch (start us, length us, event | category | flops | bytes accessed | tf_op | source)
XLA Modules:
  0.0 198.9 jit_solution(5691197149703721140)
XLA Ops:
  0.0 0.8 constant_dynamic-slice_fusion.2.refs_11_
  0.8 1.2 fusion
  2.1 1.1 pad_maximum_fusion.refs_0_.refs_4_
  3.2 3.0 %collective-permute-start.3 = (bf16[1024,512]{1,0:T(8,128)(2,1)S(1)}, bf16[1024,512]{1,0:T(8,128)(2,1)}, u32[]{:S(2)}, u32[]{:S(2)}) collective-permute-start(bf16[1024,512]{1,0:T(8,128)(2,1)S(1)} %pad_maximum_fusion.refs_0_.refs_4_), channel_id=1, source_target_pairs={{0,16},{8,24},{16,0},{24,8},{1,17},{9,25},{17,1},{25,9},{2,18},{10... | collective-permute-start | bytes 3145736 | tf_op jit(solution)/shard_map/ppermute | solution.py:27
  6.3 0.3 copy.35
  6.6 1.3 multiply_reduce_fusion
  7.9 0.3 copy.34
  8.2 0.1 maximum_bitcast_fusion
  8.3 0.0 copy-start.8
  8.3 0.0 copy-start.7
  8.3 1.5 copy.28
  9.9 5.8 %all-to-all-start = ((bf16[8,2,32,1024]{3,2,1,0:T(8,128)(2,1)}), bf16[8,2,32,1024]{3,2,1,0:T(8,128)(2,1)}, u32[]{:S(2)}, u32[]{:S(2)}) async-start(bf16[8,2,32,1024]{3,2,1,0:T(8,128)(2,1)} %copy.28), calls=%async_computation | async-start | bytes 2097152 | tf_op jit(solution)/shard_map/all_to_all | solution.py:190
  15.7 0.1 collective-permute-start.4
  15.8 13.8 %collective-permute-done.3.refs_1_.refs_5_ = bf16[1024,512]{1,0:T(8,128)(2,1)} collective-permute-done((bf16[1024,512]{1,0:T(8,128)(2,1)S(1)}, bf16[1024,512]{1,0:T(8,128)(2,1)}, u32[]{:S(2)}, u32[]{:S(2)}) %collective-permute-start.3) | collective-permute-done | bytes 1048608 | tf_op jit(solution)/shard_map/ppermute | solution.py:27
  29.5 0.6 dynamic_slice.24.left
  30.1 0.7 dynamic_slice.25.right
  30.8 0.6 broadcast_multiply_fusion
  31.4 10.0 %all-to-all-done.rows_ref = bf16[8,2,32,1024]{3,2,1,0:T(8,128)(2,1)} async-done(((bf16[8,2,32,1024]{3,2,1,0:T(8,128)(2,1)}), bf16[8,2,32,1024]{3,2,1,0:T(8,128)(2,1)}, u32[]{:S(2)}, u32[]{:S(2)}) %all-to-all-start) | async-done | bytes 1048608 | tf_op jit(solution)/shard_map/all_to_all | solution.py:190
  41.4 5.8 %project.1 = (bf16[8,11,32,256]{3,2,1,0:T(8,128)(2,1)}, bf16[3,256,256]{2,1,0:T(8,128)(2,1)}) custom-call(s32[4]{0:T(128)} %get-tuple-element.22.order, s32[3]{0:T(128)} %dynamic_slice.24.left, s32[3]{0:T(128)} %dynamic_slice.25.right, bf16[8,2,32,1024]{3,2,1,0:T(8,128)(2,1)} %all-to-all-done.rows_ref, bf16[1024,512]{1,0:T(8,128)(2,1)} %copy-done.1, ...), custom_call_target="tpu_custom_call" | custom-call | tf_op jit(solution)/shard_map/project/pallas_call | solution.py:195
  47.2 1.0 pad_maximum_fusion.1
  48.2 16.6 %all_to_all.25 = bf16[8,112,256]{2,1,0:T(8,128)(2,1)S(1)} all-to-all(bf16[8,112,256]{2,1,0:T(8,128)(2,1)S(1)} %pad_maximum_fusion.1), channel_id=1, replica_groups=mesh['section'=4,'dp'=8] {'dp'}, dimensions={0} | all-to-all | bytes 917504 | tf_op jit(solution)/shard_map/all_to_all | solution.py:211
  64.9 0.8 copy-done.4
  65.6 0.1 slice_reduce_fusion
  65.7 15.3 %all_to_all.26 = bf16[8,96,256]{2,1,0:T(8,128)(2,1)} all-to-all(bf16[8,96,256]{2,1,0:T(8,128)(2,1)S(1)} %broadcast_in_dim.12), channel_id=1, replica_groups=mesh['section'=4,'dp'=8] {'dp'}, dimensions={0} | all-to-all | bytes 786432 | tf_op jit(solution)/shard_map/all_to_all | solution.py:46
  81.0 3.6 %all-to-all-start.1 = ((bf16[8,11,32,256]{3,2,1,0:T(8,128)(2,1)}), bf16[8,11,32,256]{3,2,1,0:T(8,128)(2,1)S(1)}, u32[]{:S(2)}, u32[]{:S(2)}) async-start(bf16[8,11,32,256]{3,2,1,0:T(8,128)(2,1)} %get-tuple-element.19), calls=%async_computation.1 | async-start | bytes 2883584 | tf_op jit(solution)/shard_map/all_to_all | solution.py:214
  84.6 0.6 collective-permute-start.6
  85.1 9.5 %collective-permute-done.6.refs_1_ = bf16[3,256,256]{2,1,0:T(8,128)(2,1)} collective-permute-done((bf16[3,256,256]{2,1,0:T(8,128)(2,1)}, bf16[3,256,256]{2,1,0:T(8,128)(2,1)}, u32[]{:S(2)}, u32[]{:S(2)}) %collective-permute-start.6) | collective-permute-done | bytes 393248 | tf_op jit(solution)/shard_map/ppermute | solution.py:27
  94.7 0.7 copy.30.sq_ref
  95.4 1.4 collective-permute-done.8.refs_3_
  96.8 21.4 %all-to-all-done.1.sums_ref = bf16[8,11,32,256]{3,2,1,0:T(8,128)(2,1)S(1)} async-done(((bf16[8,11,32,256]{3,2,1,0:T(8,128)(2,1)}), bf16[8,11,32,256]{3,2,1,0:T(8,128)(2,1)S(1)}, u32[]{:S(2)}, u32[]{:S(2)}) %all-to-all-start.1) | async-done | bytes 1441824 | tf_op jit(solution)/shard_map/all_to_all | solution.py:214
  118.1 1.1 copy-done.2
  119.2 4.2 %recur.1 = bf16[7,32,256]{2,1,0:T(8,128)(2,1)} custom-call(s32[4]{0:T(128)} %get-tuple-element.22.order, bf16[8,11,32,256]{3,2,1,0:T(8,128)(2,1)} %copy-done.2, f32[32,1]{1,0:T(8,128)} %copy.30.sq_ref, bf16[3,256,256]{2,1,0:T(8,128)(2,1)} %bitcast.39, bf16[3,256,256]{2,1,0:T(8,128)(2,1)} %collective-permute-done.6.refs_1_, ...), custom_call_target="tpu_custom_call" | custom-call | tf_op jit(solution)/shard_map/recur/pallas_call | solution.py:217
  123.4 0.8 slice.42
  124.2 0.8 constant_dynamic-slice_fusion.1
  125.0 0.6 collective-permute-start.9
  125.6 3.9 %collective-permute-done.9 = bf16[5,32,256]{2,1,0:T(8,128)(2,1)S(1)} collective-permute-done((bf16[5,32,256]{2,1,0:T(8,128)(2,1)S(1)}, bf16[5,32,256]{2,1,0:T(8,128)(2,1)S(1)}, u32[]{:S(2)}, u32[]{:S(2)}) %collective-permute-start.9) | collective-permute-done | bytes 81952 | tf_op jit(solution)/shard_map/ppermute | solution.py:27
  129.5 0.1 broadcast_in_dim.13
  129.7 33.7 %all_to_all.27.refs_8_ = bf16[8,2,5,32,256]{4,3,2,1,0:T(8,128)(2,1)S(1)} all-to-all(bf16[8,2,5,32,256]{4,3,2,1,0:T(8,128)(2,1)S(1)} %broadcast_in_dim.13), channel_id=1, replica_groups=mesh['section'=4,'dp'=8] {'dp'}, dimensions={0} | all-to-all | bytes 2621440 | tf_op jit(solution)/shard_map/all_to_all | solution.py:46
  163.4 2.3 %slice_bitcast_fusion.refs_0_ = bf16[8,32,1024]{2,1,0:T(8,128)(2,1)} fusion(bf16[8,2,32,1024]{3,2,1,0:T(8,128)(2,1)} %all-to-all-done.rows_ref), kind=kLoop, calls=%fused_computation.5 | loop fusion | bytes 1048576 | tf_op jit(solution)/shard_map/squeeze | solution.py:236
  165.7 0.5 collective-permute-start
  166.2 13.8 %collective-permute-done.refs_1_ = bf16[8,32,1024]{2,1,0:T(8,128)(2,1)} collective-permute-done((bf16[8,32,1024]{2,1,0:T(8,128)(2,1)}, bf16[8,32,1024]{2,1,0:T(8,128)(2,1)}, u32[]{:S(2)}, u32[]{:S(2)}) %collective-permute-start) | collective-permute-done | bytes 524320 | tf_op jit(solution)/shard_map/ppermute | solution.py:27
  180.0 0.1 iota_add_fusion
  180.1 0.1 add.78
  180.1 0.7 slice.43
  180.9 0.1 copy.33
  181.0 0.7 convert_reduce_fusion
  181.7 0.5 collective-permute-done.2.refs_3_
  182.2 16.6 %squares.1 = f32[1024,256]{1,0:T(8,128)} custom-call(s32[4]{0:T(128)} %get-tuple-element.22.order, s32[1]{0:T(128)} %bitcast.4.me, bf16[8,32,1024]{2,1,0:T(8,128)(2,1)} %slice_bitcast_fusion.refs_0_, bf16[8,32,1024]{2,1,0:T(8,128)(2,1)} %collective-permute-done.refs_1_, bf16[8,32,1024]{2,1,0:T(8,128)(2,1)} %collective-permute-done.1.refs_2_, ...), custom_call_target="tpu_custom_call" | custom-call | tf_op jit(solution)/shard_map/squares/pallas_call | solution.py:249
  (34 shorter events, 0.2 us)
Async XLA Ops:
  0.0 6.3 %copy-start = (bf16[128,8192]{1,0:T(8,128)(2,1)S(1)}, bf16[128,8192]{1,0:T(8,128)(2,1)}, u32[]{:S(2)}) copy-start(bf16[128,8192]{1,0:T(8,128)(2,1)} %param.11) | copy-start | bytes 6291460
  0.8 5.5 %copy-start.5 = (f32[1,1024]{1,0:T(1,128)}, f32[1,1024]{1,0:T(1,128)S(1)}, u32[]{:S(2)}) copy-start(f32[1,1024]{1,0:T(1,128)S(1)} %constant_dynamic-slice_fusion.2.refs_11_) | copy-start | bytes 12292
  3.2 12.5 %copy-start.1 = (bf16[1024,512]{1,0:T(8,128)(2,1)}, bf16[1024,512]{1,0:T(8,128)(2,1)S(1)}, u32[]{:S(2)}) copy-start(bf16[1024,512]{1,0:T(8,128)(2,1)S(1)} %pad_maximum_fusion.refs_0_.refs_4_) | copy-start | bytes 3145732
  3.2 26.3 %collective-permute-start.3 = (bf16[1024,512]{1,0:T(8,128)(2,1)S(1)}, bf16[1024,512]{1,0:T(8,128)(2,1)}, u32[]{:S(2)}, u32[]{:S(2)}) collective-permute-start(bf16[1024,512]{1,0:T(8,128)(2,1)S(1)} %pad_maximum_fusion.refs_0_.refs_4_), channel_id=1, source_target_pairs={{0,16},{8,24},{16,0},{24,8},{1,17},{9,25},{17,1},{25,9},{2,18},{10... | collective-permute-start | bytes 3145736 | tf_op jit(solution)/shard_map/ppermute | solution.py:27
  8.3 21.2 %copy-start.8 = (s32[12]{0:T(128)S(1)}, s32[12]{0:T(128)}, u32[]{:S(2)}) copy-start(s32[12]{0:T(128)} %constant.101.clone) | copy-start | bytes 148
  8.3 21.8 %copy-start.7 = (s32[12]{0:T(128)S(1)}, s32[12]{0:T(128)}, u32[]{:S(2)}) copy-start(s32[12]{0:T(128)} %constant.102.clone) | copy-start | bytes 148
  8.3 22.5 %copy-start.6 = (s32[1,4]{1,0:T(1,128)S(1)}, s32[1,4]{1,0:T(1,128)}, u32[]{:S(2)}) copy-start(s32[1,4]{1,0:T(1,128)} %param.15) | copy-start | bytes 52
  9.9 31.5 %all-to-all-start = ((bf16[8,2,32,1024]{3,2,1,0:T(8,128)(2,1)}), bf16[8,2,32,1024]{3,2,1,0:T(8,128)(2,1)}, u32[]{:S(2)}, u32[]{:S(2)}) async-start(bf16[8,2,32,1024]{3,2,1,0:T(8,128)(2,1)} %copy.28), calls=%async_computation | async-start | bytes 2097152 | tf_op jit(solution)/shard_map/all_to_all | solution.py:190
  15.7 15.7 %collective-permute-start.4 = (bf16[1024,512]{1,0:T(8,128)(2,1)S(1)}, bf16[1024,512]{1,0:T(8,128)(2,1)}, u32[]{:S(2)}, u32[]{:S(2)}) collective-permute-start(bf16[1024,512]{1,0:T(8,128)(2,1)S(1)} %pad_maximum_fusion.refs_0_.refs_4_), channel_id=1, source_target_pairs={{0,8},{8,0},{16,24},{24,16},{1,9},{9,1},{17,25},{25,17},{2,10},{10... | collective-permute-start | bytes 3145736 | tf_op jit(solution)/shard_map/ppermute | solution.py:22
  29.5 11.9 %collective-permute-start.5 = (bf16[1024,512]{1,0:T(8,128)(2,1)}, bf16[1024,512]{1,0:T(8,128)(2,1)}, u32[]{:S(2)}, u32[]{:S(2)}) collective-permute-start(bf16[1024,512]{1,0:T(8,128)(2,1)} %collective-permute-done.3.refs_1_.refs_5_), channel_id=1, source_target_pairs={{0,8},{8,0},{16,24},{24,16},{1,9},{9,1},{17,25},{25,17},{2,10},{10... | collective-permute-start | bytes 3145736 | tf_op jit(solution)/shard_map/ppermute | solution.py:22
  64.9 0.8 copy-start.4
  81.0 37.1 %all-to-all-start.1 = ((bf16[8,11,32,256]{3,2,1,0:T(8,128)(2,1)}), bf16[8,11,32,256]{3,2,1,0:T(8,128)(2,1)S(1)}, u32[]{:S(2)}, u32[]{:S(2)}) async-start(bf16[8,11,32,256]{3,2,1,0:T(8,128)(2,1)} %get-tuple-element.19), calls=%async_computation.1 | async-start | bytes 2883584 | tf_op jit(solution)/shard_map/all_to_all | solution.py:214
  84.6 10.1 %collective-permute-start.6 = (bf16[3,256,256]{2,1,0:T(8,128)(2,1)}, bf16[3,256,256]{2,1,0:T(8,128)(2,1)}, u32[]{:S(2)}, u32[]{:S(2)}) collective-permute-start(bf16[3,256,256]{2,1,0:T(8,128)(2,1)} %bitcast.37), channel_id=1, source_target_pairs={{0,16},{8,24},{16,0},{24,8},{1,17},{9,25},{17,1},{25,9},{2,18},{10... | collective-permute-start | bytes 1179656 | tf_op jit(solution)/shard_map/ppermute | solution.py:27
  85.1 10.2 %collective-permute-start.7 = (bf16[3,256,256]{2,1,0:T(8,128)(2,1)}, bf16[3,256,256]{2,1,0:T(8,128)(2,1)}, u32[]{:S(2)}, u32[]{:S(2)}) collective-permute-start(bf16[3,256,256]{2,1,0:T(8,128)(2,1)} %bitcast.38), channel_id=1, source_target_pairs={{0,8},{8,0},{16,24},{24,16},{1,9},{9,1},{17,25},{25,17},{2,10},{10... | collective-permute-start | bytes 1179656 | tf_op jit(solution)/shard_map/ppermute | solution.py:22
  94.7 2.1 %collective-permute-start.8 = (bf16[3,256,256]{2,1,0:T(8,128)(2,1)}, bf16[3,256,256]{2,1,0:T(8,128)(2,1)}, u32[]{:S(2)}, u32[]{:S(2)}) collective-permute-start(bf16[3,256,256]{2,1,0:T(8,128)(2,1)} %collective-permute-done.6.refs_1_), channel_id=1, source_target_pairs={{0,8},{8,0},{16,24},{24,16},{1,9},{9,1},{17,25},{25,17},{2,10},{10... | collective-permute-start | bytes 1179656 | tf_op jit(solution)/shard_map/ppermute | solution.py:22
  118.1 1.1 copy-start.2
  125.0 4.5 %collective-permute-start.9 = (bf16[5,32,256]{2,1,0:T(8,128)(2,1)S(1)}, bf16[5,32,256]{2,1,0:T(8,128)(2,1)S(1)}, u32[]{:S(2)}, u32[]{:S(2)}) collective-permute-start(bf16[5,32,256]{2,1,0:T(8,128)(2,1)S(1)} %get-tuple-element.28), channel_id=1, source_target_pairs={{0,16},{8,24},{16,0},{24,8},{1,17},{9,25},{17,1},{25,9},{2,18},{10... | collective-permute-start | bytes 245768 | tf_op jit(solution)/shard_map/ppermute | solution.py:27
  163.4 18.8 %copy-start.3 = (bf16[8,2,5,32,256]{4,3,2,1,0:T(8,128)(2,1)}, bf16[8,2,5,32,256]{4,3,2,1,0:T(8,128)(2,1)S(1)}, u32[]{:S(2)}) copy-start(bf16[8,2,5,32,256]{4,3,2,1,0:T(8,128)(2,1)S(1)} %all_to_all.27.refs_8_) | copy-start | bytes 3932164
  163.4 18.8 %collective-permute-start.10 = (bf16[8,2,5,32,256]{4,3,2,1,0:T(8,128)(2,1)S(1)}, bf16[8,2,5,32,256]{4,3,2,1,0:T(8,128)(2,1)}, u32[]{:S(2)}, u32[]{:S(2)}) collective-permute-start(bf16[8,2,5,32,256]{4,3,2,1,0:T(8,128)(2,1)S(1)} %all_to_all.27.refs_8_), channel_id=1, source_target_pairs={{0,8},{8,0},{16,24},{24,16},{1,9},{9,1},{17,25},{25,17},{2,10},{10... | collective-permute-start | bytes 3932168 | tf_op jit(solution)/shard_map/ppermute | solution.py:22
  165.7 14.3 %collective-permute-start = (bf16[8,32,1024]{2,1,0:T(8,128)(2,1)}, bf16[8,32,1024]{2,1,0:T(8,128)(2,1)}, u32[]{:S(2)}, u32[]{:S(2)}) collective-permute-start(bf16[8,32,1024]{2,1,0:T(8,128)(2,1)} %slice_bitcast_fusion.refs_0_), channel_id=1, source_target_pairs={{0,16},{8,24},{16,0},{24,8},{1,17},{9,25},{17,1},{25,9},{2,18},{10... | collective-permute-start | bytes 1572872 | tf_op jit(solution)/shard_map/ppermute | solution.py:27
  166.2 15.5 %collective-permute-start.1 = (bf16[8,32,1024]{2,1,0:T(8,128)(2,1)}, bf16[8,32,1024]{2,1,0:T(8,128)(2,1)}, u32[]{:S(2)}, u32[]{:S(2)}) collective-permute-start(bf16[8,32,1024]{2,1,0:T(8,128)(2,1)} %slice_bitcast_fusion.refs_0_), channel_id=1, source_target_pairs={{0,8},{8,0},{16,24},{24,16},{1,9},{9,1},{17,25},{25,17},{2,10},{10... | collective-permute-start | bytes 1572872 | tf_op jit(solution)/shard_map/ppermute | solution.py:22
  180.0 2.3 %collective-permute-start.2 = (bf16[8,32,1024]{2,1,0:T(8,128)(2,1)}, bf16[8,32,1024]{2,1,0:T(8,128)(2,1)}, u32[]{:S(2)}, u32[]{:S(2)}) collective-permute-start(bf16[8,32,1024]{2,1,0:T(8,128)(2,1)} %collective-permute-done.refs_1_), channel_id=1, source_target_pairs={{0,8},{8,0},{16,24},{24,16},{1,9},{9,1},{17,25},{25,17},{2,10},{10... | collective-permute-start | bytes 1572872 | tf_op jit(solution)/shard_map/ppermute | solution.py:22

commit v2 on v1

v2 whole, which is shorter than its diff:
```python
import functools

import jax
import jax.numpy as jnp
from jax import lax
from jax.experimental import pallas as pl
from jax.experimental.pallas import tpu as pltpu
from jax.sharding import PartitionSpec as P

epsilon = 1e-05
bf16 = jnp.bfloat16
f32 = jnp.float32
VMEM_BYTES = 56 * 1024 * 1024


def dot(a, b, ca, cb):
    return lax.dot_general(a, b, (((ca,), (cb,)), ((), ())), preferred_element_type=f32)


def core_swap(x):
    count = lax.axis_size("section")
    return lax.ppermute(x, "section", [(i, i ^ 1) for i in range(count)])


def chip_shift(x, by):
    count = lax.axis_size("section")
    return lax.ppermute(x, "section", [(i, (i - 2 * by) % count) for i in range(count)])


def section_order():
    count = lax.axis_size("section")
    me = lax.axis_index("section")
    same = [(me + 2 * j) % count for j in range(count // 2)]
    other = [((me ^ 1) + 2 * j) % count for j in range(count // 2)]
    return jnp.stack(same + other).astype(jnp.int32)


def gather_section(x):
    count = lax.axis_size("section")
    same = [x] + [chip_shift(x, j) for j in range(1, count // 2)]
    return same + [core_swap(b) for b in same]


def spread(x):
    peers = lax.axis_size("dp")
    return lax.all_to_all(jnp.broadcast_to(x[None], (peers,) + x.shape), "dp", 0, 0, tiled=True)


def gram_pairs(count):
    ups = [(k, count + j) for j in range(count - 1) for k in range(j + 1)]
    listed = []
    for chip in range(count // 2):
        own = [(k, l) for l in (2 * chip, 2 * chip + 1) for k in range(l)]
        spare = 2 * (count - 1) - len(own)
        listed += own + ups[:spare]
        ups = ups[spare:]
    return listed


def prepare_kernel(place, tokens_ref, cot_ref, down_ref, gain_ref, rows_ref, cot_rows_ref, square_ref, weight_ref):
    peers, t, block = rows_ref.shape
    r = down_ref.shape[2]
    pieces = block // r
    total = jnp.zeros((t, 1), f32)
    for n in range(peers):
        piece = tokens_ref[:, n * block : (n + 1) * block]
        wide = piece.astype(f32)
        total = total + jnp.sum(wide * wide, axis=-1, keepdims=True)
        rows_ref[n] = piece
        for b in range(pieces):
            start = n * block + b * r
            cot_rows_ref[n, b * t : (b + 1) * t] = cot_ref[:, start : start + r]
    square_ref[...] = total
    gain = gain_ref[...].reshape(block, 1)
    weight_ref[...] = (down_ref[0].astype(f32) * gain).astype(bf16)


def gram_kernel(count, order, left, right, *refs):
    ups = refs[:count]
    mine, partner, gram_ref, table = refs[count:]
    core = lax.rem(order[0], 2)
    table[core] = mine[...]
    table[1 - core] = partner[...]
    for i in range(count):
        table[2 + order[i]] = ups[i][...]
    for p in range(count - 1):
        gram_ref[p] = dot(table[2 + left[p]], table[right[p]], 0, 0).astype(bf16)


def project_kernel(count, room, order, rows_ref, *refs):
    downs = refs[:count]
    ups = refs[count : 2 * count]
    part_ref = refs[2 * count]
    peers, t, width = rows_ref.shape
    r = part_ref.shape[2]
    x = rows_ref[...].reshape(peers * t, width)

    def place(m):
        return pl.ds(pl.multiple_of(room + m * t, t), t)

    for i in range(count):
        layer = order[i]
        out = dot(x, downs[i][...], 1, 0)
        part_ref[:, place(layer), :] = out.astype(bf16).reshape(peers, t, r)

        @pl.when(layer < count - 1)
        def _():
            out = dot(x, ups[i][...], 1, 0)
            part_ref[:, place(count + layer), :] = out.astype(bf16).reshape(peers, t, r)


def project_cot_kernel(count, order, packed_ref, *refs):
    ups = refs[:count]
    part_ref = refs[count]
    peers, rows, r = part_ref.shape
    t = rows // count
    width = ups[0].shape[0]
    c = jnp.concatenate(
        [packed_ref[:, b * t : (b + 1) * t].reshape(peers * t, r) for b in range(width // r)], axis=1
    )
    for i in range(count):
        out = dot(c, ups[i][...], 1, 0)
        start = pl.multiple_of(order[i] * t, t)
        part_ref[:, pl.ds(start, t), :] = out.astype(bf16).reshape(peers, t, r)


def recur_kernel(count, width, room, order, sums_ref, back_ref, sq_ref, *refs):
    grams = refs[:count]
    out_ref, table, grads = refs[count:]
    half, _, t, _ = out_ref.shape
    per = count - 1
    for i in range(count):
        for p in range(per):
            table[order[i] * per + p] = grams[i][p]
    place = {pair: n for n, pair in enumerate(gram_pairs(count))}

    def mixed(k, l):
        return table[place[(k, l)]]

    def ups(k, j, a):
        if k <= j:
            return dot(a, table[place[(k, count + j)]], 1, 0)
        return dot(a, table[place[(j, count + k)]], 1, 1)

    def total(ref, start):
        return jnp.sum(ref[:, start : start + t].astype(f32), axis=0)

    proj = [total(sums_ref, room + l * t) for l in range(count)]
    hu = [total(sums_ref, room + (count + k) * t) for k in range(count - 1)]
    back = [total(back_ref, l * t) for l in range(count)]
    norm = sq_ref[...]
    invs, pres, hus = [], [], []
    for l in range(count):
        inv = lax.rsqrt(norm / width + epsilon)
        pre = inv * proj[l]
        invs.append(inv)
        pres.append(pre)
        hus.append(list(hu))
        if l < count - 1:
            act = (pre * jax.nn.sigmoid(pre)).astype(bf16)
            for j in range(half):
                out_ref[j, 2 + l] = act
            wide = act.astype(f32)
            for j in range(l + 1, count):
                proj[j] = proj[j] + dot(act, mixed(l, j), 1, 0)
            step = [ups(l, j, act) for j in range(count - 1)]
            norm = norm + jnp.sum(wide * (2.0 * hu[l] + step[l]), axis=-1, keepdims=True)
            hu = [hu[j] + step[j] for j in range(count - 1)]
    for l in reversed(range(count)):
        s = jax.nn.sigmoid(pres[l])
        grad = (back[l] * s * (1.0 + pres[l] * (1.0 - s))).astype(bf16)
        wide = grad.astype(f32)
        grads[l] = (wide * invs[l]).astype(bf16)
        inner = jnp.sum(wide * proj[l], axis=-1, keepdims=True) / width
        for j in range(l):
            back[j] = back[j] + invs[l] * (
                dot(grad, mixed(j, l), 1, 1) - invs[l] * invs[l] * inner * hus[l][j]
            )
    chip = order[0] // 2
    for j in range(half):
        other = lax.rem(chip + half - j, half)
        out_ref[j, 0] = grads[2 * other]
        out_ref[j, 1] = grads[2 * other + 1]


def fisher_kernel(count, seqs, scale, order, me, *refs):
    rows = refs[:count]
    ups = refs[count : 2 * count]
    same_ref, other_ref, seg_ref, gain_ref, out_ref, acc, hidden, masks = refs[2 * count :]
    half = count // 2
    peers, t, width = rows[0].shape
    r = out_ref.shape[1]
    chunk = min(r, width)
    span = count * t

    def column(n, m):
        parts = [same_ref[n, j, m] for j in range(half)] + [other_ref[n, j, m] for j in range(half)]
        return jnp.concatenate(parts, axis=0)

    acts = []
    for i in range(1, count):
        act = jnp.concatenate([column(n, 2 + jnp.minimum(order[i], count - 2)) for n in range(peers)], axis=0)
        acts.append(jnp.where(order[i] < me[0], act, jnp.zeros_like(act)))
    for n in range(peers):
        grad = column(n, lax.rem(me[0], 2)).astype(f32).T
        seg = seg_ref[n]
        for q in range(seqs):
            masks[n, q * r : (q + 1) * r] = jnp.where(seg == q, grad, 0.0).astype(bf16)
    for f in range(width // chunk):
        cols = slice(f * chunk, (f + 1) * chunk)
        update = dot(acts[0], ups[1][cols], 1, 1)
        for i in range(2, count):
            update = update + dot(acts[i - 1], ups[i][cols], 1, 1)
        for n in range(peers):
            h = jnp.concatenate([rows[i][n, :, cols] for i in range(count)], axis=0).astype(f32)
            hidden[n] = (h + update[n * span : (n + 1) * span]).astype(bf16)
        for n in range(peers):
            g = dot(masks[n], hidden[n], 1, 0)
            g = g * g
            total = g[:r]
            for q in range(1, seqs):
                total = total + g[q * r : (q + 1) * r]
            if n == 0:
                acc[...] = total
            else:
                acc[...] = acc[...] + total
        gain = gain_ref[:, cols]
        out_ref[cols] = (acc[...] * (gain * gain * scale)).T


def per_device(tokens, cotangent, down_weight, up_weight, norm_gain, lengths):
    count = lax.axis_size("section")
    peers = lax.axis_size("dp")
    me = lax.axis_index("section")
    spot = lax.axis_index("dp")
    row_count, width = tokens.shape
    block = width // peers
    t = row_count // count
    r = down_weight.shape[2]
    order = section_order()
    params = pltpu.CompilerParams(vmem_limit_bytes=VMEM_BYTES)
    smem = pl.BlockSpec(memory_space=pltpu.SMEM)
    vmem = pl.BlockSpec(memory_space=pltpu.VMEM)

    ups = gather_section(up_weight[0])
    token_send, cot_send, square, weight = pl.pallas_call(
        prepare_kernel,
        grid_spec=pltpu.PrefetchScalarGridSpec(
            num_scalar_prefetch=1,
            grid=(1,),
            in_specs=[
                pl.BlockSpec((t, width), lambda n, place: (place[0], 0)),
                pl.BlockSpec((t, width), lambda n, place: (place[0], 0)),
                pl.BlockSpec((1, block, r), lambda n, place: (0, 0, 0)),
                pl.BlockSpec((1, block), lambda n, place: (0, place[1])),
            ],
            out_specs=[
                pl.BlockSpec((peers, t, block), lambda n, place: (0, 0, 0)),
                pl.BlockSpec((peers, t * (block // r), r), lambda n, place: (0, 0, 0)),
                pl.BlockSpec((t, 1), lambda n, place: (0, 0)),
                pl.BlockSpec((block, r), lambda n, place: (0, 0)),
            ],
        ),
        out_shape=(
            jax.ShapeDtypeStruct((peers, t, block), bf16),
            jax.ShapeDtypeStruct((peers, t * (block // r), r), bf16),
            jax.ShapeDtypeStruct((t, 1), f32),
            jax.ShapeDtypeStruct((block, r), bf16),
        ),
        compiler_params=params,
        name="prepare",
    )(jnp.stack([me, spot]).astype(jnp.int32), tokens, cotangent, down_weight, norm_gain)
    downs = gather_section(weight)
    token_rows = lax.all_to_all(token_send, "dp", 0, 0, tiled=True)

    pairs = gram_pairs(count)
    left = lax.dynamic_slice_in_dim(jnp.array([a for a, _ in pairs], jnp.int32), me * (count - 1), count - 1)
    codes = jnp.array([b % 2 if b < count else 2 + b - count for _, b in pairs], jnp.int32)
    right = lax.dynamic_slice_in_dim(codes, me * (count - 1), count - 1)
    gram = pl.pallas_call(
        functools.partial(gram_kernel, count),
        out_shape=jax.ShapeDtypeStruct((count - 1, r, r), bf16),
        in_specs=[smem] * 3 + [vmem] * (count + 2),
        out_specs=vmem,
        scratch_shapes=[pltpu.VMEM((2 + count, block, r), bf16)],
        compiler_params=params,
        name="gram",
    )(order, left, right, *ups, downs[0], downs[count // 2])
    line = jnp.zeros((peers, 16, r), bf16).at[:, 0, : lengths.shape[1]].set(lengths.astype(bf16))
    gram_rows = (count - 1) * r // peers
    cot_rows = cot_send.shape[1]
    packed = jnp.concatenate([cot_send, gram.reshape(peers, gram_rows, r), line], axis=1)
    packed, token_rows = lax.optimization_barrier((packed, token_rows))
    packed = lax.all_to_all(packed, "dp", 0, 0, tiled=True)

    room = -(-gram_rows // t) * t
    part = pl.pallas_call(
        functools.partial(project_kernel, count, room),
        out_shape=jax.ShapeDtypeStruct((peers, room + (2 * count - 1) * t, r), bf16),
        in_specs=[smem] + [vmem] * (1 + 2 * count),
        out_specs=vmem,
        compiler_params=params,
        name="project",
    )(order, token_rows, *downs, *ups)
    gram_sum = jnp.sum(packed[:, cot_rows : cot_rows + gram_rows].astype(f32), axis=0).astype(bf16)
    all_lengths = packed[:, cot_rows + gram_rows, : lengths.shape[1]].astype(jnp.int32)
    part = part.at[:, :gram_rows].set(jnp.broadcast_to(gram_sum[None], (peers,) + gram_sum.shape))
    sums = lax.all_to_all(part, "dp", 0, 0, tiled=True)

    back_part = pl.pallas_call(
        functools.partial(project_cot_kernel, count),
        out_shape=jax.ShapeDtypeStruct((peers, count * t, r), bf16),
        in_specs=[smem] + [vmem] * (1 + count),
        out_specs=vmem,
        compiler_params=params,
        name="project_cot",
    )(order, packed, *ups)
    all_rows = gather_section(token_rows)
    sums, all_rows = lax.optimization_barrier((sums, all_rows))
    back_sums = lax.all_to_all(back_part, "dp", 0, 0, tiled=True)
    grams = gather_section(sums[:, :gram_rows].reshape(count - 1, r, r))

    held = pl.pallas_call(
        functools.partial(recur_kernel, count, width, room),
        out_shape=jax.ShapeDtypeStruct((count // 2, count + 1, t, r), bf16),
        in_specs=[smem] + [vmem] * (3 + count),
        out_specs=vmem,
        scratch_shapes=[
            pltpu.VMEM((count * (count - 1), r, r), bf16),
            pltpu.VMEM((count, t, r), bf16),
        ],
        compiler_params=params,
        name="recur",
    )(order, sums, back_sums, square, *grams)
    same = spread(jnp.stack([held[0]] + [chip_shift(held[j], j) for j in range(1, count // 2)]))
    other = core_swap(same)

    ends = jnp.cumsum(all_lengths, axis=1)
    position = (order[:, None] * t + jnp.arange(t, dtype=jnp.int32)[None]).reshape(-1)
    seg = jnp.sum(position[None, None, :] >= ends[:, :, None], axis=1).astype(jnp.int32)
    seg = seg.reshape(peers, 1, row_count)
    gain = lax.dynamic_slice_in_dim(norm_gain, spot * block, block, 1)

    seqs = lengths.shape[1]
    chunk = min(r, block)
    fisher = pl.pallas_call(
        functools.partial(fisher_kernel, count, seqs, 1.0 / (row_count * peers)),
        out_shape=jax.ShapeDtypeStruct((block, r), f32),
        in_specs=[smem, smem] + [vmem] * (2 * count + 4),
        out_specs=vmem,
        scratch_shapes=[
            pltpu.VMEM((r, chunk), f32),
            pltpu.VMEM((peers, row_count, chunk), bf16),
            pltpu.VMEM((peers, seqs * r, row_count), bf16),
        ],
        compiler_params=params,
        name="squares",
    )(order, me.astype(jnp.int32)[None], *all_rows, *ups, same, other, seg, gain)
    return fisher[None]


def solution(mesh):
    in_specs = (
        P("dp", None),
        P("dp", None),
        P("section", "dp", None),
        P("section", "dp", None),
        P("section", None),
        P("dp", None),
    )
    out_specs = P("section", "dp", None)
    return jax.shard_map(
        per_device, mesh=mesh, in_specs=in_specs, out_specs=out_specs, check_vma=False
    )
```

time: 200 us -> 172 us (0.86)
  blocking collectives: 65.6 us -> 33.9 us
  starting transfers between devices: 14.2 us -> 25.9 us
  waiting for transfers between devices: 74.3 us -> 64.5 us
  Pallas kernels: 26.6 us -> 32.4 us
  local copies, waits for them, and re-layouts: 11.8 us -> 9.09 us
    all_to_all x1 -> x0, blocking collectives: 16.6 us -> none  [per_device(): packed = lax.all_to_all(packed, 'dp', 0, 0, tiled=True)]
    all_to_all x2 -> x1, blocking collectives: 49 us -> 33.9 us  [spread(): lax.all_to_all(jnp.broadcast_to(x[None], (peers,) + x.shape), 'dp', 0, 0,...]
    all_to_all x1 -> x3, starting transfers between devices: 5.81 us -> 13.1 us  [the longest x1 5.81 us: per_device(): token_rows = lax.all_to_all(token_send, 'dp', 0, 0, tiled=True)]
    all_to_all x1, waiting for transfers between devices: 21.4 us -> 14.4 us  [per_device(): sums = lax.all_to_all(part, 'dp', 0, 0, tiled=True)]
    pallas_call x3 -> x6, Pallas kernels: 26.6 us -> 32.4 us  [the longest x1 12.1 us: per_device(): pl.pallas_call(functools.partial(fisher_kernel, count, seqs, 1.0 / (row_c...]
    ppermute x4 -> x5, starting transfers between devices: 4.68 us -> 8.56 us  [chip_shift(): lax.ppermute(x, 'section', [(i, (i - 2 * by) % count) for i in range(coun...]
    ppermute x4 -> x5, waiting for transfers between devices: 41 us -> 38.4 us  [chip_shift(): lax.ppermute(x, 'section', [(i, (i - 2 * by) % count) for i in range(coun...]
    squeeze x1 -> x0, local copies, waits for them, and re-layouts: 2.3 us -> none  [per_device(): all_rows = gather_section(rows[:, 0])]
  transfers between devices with their start and end apart: 13 -> 18, of which waited for: 8 -> 10; matrix products, arithmetic and copies ran while one was open for 5% -> 5% of each run, Pallas kernels for 0% -> 9%
where the time goes in v2:
time: 172 us; the launch traced here: 171 us
  waiting for transfers between devices  64.5 us (38%)
  blocking collectives  33.9 us (20%)
  Pallas kernels  32.4 us (19%)
  starting transfers between devices  25.9 us (15%)
  local copies, waits for them, and re-layouts  9.09 us (5%)
  other arithmetic  4.89 us (3%)
    ppermute x5, waiting for transfers between devices, chip_shift(): lax.ppermute(x, 'section', [(i, (i - 2 * by) % count) for i in range(coun...  38.4 us
    all_to_all x1, blocking collectives, spread(): lax.all_to_all(jnp.broadcast_to(x[None], (peers,) + x.shape), 'dp', 0, 0,...  33.9 us
    all_to_all x1, waiting for transfers between devices, per_device(): sums = lax.all_to_all(part, 'dp', 0, 0, tiled=True)  14.4 us
    pallas_call x1, Pallas kernels, per_device(): pl.pallas_call(functools.partial(fisher_kernel, count, seqs, 1.0 / (row_c...  12.1 us
    ppermute x5, starting transfers between devices, chip_shift(): lax.ppermute(x, 'section', [(i, (i - 2 * by) % count) for i in range(coun...  8.56 us
    all_to_all x1, starting transfers between devices, per_device(): token_rows = lax.all_to_all(token_send, 'dp', 0, 0, tiled=True)  5.81 us
    pallas_call x1, Pallas kernels, per_device(): pl.pallas_call(functools.partial(project_kernel, count, room), out_shape=...  5.51 us
    pallas_call x1, Pallas kernels, per_device(): pl.pallas_call(functools.partial(recur_kernel, count, width, room), out_s...  4.28 us
  transfers between devices with their start and end apart: 18, of which 10 were waited for; matrix products, arithmetic and copies ran while one was open for 5% of the time, Pallas kernels for 9%

profile of v2, /device:TPU:0, one launch (start us, length us, event | category | flops | bytes accessed | tf_op | source)
XLA Modules:
  0.0 170.9 jit_solution(17814643292388040054)
XLA Ops:
  0.0 3.0 %collective-permute-start = (bf16[1024,256]{1,0:T(8,128)(2,1)}, bf16[1024,256]{1,0:T(8,128)(2,1)S(1)}, u32[]{:S(2)}, u32[]{:S(2)}) collective-permute-start(bf16[1024,256]{1,0:T(8,128)(2,1)} %bitcast.15), channel_id=1, source_target_pairs={{0,16},{8,24},{16,0},{24,8},{1,17},{9,25},{17,1},{25,9},{2,18},{10... | collective-permute-start | bytes 1572872 | tf_op jit(solution)/shard_map/ppermute | solution.py:27
  3.0 0.6 pad_add_fusion.1.place
  3.6 3.4 %prepare.1 = (bf16[8,32,1024]{2,1,0:T(8,128)(2,1)}, bf16[8,128,256]{2,1,0:T(8,128)(2,1)}, f32[32,1]{1,0:T(8,128)}, bf16[1024,256]{1,0:T(8,128)(2,1)}) custom-call(s32[2]{0:T(128)} %pad_add_fusion.1.place, bf16[128,8192]{1,0:T(8,128)(2,1)} %tokens_ref.1, bf16[128,8192]{1,0:T(8,128)(2,1)} %cot_ref.1, bf16[1,1024,256]{2,1,0:T(8,128)(2,1)} %down_ref.1, ...), custom_call_target="tpu_custom_call" | custom-call | tf_op jit(solution)/shard_map/prepare/pallas_call | solution.py:246
  7.1 5.8 %all-to-all-start = ((bf16[8,32,1024]{2,1,0:T(8,128)(2,1)}), bf16[8,32,1024]{2,1,0:T(8,128)(2,1)S(1)}, u32[]{:S(2)}, u32[]{:S(2)}) async-start(bf16[8,32,1024]{2,1,0:T(8,128)(2,1)} %get-tuple-element.42), calls=%async_computation | async-start | bytes 1048576 | tf_op jit(solution)/shard_map/all_to_all | solution.py:274
  12.9 0.5 collective-permute-start.3
  13.4 1.7 collective-permute-done.refs_1_.refs_5_
  15.1 0.7 dynamic_slice.9.left
  15.8 0.7 dynamic_slice.10.right
  16.5 0.7 broadcast_multiply_fusion
  17.2 0.7 copy-done.2
  18.0 0.2 copy-done.10
  18.2 0.2 copy-done.3
  18.4 3.5 %gram.1 = bf16[3,256,256]{2,1,0:T(8,128)(2,1)} custom-call(s32[4]{0:T(128)} %get-tuple-element.52.order, s32[3]{0:T(128)} %dynamic_slice.9.left, s32[3]{0:T(128)} %dynamic_slice.10.right, bf16[1024,256]{1,0:T(8,128)(2,1)} %bitcast.16, bf16[1024,256]{1,0:T(8,128)(2,1)} %copy-done.1, bf16[1024,256]{1,0:T(8,128)(2,1)} %copy-done.2, ...), custom_call_target="tpu_custom_call" | custom-call | tf_op jit(solution)/shard_map/gram/pallas_call | solution.py:280
  21.9 2.0 %pad_maximum_fusion = bf16[8,240,256]{2,1,0:T(8,128)(2,1)} fusion(bf16[8,16,256]{2,1,0:T(8,128)(2,1)S(1)} %scatter.13, bf16[8,96,256]{2,1,0:T(8,128)(2,1)} %bitcast.24, bf16[8,128,256]{2,1,0:T(8,128)(2,1)S(1)} %copy-done.17), kind=kLoop, calls=%fused_computation | loop fusion | flops 2949120 | bytes 1966080 | tf_op jit(solution)/shard_map/concatenate | solution.py:292
  23.9 3.2 %all-to-all-done.rows_ref.refs_0_ = bf16[8,32,1024]{2,1,0:T(8,128)(2,1)S(1)} async-done(((bf16[8,32,1024]{2,1,0:T(8,128)(2,1)}), bf16[8,32,1024]{2,1,0:T(8,128)(2,1)S(1)}, u32[]{:S(2)}, u32[]{:S(2)}) %all-to-all-start) | async-done | bytes 524320 | tf_op jit(solution)/shard_map/all_to_all | solution.py:274
  27.1 3.6 %all-to-all-start.1 = ((bf16[8,240,256]{2,1,0:T(8,128)(2,1)}), bf16[8,240,256]{2,1,0:T(8,128)(2,1)S(1)}, u32[]{:S(2)}, u32[]{:S(2)}) async-start(bf16[8,240,256]{2,1,0:T(8,128)(2,1)} %pad_maximum_fusion), calls=%async_computation.1 | async-start | bytes 1966080 | tf_op jit(solution)/shard_map/all_to_all | solution.py:294
  30.8 0.9 collective-permute-start.4
  31.7 12.5 %collective-permute-done.4.refs_1_ = bf16[1024,256]{1,0:T(8,128)(2,1)S(1)} collective-permute-done((bf16[1024,256]{1,0:T(8,128)(2,1)S(1)}, bf16[1024,256]{1,0:T(8,128)(2,1)S(1)}, u32[]{:S(2)}, u32[]{:S(2)}) %collective-permute-start.4) | collective-permute-done | bytes 524320 | tf_op jit(solution)/shard_map/ppermute | solution.py:27
  44.2 1.9 %collective-permute-done.5.refs_3_ = bf16[1024,256]{1,0:T(8,128)(2,1)S(1)} collective-permute-done((bf16[1024,256]{1,0:T(8,128)(2,1)S(1)}, bf16[1024,256]{1,0:T(8,128)(2,1)S(1)}, u32[]{:S(2)}, u32[]{:S(2)}) %collective-permute-start.5) | collective-permute-done | bytes 524320 | tf_op jit(solution)/shard_map/ppermute | solution.py:22
  46.1 0.8 copy-done.16
  46.9 5.5 %project.1 = bf16[8,320,256]{2,1,0:T(8,128)(2,1)} custom-call(s32[4]{0:T(128)} %get-tuple-element.52.order, bf16[8,32,1024]{2,1,0:T(8,128)(2,1)} %copy-done.7, bf16[1024,256]{1,0:T(8,128)(2,1)} %get-tuple-element.41.refs_4_.refs_0_, bf16[1024,256]{1,0:T(8,128)(2,1)} %copy-done.15, bf16[1024,256]{1,0:T(8,128)(2,1)} %copy-done.10, ...), custom_call_target="tpu_custom_call" | custom-call | tf_op jit(solution)/shard_map/project/pallas_call | solution.py:297
  52.4 2.7 %all-to-all-done.1.packed_ref = bf16[8,240,256]{2,1,0:T(8,128)(2,1)S(1)} async-done(((bf16[8,240,256]{2,1,0:T(8,128)(2,1)}), bf16[8,240,256]{2,1,0:T(8,128)(2,1)S(1)}, u32[]{:S(2)}, u32[]{:S(2)}) %all-to-all-start.1) | async-done | bytes 983072 | tf_op jit(solution)/shard_map/all_to_all | solution.py:294
  55.2 0.9 broadcast_dynamic-update-slice_fusion
  56.1 0.1 copy-done.5
  56.2 3.7 %all-to-all-start.2 = ((bf16[8,320,256]{2,1,0:T(8,128)(2,1)}), bf16[8,320,256]{2,1,0:T(8,128)(2,1)S(1)}, u32[]{:S(2)}, u32[]{:S(2)}) async-start(bf16[8,320,256]{2,1,0:T(8,128)(2,1)} %broadcast_dynamic-update-slice_fusion), calls=%async_computation.2 | async-start | bytes 2621440 | tf_op jit(solution)/shard_map/all_to_all | solution.py:308
  59.9 1.5 collective-permute-start.6
  61.5 12.1 %collective-permute-done.6.refs_1_ = bf16[8,32,1024]{2,1,0:T(8,128)(2,1)S(1)} collective-permute-done((bf16[8,32,1024]{2,1,0:T(8,128)(2,1)S(1)}, bf16[8,32,1024]{2,1,0:T(8,128)(2,1)S(1)}, u32[]{:S(2)}, u32[]{:S(2)}) %collective-permute-start.6) | collective-permute-done | bytes 524320 | tf_op jit(solution)/shard_map/ppermute | solution.py:27
  73.5 3.5 %project_cot.1 = bf16[8,128,256]{2,1,0:T(8,128)(2,1)} custom-call(s32[4]{0:T(128)} %get-tuple-element.52.order, bf16[8,240,256]{2,1,0:T(8,128)(2,1)} %copy-done.5, bf16[1024,256]{1,0:T(8,128)(2,1)} %bitcast.18, bf16[1024,256]{1,0:T(8,128)(2,1)} %copy-done.1, bf16[1024,256]{1,0:T(8,128)(2,1)} %copy-done.2, bf16[1024,256]{1,0:T(8,128)(2,1)} %copy-done.3), custom_call_target="tpu_custom_call" | custom-call | tf_op jit(solution)/shard_map/project_cot/pallas_call | solution.py:310
  77.1 14.4 %all-to-all-done.2.sums_ref = bf16[8,320,256]{2,1,0:T(8,128)(2,1)S(1)} async-done(((bf16[8,320,256]{2,1,0:T(8,128)(2,1)}), bf16[8,320,256]{2,1,0:T(8,128)(2,1)S(1)}, u32[]{:S(2)}, u32[]{:S(2)}) %all-to-all-start.2) | async-done | bytes 1310752 | tf_op jit(solution)/shard_map/all_to_all | solution.py:308
  91.5 3.6 %all-to-all-start.3 = ((bf16[8,128,256]{2,1,0:T(8,128)(2,1)}), bf16[8,128,256]{2,1,0:T(8,128)(2,1)S(1)}, u32[]{:S(2)}, u32[]{:S(2)}) async-start(bf16[8,128,256]{2,1,0:T(8,128)(2,1)} %project_cot.1), calls=%async_computation.3 | async-start | bytes 1048576 | tf_op jit(solution)/shard_map/all_to_all | solution.py:320
  95.2 1.6 collective-permute-start.9
  96.7 9.2 %collective-permute-done.9.refs_1_ = bf16[3,256,256]{2,1,0:T(8,128)(2,1)S(1)} collective-permute-done((bf16[3,256,256]{2,1,0:T(8,128)(2,1)S(1)}, bf16[3,256,256]{2,1,0:T(8,128)(2,1)S(1)}, u32[]{:S(2)}, u32[]{:S(2)}) %collective-permute-start.9) | collective-permute-done | bytes 393248 | tf_op jit(solution)/shard_map/ppermute | solution.py:27
  106.0 3.8 %all-to-all-done.3.back_ref = bf16[8,128,256]{2,1,0:T(8,128)(2,1)S(1)} async-done(((bf16[8,128,256]{2,1,0:T(8,128)(2,1)}), bf16[8,128,256]{2,1,0:T(8,128)(2,1)S(1)}, u32[]{:S(2)}, u32[]{:S(2)}) %all-to-all-start.3) | async-done | bytes 524320 | tf_op jit(solution)/shard_map/all_to_all | solution.py:320
  109.8 0.8 copy-done.11
  110.6 0.1 copy-done.19
  110.7 0.1 copy-done.20
  110.9 4.3 %recur.1 = bf16[2,5,32,256]{3,2,1,0:T(8,128)(2,1)} custom-call(s32[4]{0:T(128)} %get-tuple-element.52.order, bf16[8,320,256]{2,1,0:T(8,128)(2,1)} %copy-done.4, bf16[8,128,256]{2,1,0:T(8,128)(2,1)} %copy-done.11, f32[32,1]{1,0:T(8,128)} %get-tuple-element.50.sq_ref, bf16[3,256,256]{2,1,0:T(8,128)(2,1)} %bitcast.23, bf16[3,256,256]{2,1,0:T(8,128)(2,1)} %copy-done.18, ...), custom_call_target="tpu_custom_call" | custom-call | tf_op jit(solution)/shard_map/recur/pallas_call | solution.py:323
  115.1 0.9 fusion
  116.1 1.6 collective-permute-start.12
  117.7 2.9 %collective-permute-done.12 = bf16[5,32,256]{2,1,0:T(8,128)(2,1)S(1)} collective-permute-done((bf16[5,32,256]{2,1,0:T(8,128)(2,1)S(1)}, bf16[5,32,256]{2,1,0:T(8,128)(2,1)S(1)}, u32[]{:S(2)}, u32[]{:S(2)}) %collective-permute-start.12) | collective-permute-done | bytes 81952 | tf_op jit(solution)/shard_map/ppermute | solution.py:27
  120.6 0.1 broadcast_in_dim.7
  120.8 33.9 %all_to_all.25.refs_8_ = bf16[8,2,5,32,256]{4,3,2,1,0:T(8,128)(2,1)S(1)} all-to-all(bf16[8,2,5,32,256]{4,3,2,1,0:T(8,128)(2,1)S(1)} %broadcast_in_dim.7), channel_id=1, replica_groups=mesh['section'=4,'dp'=8] {'dp'}, dimensions={0} | all-to-all | bytes 2621440 | tf_op jit(solution)/shard_map/all_to_all | solution.py:46
  154.7 0.1 add.62
  154.8 1.3 constant_dynamic-slice_fusion.refs_11_
  156.2 0.7 slice_convert_fusion
  157.0 0.7 convert_reduce_fusion
  157.7 1.1 copy-done.13
  158.8 12.1 %squares.1 = f32[1024,256]{1,0:T(8,128)} custom-call(s32[4]{0:T(128)} %get-tuple-element.52.order, s32[1]{0:T(128)} %bitcast.4.me, bf16[8,32,1024]{2,1,0:T(8,128)(2,1)} %copy-done.7, bf16[8,32,1024]{2,1,0:T(8,128)(2,1)} %copy-done.14, bf16[8,32,1024]{2,1,0:T(8,128)(2,1)} %collective-permute-done.7.refs_2_, ...), custom_call_target="tpu_custom_call" | custom-call | tf_op jit(solution)/shard_map/squares/pallas_call | solution.py:346
  (64 shorter events, 0.5 us)
Async XLA Ops:
  0.0 15.1 %collective-permute-start = (bf16[1024,256]{1,0:T(8,128)(2,1)}, bf16[1024,256]{1,0:T(8,128)(2,1)S(1)}, u32[]{:S(2)}, u32[]{:S(2)}) collective-permute-start(bf16[1024,256]{1,0:T(8,128)(2,1)} %bitcast.15), channel_id=1, source_target_pairs={{0,16},{8,24},{16,0},{24,8},{1,17},{9,25},{17,1},{25,9},{2,18},{10... | collective-permute-start | bytes 1572872 | tf_op jit(solution)/shard_map/ppermute | solution.py:27
  3.6 9.3 %copy-start = (bf16[1,1024,256]{2,1,0:T(8,128)(2,1)S(1)}, bf16[1,1024,256]{2,1,0:T(8,128)(2,1)}, u32[]{:S(2)}) copy-start(bf16[1,1024,256]{2,1,0:T(8,128)(2,1)} %param.15) | copy-start | bytes 1572868
  3.6 11.5 %copy-start.23 = (s32[12]{0:T(128)S(1)}, s32[12]{0:T(128)}, u32[]{:S(2)}) copy-start(s32[12]{0:T(128)} %constant.112.clone) | copy-start | bytes 148
  3.6 12.2 %copy-start.22 = (s32[12]{0:T(128)S(1)}, s32[12]{0:T(128)}, u32[]{:S(2)}) copy-start(s32[12]{0:T(128)} %constant.113.clone) | copy-start | bytes 148
  3.6 12.9 %copy-start.21 = (s32[1,4]{1,0:T(1,128)S(1)}, s32[1,4]{1,0:T(1,128)}, u32[]{:S(2)}) copy-start(s32[1,4]{1,0:T(1,128)} %param.17) | copy-start | bytes 52
  7.1 20.1 %all-to-all-start = ((bf16[8,32,1024]{2,1,0:T(8,128)(2,1)}), bf16[8,32,1024]{2,1,0:T(8,128)(2,1)S(1)}, u32[]{:S(2)}, u32[]{:S(2)}) async-start(bf16[8,32,1024]{2,1,0:T(8,128)(2,1)} %get-tuple-element.42), calls=%async_computation | async-start | bytes 1048576 | tf_op jit(solution)/shard_map/all_to_all | solution.py:274
  12.9 4.3 %collective-permute-start.1 = (bf16[1024,256]{1,0:T(8,128)(2,1)S(1)}, bf16[1024,256]{1,0:T(8,128)(2,1)S(1)}, u32[]{:S(2)}, u32[]{:S(2)}) collective-permute-start(bf16[1024,256]{1,0:T(8,128)(2,1)S(1)} %bitcast.20), channel_id=1, source_target_pairs={{0,8},{8,0},{16,24},{24,16},{1,9},{9,1},{17,25},{25,17},{2,10},{10... | collective-permute-start | bytes 1572872 | tf_op jit(solution)/shard_map/ppermute | solution.py:22
  12.9 4.3 %collective-permute-start.3 = (bf16[1024,256]{1,0:T(8,128)(2,1)}, bf16[1024,256]{1,0:T(8,128)(2,1)S(1)}, u32[]{:S(2)}, u32[]{:S(2)}) collective-permute-start(bf16[1024,256]{1,0:T(8,128)(2,1)} %get-tuple-element.41.refs_4_.refs_0_), channel_id=1, source_target_pairs={{0,8},{8,0},{16,24},{24,16},{1,9},{9,1},{17,25},{25,17},{2,10},{10... | collective-permute-start | bytes 1572872 | tf_op jit(solution)/shard_map/ppermute | solution.py:22
  15.1 2.1 %copy-start.1 = (bf16[1024,256]{1,0:T(8,128)(2,1)}, bf16[1024,256]{1,0:T(8,128)(2,1)S(1)}, u32[]{:S(2)}) copy-start(bf16[1024,256]{1,0:T(8,128)(2,1)S(1)} %collective-permute-done.refs_1_.refs_5_) | copy-start | bytes 1572868
  15.1 2.1 %collective-permute-start.2 = (bf16[1024,256]{1,0:T(8,128)(2,1)S(1)}, bf16[1024,256]{1,0:T(8,128)(2,1)S(1)}, u32[]{:S(2)}, u32[]{:S(2)}) collective-permute-start(bf16[1024,256]{1,0:T(8,128)(2,1)S(1)} %collective-permute-done.refs_1_.refs_5_), channel_id=1, source_target_pairs={{0,8},{8,0},{16,24},{24,16},{1,9},{9,1},{17,25},{25,17},{2,10},{10... | collective-permute-start | bytes 1572872 | tf_op jit(solution)/shard_map/ppermute | solution.py:22
  17.2 0.8 copy-start.2
  17.2 1.0 copy-start.10
  17.2 1.1 copy-start.3
  18.4 3.5 %copy-start.17 = (bf16[8,128,256]{2,1,0:T(8,128)(2,1)S(1)}, bf16[8,128,256]{2,1,0:T(8,128)(2,1)}, u32[]{:S(2)}) copy-start(bf16[8,128,256]{2,1,0:T(8,128)(2,1)} %get-tuple-element.40) | copy-start | bytes 1572868
  23.9 6.9 %copy-start.9 = (bf16[1024,256]{1,0:T(8,128)(2,1)S(1)}, bf16[1024,256]{1,0:T(8,128)(2,1)}, u32[]{:S(2)}) copy-start(bf16[1024,256]{1,0:T(8,128)(2,1)} %get-tuple-element.41.refs_4_.refs_0_) | copy-start | bytes 1572868
  27.1 19.0 %copy-start.7 = (bf16[8,32,1024]{2,1,0:T(8,128)(2,1)}, bf16[8,32,1024]{2,1,0:T(8,128)(2,1)S(1)}, u32[]{:S(2)}) copy-start(bf16[8,32,1024]{2,1,0:T(8,128)(2,1)S(1)} %all-to-all-done.rows_ref.refs_0_) | copy-start | bytes 1572868
  27.1 28.0 %all-to-all-start.1 = ((bf16[8,240,256]{2,1,0:T(8,128)(2,1)}), bf16[8,240,256]{2,1,0:T(8,128)(2,1)S(1)}, u32[]{:S(2)}, u32[]{:S(2)}) async-start(bf16[8,240,256]{2,1,0:T(8,128)(2,1)} %pad_maximum_fusion), calls=%async_computation.1 | async-start | bytes 1966080 | tf_op jit(solution)/shard_map/all_to_all | solution.py:294
  30.8 13.4 %collective-permute-start.4 = (bf16[1024,256]{1,0:T(8,128)(2,1)S(1)}, bf16[1024,256]{1,0:T(8,128)(2,1)S(1)}, u32[]{:S(2)}, u32[]{:S(2)}) collective-permute-start(bf16[1024,256]{1,0:T(8,128)(2,1)S(1)} %copy-done.9), channel_id=1, source_target_pairs={{0,16},{8,24},{16,0},{24,8},{1,17},{9,25},{17,1},{25,9},{2,18},{10... | collective-permute-start | bytes 1572872 | tf_op jit(solution)/shard_map/ppermute | solution.py:27
  44.2 1.9 %copy-start.15 = (bf16[1024,256]{1,0:T(8,128)(2,1)}, bf16[1024,256]{1,0:T(8,128)(2,1)S(1)}, u32[]{:S(2)}) copy-start(bf16[1024,256]{1,0:T(8,128)(2,1)S(1)} %collective-permute-done.4.refs_1_) | copy-start | bytes 1572868
  44.2 1.9 %collective-permute-start.5 = (bf16[1024,256]{1,0:T(8,128)(2,1)S(1)}, bf16[1024,256]{1,0:T(8,128)(2,1)S(1)}, u32[]{:S(2)}, u32[]{:S(2)}) collective-permute-start(bf16[1024,256]{1,0:T(8,128)(2,1)S(1)} %collective-permute-done.4.refs_1_), channel_id=1, source_target_pairs={{0,8},{8,0},{16,24},{24,16},{1,9},{9,1},{17,25},{25,17},{2,10},{10... | collective-permute-start | bytes 1572872 | tf_op jit(solution)/shard_map/ppermute | solution.py:22
  46.1 0.8 copy-start.16
  55.1 1.1 copy-start.5
  56.1 3.8 %copy-start.8 = (bf16[8,32,1024]{2,1,0:T(8,128)(2,1)S(1)}, bf16[8,32,1024]{2,1,0:T(8,128)(2,1)}, u32[]{:S(2)}) copy-start(bf16[8,32,1024]{2,1,0:T(8,128)(2,1)} %copy-done.7) | copy-start | bytes 1572868
  56.2 35.3 %all-to-all-start.2 = ((bf16[8,320,256]{2,1,0:T(8,128)(2,1)}), bf16[8,320,256]{2,1,0:T(8,128)(2,1)S(1)}, u32[]{:S(2)}, u32[]{:S(2)}) async-start(bf16[8,320,256]{2,1,0:T(8,128)(2,1)} %broadcast_dynamic-update-slice_fusion), calls=%async_computation.2 | async-start | bytes 2621440 | tf_op jit(solution)/shard_map/all_to_all | solution.py:308
  59.9 13.6 %collective-permute-start.6 = (bf16[8,32,1024]{2,1,0:T(8,128)(2,1)S(1)}, bf16[8,32,1024]{2,1,0:T(8,128)(2,1)S(1)}, u32[]{:S(2)}, u32[]{:S(2)}) collective-permute-start(bf16[8,32,1024]{2,1,0:T(8,128)(2,1)S(1)} %copy-done.8), channel_id=1, source_target_pairs={{0,16},{8,24},{16,0},{24,8},{1,17},{9,25},{17,1},{25,9},{2,18},{10... | collective-permute-start | bytes 1572872 | tf_op jit(solution)/shard_map/ppermute | solution.py:27
  61.5 33.6 %collective-permute-start.7 = (bf16[8,32,1024]{2,1,0:T(8,128)(2,1)S(1)}, bf16[8,32,1024]{2,1,0:T(8,128)(2,1)}, u32[]{:S(2)}, u32[]{:S(2)}) collective-permute-start(bf16[8,32,1024]{2,1,0:T(8,128)(2,1)S(1)} %copy-done.8), channel_id=1, source_target_pairs={{0,8},{8,0},{16,24},{24,16},{1,9},{9,1},{17,25},{25,17},{2,10},{10... | collective-permute-start | bytes 1572872 | tf_op jit(solution)/shard_map/ppermute | solution.py:22
  73.5 3.5 %copy-start.14 = (bf16[8,32,1024]{2,1,0:T(8,128)(2,1)}, bf16[8,32,1024]{2,1,0:T(8,128)(2,1)S(1)}, u32[]{:S(2)}) copy-start(bf16[8,32,1024]{2,1,0:T(8,128)(2,1)S(1)} %collective-permute-done.6.refs_1_) | copy-start | bytes 1572868
  73.5 21.6 %collective-permute-start.8 = (bf16[8,32,1024]{2,1,0:T(8,128)(2,1)S(1)}, bf16[8,32,1024]{2,1,0:T(8,128)(2,1)}, u32[]{:S(2)}, u32[]{:S(2)}) collective-permute-start(bf16[8,32,1024]{2,1,0:T(8,128)(2,1)S(1)} %collective-permute-done.6.refs_1_), channel_id=1, source_target_pairs={{0,8},{8,0},{16,24},{24,16},{1,9},{9,1},{17,25},{25,17},{2,10},{10... | collective-permute-start | bytes 1572872 | tf_op jit(solution)/shard_map/ppermute | solution.py:22
  91.5 18.3 %copy-start.4 = (bf16[8,320,256]{2,1,0:T(8,128)(2,1)}, bf16[8,320,256]{2,1,0:T(8,128)(2,1)S(1)}, u32[]{:S(2)}) copy-start(bf16[8,320,256]{2,1,0:T(8,128)(2,1)S(1)} %all-to-all-done.2.sums_ref) | copy-start | bytes 3932164
  91.5 18.3 %all-to-all-start.3 = ((bf16[8,128,256]{2,1,0:T(8,128)(2,1)}), bf16[8,128,256]{2,1,0:T(8,128)(2,1)S(1)}, u32[]{:S(2)}, u32[]{:S(2)}) async-start(bf16[8,128,256]{2,1,0:T(8,128)(2,1)} %project_cot.1), calls=%async_computation.3 | async-start | bytes 1048576 | tf_op jit(solution)/shard_map/all_to_all | solution.py:320
  95.1 14.7 %copy-start.12 = (bf16[8,96,256]{2,1,0:T(8,128)(2,1)}, bf16[8,96,256]{2,1,0:T(8,128)(2,1)S(1)}, u32[]{:S(2)}) copy-start(bf16[8,96,256]{2,1,0:T(8,128)(2,1)S(1)} %slice.61) | copy-start | bytes 1179652
  95.2 10.8 %collective-permute-start.9 = (bf16[3,256,256]{2,1,0:T(8,128)(2,1)S(1)}, bf16[3,256,256]{2,1,0:T(8,128)(2,1)S(1)}, u32[]{:S(2)}, u32[]{:S(2)}) collective-permute-start(bf16[3,256,256]{2,1,0:T(8,128)(2,1)S(1)} %bitcast.21), channel_id=1, source_target_pairs={{0,16},{8,24},{16,0},{24,8},{1,17},{9,25},{17,1},{25,9},{2,18},{10... | collective-permute-start | bytes 1179656 | tf_op jit(solution)/shard_map/ppermute | solution.py:27
  96.7 13.0 %collective-permute-start.10 = (bf16[3,256,256]{2,1,0:T(8,128)(2,1)S(1)}, bf16[3,256,256]{2,1,0:T(8,128)(2,1)S(1)}, u32[]{:S(2)}, u32[]{:S(2)}) collective-permute-start(bf16[3,256,256]{2,1,0:T(8,128)(2,1)S(1)} %bitcast.22), channel_id=1, source_target_pairs={{0,8},{8,0},{16,24},{24,16},{1,9},{9,1},{17,25},{25,17},{2,10},{10... | collective-permute-start | bytes 1179656 | tf_op jit(solution)/shard_map/ppermute | solution.py:22
  106.0 3.8 %copy-start.18 = (bf16[3,256,256]{2,1,0:T(8,128)(2,1)}, bf16[3,256,256]{2,1,0:T(8,128)(2,1)S(1)}, u32[]{:S(2)}) copy-start(bf16[3,256,256]{2,1,0:T(8,128)(2,1)S(1)} %collective-permute-done.9.refs_1_) | copy-start | bytes 1179652
  106.0 3.8 %collective-permute-start.11 = (bf16[3,256,256]{2,1,0:T(8,128)(2,1)S(1)}, bf16[3,256,256]{2,1,0:T(8,128)(2,1)S(1)}, u32[]{:S(2)}, u32[]{:S(2)}) collective-permute-start(bf16[3,256,256]{2,1,0:T(8,128)(2,1)S(1)} %collective-permute-done.9.refs_1_), channel_id=1, source_target_pairs={{0,8},{8,0},{16,24},{24,16},{1,9},{9,1},{17,25},{25,17},{2,10},{10... | collective-permute-start | bytes 1179656 | tf_op jit(solution)/shard_map/ppermute | solution.py:22
  109.8 0.8 copy-start.11
  109.8 0.9 copy-start.19
  109.8 1.1 copy-start.20
  116.1 4.5 %collective-permute-start.12 = (bf16[5,32,256]{2,1,0:T(8,128)(2,1)S(1)}, bf16[5,32,256]{2,1,0:T(8,128)(2,1)S(1)}, u32[]{:S(2)}, u32[]{:S(2)}) collective-permute-start(bf16[5,32,256]{2,1,0:T(8,128)(2,1)S(1)} %get-tuple-element.54), channel_id=1, source_target_pairs={{0,16},{8,24},{16,0},{24,8},{1,17},{9,25},{17,1},{25,9},{2,18},{10... | collective-permute-start | bytes 245768 | tf_op jit(solution)/shard_map/ppermute | solution.py:27
  154.7 3.0 %copy-start.6 = (bf16[8,2,5,32,256]{4,3,2,1,0:T(8,128)(2,1)}, bf16[8,2,5,32,256]{4,3,2,1,0:T(8,128)(2,1)S(1)}, u32[]{:S(2)}) copy-start(bf16[8,2,5,32,256]{4,3,2,1,0:T(8,128)(2,1)S(1)} %all_to_all.25.refs_8_) | copy-start | bytes 3932164
  154.7 3.0 %collective-permute-start.13 = (bf16[8,2,5,32,256]{4,3,2,1,0:T(8,128)(2,1)S(1)}, bf16[8,2,5,32,256]{4,3,2,1,0:T(8,128)(2,1)S(1)}, u32[]{:S(2)}, u32[]{:S(2)}) collective-permute-start(bf16[8,2,5,32,256]{4,3,2,1,0:T(8,128)(2,1)S(1)} %all_to_all.25.refs_8_), channel_id=1, source_target_pairs={{0,8},{8,0},{16,24},{24,16},{1,9},{9,1},{17,25},{25,17},{2,10},{10... | collective-permute-start | bytes 3932168 | tf_op jit(solution)/shard_map/ppermute | solution.py:22
  157.7 1.1 copy-start.13

commit v3 on v2

--- a/solution.py
+++ b/solution.py
@@ -41,9 +41,19 @@
     return same + [core_swap(b) for b in same]
 
 
-def spread(x):
+def pair_swap(x):
     peers = lax.axis_size("dp")
-    return lax.all_to_all(jnp.broadcast_to(x[None], (peers,) + x.shape), "dp", 0, 0, tiled=True)
+    return lax.ppermute(x, "dp", [(i, i ^ 1) for i in range(peers)])
+
+
+def line_exchange(x):
+    peers = lax.axis_size("dp")
+    groups = [list(range(p, peers, 2)) for p in range(2)]
+    return lax.all_to_all(x, "dp", 0, 0, axis_index_groups=groups, tiled=True)
+
+
+def repeated(x, times):
+    return jnp.broadcast_to(x[None], (times,) + x.shape)
 
 
 def gram_pairs(count):
@@ -57,19 +67,16 @@
     return listed
 
 
-def prepare_kernel(place, tokens_ref, cot_ref, down_ref, gain_ref, rows_ref, cot_rows_ref, square_ref, weight_ref):
-    peers, t, block = rows_ref.shape
-    r = down_ref.shape[2]
-    pieces = block // r
+def prepare_kernel(place, tokens_ref, cot_ref, down_ref, gain_ref, rows_ref, square_ref, weight_ref):
+    peers, rows, block = rows_ref.shape
+    t = rows // 2
     total = jnp.zeros((t, 1), f32)
     for n in range(peers):
         piece = tokens_ref[:, n * block : (n + 1) * block]
         wide = piece.astype(f32)
         total = total + jnp.sum(wide * wide, axis=-1, keepdims=True)
-        rows_ref[n] = piece
-        for b in range(pieces):
-            start = n * block + b * r
-            cot_rows_ref[n, b * t : (b + 1) * t] = cot_ref[:, start : start + r]
+        rows_ref[n, :t] = piece
+        rows_ref[n, t:] = cot_ref[:, n * block : (n + 1) * block]
     square_ref[...] = total
     gain = gain_ref[...].reshape(block, 1)
     weight_ref[...] = (down_ref[0].astype(f32) * gain).astype(bf16)
@@ -87,40 +94,43 @@
         gram_ref[p] = dot(table[2 + left[p]], table[right[p]], 0, 0).astype(bf16)
 
 
-def project_kernel(count, room, order, rows_ref, *refs):
+def project_kernel(count, order, spot, rows_ref, *refs):
     downs = refs[:count]
     ups = refs[count : 2 * count]
-    part_ref = refs[2 * count]
-    peers, t, width = rows_ref.shape
-    r = part_ref.shape[2]
-    x = rows_ref[...].reshape(peers * t, width)
-
-    def place(m):
-        return pl.ds(pl.multiple_of(room + m * t, t), t)
+    keep_ref, send_ref, tokens_ref = refs[2 * count :]
+    peers, rows, width = rows_ref.shape
+    t = rows // 2
+    half, _, r = keep_ref.shape
+    mine = lax.rem(spot[0], 2)
+    tokens_ref[...] = rows_ref[:, :t]
+    picked = [rows_ref[2 * z + mine, :t] for z in range(half)]
+    picked += [rows_ref[2 * z + 1 - mine, :t] for z in range(half)]
+    x = jnp.concatenate(picked, axis=0)
+
+    def store(m, out):
+        place = pl.ds(pl.multiple_of(m * t, t), t)
+        keep_ref[:, place, :] = out[: half * t].reshape(half, t, r)
+        send_ref[:, place, :] = out[half * t :].astype(bf16).reshape(half, t, r)
 
     for i in range(count):
         layer = order[i]
-        out = dot(x, downs[i][...], 1, 0)
-        part_ref[:, place(layer), :] = out.astype(bf16).reshape(peers, t, r)
+        store(layer, dot(x, downs[i][...], 1, 0))
 
         @pl.when(layer < count - 1)
         def _():
-            out = dot(x, ups[i][...], 1, 0)
-            part_ref[:, place(count + layer), :] = out.astype(bf16).reshape(peers, t, r)
-
-
-def project_cot_kernel(count, order, packed_ref, *refs):
+            store(count + layer, dot(x, ups[i][...], 1, 0))
+
+
+def project_cot_kernel(count, room, order, rows_ref, *refs):
     ups = refs[:count]
     part_ref = refs[count]
-    peers, rows, r = part_ref.shape
-    t = rows // count
-    width = ups[0].shape[0]
-    c = jnp.concatenate(
-        [packed_ref[:, b * t : (b + 1) * t].reshape(peers * t, r) for b in range(width // r)], axis=1
-    )
+    peers, rows, width = rows_ref.shape
+    t = rows // 2
+    r = part_ref.shape[2]
+    c = rows_ref[:, t:].reshape(peers * t, width)
     for i in range(count):
         out = dot(c, ups[i][...], 1, 0)
-        start = pl.multiple_of(order[i] * t, t)
+        start = pl.multiple_of(room + order[i] * t, t)
         part_ref[:, pl.ds(start, t), :] = out.astype(bf16).reshape(peers, t, r)
 
 
@@ -145,9 +155,9 @@
     def total(ref, start):
         return jnp.sum(ref[:, start : start + t].astype(f32), axis=0)
 
-    proj = [total(sums_ref, room + l * t) for l in range(count)]
-    hu = [total(sums_ref, room + (count + k) * t) for k in range(count - 1)]
-    back = [total(back_ref, l * t) for l in range(count)]
+    proj = [total(sums_ref, l * t) for l in range(count)]
+    hu = [total(sums_ref, (count + k) * t) for k in range(count - 1)]
+    back = [total(back_ref, room + l * t) for l in range(count)]
     norm = sq_ref[...]
     invs, pres, hus = [], [], []
     for l in range(count):
@@ -183,27 +193,32 @@
         out_ref[j, 1] = grads[2 * other + 1]
 
 
-def fisher_kernel(count, seqs, scale, order, me, *refs):
+def fisher_kernel(count, seqs, scale, order, place, *refs):
+    half = count // 2
     rows = refs[:count]
     ups = refs[count : 2 * count]
-    same_ref, other_ref, seg_ref, gain_ref, out_ref, acc, hidden, masks = refs[2 * count :]
-    half = count // 2
+    states = refs[2 * count : 4 * count]
+    seg_ref, gain_ref, out_ref, acc, hidden, masks = refs[4 * count :]
     peers, t, width = rows[0].shape
     r = out_ref.shape[1]
     chunk = min(r, width)
     span = count * t
+    me = place[0]
+    mine = lax.rem(place[1], 2)
+    line = peers // 2
+    names = [2 * (n % line) + (mine if n < line else 1 - mine) for n in range(peers)]
 
     def column(n, m):
-        parts = [same_ref[n, j, m] for j in range(half)] + [other_ref[n, j, m] for j in range(half)]
-        return jnp.concatenate(parts, axis=0)
+        first = n // line * count
+        return jnp.concatenate([states[first + i][n % line, m] for i in range(count)], axis=0)
 
     acts = []
     for i in range(1, count):
         act = jnp.concatenate([column(n, 2 + jnp.minimum(order[i], count - 2)) for n in range(peers)], axis=0)
-        acts.append(jnp.where(order[i] < me[0], act, jnp.zeros_like(act)))
+        acts.append(jnp.where(order[i] < me, act, jnp.zeros_like(act)))
     for n in range(peers):
-        grad = column(n, lax.rem(me[0], 2)).astype(f32).T
-        seg = seg_ref[n]
+        grad = column(n, lax.rem(me, 2)).astype(f32).T
+        seg = seg_ref[names[n]]
         for q in range(seqs):
             masks[n, q * r : (q + 1) * r] = jnp.where(seg == q, grad, 0.0).astype(bf16)
     for f in range(width // chunk):
@@ -212,7 +227,7 @@
         for i in range(2, count):
             update = update + dot(acts[i - 1], ups[i][cols], 1, 1)
         for n in range(peers):
-            h = jnp.concatenate([rows[i][n, :, cols] for i in range(count)], axis=0).astype(f32)
+            h = jnp.concatenate([rows[i][names[n], :, cols] for i in range(count)], axis=0).astype(f32)
             hidden[n] = (h + update[n * span : (n + 1) * span]).astype(bf16)
         for n in range(peers):
             g = dot(masks[n], hidden[n], 1, 0)
@@ -243,7 +258,8 @@
     vmem = pl.BlockSpec(memory_space=pltpu.VMEM)
 
     ups = gather_section(up_weight[0])
-    token_send, cot_send, square, weight = pl.pallas_call(
+    place = jnp.stack([me, spot]).astype(jnp.int32)
+    send, square, weight = pl.pallas_call(
         prepare_kernel,
         grid_spec=pltpu.PrefetchScalarGridSpec(
             num_scalar_prefetch=1,
@@ -255,23 +271,21 @@
                 pl.BlockSpec((1, block), lambda n, place: (0, place[1])),
             ],
             out_specs=[
-                pl.BlockSpec((peers, t, block), lambda n, place: (0, 0, 0)),
-                pl.BlockSpec((peers, t * (block // r), r), lambda n, place: (0, 0, 0)),
+                pl.BlockSpec((peers, 2 * t, block), lambda n, place: (0, 0, 0)),
                 pl.BlockSpec((t, 1), lambda n, place: (0, 0)),
                 pl.BlockSpec((block, r), lambda n, place: (0, 0)),
             ],
         ),
         out_shape=(
-            jax.ShapeDtypeStruct((peers, t, block), bf16),
-            jax.ShapeDtypeStruct((peers, t * (block // r), r), bf16),
+            jax.ShapeDtypeStruct((peers, 2 * t, block), bf16),
             jax.ShapeDtypeStruct((t, 1), f32),
             jax.ShapeDtypeStruct((block, r), bf16),
         ),
         compiler_params=params,
         name="prepare",
-    )(jnp.stack([me, spot]).astype(jnp.int32), tokens, cotangent, down_weight, norm_gain)
+    )(place, tokens, cotangent, down_weight, norm_gain)
     downs = gather_section(weight)
-    token_rows = lax.all_to_all(token_send, "dp", 0, 0, tiled=True)
+    rows = lax.all_to_all(send, "dp", 0, 0, tiled=True)
 
     pairs = gram_pairs(count)
     left = lax.dynamic_slice_in_dim(jnp.array([a for a, _ in pairs], jnp.int32), me * (count - 1), count - 1)
@@ -288,37 +302,40 @@
     )(order, left, right, *ups, downs[0], downs[count // 2])
     line = jnp.zeros((peers, 16, r), bf16).at[:, 0, : lengths.shape[1]].set(lengths.astype(bf16))
     gram_rows = (count - 1) * r // peers
-    cot_rows = cot_send.shape[1]
-    packed = jnp.concatenate([cot_send, gram.reshape(peers, gram_rows, r), line], axis=1)
-    packed, token_rows = lax.optimization_barrier((packed, token_rows))
+    packed = jnp.concatenate([gram.reshape(peers, gram_rows, r), line], axis=1)
+    packed, rows = lax.optimization_barrier((packed, rows))
     packed = lax.all_to_all(packed, "dp", 0, 0, tiled=True)
 
     room = -(-gram_rows // t) * t
-    part = pl.pallas_call(
-        functools.partial(project_kernel, count, room),
-        out_shape=jax.ShapeDtypeStruct((peers, room + (2 * count - 1) * t, r), bf16),
-        in_specs=[smem] + [vmem] * (1 + 2 * count),
-        out_specs=vmem,
-        compiler_params=params,
-        name="project",
-    )(order, token_rows, *downs, *ups)
-    gram_sum = jnp.sum(packed[:, cot_rows : cot_rows + gram_rows].astype(f32), axis=0).astype(bf16)
-    all_lengths = packed[:, cot_rows + gram_rows, : lengths.shape[1]].astype(jnp.int32)
-    part = part.at[:, :gram_rows].set(jnp.broadcast_to(gram_sum[None], (peers,) + gram_sum.shape))
-    sums = lax.all_to_all(part, "dp", 0, 0, tiled=True)
-
     back_part = pl.pallas_call(
-        functools.partial(project_cot_kernel, count),
-        out_shape=jax.ShapeDtypeStruct((peers, count * t, r), bf16),
+        functools.partial(project_cot_kernel, count, room),
+        out_shape=jax.ShapeDtypeStruct((peers, room + count * t, r), bf16),
         in_specs=[smem] + [vmem] * (1 + count),
         out_specs=vmem,
         compiler_params=params,
         name="project_cot",
-    )(order, packed, *ups)
+    )(order, rows, *ups)
+    keep, give, token_rows = pl.pallas_call(
+        functools.partial(project_kernel, count),
+        out_shape=(
+            jax.ShapeDtypeStruct((peers // 2, (2 * count - 1) * t, r), f32),
+            jax.ShapeDtypeStruct((peers // 2, (2 * count - 1) * t, r), bf16),
+            jax.ShapeDtypeStruct((peers, t, block), bf16),
+        ),
+        in_specs=[smem, smem] + [vmem] * (1 + 2 * count),
+        out_specs=(vmem, vmem, vmem),
+        compiler_params=params,
+        name="project",
+    )(order, spot.astype(jnp.int32)[None], rows, *downs, *ups)
+    part = (keep + pair_swap(give).astype(f32)).astype(bf16)
+    gram_sum = jnp.sum(packed[:, :gram_rows].astype(f32), axis=0).astype(bf16)
+    all_lengths = packed[:, gram_rows, : lengths.shape[1]].astype(jnp.int32)
+    back_part = back_part.at[:, :gram_rows].set(repeated(gram_sum, peers))
+    back_sums = lax.all_to_all(back_part, "dp", 0, 0, tiled=True)
     all_rows = gather_section(token_rows)
-    sums, all_rows = lax.optimization_barrier((sums, all_rows))
-    back_sums = lax.all_to_all(back_part, "dp", 0, 0, tiled=True)
-    grams = gather_section(sums[:, :gram_rows].reshape(count - 1, r, r))
+    back_sums, part, all_rows = lax.optimization_barrier((back_sums, part, all_rows))
+    sums = line_exchange(part)
+    grams = gather_section(back_sums[:, :gram_rows].reshape(count - 1, r, r))
 
     held = pl.pallas_call(
         functools.partial(recur_kernel, count, width, room),
@@ -332,21 +349,28 @@
         compiler_params=params,
         name="recur",
     )(order, sums, back_sums, square, *grams)
-    same = spread(jnp.stack([held[0]] + [chip_shift(held[j], j) for j in range(1, count // 2)]))
-    other = core_swap(same)
-
     ends = jnp.cumsum(all_lengths, axis=1)
     position = (order[:, None] * t + jnp.arange(t, dtype=jnp.int32)[None]).reshape(-1)
     seg = jnp.sum(position[None, None, :] >= ends[:, :, None], axis=1).astype(jnp.int32)
     seg = seg.reshape(peers, 1, row_count)
     gain = lax.dynamic_slice_in_dim(norm_gain, spot * block, block, 1)
+    held, seg, gain = lax.optimization_barrier((held, seg, gain))
+
+    line = peers // 2
+    states = [[None] * count, [None] * count]
+    for j in range(count // 2):
+        block_j = chip_shift(held[j], j) if j else held[0]
+        got = line_exchange(repeated(block_j, line))
+        for p, part in enumerate((got, pair_swap(got))):
+            states[p][j] = part
+            states[p][count // 2 + j] = core_swap(part)
 
     seqs = lengths.shape[1]
     chunk = min(r, block)
     fisher = pl.pallas_call(
         functools.partial(fisher_kernel, count, seqs, 1.0 / (row_count * peers)),
         out_shape=jax.ShapeDtypeStruct((block, r), f32),
-        in_specs=[smem, smem] + [vmem] * (2 * count + 4),
+        in_specs=[smem, smem] + [vmem] * (4 * count + 2),
         out_specs=vmem,
         scratch_shapes=[
             pltpu.VMEM((r, chunk), f32),
@@ -355,7 +379,7 @@
         ],
         compiler_params=params,
         name="squares",
-    )(order, me.astype(jnp.int32)[None], *all_rows, *ups, same, other, seg, gain)
+    )(order, place, *all_rows, *ups, *states[0], *states[1], seg, gain)
     return fisher[None]
 
 

time: 172 us -> 160 us (0.930)
  blocking collectives: 33.9 us -> 0 us
  starting transfers between devices: 25.9 us -> 38 us
  waiting for transfers between devices: 64.5 us -> 72.6 us
    all_to_all x1 -> x0, blocking collectives: 33.9 us -> none  [spread(): lax.all_to_all(jnp.broadcast_to(x[None], (peers,) + x.shape), 'dp', 0, 0,...]
    all_to_all x2 -> x4, starting transfers between devices: 9.51 us -> 19.2 us  [the longest x3 11.8 us: line_exchange(): return lax.all_to_all(x, 'dp', 0, 0, axis_index_groups=groups, tiled=True)]
    ppermute x0 -> x3, waiting for transfers between devices: none -> 8.17 us  [pair_swap(): return lax.ppermute(x, 'dp', [(i, i ^ 1) for i in range(peers)])]
    ppermute x5, waiting for transfers between devices: 38.4 us -> 30.4 us  [chip_shift(): lax.ppermute(x, 'section', [(i, (i - 2 * by) % count) for i in range(coun...]
    all_to_all x1, waiting for transfers between devices: 2.72 us -> 8.26 us  [per_device(): packed = lax.all_to_all(packed, 'dp', 0, 0, tiled=True)]
    all_to_all x2 -> x4, waiting for transfers between devices: 17.6 us -> 22.3 us  [the longest x3 18.1 us: line_exchange(): return lax.all_to_all(x, 'dp', 0, 0, axis_index_groups=groups, tiled=True)]
    ppermute x0 -> x3, starting transfers between devices: none -> 3.84 us  [pair_swap(): return lax.ppermute(x, 'dp', [(i, i ^ 1) for i in range(peers)])]
    all_to_all x1, waiting for transfers between devices: 3.78 us -> 0.01 us  [per_device(): back_sums = lax.all_to_all(back_part, 'dp', 0, 0, tiled=True)]
  transfers between devices with their start and end apart: 18 -> 26, of which waited for: 10 -> 13; matrix products, arithmetic and copies ran while one was open for 5% -> 6% of each run, Pallas kernels for 9% -> 8%
where the time goes in v3:
time: 160 us; the launch traced here: 159 us
  waiting for transfers between devices  72.6 us (45%)
  starting transfers between devices  38 us (24%)
  Pallas kernels  32.5 us (20%)
  local copies, waits for them, and re-layouts  10.3 us (6%)
  other arithmetic  5.93 us (4%)
    ppermute x5, waiting for transfers between devices, chip_shift(): lax.ppermute(x, 'section', [(i, (i - 2 * by) % count) for i in range(coun...  30.4 us
    all_to_all x3, waiting for transfers between devices, line_exchange(): return lax.all_to_all(x, 'dp', 0, 0, axis_index_groups=groups, tiled=True)  18.1 us
    pallas_call x1, Pallas kernels, per_device(): pl.pallas_call(functools.partial(fisher_kernel, count, seqs, 1.0 / (row_c...  12 us
    all_to_all x3, starting transfers between devices, line_exchange(): return lax.all_to_all(x, 'dp', 0, 0, axis_index_groups=groups, tiled=True)  11.8 us
    all_to_all x1, waiting for transfers between devices, per_device(): packed = lax.all_to_all(packed, 'dp', 0, 0, tiled=True)  8.26 us
    ppermute x3, waiting for transfers between devices, pair_swap(): return lax.ppermute(x, 'dp', [(i, i ^ 1) for i in range(peers)])  8.17 us
    all_to_all x1, starting transfers between devices, per_device(): rows = lax.all_to_all(send, 'dp', 0, 0, tiled=True)  7.4 us
    ppermute x5, starting transfers between devices, chip_shift(): lax.ppermute(x, 'section', [(i, (i - 2 * by) % count) for i in range(coun...  6.52 us
  transfers between devices with their start and end apart: 26, of which 13 were waited for; matrix products, arithmetic and copies ran while one was open for 6% of the time, Pallas kernels for 8%

profile of v3, /device:TPU:0, one launch (start us, length us, event | category | flops | bytes accessed | tf_op | source)
XLA Modules:
  0.0 159.5 jit_solution(12765346381516962244)
XLA Ops:
  0.6 3.5 %prepare.1 = (bf16[8,64,1024]{2,1,0:T(8,128)(2,1)}, f32[32,1]{1,0:T(8,128)}, bf16[1024,256]{1,0:T(8,128)(2,1)}) custom-call(s32[2]{0:T(128)} %pad_add_fusion.1.place, bf16[128,8192]{1,0:T(8,128)(2,1)} %tokens_ref.1, bf16[128,8192]{1,0:T(8,128)(2,1)} %cot_ref.1, bf16[1,1024,256]{2,1,0:T(8,128)(2,1)} %down_ref.1, f32[1,8192]{1,0:T(1,128)} %gain_ref.1), custom_call_target="tpu_custom_call" | custom-call | tf_op jit(solution)/shard_map/prepare/pallas_call | solution.py:262
  4.1 7.4 %all-to-all-start = ((bf16[8,64,1024]{2,1,0:T(8,128)(2,1)}), bf16[8,64,1024]{2,1,0:T(8,128)(2,1)S(1)}, u32[]{:S(2)}, u32[]{:S(2)}) async-start(bf16[8,64,1024]{2,1,0:T(8,128)(2,1)} %get-tuple-element.47), calls=%async_computation | async-start | bytes 2097152 | tf_op jit(solution)/shard_map/all_to_all | solution.py:288
  11.5 1.6 collective-permute-start
  13.6 11.4 %collective-permute-done.refs_1_.refs_5_ = bf16[1024,256]{1,0:T(8,128)(2,1)S(1)} collective-permute-done((bf16[1024,256]{1,0:T(8,128)(2,1)S(1)}, bf16[1024,256]{1,0:T(8,128)(2,1)S(1)}, u32[]{:S(2)}, u32[]{:S(2)}) %collective-permute-start) | collective-permute-done | bytes 524320 | tf_op jit(solution)/shard_map/ppermute | solution.py:27
  25.0 0.7 dynamic_slice.9.left
  25.6 0.6 dynamic_slice.10.right
  26.9 0.7 copy-done.3
  27.9 3.4 %gram.1 = bf16[3,256,256]{2,1,0:T(8,128)(2,1)} custom-call(s32[4]{0:T(128)} %get-tuple-element.64.order, s32[3]{0:T(128)} %dynamic_slice.9.left, s32[3]{0:T(128)} %dynamic_slice.10.right, bf16[1024,256]{1,0:T(8,128)(2,1)} %bitcast.18, bf16[1024,256]{1,0:T(8,128)(2,1)} %copy-done.2, bf16[1024,256]{1,0:T(8,128)(2,1)} %copy-done.3, ...), custom_call_target="tpu_custom_call" | custom-call | tf_op jit(solution)/shard_map/gram/pallas_call | solution.py:294
  31.3 1.8 %pad_maximum_fusion = bf16[8,112,256]{2,1,0:T(8,128)(2,1)} fusion(bf16[8,16,256]{2,1,0:T(8,128)(2,1)S(1)} %scatter.13, bf16[8,96,256]{2,1,0:T(8,128)(2,1)} %bitcast.24), kind=kLoop, calls=%fused_computation.1 | loop fusion | flops 917504 | bytes 917504 | tf_op jit(solution)/shard_map/concatenate | solution.py:305
  33.1 4.1 %all-to-all-done.rows_ref = bf16[8,64,1024]{2,1,0:T(8,128)(2,1)S(1)} async-done(((bf16[8,64,1024]{2,1,0:T(8,128)(2,1)}), bf16[8,64,1024]{2,1,0:T(8,128)(2,1)S(1)}, u32[]{:S(2)}, u32[]{:S(2)}) %all-to-all-start) | async-done | bytes 1048608 | tf_op jit(solution)/shard_map/all_to_all | solution.py:288
  37.3 3.6 %all-to-all-start.1 = ((bf16[8,112,256]{2,1,0:T(8,128)(2,1)}), bf16[8,112,256]{2,1,0:T(8,128)(2,1)S(1)}, u32[]{:S(2)}, u32[]{:S(2)}) async-start(bf16[8,112,256]{2,1,0:T(8,128)(2,1)} %pad_maximum_fusion), calls=%async_computation.1 | async-start | bytes 917504 | tf_op jit(solution)/shard_map/all_to_all | solution.py:307
  40.9 1.5 collective-permute-start.4
  42.4 3.5 %project_cot.1 = bf16[8,224,256]{2,1,0:T(8,128)(2,1)} custom-call(s32[4]{0:T(128)} %get-tuple-element.64.order, bf16[8,64,1024]{2,1,0:T(8,128)(2,1)} %copy-done, bf16[1024,256]{1,0:T(8,128)(2,1)} %bitcast.19, bf16[1024,256]{1,0:T(8,128)(2,1)} %copy-done.2, bf16[1024,256]{1,0:T(8,128)(2,1)} %copy-done.3, bf16[1024,256]{1,0:T(8,128)(2,1)} %copy-done.4), custom_call_target="tpu_custom_call" | custom-call | tf_op jit(solution)/shard_map/project_cot/pallas_call | solution.py:310
  45.9 8.3 %all-to-all-done.1 = bf16[8,112,256]{2,1,0:T(8,128)(2,1)S(1)} async-done(((bf16[8,112,256]{2,1,0:T(8,128)(2,1)}), bf16[8,112,256]{2,1,0:T(8,128)(2,1)S(1)}, u32[]{:S(2)}, u32[]{:S(2)}) %all-to-all-start.1) | async-done | bytes 458784 | tf_op jit(solution)/shard_map/all_to_all | solution.py:307
  54.2 0.8 broadcast_dynamic-update-slice_fusion
  55.0 3.6 %all-to-all-start.2 = ((bf16[8,224,256]{2,1,0:T(8,128)(2,1)}), bf16[8,224,256]{2,1,0:T(8,128)(2,1)S(1)}, u32[]{:S(2)}, u32[]{:S(2)}) async-start(bf16[8,224,256]{2,1,0:T(8,128)(2,1)} %broadcast_dynamic-update-slice_fusion), calls=%async_computation.2 | async-start | bytes 1835008 | tf_op jit(solution)/shard_map/all_to_all | solution.py:334
  58.7 1.9 %collective-permute-done.5.refs_3_ = bf16[1024,256]{1,0:T(8,128)(2,1)S(1)} collective-permute-done((bf16[1024,256]{1,0:T(8,128)(2,1)S(1)}, bf16[1024,256]{1,0:T(8,128)(2,1)S(1)}, u32[]{:S(2)}, u32[]{:S(2)}) %collective-permute-start.5) | collective-permute-done | bytes 524320 | tf_op jit(solution)/shard_map/ppermute | solution.py:22
  60.6 0.8 copy-done.14
  61.4 5.9 %project.1 = (f32[4,224,256]{2,1,0:T(8,128)}, bf16[4,224,256]{2,1,0:T(8,128)(2,1)}, bf16[8,32,1024]{2,1,0:T(8,128)(2,1)}) custom-call(s32[4]{0:T(128)} %get-tuple-element.64.order, s32[1]{0:T(128)} %bitcast.5.spot, bf16[8,64,1024]{2,1,0:T(8,128)(2,1)} %copy-done, bf16[1024,256]{1,0:T(8,128)(2,1)} %get-tuple-element.46.refs_4_.refs_0_, ...), custom_call_target="tpu_custom_call" | custom-call | tf_op jit(solution)/shard_map/project/pallas_call | solution.py:318
  67.3 1.5 collective-permute-start.7
  68.8 2.0 %collective-permute-start.6 = (bf16[4,224,256]{2,1,0:T(8,128)(2,1)}, bf16[4,224,256]{2,1,0:T(8,128)(2,1)S(1)}, u32[]{:S(2)}, u32[]{:S(2)}) collective-permute-start(bf16[4,224,256]{2,1,0:T(8,128)(2,1)} %get-tuple-element.51), channel_id=1, source_target_pairs={{0,1},{1,0},{2,3},{3,2},{4,5},{5,4},{6,7},{7,6},{8,9},{9,8},{10,11... | collective-permute-start | bytes 1376264 | tf_op jit(solution)/shard_map/ppermute | solution.py:46
  70.8 10.6 %collective-permute-done.7.refs_1_ = bf16[8,32,1024]{2,1,0:T(8,128)(2,1)S(1)} collective-permute-done((bf16[8,32,1024]{2,1,0:T(8,128)(2,1)}, bf16[8,32,1024]{2,1,0:T(8,128)(2,1)S(1)}, u32[]{:S(2)}, u32[]{:S(2)}) %collective-permute-start.7) | collective-permute-done | bytes 524320 | tf_op jit(solution)/shard_map/ppermute | solution.py:27
  81.5 2.6 %collective-permute-done.6 = bf16[4,224,256]{2,1,0:T(8,128)(2,1)S(1)} collective-permute-done((bf16[4,224,256]{2,1,0:T(8,128)(2,1)}, bf16[4,224,256]{2,1,0:T(8,128)(2,1)S(1)}, u32[]{:S(2)}, u32[]{:S(2)}) %collective-permute-start.6) | collective-permute-done | bytes 458784 | tf_op jit(solution)/shard_map/ppermute | solution.py:46
  84.1 2.1 %add_convert_fusion = bf16[4,224,256]{2,1,0:T(8,128)(2,1)} fusion(f32[4,224,256]{2,1,0:T(8,128)} %get-tuple-element.50, bf16[4,224,256]{2,1,0:T(8,128)(2,1)S(1)} %collective-permute-done.6), kind=kLoop, calls=%fused_computation | loop fusion | flops 688128 | bytes 1835008 | tf_op jit(solution)/shard_map/convert_element_type | solution.py:330
  86.1 0.8 copy-done.12
  87.0 0.8 collective-permute-start.10
  87.8 4.7 %all-to-all-start.3 = ((bf16[4,224,256]{2,1,0:T(8,128)(2,1)}), bf16[4,224,256]{2,1,0:T(8,128)(2,1)S(1)}, u32[]{:S(2)}, u32[]{:S(2)}) async-start(bf16[4,224,256]{2,1,0:T(8,128)(2,1)} %add_convert_fusion), calls=%async_computation.3 | async-start | bytes 917504 | tf_op jit(solution)/shard_map/all_to_all | solution.py:52
  92.6 4.9 %collective-permute-done.10.refs_1_ = bf16[3,256,256]{2,1,0:T(8,128)(2,1)} collective-permute-done((bf16[3,256,256]{2,1,0:T(8,128)(2,1)S(1)}, bf16[3,256,256]{2,1,0:T(8,128)(2,1)}, u32[]{:S(2)}, u32[]{:S(2)}) %collective-permute-start.10) | collective-permute-done | bytes 393248 | tf_op jit(solution)/shard_map/ppermute | solution.py:27
  97.6 1.3 constant_dynamic-slice_fusion.refs_17_
  99.1 0.7 convert_reduce_fusion
  99.8 5.3 %all-to-all-done.3.sums_ref = bf16[4,224,256]{2,1,0:T(8,128)(2,1)S(1)} async-done(((bf16[4,224,256]{2,1,0:T(8,128)(2,1)}), bf16[4,224,256]{2,1,0:T(8,128)(2,1)S(1)}, u32[]{:S(2)}, u32[]{:S(2)}) %all-to-all-start.3) | async-done | bytes 458784 | tf_op jit(solution)/shard_map/all_to_all | solution.py:52
  105.1 0.8 copy-done.6
  105.9 4.2 %recur.1 = bf16[2,5,32,256]{3,2,1,0:T(8,128)(2,1)} custom-call(s32[4]{0:T(128)} %get-tuple-element.64.order, bf16[4,224,256]{2,1,0:T(8,128)(2,1)} %copy-done.6, bf16[8,224,256]{2,1,0:T(8,128)(2,1)} %copy-done.5, f32[32,1]{1,0:T(8,128)} %get-tuple-element.59.sq_ref, bf16[3,256,256]{2,1,0:T(8,128)(2,1)} %bitcast.27, ...), custom_call_target="tpu_custom_call" | custom-call | tf_op jit(solution)/shard_map/recur/pallas_call | solution.py:340
  110.0 0.9 slice_bitcast_fusion
  111.0 0.8 broadcast_in_dim.9
  111.7 3.5 %all-to-all-start.4 = ((bf16[4,5,32,256]{3,2,1,0:T(8,128)(2,1)}), bf16[4,5,32,256]{3,2,1,0:T(8,128)(2,1)S(1)}, u32[]{:S(2)}, u32[]{:S(2)}) async-start(bf16[4,5,32,256]{3,2,1,0:T(8,128)(2,1)} %broadcast_in_dim.9), calls=%async_computation.4 | async-start | bytes 655360 | tf_op jit(solution)/shard_map/all_to_all | solution.py:52
  115.2 1.1 collective-permute-start.13
  116.3 3.4 %collective-permute-done.13 = bf16[5,32,256]{2,1,0:T(8,128)(2,1)S(1)} collective-permute-done((bf16[5,32,256]{2,1,0:T(8,128)(2,1)S(1)}, bf16[5,32,256]{2,1,0:T(8,128)(2,1)S(1)}, u32[]{:S(2)}, u32[]{:S(2)}) %collective-permute-start.13) | collective-permute-done | bytes 81952 | tf_op jit(solution)/shard_map/ppermute | solution.py:27
  119.7 5.3 %all-to-all-done.4.refs_8_ = bf16[4,5,32,256]{3,2,1,0:T(8,128)(2,1)S(1)} async-done(((bf16[4,5,32,256]{3,2,1,0:T(8,128)(2,1)}), bf16[4,5,32,256]{3,2,1,0:T(8,128)(2,1)S(1)}, u32[]{:S(2)}, u32[]{:S(2)}) %all-to-all-start.4) | async-done | bytes 327712 | tf_op jit(solution)/shard_map/all_to_all | solution.py:52
  125.0 0.8 broadcast_in_dim.10
  125.9 3.6 %all-to-all-start.5 = ((bf16[4,5,32,256]{3,2,1,0:T(8,128)(2,1)}), bf16[4,5,32,256]{3,2,1,0:T(8,128)(2,1)S(1)}, u32[]{:S(2)}, u32[]{:S(2)}) async-start(bf16[4,5,32,256]{3,2,1,0:T(8,128)(2,1)} %broadcast_in_dim.10), calls=%async_computation.5 | async-start | bytes 655360 | tf_op jit(solution)/shard_map/all_to_all | solution.py:52
  129.5 1.0 collective-permute-start.16
  130.5 7.5 %all-to-all-done.5.refs_9_ = bf16[4,5,32,256]{3,2,1,0:T(8,128)(2,1)S(1)} async-done(((bf16[4,5,32,256]{3,2,1,0:T(8,128)(2,1)}), bf16[4,5,32,256]{3,2,1,0:T(8,128)(2,1)S(1)}, u32[]{:S(2)}, u32[]{:S(2)}) %all-to-all-start.5) | async-done | bytes 327712 | tf_op jit(solution)/shard_map/all_to_all | solution.py:52
  138.0 0.9 collective-permute-start.17
  139.4 5.6 %collective-permute-done.17.refs_13_ = bf16[4,5,32,256]{3,2,1,0:T(8,128)(2,1)S(1)} collective-permute-done((bf16[4,5,32,256]{3,2,1,0:T(8,128)(2,1)S(1)}, bf16[4,5,32,256]{3,2,1,0:T(8,128)(2,1)S(1)}, u32[]{:S(2)}, u32[]{:S(2)}) %collective-permute-start.17) | collective-permute-done | bytes 327712 | tf_op jit(solution)/shard_map/ppermute | solution.py:46
  145.1 1.6 collective-permute-done.19.refs_15_
  146.8 0.7 copy-done.20
  147.5 12.0 %squares.1 = f32[1024,256]{1,0:T(8,128)} custom-call(s32[4]{0:T(128)} %get-tuple-element.64.order, s32[2]{0:T(128)} %pad_add_fusion.1.place, bf16[8,32,1024]{2,1,0:T(8,128)(2,1)} %get-tuple-element.53.refs_0_, bf16[8,32,1024]{2,1,0:T(8,128)(2,1)} %copy-done.10, bf16[8,32,1024]{2,1,0:T(8,128)(2,1)} %copy-done.11, bf16[8,32,1024]{2,1,0:T(8,128)(2,1)} %copy-done.12, ...), custom_call_target="tpu_custom_call" | custom-call | tf_op jit(solution)/shard_map/squares/pallas_call | solution.py:370
  (81 shorter events, 3.1 us)
Async XLA Ops:
  4.1 7.4 %copy-start.1 = (bf16[1,1024,256]{2,1,0:T(8,128)(2,1)S(1)}, bf16[1,1024,256]{2,1,0:T(8,128)(2,1)}, u32[]{:S(2)}) copy-start(bf16[1,1024,256]{2,1,0:T(8,128)(2,1)} %param.15) | copy-start | bytes 1572868
  4.1 20.9 %copy-start.23 = (s32[12]{0:T(128)S(1)}, s32[12]{0:T(128)}, u32[]{:S(2)}) copy-start(s32[12]{0:T(128)} %constant.112.clone) | copy-start | bytes 148
  4.1 21.5 %copy-start.22 = (s32[12]{0:T(128)S(1)}, s32[12]{0:T(128)}, u32[]{:S(2)}) copy-start(s32[12]{0:T(128)} %constant.113.clone) | copy-start | bytes 148
  4.1 22.2 %copy-start.21 = (s32[1,4]{1,0:T(1,128)S(1)}, s32[1,4]{1,0:T(1,128)}, u32[]{:S(2)}) copy-start(s32[1,4]{1,0:T(1,128)} %param.17) | copy-start | bytes 52
  4.1 33.2 %all-to-all-start = ((bf16[8,64,1024]{2,1,0:T(8,128)(2,1)}), bf16[8,64,1024]{2,1,0:T(8,128)(2,1)S(1)}, u32[]{:S(2)}, u32[]{:S(2)}) async-start(bf16[8,64,1024]{2,1,0:T(8,128)(2,1)} %get-tuple-element.47), calls=%async_computation | async-start | bytes 2097152 | tf_op jit(solution)/shard_map/all_to_all | solution.py:288
  11.5 13.4 %collective-permute-start = (bf16[1024,256]{1,0:T(8,128)(2,1)S(1)}, bf16[1024,256]{1,0:T(8,128)(2,1)S(1)}, u32[]{:S(2)}, u32[]{:S(2)}) collective-permute-start(bf16[1024,256]{1,0:T(8,128)(2,1)S(1)} %bitcast.22), channel_id=1, source_target_pairs={{0,16},{8,24},{16,0},{24,8},{1,17},{9,25},{17,1},{25,9},{2,18},{10... | collective-permute-start | bytes 1572872 | tf_op jit(solution)/shard_map/ppermute | solution.py:27
  13.1 13.8 %collective-permute-start.1 = (bf16[1024,256]{1,0:T(8,128)(2,1)S(1)}, bf16[1024,256]{1,0:T(8,128)(2,1)S(1)}, u32[]{:S(2)}, u32[]{:S(2)}) collective-permute-start(bf16[1024,256]{1,0:T(8,128)(2,1)S(1)} %bitcast.23), channel_id=1, source_target_pairs={{0,8},{8,0},{16,24},{24,16},{1,9},{9,1},{17,25},{25,17},{2,10},{10... | collective-permute-start | bytes 1572872 | tf_op jit(solution)/shard_map/ppermute | solution.py:22
  13.1 13.8 %collective-permute-start.3 = (bf16[1024,256]{1,0:T(8,128)(2,1)}, bf16[1024,256]{1,0:T(8,128)(2,1)}, u32[]{:S(2)}, u32[]{:S(2)}) collective-permute-start(bf16[1024,256]{1,0:T(8,128)(2,1)} %get-tuple-element.46.refs_4_.refs_0_), channel_id=1, source_target_pairs={{0,8},{8,0},{16,24},{24,16},{1,9},{9,1},{17,25},{25,17},{2,10},{10... | collective-permute-start | bytes 1572872 | tf_op jit(solution)/shard_map/ppermute | solution.py:22
  24.9 2.0 %copy-start.2 = (bf16[1024,256]{1,0:T(8,128)(2,1)}, bf16[1024,256]{1,0:T(8,128)(2,1)S(1)}, u32[]{:S(2)}) copy-start(bf16[1024,256]{1,0:T(8,128)(2,1)S(1)} %collective-permute-done.refs_1_.refs_5_) | copy-start | bytes 1572868
  25.0 2.0 %collective-permute-start.2 = (bf16[1024,256]{1,0:T(8,128)(2,1)S(1)}, bf16[1024,256]{1,0:T(8,128)(2,1)S(1)}, u32[]{:S(2)}, u32[]{:S(2)}) collective-permute-start(bf16[1024,256]{1,0:T(8,128)(2,1)S(1)} %collective-permute-done.refs_1_.refs_5_), channel_id=1, source_target_pairs={{0,8},{8,0},{16,24},{24,16},{1,9},{9,1},{17,25},{25,17},{2,10},{10... | collective-permute-start | bytes 1572872 | tf_op jit(solution)/shard_map/ppermute | solution.py:22
  26.9 1.0 copy-start.4
  37.3 5.1 %copy-start = (bf16[8,64,1024]{2,1,0:T(8,128)(2,1)}, bf16[8,64,1024]{2,1,0:T(8,128)(2,1)S(1)}, u32[]{:S(2)}) copy-start(bf16[8,64,1024]{2,1,0:T(8,128)(2,1)S(1)} %all-to-all-done.rows_ref) | copy-start | bytes 3145732
  37.3 16.9 %all-to-all-start.1 = ((bf16[8,112,256]{2,1,0:T(8,128)(2,1)}), bf16[8,112,256]{2,1,0:T(8,128)(2,1)S(1)}, u32[]{:S(2)}, u32[]{:S(2)}) async-start(bf16[8,112,256]{2,1,0:T(8,128)(2,1)} %pad_maximum_fusion), calls=%async_computation.1 | async-start | bytes 917504 | tf_op jit(solution)/shard_map/all_to_all | solution.py:307
  40.9 17.8 %collective-permute-start.4 = (bf16[1024,256]{1,0:T(8,128)(2,1)}, bf16[1024,256]{1,0:T(8,128)(2,1)S(1)}, u32[]{:S(2)}, u32[]{:S(2)}) collective-permute-start(bf16[1024,256]{1,0:T(8,128)(2,1)} %get-tuple-element.46.refs_4_.refs_0_), channel_id=1, source_target_pairs={{0,16},{8,24},{16,0},{24,8},{1,17},{9,25},{17,1},{25,9},{2,18},{10... | collective-permute-start | bytes 1572872 | tf_op jit(solution)/shard_map/ppermute | solution.py:27
  55.0 32.0 %all-to-all-start.2 = ((bf16[8,224,256]{2,1,0:T(8,128)(2,1)}), bf16[8,224,256]{2,1,0:T(8,128)(2,1)S(1)}, u32[]{:S(2)}, u32[]{:S(2)}) async-start(bf16[8,224,256]{2,1,0:T(8,128)(2,1)} %broadcast_dynamic-update-slice_fusion), calls=%async_computation.2 | async-start | bytes 1835008 | tf_op jit(solution)/shard_map/all_to_all | solution.py:334
  58.6 2.0 %copy-start.13 = (bf16[1024,256]{1,0:T(8,128)(2,1)}, bf16[1024,256]{1,0:T(8,128)(2,1)S(1)}, u32[]{:S(2)}) copy-start(bf16[1024,256]{1,0:T(8,128)(2,1)S(1)} %collective-permute-done.4.refs_1_) | copy-start | bytes 1572868
  58.6 2.0 %collective-permute-start.5 = (bf16[1024,256]{1,0:T(8,128)(2,1)S(1)}, bf16[1024,256]{1,0:T(8,128)(2,1)S(1)}, u32[]{:S(2)}, u32[]{:S(2)}) collective-permute-start(bf16[1024,256]{1,0:T(8,128)(2,1)S(1)} %collective-permute-done.4.refs_1_), channel_id=1, source_target_pairs={{0,8},{8,0},{16,24},{24,16},{1,9},{9,1},{17,25},{25,17},{2,10},{10... | collective-permute-start | bytes 1572872 | tf_op jit(solution)/shard_map/ppermute | solution.py:22
  60.6 0.8 copy-start.14
  67.3 14.2 %collective-permute-start.7 = (bf16[8,32,1024]{2,1,0:T(8,128)(2,1)}, bf16[8,32,1024]{2,1,0:T(8,128)(2,1)S(1)}, u32[]{:S(2)}, u32[]{:S(2)}) collective-permute-start(bf16[8,32,1024]{2,1,0:T(8,128)(2,1)} %get-tuple-element.53.refs_0_), channel_id=1, source_target_pairs={{0,16},{8,24},{16,0},{24,8},{1,17},{9,25},{17,1},{25,9},{2,18},{10... | collective-permute-start | bytes 1572872 | tf_op jit(solution)/shard_map/ppermute | solution.py:27
  68.8 15.2 %collective-permute-start.6 = (bf16[4,224,256]{2,1,0:T(8,128)(2,1)}, bf16[4,224,256]{2,1,0:T(8,128)(2,1)S(1)}, u32[]{:S(2)}, u32[]{:S(2)}) collective-permute-start(bf16[4,224,256]{2,1,0:T(8,128)(2,1)} %get-tuple-element.51), channel_id=1, source_target_pairs={{0,1},{1,0},{2,3},{3,2},{4,5},{5,4},{6,7},{7,6},{8,9},{9,8},{10,11... | collective-permute-start | bytes 1376264 | tf_op jit(solution)/shard_map/ppermute | solution.py:46
  70.8 15.3 %collective-permute-start.8 = (bf16[8,32,1024]{2,1,0:T(8,128)(2,1)}, bf16[8,32,1024]{2,1,0:T(8,128)(2,1)S(1)}, u32[]{:S(2)}, u32[]{:S(2)}) collective-permute-start(bf16[8,32,1024]{2,1,0:T(8,128)(2,1)} %get-tuple-element.53.refs_0_), channel_id=1, source_target_pairs={{0,8},{8,0},{16,24},{24,16},{1,9},{9,1},{17,25},{25,17},{2,10},{10... | collective-permute-start | bytes 1572872 | tf_op jit(solution)/shard_map/ppermute | solution.py:22
  81.5 28.6 %copy-start.10 = (bf16[8,32,1024]{2,1,0:T(8,128)(2,1)}, bf16[8,32,1024]{2,1,0:T(8,128)(2,1)S(1)}, u32[]{:S(2)}) copy-start(bf16[8,32,1024]{2,1,0:T(8,128)(2,1)S(1)} %collective-permute-done.7.refs_1_) | copy-start | bytes 1572868
  81.5 4.6 %collective-permute-start.9 = (bf16[8,32,1024]{2,1,0:T(8,128)(2,1)S(1)}, bf16[8,32,1024]{2,1,0:T(8,128)(2,1)S(1)}, u32[]{:S(2)}, u32[]{:S(2)}) collective-permute-start(bf16[8,32,1024]{2,1,0:T(8,128)(2,1)S(1)} %collective-permute-done.7.refs_1_), channel_id=1, source_target_pairs={{0,8},{8,0},{16,24},{24,16},{1,9},{9,1},{17,25},{25,17},{2,10},{10... | collective-permute-start | bytes 1572872 | tf_op jit(solution)/shard_map/ppermute | solution.py:22
  86.1 60.6 %copy-start.11 = (bf16[8,32,1024]{2,1,0:T(8,128)(2,1)}, bf16[8,32,1024]{2,1,0:T(8,128)(2,1)S(1)}, u32[]{:S(2)}) copy-start(bf16[8,32,1024]{2,1,0:T(8,128)(2,1)S(1)} %collective-permute-done.8.refs_2_) | copy-start | bytes 1572868
  86.1 0.8 copy-start.12
  87.0 18.1 %copy-start.5 = (bf16[8,224,256]{2,1,0:T(8,128)(2,1)}, bf16[8,224,256]{2,1,0:T(8,128)(2,1)S(1)}, u32[]{:S(2)}) copy-start(bf16[8,224,256]{2,1,0:T(8,128)(2,1)S(1)} %all-to-all-done.2.back_ref) | copy-start | bytes 2752516
  87.0 18.1 %copy-start.7 = (bf16[8,96,256]{2,1,0:T(8,128)(2,1)}, bf16[8,96,256]{2,1,0:T(8,128)(2,1)S(1)}, u32[]{:S(2)}) copy-start(bf16[8,96,256]{2,1,0:T(8,128)(2,1)S(1)} %slice.61) | copy-start | bytes 1179652
  87.0 10.5 %collective-permute-start.10 = (bf16[3,256,256]{2,1,0:T(8,128)(2,1)S(1)}, bf16[3,256,256]{2,1,0:T(8,128)(2,1)}, u32[]{:S(2)}, u32[]{:S(2)}) collective-permute-start(bf16[3,256,256]{2,1,0:T(8,128)(2,1)S(1)} %bitcast.25), channel_id=1, source_target_pairs={{0,16},{8,24},{16,0},{24,8},{1,17},{9,25},{17,1},{25,9},{2,18},{10... | collective-permute-start | bytes 1179656 | tf_op jit(solution)/shard_map/ppermute | solution.py:27
  87.8 17.2 %all-to-all-start.3 = ((bf16[4,224,256]{2,1,0:T(8,128)(2,1)}), bf16[4,224,256]{2,1,0:T(8,128)(2,1)S(1)}, u32[]{:S(2)}, u32[]{:S(2)}) async-start(bf16[4,224,256]{2,1,0:T(8,128)(2,1)} %add_convert_fusion), calls=%async_computation.3 | async-start | bytes 917504 | tf_op jit(solution)/shard_map/all_to_all | solution.py:52
  92.6 7.1 %collective-permute-start.11 = (bf16[3,256,256]{2,1,0:T(8,128)(2,1)S(1)}, bf16[3,256,256]{2,1,0:T(8,128)(2,1)}, u32[]{:S(2)}, u32[]{:S(2)}) collective-permute-start(bf16[3,256,256]{2,1,0:T(8,128)(2,1)S(1)} %bitcast.26), channel_id=1, source_target_pairs={{0,8},{8,0},{16,24},{24,16},{1,9},{9,1},{17,25},{25,17},{2,10},{10... | collective-permute-start | bytes 1179656 | tf_op jit(solution)/shard_map/ppermute | solution.py:22
  97.6 7.5 %collective-permute-start.12 = (bf16[3,256,256]{2,1,0:T(8,128)(2,1)}, bf16[3,256,256]{2,1,0:T(8,128)(2,1)}, u32[]{:S(2)}, u32[]{:S(2)}) collective-permute-start(bf16[3,256,256]{2,1,0:T(8,128)(2,1)} %collective-permute-done.10.refs_1_), channel_id=1, source_target_pairs={{0,8},{8,0},{16,24},{24,16},{1,9},{9,1},{17,25},{25,17},{2,10},{10... | collective-permute-start | bytes 1179656 | tf_op jit(solution)/shard_map/ppermute | solution.py:22
  105.1 0.8 copy-start.6
  111.7 13.3 %all-to-all-start.4 = ((bf16[4,5,32,256]{3,2,1,0:T(8,128)(2,1)}), bf16[4,5,32,256]{3,2,1,0:T(8,128)(2,1)S(1)}, u32[]{:S(2)}, u32[]{:S(2)}) async-start(bf16[4,5,32,256]{3,2,1,0:T(8,128)(2,1)} %broadcast_in_dim.9), calls=%async_computation.4 | async-start | bytes 655360 | tf_op jit(solution)/shard_map/all_to_all | solution.py:52
  115.2 4.5 %collective-permute-start.13 = (bf16[5,32,256]{2,1,0:T(8,128)(2,1)S(1)}, bf16[5,32,256]{2,1,0:T(8,128)(2,1)S(1)}, u32[]{:S(2)}, u32[]{:S(2)}) collective-permute-start(bf16[5,32,256]{2,1,0:T(8,128)(2,1)S(1)} %get-tuple-element.65), channel_id=1, source_target_pairs={{0,16},{8,24},{16,0},{24,8},{1,17},{9,25},{17,1},{25,9},{2,18},{10... | collective-permute-start | bytes 245768 | tf_op jit(solution)/shard_map/ppermute | solution.py:27
  125.0 21.6 %copy-start.8 = (bf16[4,5,32,256]{3,2,1,0:T(8,128)(2,1)}, bf16[4,5,32,256]{3,2,1,0:T(8,128)(2,1)S(1)}, u32[]{:S(2)}) copy-start(bf16[4,5,32,256]{3,2,1,0:T(8,128)(2,1)S(1)} %all-to-all-done.4.refs_8_) | copy-start | bytes 983044
  125.9 12.1 %all-to-all-start.5 = ((bf16[4,5,32,256]{3,2,1,0:T(8,128)(2,1)}), bf16[4,5,32,256]{3,2,1,0:T(8,128)(2,1)S(1)}, u32[]{:S(2)}, u32[]{:S(2)}) async-start(bf16[4,5,32,256]{3,2,1,0:T(8,128)(2,1)} %broadcast_in_dim.10), calls=%async_computation.5 | async-start | bytes 655360 | tf_op jit(solution)/shard_map/all_to_all | solution.py:52
  129.5 9.9 %collective-permute-start.16 = (bf16[4,5,32,256]{3,2,1,0:T(8,128)(2,1)S(1)}, bf16[4,5,32,256]{3,2,1,0:T(8,128)(2,1)S(1)}, u32[]{:S(2)}, u32[]{:S(2)}) collective-permute-start(bf16[4,5,32,256]{3,2,1,0:T(8,128)(2,1)S(1)} %all-to-all-done.4.refs_8_), channel_id=1, source_target_pairs={{0,1},{1,0},{2,3},{3,2},{4,5},{5,4},{6,7},{7,6},{8,9},{9,8},{10,11... | collective-permute-start | bytes 983048 | tf_op jit(solution)/shard_map/ppermute | solution.py:46
  138.0 8.7 %copy-start.9 = (bf16[4,5,32,256]{3,2,1,0:T(8,128)(2,1)}, bf16[4,5,32,256]{3,2,1,0:T(8,128)(2,1)S(1)}, u32[]{:S(2)}) copy-start(bf16[4,5,32,256]{3,2,1,0:T(8,128)(2,1)S(1)} %all-to-all-done.5.refs_9_) | copy-start | bytes 983044
  138.0 7.1 %collective-permute-start.17 = (bf16[4,5,32,256]{3,2,1,0:T(8,128)(2,1)S(1)}, bf16[4,5,32,256]{3,2,1,0:T(8,128)(2,1)S(1)}, u32[]{:S(2)}, u32[]{:S(2)}) collective-permute-start(bf16[4,5,32,256]{3,2,1,0:T(8,128)(2,1)S(1)} %all-to-all-done.5.refs_9_), channel_id=1, source_target_pairs={{0,1},{1,0},{2,3},{3,2},{4,5},{5,4},{6,7},{7,6},{8,9},{9,8},{10,11... | collective-permute-start | bytes 983048 | tf_op jit(solution)/shard_map/ppermute | solution.py:46
  138.9 6.2 %collective-permute-start.14 = (bf16[4,5,32,256]{3,2,1,0:T(8,128)(2,1)S(1)}, bf16[4,5,32,256]{3,2,1,0:T(8,128)(2,1)S(1)}, u32[]{:S(2)}, u32[]{:S(2)}) collective-permute-start(bf16[4,5,32,256]{3,2,1,0:T(8,128)(2,1)S(1)} %all-to-all-done.4.refs_8_), channel_id=1, source_target_pairs={{0,8},{8,0},{16,24},{24,16},{1,9},{9,1},{17,25},{25,17},{2,10},{10... | collective-permute-start | bytes 983048 | tf_op jit(solution)/shard_map/ppermute | solution.py:22
  138.9 6.2 %collective-permute-start.15 = (bf16[4,5,32,256]{3,2,1,0:T(8,128)(2,1)S(1)}, bf16[4,5,32,256]{3,2,1,0:T(8,128)(2,1)S(1)}, u32[]{:S(2)}, u32[]{:S(2)}) collective-permute-start(bf16[4,5,32,256]{3,2,1,0:T(8,128)(2,1)S(1)} %all-to-all-done.5.refs_9_), channel_id=1, source_target_pairs={{0,8},{8,0},{16,24},{24,16},{1,9},{9,1},{17,25},{25,17},{2,10},{10... | collective-permute-start | bytes 983048 | tf_op jit(solution)/shard_map/ppermute | solution.py:22
  139.4 7.3 %copy-start.15 = (bf16[4,5,32,256]{3,2,1,0:T(8,128)(2,1)}, bf16[4,5,32,256]{3,2,1,0:T(8,128)(2,1)S(1)}, u32[]{:S(2)}) copy-start(bf16[4,5,32,256]{3,2,1,0:T(8,128)(2,1)S(1)} %collective-permute-done.16.refs_12_) | copy-start | bytes 983044
  139.4 5.7 %collective-permute-start.18 = (bf16[4,5,32,256]{3,2,1,0:T(8,128)(2,1)S(1)}, bf16[4,5,32,256]{3,2,1,0:T(8,128)(2,1)S(1)}, u32[]{:S(2)}, u32[]{:S(2)}) collective-permute-start(bf16[4,5,32,256]{3,2,1,0:T(8,128)(2,1)S(1)} %collective-permute-done.16.refs_12_), channel_id=1, source_target_pairs={{0,8},{8,0},{16,24},{24,16},{1,9},{9,1},{17,25},{25,17},{2,10},{10... | collective-permute-start | bytes 983048 | tf_op jit(solution)/shard_map/ppermute | solution.py:22
  145.0 1.7 %copy-start.16 = (bf16[4,5,32,256]{3,2,1,0:T(8,128)(2,1)}, bf16[4,5,32,256]{3,2,1,0:T(8,128)(2,1)S(1)}, u32[]{:S(2)}) copy-start(bf16[4,5,32,256]{3,2,1,0:T(8,128)(2,1)S(1)} %collective-permute-done.17.refs_13_) | copy-start | bytes 983044
  145.1 1.6 %collective-permute-start.19 = (bf16[4,5,32,256]{3,2,1,0:T(8,128)(2,1)S(1)}, bf16[4,5,32,256]{3,2,1,0:T(8,128)(2,1)S(1)}, u32[]{:S(2)}, u32[]{:S(2)}) collective-permute-start(bf16[4,5,32,256]{3,2,1,0:T(8,128)(2,1)S(1)} %collective-permute-done.17.refs_13_), channel_id=1, source_target_pairs={{0,8},{8,0},{16,24},{24,16},{1,9},{9,1},{17,25},{25,17},{2,10},{10... | collective-permute-start | bytes 983048 | tf_op jit(solution)/shard_map/ppermute | solution.py:22
  145.1 1.7 %copy-start.17 = (bf16[4,5,32,256]{3,2,1,0:T(8,128)(2,1)}, bf16[4,5,32,256]{3,2,1,0:T(8,128)(2,1)S(1)}, u32[]{:S(2)}) copy-start(bf16[4,5,32,256]{3,2,1,0:T(8,128)(2,1)S(1)} %collective-permute-done.14.refs_10_) | copy-start | bytes 983044
  145.1 1.6 %copy-start.18 = (bf16[4,5,32,256]{3,2,1,0:T(8,128)(2,1)}, bf16[4,5,32,256]{3,2,1,0:T(8,128)(2,1)S(1)}, u32[]{:S(2)}) copy-start(bf16[4,5,32,256]{3,2,1,0:T(8,128)(2,1)S(1)} %collective-permute-done.15.refs_11_) | copy-start | bytes 983044
  145.1 1.6 %copy-start.19 = (bf16[4,5,32,256]{3,2,1,0:T(8,128)(2,1)}, bf16[4,5,32,256]{3,2,1,0:T(8,128)(2,1)S(1)}, u32[]{:S(2)}) copy-start(bf16[4,5,32,256]{3,2,1,0:T(8,128)(2,1)S(1)} %collective-permute-done.18.refs_14_) | copy-start | bytes 983044
  (2 other events, 1.5 us)

commit v4 on v3

v4 whole, which is shorter than its diff:
```python
import functools

import jax
import jax.numpy as jnp
from jax import lax
from jax.experimental import pallas as pl
from jax.experimental.pallas import tpu as pltpu
from jax.sharding import PartitionSpec as P

epsilon = 1e-05
bf16 = jnp.bfloat16
f32 = jnp.float32
MIB = 1024 * 1024


def dot(a, b, ca, cb):
    return lax.dot_general(a, b, (((ca,), (cb,)), ((), ())), preferred_element_type=f32)


def core_swap(x):
    count = lax.axis_size("section")
    return lax.ppermute(x, "section", [(i, i ^ 1) for i in range(count)])


def chip_shift(x, by):
    count = lax.axis_size("section")
    return lax.ppermute(x, "section", [(i, (i - 2 * by) % count) for i in range(count)])


def section_order():
    count = lax.axis_size("section")
    me = lax.axis_index("section")
    same = [(me + 2 * j) % count for j in range(count // 2)]
    other = [((me ^ 1) + 2 * j) % count for j in range(count // 2)]
    return jnp.stack(same + other).astype(jnp.int32)


def gather_section(x):
    count = lax.axis_size("section")
    same = [x] + [chip_shift(x, j) for j in range(1, count // 2)]
    return same + [core_swap(b) for b in same]


def far_away(*arrays):
    return [pltpu.with_memory_space_constraint(a, pltpu.HBM) for a in arrays]


def pair_swap(x):
    peers = lax.axis_size("dp")
    return lax.ppermute(x, "dp", [(i, i ^ 1) for i in range(peers)])


def line_exchange(x):
    peers = lax.axis_size("dp")
    groups = [list(range(p, peers, 2)) for p in range(2)]
    return lax.all_to_all(x, "dp", 0, 0, axis_index_groups=groups, tiled=True)


def repeated(x, times):
    return jnp.broadcast_to(x[None], (times,) + x.shape)


def gram_pairs(count):
    ups = [(k, count + j) for j in range(count - 1) for k in range(j + 1)]
    listed = []
    for chip in range(count // 2):
        own = [(k, l) for l in (2 * chip, 2 * chip + 1) for k in range(l)]
        spare = 2 * (count - 1) - len(own)
        listed += own + ups[:spare]
        ups = ups[spare:]
    return listed


def prepare_kernel(tokens_ref, cot_ref, rows_ref, sems):
    peers, rows, block = rows_ref.shape
    t = rows // 2
    start = pl.multiple_of(lax.axis_index("section") * t, t)
    copies = []
    for n in range(peers):
        for k, ref in enumerate((tokens_ref, cot_ref)):
            source = ref.at[pl.ds(start, t), pl.ds(n * block, block)]
            copies.append(pltpu.make_async_copy(source, rows_ref.at[n, pl.ds(k * t, t)], sems.at[k, n]))
    for copy in copies:
        copy.start()
    for copy in copies:
        copy.wait()


def weight_kernel(place, rows_ref, down_ref, gain_ref, square_ref, weight_ref):
    peers, rows, block = rows_ref.shape
    t = rows // 2
    total = jnp.zeros((t, 1), f32)
    for n in range(peers):
        wide = rows_ref[n, :t].astype(f32)
        total = total + jnp.sum(wide * wide, axis=-1, keepdims=True)
    square_ref[...] = total
    gain = gain_ref[...].reshape(block, 1)
    weight_ref[...] = (down_ref[0].astype(f32) * gain).astype(bf16)


def gram_kernel(count, seqs, order, left, right, lengths, *refs):
    ups = refs[:count]
    mine, partner, gram_ref, table = refs[count:]
    peers, rows, r = gram_ref.shape
    core = lax.rem(order[0], 2)
    table[core] = mine[...]
    table[1 - core] = partner[...]
    for i in range(count):
        table[2 + order[i]] = ups[i][...]
    share = r // peers
    for p in range(count - 1):
        out = dot(table[2 + left[p]], table[right[p]], 0, 0).astype(bf16)
        gram_ref[:, p * share : (p + 1) * share] = out.reshape(peers, share, r)
    used = (count - 1) * share
    lane = lax.broadcasted_iota(jnp.int32, (rows - used, r), 1)
    line = jnp.zeros((rows - used, r), f32)
    for q in range(seqs):
        line = jnp.where(lane == q, lengths[0, q].astype(f32), line)
    gram_ref[:, used:] = jnp.broadcast_to(line.astype(bf16)[None], (peers, rows - used, r))


def paired(rows, mine):
    return jnp.concatenate(rows(mine) + rows(1 - mine), axis=0)


def store_pair(keep_ref, send_ref, m, t, out):
    line, _, r = keep_ref.shape
    place = pl.ds(pl.multiple_of(m * t, t), t)
    keep_ref[:, place, :] = out[: line * t].reshape(line, t, r)
    send_ref[:, place, :] = out[line * t :].astype(bf16).reshape(line, t, r)


def project_kernel(count, order, spot, rows_ref, *refs):
    downs = refs[:count]
    ups = refs[count : 2 * count]
    keep_ref, send_ref, tokens_ref = refs[2 * count :]
    peers, rows, _ = rows_ref.shape
    t = rows // 2
    mine = lax.rem(spot[0], 2)
    tokens_ref[...] = rows_ref[:, :t]
    x = paired(lambda p: [rows_ref[2 * z + p, :t] for z in range(peers // 2)], mine)
    c = paired(lambda p: [rows_ref[2 * z + p, t:] for z in range(peers // 2)], mine)
    for i in range(count):
        layer = order[i]
        store_pair(keep_ref, send_ref, layer, t, dot(x, downs[i][...], 1, 0))
        store_pair(keep_ref, send_ref, 2 * count - 1 + layer, t, dot(c, ups[i][...], 1, 0))

        @pl.when(layer < count - 1)
        def _():
            store_pair(keep_ref, send_ref, count + layer, t, dot(x, ups[i][...], 1, 0))


def recur_kernel(count, width, order, spot, sums_ref, sq_ref, *refs):
    grams = refs[: 2 * count]
    own_ref, out_ref, table, grads = refs[2 * count :]
    copies, _, t, _ = own_ref.shape
    half = count // 2

    def put(j, m, value):
        if j:
            out_ref[j - 1, m] = value
        else:
            for z in range(copies):
                own_ref[z, m] = value

    per = count - 1
    mine = lax.rem(spot[0], 2)
    line = grams[0].shape[0]
    _, _, peers, share, r = table.shape
    for i in range(count):
        for z in range(line):
            for p in range(per):
                rows = slice(p * share, (p + 1) * share)
                table[order[i], p, 2 * z + mine] = grams[i][z, rows]
                table[order[i], p, 2 * z + 1 - mine] = grams[count + i][z, rows]
    place = {pair: n for n, pair in enumerate(gram_pairs(count))}

    def product(pair):
        n = place[pair]
        return table[n // per, n % per].reshape(peers * share, r)

    def mixed(k, l):
        return product((k, l))

    def ups(k, j, a):
        if k <= j:
            return dot(a, product((k, count + j)), 1, 0)
        return dot(a, product((j, count + k)), 1, 1)

    def total(ref, start):
        return jnp.sum(ref[:, start : start + t].astype(f32), axis=0)

    proj = [total(sums_ref, l * t) for l in range(count)]
    hu = [total(sums_ref, (count + k) * t) for k in range(count - 1)]
    back = [total(sums_ref, (2 * count - 1 + l) * t) for l in range(count)]
    norm = sq_ref[...]
    invs, pres, hus = [], [], []
    for l in range(count):
        inv = lax.rsqrt(norm / width + epsilon)
        pre = inv * proj[l]
        invs.append(inv)
        pres.append(pre)
        hus.append(list(hu))
        if l < count - 1:
            act = (pre * jax.nn.sigmoid(pre)).astype(bf16)
            for j in range(half):
                put(j, 2 + l, act)
            wide = act.astype(f32)
            for j in range(l + 1, count):
                proj[j] = proj[j] + dot(act, mixed(l, j), 1, 0)
            step = [ups(l, j, act) for j in range(count - 1)]
            norm = norm + jnp.sum(wide * (2.0 * hu[l] + step[l]), axis=-1, keepdims=True)
            hu = [hu[j] + step[j] for j in range(count - 1)]
    for l in reversed(range(count)):
        s = jax.nn.sigmoid(pres[l])
        grad = (back[l] * s * (1.0 + pres[l] * (1.0 - s))).astype(bf16)
        wide = grad.astype(f32)
        grads[l] = (wide * invs[l]).astype(bf16)
        inner = jnp.sum(wide * proj[l], axis=-1, keepdims=True) / width
        for j in range(l):
            back[j] = back[j] + invs[l] * (
                dot(grad, mixed(j, l), 1, 1) - invs[l] * invs[l] * inner * hus[l][j]
            )
    chip = order[0] // 2
    for j in range(half):
        other = lax.rem(chip + half - j, half)
        put(j, 0, grads[2 * other])
        put(j, 1, grads[2 * other + 1])


def fisher_kernel(count, seqs, scale, order, place, lengths, *refs):
    half = count // 2
    sources = refs[:count]
    ups = refs[count : 2 * count]
    states = refs[2 * count : 4 * count]
    gain_ref, out_ref, rows, acc, hidden, masks, sems = refs[4 * count :]
    copies = [pltpu.make_async_copy(sources[i], rows.at[i], sems.at[i]) for i in range(count)]
    for copy in copies:
        copy.start()
    _, peers, t, width = rows.shape
    r = out_ref.shape[1]
    chunk = min(r, width)
    span = count * t
    me = place[0]
    mine = lax.rem(place[1], 2)
    line = peers // 2
    names = [2 * (n % line) + (mine if n < line else 1 - mine) for n in range(peers)]
    spot = lax.broadcasted_iota(jnp.int32, (1, span), 1)
    position = spot
    for i in range(count):
        inside = (spot >= i * t) & (spot < (i + 1) * t)
        position = jnp.where(inside, spot + (order[i] - i) * t, position)

    def column(n, m):
        first = n // line * count
        return jnp.concatenate([states[first + i][n % line, m] for i in range(count)], axis=0)

    acts = []
    for i in range(1, count):
        act = jnp.concatenate([column(n, 2 + jnp.minimum(order[i], count - 2)) for n in range(peers)], axis=0)
        acts.append(jnp.where(order[i] < me, act, jnp.zeros_like(act)))
    for n in range(peers):
        grad = column(n, lax.rem(me, 2)).astype(f32).T
        start = 0
        for q in range(seqs):
            stop = start + lengths[names[n], q]
            inside = (position >= start) & (position < stop)
            masks[n, q * r : (q + 1) * r] = jnp.where(inside, grad, 0.0).astype(bf16)
            start = stop
    for f in range(width // chunk):
        cols = slice(f * chunk, (f + 1) * chunk)
        update = dot(acts[0], ups[1][cols], 1, 1)
        for i in range(2, count):
            update = update + dot(acts[i - 1], ups[i][cols], 1, 1)
        if f == 0:
            for copy in copies:
                copy.wait()
        for n in range(peers):
            h = jnp.concatenate([rows[i, names[n], :, cols] for i in range(count)], axis=0).astype(f32)
            hidden[n] = (h + update[n * span : (n + 1) * span]).astype(bf16)
        for n in range(peers):
            g = dot(masks[n], hidden[n], 1, 0)
            g = g * g
            total = g[:r]
            for q in range(1, seqs):
                total = total + g[q * r : (q + 1) * r]
            if n == 0:
                acc[...] = total
            else:
                acc[...] = acc[...] + total
        gain = gain_ref[:, cols]
        out_ref[cols] = (acc[...] * (gain * gain * scale)).T


def per_device(tokens, cotangent, down_weight, up_weight, norm_gain, lengths):
    count = lax.axis_size("section")
    peers = lax.axis_size("dp")
    me = lax.axis_index("section")
    spot = lax.axis_index("dp")
    row_count, width = tokens.shape
    block = width // peers
    t = row_count // count
    r = down_weight.shape[2]
    order = section_order()
    smem = pl.BlockSpec(memory_space=pltpu.SMEM)
    vmem = pl.BlockSpec(memory_space=pltpu.VMEM)
    anywhere = pl.BlockSpec(memory_space=pl.ANY)

    def limit(mib):
        return pltpu.CompilerParams(vmem_limit_bytes=mib * MIB)

    place = jnp.stack([me, spot]).astype(jnp.int32)
    spot_ref = place[1:]
    ups = gather_section(up_weight[0])
    send = pl.pallas_call(
        prepare_kernel,
        out_shape=jax.ShapeDtypeStruct((peers, 2 * t, block), bf16),
        in_specs=[anywhere, anywhere],
        out_specs=vmem,
        scratch_shapes=[pltpu.SemaphoreType.DMA((2, peers))],
        name="prepare",
    )(tokens, cotangent)
    square, weight = pl.pallas_call(
        weight_kernel,
        grid_spec=pltpu.PrefetchScalarGridSpec(
            num_scalar_prefetch=1,
            grid=(1,),
            in_specs=[
                pl.BlockSpec((peers, 2 * t, block), lambda n, place: (0, 0, 0)),
                pl.BlockSpec((1, block, r), lambda n, place: (0, 0, 0)),
                pl.BlockSpec((1, block), lambda n, place: (0, place[1])),
            ],
            out_specs=[
                pl.BlockSpec((t, 1), lambda n, place: (0, 0)),
                pl.BlockSpec((block, r), lambda n, place: (0, 0)),
            ],
        ),
        out_shape=(
            jax.ShapeDtypeStruct((t, 1), f32),
            jax.ShapeDtypeStruct((block, r), bf16),
        ),
        compiler_params=limit(12),
        name="weight",
    )(place, send, down_weight, norm_gain)
    partner = core_swap(weight)
    rows = lax.all_to_all(send, "dp", 0, 0, tiled=True)

    pairs = gram_pairs(count)
    left = lax.dynamic_slice_in_dim(jnp.array([a for a, _ in pairs], jnp.int32), me * (count - 1), count - 1)
    codes = jnp.array([b % 2 if b < count else 2 + b - count for _, b in pairs], jnp.int32)
    right = lax.dynamic_slice_in_dim(codes, me * (count - 1), count - 1)
    seqs = lengths.shape[1]
    gram_rows = (count - 1) * (r // peers)
    packed = pl.pallas_call(
        functools.partial(gram_kernel, count, seqs),
        out_shape=jax.ShapeDtypeStruct((peers, gram_rows + 16, r), bf16),
        in_specs=[smem] * 4 + [vmem] * (count + 2),
        out_specs=vmem,
        scratch_shapes=[pltpu.VMEM((2 + count, block, r), bf16)],
        compiler_params=limit(16),
        name="gram",
    )(order, left, right, lengths, *ups, weight, partner)
    packed, weight = lax.optimization_barrier((packed, weight))
    far = [chip_shift(weight, j) for j in range(1, count // 2)]
    downs = [weight, *far, partner, *[core_swap(b) for b in far]]

    packed = lax.all_to_all(packed, "dp", 0, 0, tiled=True)

    line = peers // 2
    sums_shape = (line, (3 * count - 1) * t, r)
    keep, give, token_rows = pl.pallas_call(
        functools.partial(project_kernel, count),
        out_shape=(
            jax.ShapeDtypeStruct(sums_shape, f32),
            jax.ShapeDtypeStruct(sums_shape, bf16),
            jax.ShapeDtypeStruct((peers, t, block), bf16),
        ),
        in_specs=[smem, smem] + [vmem] * (1 + 2 * count),
        out_specs=(vmem, vmem, vmem),
        compiler_params=limit(16),
        name="project",
    )(order, spot_ref, rows, *downs, *ups)
    gram_sum = jnp.sum(packed[:, :gram_rows].astype(f32), axis=0).astype(bf16)
    all_lengths = packed[:, gram_rows, :seqs].astype(jnp.int32)
    own_grams = line_exchange(repeated(gram_sum, line))
    part = (keep + pair_swap(give).astype(f32)).astype(bf16)
    far_rows = [chip_shift(token_rows, j) for j in range(1, count // 2)]
    own_grams, part, *far_rows = lax.optimization_barrier((own_grams, part, *far_rows))
    sums = line_exchange(part)
    all_rows = [token_rows, *far_rows]
    all_rows += [core_swap(b) for b in all_rows]
    sums, all_rows = lax.optimization_barrier((sums, all_rows))
    grams = gather_section(own_grams) + gather_section(pair_swap(own_grams))

    own_held, held = pl.pallas_call(
        functools.partial(recur_kernel, count, width),
        out_shape=(
            jax.ShapeDtypeStruct((line, count + 1, t, r), bf16),
            jax.ShapeDtypeStruct((count // 2 - 1, count + 1, t, r), bf16),
        ),
        in_specs=[smem, smem] + [vmem] * (2 + 2 * count),
        out_specs=(vmem, vmem),
        scratch_shapes=[
            pltpu.VMEM((count, count - 1, peers, r // peers, r), bf16),
            pltpu.VMEM((count, t, r), bf16),
        ],
        compiler_params=limit(16),
        name="recur",
    )(order, spot_ref, sums, square, *grams)
    gain = lax.dynamic_slice_in_dim(norm_gain, spot * block, block, 1)
    own_held, all_lengths, gain = lax.optimization_barrier((own_held, all_lengths, gain))

    states = [[None] * count, [None] * count]
    for j in range(count // 2):
        block_j = repeated(chip_shift(held[j - 1], j), line) if j else own_held
        got = line_exchange(block_j)
        for p, part in enumerate((got, pair_swap(got))):
            states[p][j] = part
            states[p][count // 2 + j] = core_swap(part)

    chunk = min(r, block)
    fisher = pl.pallas_call(
        functools.partial(fisher_kernel, count, seqs, 1.0 / (row_count * peers)),
        out_shape=jax.ShapeDtypeStruct((block, r), f32),
        in_specs=[smem, smem, smem] + [anywhere] * count + [vmem] * (3 * count + 1),
        out_specs=vmem,
        scratch_shapes=[
            pltpu.VMEM((count, peers, t, block), bf16),
            pltpu.VMEM((r, chunk), f32),
            pltpu.VMEM((peers, row_count, chunk), bf16),
            pltpu.VMEM((peers, seqs * r, row_count), bf16),
            pltpu.SemaphoreType.DMA((count,)),
        ],
        compiler_params=limit(24),
        name="squares",
    )(order, place, all_lengths, *far_away(*all_rows), *ups, *states[0], *states[1], gain)
    return fisher[None]


def solution(mesh):
    in_specs = (
        P("dp", None),
        P("dp", None),
        P("section", "dp", None),
        P("section", "dp", None),
        P("section", None),
        P("dp", None),
    )
    out_specs = P("section", "dp", None)
    return jax.shard_map(
        per_device, mesh=mesh, in_specs=in_specs, out_specs=out_specs, check_vma=False
    )
```

time: 160 us -> 146 us (0.912)
  Pallas kernels: 32.5 us -> 25.2 us
  waiting for transfers between devices: 72.6 us -> 65.6 us
  starting transfers between devices: 38 us -> 40.3 us
  other arithmetic: 5.93 us -> 4.31 us
    ppermute x5 -> x6, waiting for transfers between devices: 30.4 us -> 21.3 us  [chip_shift(): lax.ppermute(x, 'section', [(i, (i - 2 * by) % count) for i in range(coun...]
    ppermute x3 -> x4, waiting for transfers between devices: 8.17 us -> 17 us  [pair_swap(): return lax.ppermute(x, 'dp', [(i, i ^ 1) for i in range(peers)])]
    pallas_call x4, Pallas kernels: 14.5 us -> 7.57 us  [the longest x1 2.99 us: per_device(): pl.pallas_call(functools.partial(recur_kernel, count, width), out_shape=(...]
    all_to_all x1, waiting for transfers between devices: 8.26 us -> 3.92 us  [per_device(): packed = lax.all_to_all(packed, 'dp', 0, 0, tiled=True)]
    all_to_all x1 -> x0, starting transfers between devices: 3.64 us -> none  [per_device(): back_sums = lax.all_to_all(back_part, 'dp', 0, 0, tiled=True)]
    all_to_all x3 -> x4, starting transfers between devices: 11.8 us -> 14.9 us  [line_exchange(): return lax.all_to_all(x, 'dp', 0, 0, axis_index_groups=groups, tiled=True)]
    all_to_all x3 -> x4, waiting for transfers between devices: 18.1 us -> 15.3 us  [line_exchange(): return lax.all_to_all(x, 'dp', 0, 0, axis_index_groups=groups, tiled=True)]
    ppermute x3 -> x4, starting transfers between devices: 3.84 us -> 6.54 us  [pair_swap(): return lax.ppermute(x, 'dp', [(i, i ^ 1) for i in range(peers)])]
  transfers between devices with their start and end apart: 26 -> 30, of which waited for: 13 -> 15; matrix products, arithmetic and copies ran while one was open for 6% -> 4% of each run, Pallas kernels for 8% -> 7%
where the time goes in v4:
time: 146 us; the launch traced here: 145 us
  waiting for transfers between devices  65.6 us (45%)
  starting transfers between devices  40.3 us (28%)
  Pallas kernels  25.2 us (17%)
  local copies, waits for them, and re-layouts  8.92 us (6%)
  other arithmetic  4.31 us (3%)
    ppermute x6, waiting for transfers between devices, chip_shift(): lax.ppermute(x, 'section', [(i, (i - 2 * by) % count) for i in range(coun...  21.3 us
    ppermute x4, waiting for transfers between devices, pair_swap(): return lax.ppermute(x, 'dp', [(i, i ^ 1) for i in range(peers)])  17 us
    all_to_all x4, waiting for transfers between devices, line_exchange(): return lax.all_to_all(x, 'dp', 0, 0, axis_index_groups=groups, tiled=True)  15.3 us
    all_to_all x4, starting transfers between devices, line_exchange(): return lax.all_to_all(x, 'dp', 0, 0, axis_index_groups=groups, tiled=True)  14.9 us
    pallas_call x1, Pallas kernels, per_device(): pl.pallas_call(functools.partial(fisher_kernel, count, seqs, 1.0 / (row_c...  12.3 us
    ppermute x6, starting transfers between devices, chip_shift(): lax.ppermute(x, 'section', [(i, (i - 2 * by) % count) for i in range(coun...  6.85 us
    ppermute x4, starting transfers between devices, pair_swap(): return lax.ppermute(x, 'dp', [(i, i ^ 1) for i in range(peers)])  6.54 us
    unnamed x30, local copies, waits for them, and re-layouts  6.48 us
  transfers between devices with their start and end apart: 30, of which 15 were waited for; matrix products, arithmetic and copies ran while one was open for 4% of the time, Pallas kernels for 7%

profile of v4, /device:TPU:0, one launch (start us, length us, event | category | flops | bytes accessed | tf_op | source)
XLA Modules:
  0.0 144.6 jit_solution(10921401283435214563)
XLA Ops:
  0.0 3.0 %collective-permute-start = (bf16[1024,256]{1,0:T(8,128)(2,1)}, bf16[1024,256]{1,0:T(8,128)(2,1)S(1)}, u32[]{:S(2)}, u32[]{:S(2)}) collective-permute-start(bf16[1024,256]{1,0:T(8,128)(2,1)} %bitcast.10), channel_id=1, source_target_pairs={{0,16},{8,24},{16,0},{24,8},{1,17},{9,25},{17,1},{25,9},{2,18},{10... | collective-permute-start | bytes 1572872 | tf_op jit(solution)/shard_map/ppermute | solution.py:27
  3.0 2.3 %prepare.1.rows_ref = bf16[8,64,1024]{2,1,0:T(8,128)(2,1)} custom-call(bf16[128,8192]{1,0:T(8,128)(2,1)} %tokens_ref.1, bf16[128,8192]{1,0:T(8,128)(2,1)} %cot_ref.1), custom_call_target="tpu_custom_call" | custom-call | tf_op jit(solution)/shard_map/prepare/pallas_call | solution.py:315
  5.4 5.9 %all-to-all-start.2 = ((bf16[8,64,1024]{2,1,0:T(8,128)(2,1)}), bf16[8,64,1024]{2,1,0:T(8,128)(2,1)}, u32[]{:S(2)}, u32[]{:S(2)}) async-start(bf16[8,64,1024]{2,1,0:T(8,128)(2,1)} %prepare.1.rows_ref), calls=%async_computation.2 | async-start | bytes 2097152 | tf_op jit(solution)/shard_map/all_to_all | solution.py:346
  11.5 1.0 copy-done.4
  12.6 0.8 weight.1
  13.4 0.6 copy-done.9
  14.5 0.6 collective-permute-done.refs_1_.refs_5_
  15.3 0.7 collective-permute-done.3.refs_5_.refs_2_
  16.0 1.0 collective-permute-done.2.refs_3_.refs_7_
  17.0 1.4 gram.1
  18.4 1.8 %collective-permute-start.4 = (bf16[1024,256]{1,0:T(8,128)(2,1)S(1)}, bf16[1024,256]{1,0:T(8,128)(2,1)}, u32[]{:S(2)}, u32[]{:S(2)}) collective-permute-start(bf16[1024,256]{1,0:T(8,128)(2,1)S(1)} %get-tuple-element.27.refs_4_.refs_0_), channel_id=1, source_target_pairs={{0,16},{8,24},{16,0},{24,8},{1,17},{9,25},{17,1},{25,9},{2,18},{10... | collective-permute-start | bytes 1572872 | tf_op jit(solution)/shard_map/ppermute | solution.py:27
  20.2 12.3 %collective-permute-done.4.refs_1_ = bf16[1024,256]{1,0:T(8,128)(2,1)} collective-permute-done((bf16[1024,256]{1,0:T(8,128)(2,1)S(1)}, bf16[1024,256]{1,0:T(8,128)(2,1)}, u32[]{:S(2)}, u32[]{:S(2)}) %collective-permute-start.4) | collective-permute-done | bytes 524320 | tf_op jit(solution)/shard_map/ppermute | solution.py:27
  32.6 4.5 %all-to-all-done.2.rows_ref = bf16[8,64,1024]{2,1,0:T(8,128)(2,1)} async-done(((bf16[8,64,1024]{2,1,0:T(8,128)(2,1)}), bf16[8,64,1024]{2,1,0:T(8,128)(2,1)}, u32[]{:S(2)}, u32[]{:S(2)}) %all-to-all-start.2) | async-done | bytes 1048608 | tf_op jit(solution)/shard_map/all_to_all | solution.py:346
  37.1 4.1 %all-to-all-start = ((bf16[8,112,256]{2,1,0:T(8,128)(2,1)}), bf16[8,112,256]{2,1,0:T(8,128)(2,1)}, u32[]{:S(2)}, u32[]{:S(2)}) async-start(bf16[8,112,256]{2,1,0:T(8,128)(2,1)} %copy-done.2), calls=%async_computation | async-start | bytes 917504 | tf_op jit(solution)/shard_map/all_to_all | solution.py:367
  41.2 5.3 %project.1 = (f32[4,352,256]{2,1,0:T(8,128)S(1)}, bf16[4,352,256]{2,1,0:T(8,128)(2,1)}, bf16[8,32,1024]{2,1,0:T(8,128)(2,1)}) custom-call(s32[4]{0:T(128)S(1)} %pad_add_fusion.order, s32[1]{0:T(128)} %bitcast.5.spot, bf16[8,64,1024]{2,1,0:T(8,128)(2,1)} %all-to-all-done.2.rows_ref, bf16[1024,256]{1,0:T(8,128)(2,1)S(1)} %get-tuple-element.27.refs_4_.refs_0_, ...), custom_call_target="tpu_custom_call" | custom-call | tf_op jit(solution)/shard_map/project/pallas_call | solution.py:371
  46.5 1.1 copy-done.3
  47.6 1.9 %collective-permute-start.6 = (bf16[4,352,256]{2,1,0:T(8,128)(2,1)}, bf16[4,352,256]{2,1,0:T(8,128)(2,1)S(1)}, u32[]{:S(2)}, u32[]{:S(2)}) collective-permute-start(bf16[4,352,256]{2,1,0:T(8,128)(2,1)} %get-tuple-element.29), channel_id=1, source_target_pairs={{0,1},{1,0},{2,3},{3,2},{4,5},{5,4},{6,7},{7,6},{8,9},{9,8},{10,11... | collective-permute-start | bytes 2162696 | tf_op jit(solution)/shard_map/ppermute | solution.py:50
  50.0 3.9 %all-to-all-done = bf16[8,112,256]{2,1,0:T(8,128)(2,1)} async-done(((bf16[8,112,256]{2,1,0:T(8,128)(2,1)}), bf16[8,112,256]{2,1,0:T(8,128)(2,1)}, u32[]{:S(2)}, u32[]{:S(2)}) %all-to-all-start) | async-done | bytes 458784 | tf_op jit(solution)/shard_map/all_to_all | solution.py:367
  53.9 1.1 slice_reduce_fusion
  55.0 0.7 broadcast_in_dim.6
  55.7 3.4 %all-to-all-start.1 = ((bf16[4,96,256]{2,1,0:T(8,128)(2,1)}), bf16[4,96,256]{2,1,0:T(8,128)(2,1)S(1)}, u32[]{:S(2)}, u32[]{:S(2)}) async-start(bf16[4,96,256]{2,1,0:T(8,128)(2,1)} %broadcast_in_dim.6), calls=%async_computation.1 | async-start | bytes 393216 | tf_op jit(solution)/shard_map/all_to_all | solution.py:56
  59.1 6.8 %collective-permute-done.6 = bf16[4,352,256]{2,1,0:T(8,128)(2,1)S(1)} collective-permute-done((bf16[4,352,256]{2,1,0:T(8,128)(2,1)}, bf16[4,352,256]{2,1,0:T(8,128)(2,1)S(1)}, u32[]{:S(2)}, u32[]{:S(2)}) %collective-permute-start.6) | collective-permute-done | bytes 720928 | tf_op jit(solution)/shard_map/ppermute | solution.py:50
  65.8 2.4 %add_convert_fusion = bf16[4,352,256]{2,1,0:T(8,128)(2,1)} fusion(f32[4,352,256]{2,1,0:T(8,128)} %copy-done.3, bf16[4,352,256]{2,1,0:T(8,128)(2,1)S(1)} %collective-permute-done.6), kind=kLoop, calls=%fused_computation | loop fusion | flops 1081344 | bytes 2883584 | tf_op jit(solution)/shard_map/convert_element_type | solution.py:386
  68.2 4.5 %all-to-all-start.3 = ((bf16[4,352,256]{2,1,0:T(8,128)(2,1)}), bf16[4,352,256]{2,1,0:T(8,128)(2,1)S(1)}, u32[]{:S(2)}, u32[]{:S(2)}) async-start(bf16[4,352,256]{2,1,0:T(8,128)(2,1)} %add_convert_fusion), calls=%async_computation.3 | async-start | bytes 1441792 | tf_op jit(solution)/shard_map/all_to_all | solution.py:56
  72.7 1.5 %collective-permute-start.13 = (bf16[4,96,256]{2,1,0:T(8,128)(2,1)S(1)}, bf16[4,96,256]{2,1,0:T(8,128)(2,1)S(1)}, u32[]{:S(2)}, u32[]{:S(2)}) collective-permute-start(bf16[4,96,256]{2,1,0:T(8,128)(2,1)S(1)} %all-to-all-done.1.refs_0_), channel_id=1, source_target_pairs={{0,1},{1,0},{2,3},{3,2},{4,5},{5,4},{6,7},{7,6},{8,9},{9,8},{10,11... | collective-permute-start | bytes 589832 | tf_op jit(solution)/shard_map/ppermute | solution.py:50
  74.9 5.1 %collective-permute-done.13.refs_4_ = bf16[4,96,256]{2,1,0:T(8,128)(2,1)S(1)} collective-permute-done((bf16[4,96,256]{2,1,0:T(8,128)(2,1)S(1)}, bf16[4,96,256]{2,1,0:T(8,128)(2,1)S(1)}, u32[]{:S(2)}, u32[]{:S(2)}) %collective-permute-start.13) | collective-permute-done | bytes 196640 | tf_op jit(solution)/shard_map/ppermute | solution.py:50
  80.5 0.7 constant_dynamic-slice_fusion.refs_16_
  81.8 0.7 copy-done.6
  82.5 4.2 %collective-permute-done.14.refs_5_ = bf16[4,96,256]{2,1,0:T(8,128)(2,1)} collective-permute-done((bf16[4,96,256]{2,1,0:T(8,128)(2,1)S(1)}, bf16[4,96,256]{2,1,0:T(8,128)(2,1)}, u32[]{:S(2)}, u32[]{:S(2)}) %collective-permute-start.14) | collective-permute-done | bytes 196640 | tf_op jit(solution)/shard_map/ppermute | solution.py:27
  86.7 0.7 slice_convert_fusion
  87.5 3.3 %all-to-all-done.3.sums_ref = bf16[4,352,256]{2,1,0:T(8,128)(2,1)S(1)} async-done(((bf16[4,352,256]{2,1,0:T(8,128)(2,1)}), bf16[4,352,256]{2,1,0:T(8,128)(2,1)S(1)}, u32[]{:S(2)}, u32[]{:S(2)}) %all-to-all-start.3) | async-done | bytes 720928 | tf_op jit(solution)/shard_map/all_to_all | solution.py:56
  90.8 0.9 copy-done.7
  91.7 0.7 copy-done.10
  92.5 3.0 %recur.1 = (bf16[4,5,32,256]{3,2,1,0:T(8,128)(2,1)S(1)}, bf16[1,5,32,256]{3,2,1,0:T(8,128)(2,1)S(1)}) custom-call(s32[4]{0:T(128)S(1)} %pad_add_fusion.order, s32[1]{0:T(128)} %bitcast.5.spot, bf16[4,352,256]{2,1,0:T(8,128)(2,1)S(1)} %all-to-all-done.3.sums_ref, f32[32,1]{1,0:T(8,128)S(1)} %copy-done.10, bf16[4,96,256]{2,1,0:T(8,128)(2,1)S(1)} %all-to-all-done.1.refs_0_, ...), custom_call_target="tpu_custom_call" | custom-call | tf_op jit(solution)/shard_map/recur/pallas_call | solution.py:395
  95.5 0.6 copy-done.12
  96.1 0.7 copy-done.5
  96.8 3.5 %all-to-all-start.4 = ((bf16[4,5,32,256]{3,2,1,0:T(8,128)(2,1)}), bf16[4,5,32,256]{3,2,1,0:T(8,128)(2,1)S(1)}, u32[]{:S(2)}, u32[]{:S(2)}) async-start(bf16[4,5,32,256]{3,2,1,0:T(8,128)(2,1)} %copy-done.5), calls=%async_computation.4 | async-start | bytes 655360 | tf_op jit(solution)/shard_map/all_to_all | solution.py:56
  100.3 0.6 collective-permute-start.17
  100.8 4.1 %collective-permute-done.17 = bf16[5,32,256]{2,1,0:T(8,128)(2,1)S(1)} collective-permute-done((bf16[5,32,256]{2,1,0:T(8,128)(2,1)}, bf16[5,32,256]{2,1,0:T(8,128)(2,1)S(1)}, u32[]{:S(2)}, u32[]{:S(2)}) %collective-permute-start.17) | collective-permute-done | bytes 81952 | tf_op jit(solution)/shard_map/ppermute | solution.py:27
  105.0 5.1 %all-to-all-done.4.refs_8_ = bf16[4,5,32,256]{3,2,1,0:T(8,128)(2,1)S(1)} async-done(((bf16[4,5,32,256]{3,2,1,0:T(8,128)(2,1)}), bf16[4,5,32,256]{3,2,1,0:T(8,128)(2,1)S(1)}, u32[]{:S(2)}, u32[]{:S(2)}) %all-to-all-start.4) | async-done | bytes 327712 | tf_op jit(solution)/shard_map/all_to_all | solution.py:56
  110.1 0.8 broadcast_in_dim.7
  110.9 3.6 %all-to-all-start.5 = ((bf16[4,5,32,256]{3,2,1,0:T(8,128)(2,1)}), bf16[4,5,32,256]{3,2,1,0:T(8,128)(2,1)S(1)}, u32[]{:S(2)}, u32[]{:S(2)}) async-start(bf16[4,5,32,256]{3,2,1,0:T(8,128)(2,1)} %broadcast_in_dim.7), calls=%async_computation.5 | async-start | bytes 655360 | tf_op jit(solution)/shard_map/all_to_all | solution.py:56
  114.5 1.6 %collective-permute-start.20 = (bf16[4,5,32,256]{3,2,1,0:T(8,128)(2,1)S(1)}, bf16[4,5,32,256]{3,2,1,0:T(8,128)(2,1)S(1)}, u32[]{:S(2)}, u32[]{:S(2)}) collective-permute-start(bf16[4,5,32,256]{3,2,1,0:T(8,128)(2,1)S(1)} %all-to-all-done.4.refs_8_), channel_id=1, source_target_pairs={{0,1},{1,0},{2,3},{3,2},{4,5},{5,4},{6,7},{7,6},{8,9},{9,8},{10,11... | collective-permute-start | bytes 983048 | tf_op jit(solution)/shard_map/ppermute | solution.py:50
  116.1 6.9 %all-to-all-done.5.refs_9_ = bf16[4,5,32,256]{3,2,1,0:T(8,128)(2,1)S(1)} async-done(((bf16[4,5,32,256]{3,2,1,0:T(8,128)(2,1)}), bf16[4,5,32,256]{3,2,1,0:T(8,128)(2,1)S(1)}, u32[]{:S(2)}, u32[]{:S(2)}) %all-to-all-start.5) | async-done | bytes 327712 | tf_op jit(solution)/shard_map/all_to_all | solution.py:56
  123.0 1.5 %collective-permute-start.21 = (bf16[4,5,32,256]{3,2,1,0:T(8,128)(2,1)S(1)}, bf16[4,5,32,256]{3,2,1,0:T(8,128)(2,1)}, u32[]{:S(2)}, u32[]{:S(2)}) collective-permute-start(bf16[4,5,32,256]{3,2,1,0:T(8,128)(2,1)S(1)} %all-to-all-done.5.refs_9_), channel_id=1, source_target_pairs={{0,1},{1,0},{2,3},{3,2},{4,5},{5,4},{6,7},{7,6},{8,9},{9,8},{10,11... | collective-permute-start | bytes 983048 | tf_op jit(solution)/shard_map/ppermute | solution.py:50
  125.0 5.1 %collective-permute-done.21.refs_13_ = bf16[4,5,32,256]{3,2,1,0:T(8,128)(2,1)} collective-permute-done((bf16[4,5,32,256]{3,2,1,0:T(8,128)(2,1)S(1)}, bf16[4,5,32,256]{3,2,1,0:T(8,128)(2,1)}, u32[]{:S(2)}, u32[]{:S(2)}) %collective-permute-start.21) | collective-permute-done | bytes 327712 | tf_op jit(solution)/shard_map/ppermute | solution.py:50
  130.3 1.9 %collective-permute-done.23.refs_15_ = bf16[4,5,32,256]{3,2,1,0:T(8,128)(2,1)} collective-permute-done((bf16[4,5,32,256]{3,2,1,0:T(8,128)(2,1)}, bf16[4,5,32,256]{3,2,1,0:T(8,128)(2,1)}, u32[]{:S(2)}, u32[]{:S(2)}) %collective-permute-start.23) | collective-permute-done | bytes 327712 | tf_op jit(solution)/shard_map/ppermute | solution.py:22
  132.1 12.3 %squares.1 = f32[1024,256]{1,0:T(8,128)} custom-call(s32[4]{0:T(128)S(1)} %pad_add_fusion.order, s32[2]{0:T(128)S(1)} %pad_add_fusion.1.place, s32[8,4]{1,0:T(8,128)S(1)} %copy.12.lengths, bf16[8,32,1024]{2,1,0:T(8,128)(2,1)} %get-tuple-element.38.refs_0_, bf16[8,32,1024]{2,1,0:T(8,128)(2,1)} %collective-permute-done.7.refs_1_, ...), custom_call_target="tpu_custom_call" | custom-call | tf_op jit(solution)/shard_map/squares/pallas_call | solution.py:422
  (60 shorter events, 4.0 us)
Async XLA Ops:
  0.0 15.1 %collective-permute-start = (bf16[1024,256]{1,0:T(8,128)(2,1)}, bf16[1024,256]{1,0:T(8,128)(2,1)S(1)}, u32[]{:S(2)}, u32[]{:S(2)}) collective-permute-start(bf16[1024,256]{1,0:T(8,128)(2,1)} %bitcast.10), channel_id=1, source_target_pairs={{0,16},{8,24},{16,0},{24,8},{1,17},{9,25},{17,1},{25,9},{2,18},{10... | collective-permute-start | bytes 1572872 | tf_op jit(solution)/shard_map/ppermute | solution.py:27
  5.3 6.0 %copy-start.1 = (bf16[1,1024,256]{2,1,0:T(8,128)(2,1)S(1)}, bf16[1,1024,256]{2,1,0:T(8,128)(2,1)}, u32[]{:S(2)}) copy-start(bf16[1,1024,256]{2,1,0:T(8,128)(2,1)} %param.11) | copy-start | bytes 1572868
  5.3 6.2 %copy-start = (bf16[8,64,1024]{2,1,0:T(8,128)(2,1)S(1)}, bf16[8,64,1024]{2,1,0:T(8,128)(2,1)}, u32[]{:S(2)}) copy-start(bf16[8,64,1024]{2,1,0:T(8,128)(2,1)} %prepare.1.rows_ref) | copy-start | bytes 3145732
  5.3 6.2 %copy-start.8 = (f32[1,8192]{1,0:T(1,128)S(1)}, f32[1,8192]{1,0:T(1,128)}, u32[]{:S(2)}) copy-start(f32[1,8192]{1,0:T(1,128)} %gain_ref.1) | copy-start | bytes 98308
  5.4 9.7 %copy-start.14 = (s32[12]{0:T(128)S(1)}, s32[12]{0:T(128)}, u32[]{:S(2)}) copy-start(s32[12]{0:T(128)} %constant.52.clone) | copy-start | bytes 148
  5.4 9.8 %copy-start.13 = (s32[12]{0:T(128)S(1)}, s32[12]{0:T(128)}, u32[]{:S(2)}) copy-start(s32[12]{0:T(128)} %constant.53.clone) | copy-start | bytes 148
  5.4 11.6 %copy-start.11 = (s32[1,4]{1,0:T(1,128)S(1)}, s32[1,4]{1,0:T(1,128)}, u32[]{:S(2)}) copy-start(s32[1,4]{1,0:T(1,128)} %lengths.1) | copy-start | bytes 52
  5.4 31.7 %all-to-all-start.2 = ((bf16[8,64,1024]{2,1,0:T(8,128)(2,1)}), bf16[8,64,1024]{2,1,0:T(8,128)(2,1)}, u32[]{:S(2)}, u32[]{:S(2)}) async-start(bf16[8,64,1024]{2,1,0:T(8,128)(2,1)} %prepare.1.rows_ref), calls=%async_computation.2 | async-start | bytes 2097152 | tf_op jit(solution)/shard_map/all_to_all | solution.py:346
  11.4 4.0 %collective-permute-start.1 = (bf16[1024,256]{1,0:T(8,128)(2,1)S(1)}, bf16[1024,256]{1,0:T(8,128)(2,1)S(1)}, u32[]{:S(2)}, u32[]{:S(2)}) collective-permute-start(bf16[1024,256]{1,0:T(8,128)(2,1)S(1)} %bitcast.11), channel_id=1, source_target_pairs={{0,8},{8,0},{16,24},{24,16},{1,9},{9,1},{17,25},{25,17},{2,10},{10... | collective-permute-start | bytes 1572872 | tf_op jit(solution)/shard_map/ppermute | solution.py:22
  11.5 1.0 copy-start.4
  13.4 0.6 copy-start.9
  14.0 2.0 %collective-permute-start.3 = (bf16[1024,256]{1,0:T(8,128)(2,1)S(1)}, bf16[1024,256]{1,0:T(8,128)(2,1)S(1)}, u32[]{:S(2)}, u32[]{:S(2)}) collective-permute-start(bf16[1024,256]{1,0:T(8,128)(2,1)S(1)} %get-tuple-element.27.refs_4_.refs_0_), channel_id=1, source_target_pairs={{0,8},{8,0},{16,24},{24,16},{1,9},{9,1},{17,25},{25,17},{2,10},{10... | collective-permute-start | bytes 1572872 | tf_op jit(solution)/shard_map/ppermute | solution.py:22
  15.1 1.9 %collective-permute-start.2 = (bf16[1024,256]{1,0:T(8,128)(2,1)S(1)}, bf16[1024,256]{1,0:T(8,128)(2,1)S(1)}, u32[]{:S(2)}, u32[]{:S(2)}) collective-permute-start(bf16[1024,256]{1,0:T(8,128)(2,1)S(1)} %collective-permute-done.refs_1_.refs_5_), channel_id=1, source_target_pairs={{0,8},{8,0},{16,24},{24,16},{1,9},{9,1},{17,25},{25,17},{2,10},{10... | collective-permute-start | bytes 1572872 | tf_op jit(solution)/shard_map/ppermute | solution.py:22
  18.4 14.2 %copy-start.2 = (bf16[8,112,256]{2,1,0:T(8,128)(2,1)}, bf16[8,112,256]{2,1,0:T(8,128)(2,1)S(1)}, u32[]{:S(2)}) copy-start(bf16[8,112,256]{2,1,0:T(8,128)(2,1)S(1)} %gram.1) | copy-start | bytes 1376260
  18.4 14.2 %collective-permute-start.4 = (bf16[1024,256]{1,0:T(8,128)(2,1)S(1)}, bf16[1024,256]{1,0:T(8,128)(2,1)}, u32[]{:S(2)}, u32[]{:S(2)}) collective-permute-start(bf16[1024,256]{1,0:T(8,128)(2,1)S(1)} %get-tuple-element.27.refs_4_.refs_0_), channel_id=1, source_target_pairs={{0,16},{8,24},{16,0},{24,8},{1,17},{9,25},{17,1},{25,9},{2,18},{10... | collective-permute-start | bytes 1572872 | tf_op jit(solution)/shard_map/ppermute | solution.py:27
  32.6 8.6 %collective-permute-start.5 = (bf16[1024,256]{1,0:T(8,128)(2,1)}, bf16[1024,256]{1,0:T(8,128)(2,1)}, u32[]{:S(2)}, u32[]{:S(2)}) collective-permute-start(bf16[1024,256]{1,0:T(8,128)(2,1)} %collective-permute-done.4.refs_1_), channel_id=1, source_target_pairs={{0,8},{8,0},{16,24},{24,16},{1,9},{9,1},{17,25},{25,17},{2,10},{10... | collective-permute-start | bytes 1572872 | tf_op jit(solution)/shard_map/ppermute | solution.py:22
  37.1 16.9 %all-to-all-start = ((bf16[8,112,256]{2,1,0:T(8,128)(2,1)}), bf16[8,112,256]{2,1,0:T(8,128)(2,1)}, u32[]{:S(2)}, u32[]{:S(2)}) async-start(bf16[8,112,256]{2,1,0:T(8,128)(2,1)} %copy-done.2), calls=%async_computation | async-start | bytes 917504 | tf_op jit(solution)/shard_map/all_to_all | solution.py:367
  46.5 1.1 copy-start.3
  47.6 18.2 %collective-permute-start.6 = (bf16[4,352,256]{2,1,0:T(8,128)(2,1)}, bf16[4,352,256]{2,1,0:T(8,128)(2,1)S(1)}, u32[]{:S(2)}, u32[]{:S(2)}) collective-permute-start(bf16[4,352,256]{2,1,0:T(8,128)(2,1)} %get-tuple-element.29), channel_id=1, source_target_pairs={{0,1},{1,0},{2,3},{3,2},{4,5},{5,4},{6,7},{7,6},{8,9},{9,8},{10,11... | collective-permute-start | bytes 2162696 | tf_op jit(solution)/shard_map/ppermute | solution.py:50
  49.5 18.7 %collective-permute-start.7 = (bf16[8,32,1024]{2,1,0:T(8,128)(2,1)}, bf16[8,32,1024]{2,1,0:T(8,128)(2,1)}, u32[]{:S(2)}, u32[]{:S(2)}) collective-permute-start(bf16[8,32,1024]{2,1,0:T(8,128)(2,1)} %get-tuple-element.38.refs_0_), channel_id=1, source_target_pairs={{0,16},{8,24},{16,0},{24,8},{1,17},{9,25},{17,1},{25,9},{2,18},{10... | collective-permute-start | bytes 1572872 | tf_op jit(solution)/shard_map/ppermute | solution.py:27
  55.7 12.5 %all-to-all-start.1 = ((bf16[4,96,256]{2,1,0:T(8,128)(2,1)}), bf16[4,96,256]{2,1,0:T(8,128)(2,1)S(1)}, u32[]{:S(2)}, u32[]{:S(2)}) async-start(bf16[4,96,256]{2,1,0:T(8,128)(2,1)} %broadcast_in_dim.6), calls=%async_computation.1 | async-start | bytes 393216 | tf_op jit(solution)/shard_map/all_to_all | solution.py:56
  68.2 22.6 %all-to-all-start.3 = ((bf16[4,352,256]{2,1,0:T(8,128)(2,1)}), bf16[4,352,256]{2,1,0:T(8,128)(2,1)S(1)}, u32[]{:S(2)}, u32[]{:S(2)}) async-start(bf16[4,352,256]{2,1,0:T(8,128)(2,1)} %add_convert_fusion), calls=%async_computation.3 | async-start | bytes 1441792 | tf_op jit(solution)/shard_map/all_to_all | solution.py:56
  72.7 8.5 %collective-permute-start.8 = (bf16[8,32,1024]{2,1,0:T(8,128)(2,1)}, bf16[8,32,1024]{2,1,0:T(8,128)(2,1)}, u32[]{:S(2)}, u32[]{:S(2)}) collective-permute-start(bf16[8,32,1024]{2,1,0:T(8,128)(2,1)} %get-tuple-element.38.refs_0_), channel_id=1, source_target_pairs={{0,8},{8,0},{16,24},{24,16},{1,9},{9,1},{17,25},{25,17},{2,10},{10... | collective-permute-start | bytes 1572872 | tf_op jit(solution)/shard_map/ppermute | solution.py:22
  72.7 7.3 %collective-permute-start.13 = (bf16[4,96,256]{2,1,0:T(8,128)(2,1)S(1)}, bf16[4,96,256]{2,1,0:T(8,128)(2,1)S(1)}, u32[]{:S(2)}, u32[]{:S(2)}) collective-permute-start(bf16[4,96,256]{2,1,0:T(8,128)(2,1)S(1)} %all-to-all-done.1.refs_0_), channel_id=1, source_target_pairs={{0,1},{1,0},{2,3},{3,2},{4,5},{5,4},{6,7},{7,6},{8,9},{9,8},{10,11... | collective-permute-start | bytes 589832 | tf_op jit(solution)/shard_map/ppermute | solution.py:50
  74.2 13.3 %collective-permute-start.9 = (bf16[8,32,1024]{2,1,0:T(8,128)(2,1)}, bf16[8,32,1024]{2,1,0:T(8,128)(2,1)}, u32[]{:S(2)}, u32[]{:S(2)}) collective-permute-start(bf16[8,32,1024]{2,1,0:T(8,128)(2,1)} %collective-permute-done.7.refs_1_), channel_id=1, source_target_pairs={{0,8},{8,0},{16,24},{24,16},{1,9},{9,1},{17,25},{25,17},{2,10},{10... | collective-permute-start | bytes 1572872 | tf_op jit(solution)/shard_map/ppermute | solution.py:22
  74.4 7.3 %collective-permute-start.10 = (bf16[4,96,256]{2,1,0:T(8,128)(2,1)S(1)}, bf16[4,96,256]{2,1,0:T(8,128)(2,1)S(1)}, u32[]{:S(2)}, u32[]{:S(2)}) collective-permute-start(bf16[4,96,256]{2,1,0:T(8,128)(2,1)S(1)} %all-to-all-done.1.refs_0_), channel_id=1, source_target_pairs={{0,16},{8,24},{16,0},{24,8},{1,17},{9,25},{17,1},{25,9},{2,18},{10... | collective-permute-start | bytes 589832 | tf_op jit(solution)/shard_map/ppermute | solution.py:27
  80.0 6.6 %collective-permute-start.14 = (bf16[4,96,256]{2,1,0:T(8,128)(2,1)S(1)}, bf16[4,96,256]{2,1,0:T(8,128)(2,1)}, u32[]{:S(2)}, u32[]{:S(2)}) collective-permute-start(bf16[4,96,256]{2,1,0:T(8,128)(2,1)S(1)} %collective-permute-done.13.refs_4_), channel_id=1, source_target_pairs={{0,16},{8,24},{16,0},{24,8},{1,17},{9,25},{17,1},{25,9},{2,18},{10... | collective-permute-start | bytes 589832 | tf_op jit(solution)/shard_map/ppermute | solution.py:27
  81.2 9.6 %collective-permute-start.11 = (bf16[4,96,256]{2,1,0:T(8,128)(2,1)S(1)}, bf16[4,96,256]{2,1,0:T(8,128)(2,1)}, u32[]{:S(2)}, u32[]{:S(2)}) collective-permute-start(bf16[4,96,256]{2,1,0:T(8,128)(2,1)S(1)} %all-to-all-done.1.refs_0_), channel_id=1, source_target_pairs={{0,8},{8,0},{16,24},{24,16},{1,9},{9,1},{17,25},{25,17},{2,10},{10... | collective-permute-start | bytes 589832 | tf_op jit(solution)/shard_map/ppermute | solution.py:22
  81.2 9.6 %collective-permute-start.15 = (bf16[4,96,256]{2,1,0:T(8,128)(2,1)S(1)}, bf16[4,96,256]{2,1,0:T(8,128)(2,1)}, u32[]{:S(2)}, u32[]{:S(2)}) collective-permute-start(bf16[4,96,256]{2,1,0:T(8,128)(2,1)S(1)} %collective-permute-done.13.refs_4_), channel_id=1, source_target_pairs={{0,8},{8,0},{16,24},{24,16},{1,9},{9,1},{17,25},{25,17},{2,10},{10... | collective-permute-start | bytes 589832 | tf_op jit(solution)/shard_map/ppermute | solution.py:22
  81.7 9.1 %collective-permute-start.12 = (bf16[4,96,256]{2,1,0:T(8,128)(2,1)S(1)}, bf16[4,96,256]{2,1,0:T(8,128)(2,1)}, u32[]{:S(2)}, u32[]{:S(2)}) collective-permute-start(bf16[4,96,256]{2,1,0:T(8,128)(2,1)S(1)} %collective-permute-done.10.refs_1_), channel_id=1, source_target_pairs={{0,8},{8,0},{16,24},{24,16},{1,9},{9,1},{17,25},{25,17},{2,10},{10... | collective-permute-start | bytes 589832 | tf_op jit(solution)/shard_map/ppermute | solution.py:22
  81.8 0.7 copy-start.6
  86.7 4.1 %collective-permute-start.16 = (bf16[4,96,256]{2,1,0:T(8,128)(2,1)}, bf16[4,96,256]{2,1,0:T(8,128)(2,1)}, u32[]{:S(2)}, u32[]{:S(2)}) collective-permute-start(bf16[4,96,256]{2,1,0:T(8,128)(2,1)} %collective-permute-done.14.refs_5_), channel_id=1, source_target_pairs={{0,8},{8,0},{16,24},{24,16},{1,9},{9,1},{17,25},{25,17},{2,10},{10... | collective-permute-start | bytes 589832 | tf_op jit(solution)/shard_map/ppermute | solution.py:22
  90.8 0.9 copy-start.7
  91.7 0.7 copy-start.10
  95.5 0.6 copy-start.12
  96.1 0.7 copy-start.5
  96.8 13.3 %all-to-all-start.4 = ((bf16[4,5,32,256]{3,2,1,0:T(8,128)(2,1)}), bf16[4,5,32,256]{3,2,1,0:T(8,128)(2,1)S(1)}, u32[]{:S(2)}, u32[]{:S(2)}) async-start(bf16[4,5,32,256]{3,2,1,0:T(8,128)(2,1)} %copy-done.5), calls=%async_computation.4 | async-start | bytes 655360 | tf_op jit(solution)/shard_map/all_to_all | solution.py:56
  100.3 4.7 %collective-permute-start.17 = (bf16[5,32,256]{2,1,0:T(8,128)(2,1)}, bf16[5,32,256]{2,1,0:T(8,128)(2,1)S(1)}, u32[]{:S(2)}, u32[]{:S(2)}) collective-permute-start(bf16[5,32,256]{2,1,0:T(8,128)(2,1)} %bitcast.15), channel_id=1, source_target_pairs={{0,16},{8,24},{16,0},{24,8},{1,17},{9,25},{17,1},{25,9},{2,18},{10... | collective-permute-start | bytes 245768 | tf_op jit(solution)/shard_map/ppermute | solution.py:27
  110.9 12.1 %all-to-all-start.5 = ((bf16[4,5,32,256]{3,2,1,0:T(8,128)(2,1)}), bf16[4,5,32,256]{3,2,1,0:T(8,128)(2,1)S(1)}, u32[]{:S(2)}, u32[]{:S(2)}) async-start(bf16[4,5,32,256]{3,2,1,0:T(8,128)(2,1)} %broadcast_in_dim.7), calls=%async_computation.5 | async-start | bytes 655360 | tf_op jit(solution)/shard_map/all_to_all | solution.py:56
  114.5 10.5 %collective-permute-start.20 = (bf16[4,5,32,256]{3,2,1,0:T(8,128)(2,1)S(1)}, bf16[4,5,32,256]{3,2,1,0:T(8,128)(2,1)S(1)}, u32[]{:S(2)}, u32[]{:S(2)}) collective-permute-start(bf16[4,5,32,256]{3,2,1,0:T(8,128)(2,1)S(1)} %all-to-all-done.4.refs_8_), channel_id=1, source_target_pairs={{0,1},{1,0},{2,3},{3,2},{4,5},{5,4},{6,7},{7,6},{8,9},{9,8},{10,11... | collective-permute-start | bytes 983048 | tf_op jit(solution)/shard_map/ppermute | solution.py:50
  123.0 7.2 %collective-permute-start.21 = (bf16[4,5,32,256]{3,2,1,0:T(8,128)(2,1)S(1)}, bf16[4,5,32,256]{3,2,1,0:T(8,128)(2,1)}, u32[]{:S(2)}, u32[]{:S(2)}) collective-permute-start(bf16[4,5,32,256]{3,2,1,0:T(8,128)(2,1)S(1)} %all-to-all-done.5.refs_9_), channel_id=1, source_target_pairs={{0,1},{1,0},{2,3},{3,2},{4,5},{5,4},{6,7},{7,6},{8,9},{9,8},{10,11... | collective-permute-start | bytes 983048 | tf_op jit(solution)/shard_map/ppermute | solution.py:50
  124.5 5.7 %collective-permute-start.18 = (bf16[4,5,32,256]{3,2,1,0:T(8,128)(2,1)S(1)}, bf16[4,5,32,256]{3,2,1,0:T(8,128)(2,1)}, u32[]{:S(2)}, u32[]{:S(2)}) collective-permute-start(bf16[4,5,32,256]{3,2,1,0:T(8,128)(2,1)S(1)} %all-to-all-done.4.refs_8_), channel_id=1, source_target_pairs={{0,8},{8,0},{16,24},{24,16},{1,9},{9,1},{17,25},{25,17},{2,10},{10... | collective-permute-start | bytes 983048 | tf_op jit(solution)/shard_map/ppermute | solution.py:22
  124.5 5.7 %collective-permute-start.19 = (bf16[4,5,32,256]{3,2,1,0:T(8,128)(2,1)S(1)}, bf16[4,5,32,256]{3,2,1,0:T(8,128)(2,1)}, u32[]{:S(2)}, u32[]{:S(2)}) collective-permute-start(bf16[4,5,32,256]{3,2,1,0:T(8,128)(2,1)S(1)} %all-to-all-done.5.refs_9_), channel_id=1, source_target_pairs={{0,8},{8,0},{16,24},{24,16},{1,9},{9,1},{17,25},{25,17},{2,10},{10... | collective-permute-start | bytes 983048 | tf_op jit(solution)/shard_map/ppermute | solution.py:22
  125.0 5.2 %collective-permute-start.22 = (bf16[4,5,32,256]{3,2,1,0:T(8,128)(2,1)S(1)}, bf16[4,5,32,256]{3,2,1,0:T(8,128)(2,1)}, u32[]{:S(2)}, u32[]{:S(2)}) collective-permute-start(bf16[4,5,32,256]{3,2,1,0:T(8,128)(2,1)S(1)} %collective-permute-done.20.refs_12_), channel_id=1, source_target_pairs={{0,8},{8,0},{16,24},{24,16},{1,9},{9,1},{17,25},{25,17},{2,10},{10... | collective-permute-start | bytes 983048 | tf_op jit(solution)/shard_map/ppermute | solution.py:22
  130.2 2.0 %collective-permute-start.23 = (bf16[4,5,32,256]{3,2,1,0:T(8,128)(2,1)}, bf16[4,5,32,256]{3,2,1,0:T(8,128)(2,1)}, u32[]{:S(2)}, u32[]{:S(2)}) collective-permute-start(bf16[4,5,32,256]{3,2,1,0:T(8,128)(2,1)} %collective-permute-done.21.refs_13_), channel_id=1, source_target_pairs={{0,8},{8,0},{16,24},{24,16},{1,9},{9,1},{17,25},{25,17},{2,10},{10... | collective-permute-start | bytes 983048 | tf_op jit(solution)/shard_map/ppermute | solution.py:22

commit v5 on v4

--- a/solution.py
+++ b/solution.py
@@ -41,8 +41,8 @@
     return same + [core_swap(b) for b in same]
 
 
-def far_away(*arrays):
-    return [pltpu.with_memory_space_constraint(a, pltpu.HBM) for a in arrays]
+def kept(x, space):
+    return pltpu.with_memory_space_constraint(x, space)
 
 
 def pair_swap(x):
@@ -133,21 +133,28 @@
 def project_kernel(count, order, spot, rows_ref, *refs):
     downs = refs[:count]
     ups = refs[count : 2 * count]
-    keep_ref, send_ref, tokens_ref = refs[2 * count :]
+    keep_ref, send_ref = refs[2 * count :]
     peers, rows, _ = rows_ref.shape
     t = rows // 2
-    mine = lax.rem(spot[0], 2)
-    tokens_ref[...] = rows_ref[:, :t]
-    x = paired(lambda p: [rows_ref[2 * z + p, :t] for z in range(peers // 2)], mine)
-    c = paired(lambda p: [rows_ref[2 * z + p, t:] for z in range(peers // 2)], mine)
+    x = paired(lambda p: [rows_ref[2 * z + p, :t] for z in range(peers // 2)], lax.rem(spot[0], 2))
     for i in range(count):
         layer = order[i]
         store_pair(keep_ref, send_ref, layer, t, dot(x, downs[i][...], 1, 0))
-        store_pair(keep_ref, send_ref, 2 * count - 1 + layer, t, dot(c, ups[i][...], 1, 0))
 
         @pl.when(layer < count - 1)
         def _():
             store_pair(keep_ref, send_ref, count + layer, t, dot(x, ups[i][...], 1, 0))
+
+
+def project_cot_kernel(count, order, spot, rows_ref, *refs):
+    ups = refs[:count]
+    keep_ref, send_ref, tokens_ref = refs[count:]
+    peers, rows, _ = rows_ref.shape
+    t = rows // 2
+    tokens_ref[...] = rows_ref[:, :t]
+    c = paired(lambda p: [rows_ref[2 * z + p, t:] for z in range(peers // 2)], lax.rem(spot[0], 2))
+    for i in range(count):
+        store_pair(keep_ref, send_ref, order[i], t, dot(c, ups[i][...], 1, 0))
 
 
 def recur_kernel(count, width, order, spot, sums_ref, sq_ref, *refs):
@@ -156,12 +163,9 @@
     copies, _, t, _ = own_ref.shape
     half = count // 2
 
-    def put(j, m, value):
-        if j:
-            out_ref[j - 1, m] = value
-        else:
-            for z in range(copies):
-                own_ref[z, m] = value
+    def put(m, value):
+        for z in range(copies):
+            own_ref[z, m] = value
 
     per = count - 1
     mine = lax.rem(spot[0], 2)
@@ -203,8 +207,7 @@
         hus.append(list(hu))
         if l < count - 1:
             act = (pre * jax.nn.sigmoid(pre)).astype(bf16)
-            for j in range(half):
-                put(j, 2 + l, act)
+            put(2 + l, act)
             wide = act.astype(f32)
             for j in range(l + 1, count):
                 proj[j] = proj[j] + dot(act, mixed(l, j), 1, 0)
@@ -222,18 +225,25 @@
                 dot(grad, mixed(j, l), 1, 1) - invs[l] * invs[l] * inner * hus[l][j]
             )
     chip = order[0] // 2
-    for j in range(half):
-        other = lax.rem(chip + half - j, half)
-        put(j, 0, grads[2 * other])
-        put(j, 1, grads[2 * other + 1])
+    for m in range(2):
+        put(m, grads[2 * chip + m])
+        for j in range(1, half):
+            out_ref[j - 1, m] = grads[2 * lax.rem(chip + half - j, half) + m]
 
 
 def fisher_kernel(count, seqs, scale, order, place, lengths, *refs):
     half = count // 2
     sources = refs[:count]
     ups = refs[count : 2 * count]
-    states = refs[2 * count : 4 * count]
-    gain_ref, out_ref, rows, acc, hidden, masks, sems = refs[4 * count :]
+    rest = list(refs[2 * count :])
+    states = []
+    for i in range(2 * count):
+        if i % half:
+            states.append((rest.pop(0), rest.pop(0), 0))
+        else:
+            both = rest.pop(0)
+            states.append((both, both, 2))
+    gain_ref, out_ref, rows, acc, hidden, masks, sems = rest
     copies = [pltpu.make_async_copy(sources[i], rows.at[i], sems.at[i]) for i in range(count)]
     for copy in copies:
         copy.start()
@@ -251,16 +261,20 @@
         inside = (spot >= i * t) & (spot < (i + 1) * t)
         position = jnp.where(inside, spot + (order[i] - i) * t, position)
 
-    def column(n, m):
-        first = n // line * count
-        return jnp.concatenate([states[first + i][n % line, m] for i in range(count)], axis=0)
+    def grad_rows(n, m):
+        found = states[n // line * count :][:count]
+        return jnp.concatenate([grads[n % line, m] for grads, _, _ in found], axis=0)
+
+    def act_rows(n, k):
+        found = states[n // line * count :][:count]
+        return jnp.concatenate([acts[n % line, shift + k] for _, acts, shift in found], axis=0)
 
     acts = []
     for i in range(1, count):
-        act = jnp.concatenate([column(n, 2 + jnp.minimum(order[i], count - 2)) for n in range(peers)], axis=0)
+        act = jnp.concatenate([act_rows(n, jnp.minimum(order[i], count - 2)) for n in range(peers)], axis=0)
         acts.append(jnp.where(order[i] < me, act, jnp.zeros_like(act)))
     for n in range(peers):
-        grad = column(n, lax.rem(me, 2)).astype(f32).T
+        grad = grad_rows(n, lax.rem(me, 2)).astype(f32).T
         start = 0
         for q in range(seqs):
             stop = start + lengths[names[n], q]
@@ -279,11 +293,10 @@
             h = jnp.concatenate([rows[i, names[n], :, cols] for i in range(count)], axis=0).astype(f32)
             hidden[n] = (h + update[n * span : (n + 1) * span]).astype(bf16)
         for n in range(peers):
-            g = dot(masks[n], hidden[n], 1, 0)
-            g = g * g
-            total = g[:r]
-            for q in range(1, seqs):
-                total = total + g[q * r : (q + 1) * r]
+            total = None
+            for q in range(seqs):
+                g = dot(masks[n, q * r : (q + 1) * r], hidden[n], 1, 0)
+                total = g * g if total is None else total + g * g
             if n == 0:
                 acc[...] = total
             else:
@@ -367,25 +380,40 @@
     packed = lax.all_to_all(packed, "dp", 0, 0, tiled=True)
 
     line = peers // 2
-    sums_shape = (line, (3 * count - 1) * t, r)
-    keep, give, token_rows = pl.pallas_call(
+
+    def pair_shapes(blocks):
+        return (
+            jax.ShapeDtypeStruct((line, blocks * t, r), f32),
+            jax.ShapeDtypeStruct((line, blocks * t, r), bf16),
+        )
+
+    def pair_sum(keep, give):
+        return (keep + give.astype(f32)).astype(bf16)
+
+    back_keep, back_give, token_rows = pl.pallas_call(
+        functools.partial(project_cot_kernel, count),
+        out_shape=(*pair_shapes(count), jax.ShapeDtypeStruct((peers, t, block), bf16)),
+        in_specs=[smem, smem] + [vmem] * (1 + count),
+        out_specs=(vmem, vmem, vmem),
+        compiler_params=limit(16),
+        name="project_cot",
+    )(order, spot_ref, rows, *ups)
+    back_part = pair_sum(back_keep, pair_swap(back_give))
+    far_rows = [chip_shift(token_rows, j) for j in range(1, count // 2)]
+    keep, give = pl.pallas_call(
         functools.partial(project_kernel, count),
-        out_shape=(
-            jax.ShapeDtypeStruct(sums_shape, f32),
-            jax.ShapeDtypeStruct(sums_shape, bf16),
-            jax.ShapeDtypeStruct((peers, t, block), bf16),
-        ),
+        out_shape=pair_shapes(2 * count - 1),
         in_specs=[smem, smem] + [vmem] * (1 + 2 * count),
-        out_specs=(vmem, vmem, vmem),
+        out_specs=(vmem, vmem),
         compiler_params=limit(16),
         name="project",
     )(order, spot_ref, rows, *downs, *ups)
+    got, *far_rows = lax.optimization_barrier((pair_swap(give), *far_rows))
     gram_sum = jnp.sum(packed[:, :gram_rows].astype(f32), axis=0).astype(bf16)
     all_lengths = packed[:, gram_rows, :seqs].astype(jnp.int32)
     own_grams = line_exchange(repeated(gram_sum, line))
-    part = (keep + pair_swap(give).astype(f32)).astype(bf16)
-    far_rows = [chip_shift(token_rows, j) for j in range(1, count // 2)]
-    own_grams, part, *far_rows = lax.optimization_barrier((own_grams, part, *far_rows))
+    part = jnp.concatenate([pair_sum(keep, got), back_part], axis=1)
+    own_grams, part = lax.optimization_barrier((own_grams, part))
     sums = line_exchange(part)
     all_rows = [token_rows, *far_rows]
     all_rows += [core_swap(b) for b in all_rows]
@@ -395,8 +423,8 @@
     own_held, held = pl.pallas_call(
         functools.partial(recur_kernel, count, width),
         out_shape=(
-            jax.ShapeDtypeStruct((line, count + 1, t, r), bf16),
-            jax.ShapeDtypeStruct((count // 2 - 1, count + 1, t, r), bf16),
+            pltpu.HBM((line, count + 1, t, r), bf16),
+            pltpu.HBM((count // 2 - 1, 2, t, r), bf16),
         ),
         in_specs=[smem, smem] + [vmem] * (2 + 2 * count),
         out_specs=(vmem, vmem),
@@ -406,23 +434,33 @@
         ],
         compiler_params=limit(16),
         name="recur",
-    )(order, spot_ref, sums, square, *grams)
+    )(order, spot_ref, sums, kept(square, pltpu.HBM), *[kept(g, pltpu.VMEM) for g in grams])
     gain = lax.dynamic_slice_in_dim(norm_gain, spot * block, block, 1)
     own_held, all_lengths, gain = lax.optimization_barrier((own_held, all_lengths, gain))
 
+    half = count // 2
+    own = line_exchange(own_held)
+    held = [chip_shift(held[j - 1], j) for j in range(1, half)]
+    own, *held = lax.optimization_barrier((own, *held))
+    own = [own, pair_swap(own)]
+    acts = [x[:, 2:] for x in own]
     states = [[None] * count, [None] * count]
-    for j in range(count // 2):
-        block_j = repeated(chip_shift(held[j - 1], j), line) if j else own_held
-        got = line_exchange(block_j)
-        for p, part in enumerate((got, pair_swap(got))):
-            states[p][j] = part
-            states[p][count // 2 + j] = core_swap(part)
+    for j in range(half):
+        if j:
+            grads = line_exchange(repeated(held[j - 1], line))
+            blocks = [[g, chip_shift(a, j)] for g, a in zip([grads, pair_swap(grads)], acts)]
+        else:
+            blocks = [[x] for x in own]
+        for p in range(2):
+            states[p][j] = blocks[p]
+            states[p][half + j] = [core_swap(x) for x in blocks[p]]
+    flat = [x for row in states for parts in row for x in parts]
 
     chunk = min(r, block)
     fisher = pl.pallas_call(
         functools.partial(fisher_kernel, count, seqs, 1.0 / (row_count * peers)),
         out_shape=jax.ShapeDtypeStruct((block, r), f32),
-        in_specs=[smem, smem, smem] + [anywhere] * count + [vmem] * (3 * count + 1),
+        in_specs=[smem, smem, smem] + [anywhere] * count + [vmem] * (count + len(flat) + 1),
         out_specs=vmem,
         scratch_shapes=[
             pltpu.VMEM((count, peers, t, block), bf16),
@@ -433,7 +471,7 @@
         ],
         compiler_params=limit(24),
         name="squares",
-    )(order, place, all_lengths, *far_away(*all_rows), *ups, *states[0], *states[1], gain)
+    )(order, place, all_lengths, *[kept(x, pltpu.HBM) for x in all_rows], *ups, *flat, gain)
     return fisher[None]
 
 

time: 146 us -> 140 us (0.959)
  waiting for transfers between devices: 65.6 us -> 52.7 us
  Pallas kernels: 25.2 us -> 28 us
  starting transfers between devices: 40.3 us -> 42.9 us
    all_to_all x4, waiting for transfers between devices: 15.3 us -> 10.5 us  [line_exchange(): return lax.all_to_all(x, 'dp', 0, 0, axis_index_groups=groups, tiled=True)]
    all_to_all x1, waiting for transfers between devices: 3.92 us -> 0.01 us  [per_device(): packed = lax.all_to_all(packed, 'dp', 0, 0, tiled=True)]
    ppermute x4 -> x5, waiting for transfers between devices: 17 us -> 13.9 us  [pair_swap(): return lax.ppermute(x, 'dp', [(i, i ^ 1) for i in range(peers)])]
    ppermute x4 -> x5, starting transfers between devices: 6.54 us -> 4.83 us  [pair_swap(): return lax.ppermute(x, 'dp', [(i, i ^ 1) for i in range(peers)])]
    ppermute x6 -> x8, starting transfers between devices: 6.85 us -> 8.4 us  [chip_shift(): lax.ppermute(x, 'section', [(i, (i - 2 * by) % count) for i in range(coun...]
    all_to_all x1, waiting for transfers between devices: 4.5 us -> 6.05 us  [per_device(): rows = lax.all_to_all(send, 'dp', 0, 0, tiled=True)]
    pallas_call x1 -> x2, Pallas kernels: 5.28 us -> 6.77 us  [the longest x1 4.26 us: per_device(): pl.pallas_call(functools.partial(project_kernel, count), out_shape=pair_s...]
    ppermute x6 -> x8, waiting for transfers between devices: 21.3 us -> 19.9 us  [chip_shift(): lax.ppermute(x, 'section', [(i, (i - 2 * by) % count) for i in range(coun...]
  transfers between devices with their start and end apart: 30 -> 35, of which waited for: 15 -> 15; matrix products, arithmetic and copies ran while one was open for 4% -> 7% of each run, Pallas kernels for 7% -> 8%
where the time goes in v5:
time: 140 us; the launch traced here: 139 us
  waiting for transfers between devices  52.7 us (38%)
  starting transfers between devices  42.9 us (31%)
  Pallas kernels  28 us (20%)
  local copies, waits for them, and re-layouts  9.99 us (7%)
  other arithmetic  5.12 us (4%)
    ppermute x8, waiting for transfers between devices, chip_shift(): lax.ppermute(x, 'section', [(i, (i - 2 * by) % count) for i in range(coun...  19.9 us
    all_to_all x4, starting transfers between devices, line_exchange(): return lax.all_to_all(x, 'dp', 0, 0, axis_index_groups=groups, tiled=True)  16.2 us
    ppermute x5, waiting for transfers between devices, pair_swap(): return lax.ppermute(x, 'dp', [(i, i ^ 1) for i in range(peers)])  13.9 us
    pallas_call x1, Pallas kernels, per_device(): pl.pallas_call(functools.partial(fisher_kernel, count, seqs, 1.0 / (row_c...  11.7 us
    all_to_all x4, waiting for transfers between devices, line_exchange(): return lax.all_to_all(x, 'dp', 0, 0, axis_index_groups=groups, tiled=True)  10.5 us
    ppermute x8, starting transfers between devices, chip_shift(): lax.ppermute(x, 'section', [(i, (i - 2 * by) % count) for i in range(coun...  8.4 us
    all_to_all x1, starting transfers between devices, per_device(): rows = lax.all_to_all(send, 'dp', 0, 0, tiled=True)  7.4 us
    all_to_all x1, waiting for transfers between devices, per_device(): rows = lax.all_to_all(send, 'dp', 0, 0, tiled=True)  6.05 us
  transfers between devices with their start and end apart: 35, of which 15 were waited for; matrix products, arithmetic and copies ran while one was open for 7% of the time, Pallas kernels for 8%

profile of v5, /device:TPU:0, one launch (start us, length us, event | category | flops | bytes accessed | tf_op | source)
XLA Modules:
  0.0 139.1 jit_solution(15769734258802119137)
XLA Ops:
  0.0 2.3 %prepare.1.rows_ref = bf16[8,64,1024]{2,1,0:T(8,128)(2,1)} custom-call(bf16[128,8192]{1,0:T(8,128)(2,1)} %tokens_ref.1, bf16[128,8192]{1,0:T(8,128)(2,1)} %cot_ref.1), custom_call_target="tpu_custom_call" | custom-call | tf_op jit(solution)/shard_map/prepare/pallas_call | solution.py:328
  2.4 7.4 %all-to-all-start.2 = ((bf16[8,64,1024]{2,1,0:T(8,128)(2,1)}), bf16[8,64,1024]{2,1,0:T(8,128)(2,1)S(1)}, u32[]{:S(2)}, u32[]{:S(2)}) async-start(bf16[8,64,1024]{2,1,0:T(8,128)(2,1)} %prepare.1.rows_ref), calls=%async_computation.2 | async-start | bytes 2097152 | tf_op jit(solution)/shard_map/all_to_all | solution.py:359
  9.8 1.6 %collective-permute-start = (bf16[1024,256]{1,0:T(8,128)(2,1)S(1)}, bf16[1024,256]{1,0:T(8,128)(2,1)S(1)}, u32[]{:S(2)}, u32[]{:S(2)}) collective-permute-start(bf16[1024,256]{1,0:T(8,128)(2,1)S(1)} %bitcast.10), channel_id=1, source_target_pairs={{0,16},{8,24},{16,0},{24,8},{1,17},{9,25},{17,1},{25,9},{2,18},{10... | collective-permute-start | bytes 1572872 | tf_op jit(solution)/shard_map/ppermute | solution.py:27
  11.5 1.0 copy-done.5
  12.5 1.6 %weight.1 = (f32[32,1]{1,0:T(8,128)S(1)}, bf16[1024,256]{1,0:T(8,128)(2,1)}) custom-call(s32[2]{0:T(128)S(1)} %pad_add_fusion.1.place, bf16[8,64,1024]{2,1,0:T(8,128)(2,1)S(1)} %copy-done, bf16[1,1024,256]{2,1,0:T(8,128)(2,1)S(1)} %copy-done.5, f32[1,8192]{1,0:T(1,128)S(1)} %copy-done.9), custom_call_target="tpu_custom_call" | custom-call | tf_op jit(solution)/shard_map/weight/pallas_call | solution.py:336
  15.3 8.0 %collective-permute-done.refs_1_.refs_5_ = bf16[1024,256]{1,0:T(8,128)(2,1)S(1)} collective-permute-done((bf16[1024,256]{1,0:T(8,128)(2,1)S(1)}, bf16[1024,256]{1,0:T(8,128)(2,1)S(1)}, u32[]{:S(2)}, u32[]{:S(2)}) %collective-permute-start) | collective-permute-done | bytes 524320 | tf_op jit(solution)/shard_map/ppermute | solution.py:27
  23.5 1.7 %collective-permute-done.2.refs_3_.refs_7_ = bf16[1024,256]{1,0:T(8,128)(2,1)S(1)} collective-permute-done((bf16[1024,256]{1,0:T(8,128)(2,1)S(1)}, bf16[1024,256]{1,0:T(8,128)(2,1)S(1)}, u32[]{:S(2)}, u32[]{:S(2)}) %collective-permute-start.2) | collective-permute-done | bytes 524320 | tf_op jit(solution)/shard_map/ppermute | solution.py:22
  25.2 2.0 %gram.1 = bf16[8,112,256]{2,1,0:T(8,128)(2,1)S(1)} custom-call(s32[4]{0:T(128)S(1)} %pad_add_fusion.order, s32[3]{0:T(128)S(1)} %dynamic_slice.9.left, s32[3]{0:T(128)S(1)} %dynamic_slice.10.right, s32[1,4]{1,0:T(1,128)S(1)} %copy-done.11, bf16[1024,256]{1,0:T(8,128)(2,1)S(1)} %bitcast.12, bf16[1024,256]{1,0:T(8,128)(2,1)S(1)} %collective-permute-done.refs_1_.refs_5_, ...), custom_call_target="tpu_custom_call" | custom-call | tf_op jit(solution)/shard_map/gram/pallas_call | solution.py:367
  27.3 0.8 copy-done.2
  28.0 1.5 %collective-permute-start.4 = (bf16[1024,256]{1,0:T(8,128)(2,1)}, bf16[1024,256]{1,0:T(8,128)(2,1)}, u32[]{:S(2)}, u32[]{:S(2)}) collective-permute-start(bf16[1024,256]{1,0:T(8,128)(2,1)} %get-tuple-element.32.refs_4_.refs_0_), channel_id=1, source_target_pairs={{0,16},{8,24},{16,0},{24,8},{1,17},{9,25},{17,1},{25,9},{2,18},{10... | collective-permute-start | bytes 1572872 | tf_op jit(solution)/shard_map/ppermute | solution.py:27
  29.5 6.1 %all-to-all-done.2.rows_ref = bf16[8,64,1024]{2,1,0:T(8,128)(2,1)S(1)} async-done(((bf16[8,64,1024]{2,1,0:T(8,128)(2,1)}), bf16[8,64,1024]{2,1,0:T(8,128)(2,1)S(1)}, u32[]{:S(2)}, u32[]{:S(2)}) %all-to-all-start.2) | async-done | bytes 1048608 | tf_op jit(solution)/shard_map/all_to_all | solution.py:359
  35.6 4.1 %all-to-all-start = ((bf16[8,112,256]{2,1,0:T(8,128)(2,1)}), bf16[8,112,256]{2,1,0:T(8,128)(2,1)}, u32[]{:S(2)}, u32[]{:S(2)}) async-start(bf16[8,112,256]{2,1,0:T(8,128)(2,1)} %copy-done.2), calls=%async_computation | async-start | bytes 917504 | tf_op jit(solution)/shard_map/all_to_all | solution.py:380
  39.7 2.6 %collective-permute-done.4.refs_1_ = bf16[1024,256]{1,0:T(8,128)(2,1)} collective-permute-done((bf16[1024,256]{1,0:T(8,128)(2,1)}, bf16[1024,256]{1,0:T(8,128)(2,1)}, u32[]{:S(2)}, u32[]{:S(2)}) %collective-permute-start.4) | collective-permute-done | bytes 524320 | tf_op jit(solution)/shard_map/ppermute | solution.py:27
  42.3 2.5 %project_cot.1 = (f32[4,128,256]{2,1,0:T(8,128)S(1)}, bf16[4,128,256]{2,1,0:T(8,128)(2,1)S(1)}, bf16[8,32,1024]{2,1,0:T(8,128)(2,1)}) custom-call(s32[4]{0:T(128)S(1)} %pad_add_fusion.order, s32[1]{0:T(128)} %bitcast.5.spot, bf16[8,64,1024]{2,1,0:T(8,128)(2,1)S(1)} %all-to-all-done.2.rows_ref, bf16[1024,256]{1,0:T(8,128)(2,1)S(1)} %bitcast.13, ...), custom_call_target="tpu_custom_call" | custom-call | tf_op jit(solution)/shard_map/project_cot/pallas_call | solution.py:393
  44.8 1.5 %collective-permute-start.7 = (bf16[8,32,1024]{2,1,0:T(8,128)(2,1)}, bf16[8,32,1024]{2,1,0:T(8,128)(2,1)}, u32[]{:S(2)}, u32[]{:S(2)}) collective-permute-start(bf16[8,32,1024]{2,1,0:T(8,128)(2,1)} %get-tuple-element.46.refs_0_), channel_id=1, source_target_pairs={{0,16},{8,24},{16,0},{24,8},{1,17},{9,25},{17,1},{25,9},{2,18},{10... | collective-permute-start | bytes 1572872 | tf_op jit(solution)/shard_map/ppermute | solution.py:27
  46.3 1.7 %collective-permute-start.8 = (bf16[4,128,256]{2,1,0:T(8,128)(2,1)S(1)}, bf16[4,128,256]{2,1,0:T(8,128)(2,1)}, u32[]{:S(2)}, u32[]{:S(2)}) collective-permute-start(bf16[4,128,256]{2,1,0:T(8,128)(2,1)S(1)} %get-tuple-element.38), channel_id=1, source_target_pairs={{0,1},{1,0},{2,3},{3,2},{4,5},{5,4},{6,7},{7,6},{8,9},{9,8},{10,11... | collective-permute-start | bytes 786440 | tf_op jit(solution)/shard_map/ppermute | solution.py:50
  48.0 4.3 %project.1 = (f32[4,224,256]{2,1,0:T(8,128)S(1)}, bf16[4,224,256]{2,1,0:T(8,128)(2,1)}) custom-call(s32[4]{0:T(128)S(1)} %pad_add_fusion.order, s32[1]{0:T(128)} %bitcast.5.spot, bf16[8,64,1024]{2,1,0:T(8,128)(2,1)S(1)} %all-to-all-done.2.rows_ref, bf16[1024,256]{1,0:T(8,128)(2,1)} %get-tuple-element.32.refs_4_.refs_0_, ...), custom_call_target="tpu_custom_call" | custom-call | tf_op jit(solution)/shard_map/project/pallas_call | solution.py:403
  52.3 0.9 copy-done.3
  53.6 1.1 slice_reduce_fusion
  54.6 0.7 broadcast_in_dim.6
  55.3 4.7 %all-to-all-start.1 = ((bf16[4,96,256]{2,1,0:T(8,128)(2,1)}), bf16[4,96,256]{2,1,0:T(8,128)(2,1)S(1)}, u32[]{:S(2)}, u32[]{:S(2)}) async-start(bf16[4,96,256]{2,1,0:T(8,128)(2,1)} %broadcast_in_dim.6), calls=%async_computation.1 | async-start | bytes 393216 | tf_op jit(solution)/shard_map/all_to_all | solution.py:56
  60.1 1.2 add_convert_fusion.1
  61.2 4.6 %collective-permute-done.6 = bf16[4,224,256]{2,1,0:T(8,128)(2,1)S(1)} collective-permute-done((bf16[4,224,256]{2,1,0:T(8,128)(2,1)}, bf16[4,224,256]{2,1,0:T(8,128)(2,1)S(1)}, u32[]{:S(2)}, u32[]{:S(2)}) %collective-permute-start.6) | collective-permute-done | bytes 458784 | tf_op jit(solution)/shard_map/ppermute | solution.py:50
  65.8 0.8 copy-done.12
  66.6 1.1 add_convert_fusion
  67.7 0.9 pad_maximum_fusion
  68.6 4.5 %all-to-all-start.3 = ((bf16[4,352,256]{2,1,0:T(8,128)(2,1)}), bf16[4,352,256]{2,1,0:T(8,128)(2,1)S(1)}, u32[]{:S(2)}, u32[]{:S(2)}) async-start(bf16[4,352,256]{2,1,0:T(8,128)(2,1)} %pad_maximum_fusion), calls=%async_computation.3 | async-start | bytes 1441792 | tf_op jit(solution)/shard_map/all_to_all | solution.py:56
  73.1 0.8 collective-permute-start.14
  74.1 0.8 collective-permute-start.11
  75.0 5.5 %collective-permute-done.14.refs_4_ = bf16[4,96,256]{2,1,0:T(8,128)(2,1)S(1)} collective-permute-done((bf16[4,96,256]{2,1,0:T(8,128)(2,1)S(1)}, bf16[4,96,256]{2,1,0:T(8,128)(2,1)S(1)}, u32[]{:S(2)}, u32[]{:S(2)}) %collective-permute-start.14) | collective-permute-done | bytes 196640 | tf_op jit(solution)/shard_map/ppermute | solution.py:50
  81.5 5.4 %collective-permute-done.15.refs_5_ = bf16[4,96,256]{2,1,0:T(8,128)(2,1)S(1)} collective-permute-done((bf16[4,96,256]{2,1,0:T(8,128)(2,1)S(1)}, bf16[4,96,256]{2,1,0:T(8,128)(2,1)S(1)}, u32[]{:S(2)}, u32[]{:S(2)}) %collective-permute-start.15) | collective-permute-done | bytes 196640 | tf_op jit(solution)/shard_map/ppermute | solution.py:27
  87.0 0.7 slice_convert_fusion
  88.4 2.7 %all-to-all-done.3.sums_ref = bf16[4,352,256]{2,1,0:T(8,128)(2,1)S(1)} async-done(((bf16[4,352,256]{2,1,0:T(8,128)(2,1)}), bf16[4,352,256]{2,1,0:T(8,128)(2,1)S(1)}, u32[]{:S(2)}, u32[]{:S(2)}) %all-to-all-start.3) | async-done | bytes 720928 | tf_op jit(solution)/shard_map/all_to_all | solution.py:56
  91.1 3.5 %recur.1 = (bf16[4,5,32,256]{3,2,1,0:T(8,128)(2,1)}, bf16[1,2,32,256]{3,2,1,0:T(8,128)(2,1)}) custom-call(s32[4]{0:T(128)S(1)} %pad_add_fusion.order, s32[1]{0:T(128)} %bitcast.5.spot, bf16[4,352,256]{2,1,0:T(8,128)(2,1)S(1)} %all-to-all-done.3.sums_ref, f32[32,1]{1,0:T(8,128)} %copy-done.10, bf16[4,96,256]{2,1,0:T(8,128)(2,1)S(1)} %all-to-all-done.1.refs_0_, ...), custom_call_target="tpu_custom_call" | custom-call | tf_op jit(solution)/shard_map/recur/pallas_call | solution.py:423
  94.6 3.5 %all-to-all-start.4 = ((bf16[4,5,32,256]{3,2,1,0:T(8,128)(2,1)}), bf16[4,5,32,256]{3,2,1,0:T(8,128)(2,1)S(1)}, u32[]{:S(2)}, u32[]{:S(2)}) async-start(bf16[4,5,32,256]{3,2,1,0:T(8,128)(2,1)} %get-tuple-element.50), calls=%async_computation.4 | async-start | bytes 655360 | tf_op jit(solution)/shard_map/all_to_all | solution.py:56
  98.1 0.7 collective-permute-start.18
  98.8 3.4 %collective-permute-done.18 = bf16[2,32,256]{2,1,0:T(8,128)(2,1)S(1)} collective-permute-done((bf16[2,32,256]{2,1,0:T(8,128)(2,1)}, bf16[2,32,256]{2,1,0:T(8,128)(2,1)S(1)}, u32[]{:S(2)}, u32[]{:S(2)}) %collective-permute-start.18) | collective-permute-done | bytes 32800 | tf_op jit(solution)/shard_map/ppermute | solution.py:27
  102.3 5.7 %all-to-all-done.4.refs_8_ = bf16[4,5,32,256]{3,2,1,0:T(8,128)(2,1)S(1)} async-done(((bf16[4,5,32,256]{3,2,1,0:T(8,128)(2,1)}), bf16[4,5,32,256]{3,2,1,0:T(8,128)(2,1)S(1)}, u32[]{:S(2)}, u32[]{:S(2)}) %all-to-all-start.4) | async-done | bytes 327712 | tf_op jit(solution)/shard_map/all_to_all | solution.py:56
  108.0 0.8 collective-permute-start.23
  109.4 3.5 %all-to-all-start.5 = ((bf16[4,2,32,256]{3,2,1,0:T(8,128)(2,1)}), bf16[4,2,32,256]{3,2,1,0:T(8,128)(2,1)S(1)}, u32[]{:S(2)}, u32[]{:S(2)}) async-start(bf16[4,2,32,256]{3,2,1,0:T(8,128)(2,1)} %broadcast_in_dim.7), calls=%async_computation.5 | async-start | bytes 262144 | tf_op jit(solution)/shard_map/all_to_all | solution.py:56
  113.6 1.2 collective-permute-start.19
  116.6 2.0 %all-to-all-done.5.refs_9_ = bf16[4,2,32,256]{3,2,1,0:T(8,128)(2,1)S(1)} async-done(((bf16[4,2,32,256]{3,2,1,0:T(8,128)(2,1)}), bf16[4,2,32,256]{3,2,1,0:T(8,128)(2,1)S(1)}, u32[]{:S(2)}, u32[]{:S(2)}) %all-to-all-start.5) | async-done | bytes 131104 | tf_op jit(solution)/shard_map/all_to_all | solution.py:56
  118.6 1.2 collective-permute-start.24
  120.4 3.2 %collective-permute-done.24.refs_15_ = bf16[4,2,32,256]{3,2,1,0:T(8,128)(2,1)S(1)} collective-permute-done((bf16[4,2,32,256]{3,2,1,0:T(8,128)(2,1)S(1)}, bf16[4,2,32,256]{3,2,1,0:T(8,128)(2,1)S(1)}, u32[]{:S(2)}, u32[]{:S(2)}) %collective-permute-start.24) | collective-permute-done | bytes 131104 | tf_op jit(solution)/shard_map/ppermute | solution.py:50
  124.8 0.8 copy.12.lengths
  125.6 0.7 collective-permute-done.27.refs_18_
  126.3 0.9 copy-done.8
  127.2 11.7 %squares.1 = f32[1024,256]{1,0:T(8,128)} custom-call(s32[4]{0:T(128)S(1)} %pad_add_fusion.order, s32[2]{0:T(128)S(1)} %pad_add_fusion.1.place, s32[8,4]{1,0:T(8,128)S(1)} %copy.12.lengths, bf16[8,32,1024]{2,1,0:T(8,128)(2,1)} %get-tuple-element.46.refs_0_, bf16[8,32,1024]{2,1,0:T(8,128)(2,1)} %collective-permute-done.7.refs_1_, ...), custom_call_target="tpu_custom_call" | custom-call | tf_op jit(solution)/shard_map/squares/pallas_call | solution.py:460
  (75 shorter events, 8.7 us)
Async XLA Ops:
  2.4 7.5 %copy-start.1 = (bf16[1,1024,256]{2,1,0:T(8,128)(2,1)S(1)}, bf16[1,1024,256]{2,1,0:T(8,128)(2,1)}, u32[]{:S(2)}) copy-start(bf16[1,1024,256]{2,1,0:T(8,128)(2,1)} %param.11) | copy-start | bytes 1572868
  2.4 9.1 %copy-start = (bf16[8,64,1024]{2,1,0:T(8,128)(2,1)S(1)}, bf16[8,64,1024]{2,1,0:T(8,128)(2,1)}, u32[]{:S(2)}) copy-start(bf16[8,64,1024]{2,1,0:T(8,128)(2,1)} %prepare.1.rows_ref) | copy-start | bytes 3145732
  2.4 9.1 %copy-start.9 = (f32[1,8192]{1,0:T(1,128)S(1)}, f32[1,8192]{1,0:T(1,128)}, u32[]{:S(2)}) copy-start(f32[1,8192]{1,0:T(1,128)} %gain_ref.1) | copy-start | bytes 98308
  2.4 20.9 %copy-start.14 = (s32[12]{0:T(128)S(1)}, s32[12]{0:T(128)}, u32[]{:S(2)}) copy-start(s32[12]{0:T(128)} %constant.52.clone) | copy-start | bytes 148
  2.4 21.0 %copy-start.13 = (s32[12]{0:T(128)S(1)}, s32[12]{0:T(128)}, u32[]{:S(2)}) copy-start(s32[12]{0:T(128)} %constant.53.clone) | copy-start | bytes 148
  2.4 22.8 %copy-start.11 = (s32[1,4]{1,0:T(1,128)S(1)}, s32[1,4]{1,0:T(1,128)}, u32[]{:S(2)}) copy-start(s32[1,4]{1,0:T(1,128)} %lengths.1) | copy-start | bytes 52
  2.4 33.2 %all-to-all-start.2 = ((bf16[8,64,1024]{2,1,0:T(8,128)(2,1)}), bf16[8,64,1024]{2,1,0:T(8,128)(2,1)S(1)}, u32[]{:S(2)}, u32[]{:S(2)}) async-start(bf16[8,64,1024]{2,1,0:T(8,128)(2,1)} %prepare.1.rows_ref), calls=%async_computation.2 | async-start | bytes 2097152 | tf_op jit(solution)/shard_map/all_to_all | solution.py:359
  9.8 13.4 %collective-permute-start = (bf16[1024,256]{1,0:T(8,128)(2,1)S(1)}, bf16[1024,256]{1,0:T(8,128)(2,1)S(1)}, u32[]{:S(2)}, u32[]{:S(2)}) collective-permute-start(bf16[1024,256]{1,0:T(8,128)(2,1)S(1)} %bitcast.10), channel_id=1, source_target_pairs={{0,16},{8,24},{16,0},{24,8},{1,17},{9,25},{17,1},{25,9},{2,18},{10... | collective-permute-start | bytes 1572872 | tf_op jit(solution)/shard_map/ppermute | solution.py:27
  11.4 12.1 %collective-permute-start.1 = (bf16[1024,256]{1,0:T(8,128)(2,1)S(1)}, bf16[1024,256]{1,0:T(8,128)(2,1)}, u32[]{:S(2)}, u32[]{:S(2)}) collective-permute-start(bf16[1024,256]{1,0:T(8,128)(2,1)S(1)} %bitcast.11), channel_id=1, source_target_pairs={{0,8},{8,0},{16,24},{24,16},{1,9},{9,1},{17,25},{25,17},{2,10},{10... | collective-permute-start | bytes 1572872 | tf_op jit(solution)/shard_map/ppermute | solution.py:22
  11.5 1.0 copy-start.5
  14.8 8.7 %collective-permute-start.3 = (bf16[1024,256]{1,0:T(8,128)(2,1)}, bf16[1024,256]{1,0:T(8,128)(2,1)S(1)}, u32[]{:S(2)}, u32[]{:S(2)}) collective-permute-start(bf16[1024,256]{1,0:T(8,128)(2,1)} %get-tuple-element.32.refs_4_.refs_0_), channel_id=1, source_target_pairs={{0,8},{8,0},{16,24},{24,16},{1,9},{9,1},{17,25},{25,17},{2,10},{10... | collective-permute-start | bytes 1572872 | tf_op jit(solution)/shard_map/ppermute | solution.py:22
  23.3 1.9 %collective-permute-start.2 = (bf16[1024,256]{1,0:T(8,128)(2,1)S(1)}, bf16[1024,256]{1,0:T(8,128)(2,1)S(1)}, u32[]{:S(2)}, u32[]{:S(2)}) collective-permute-start(bf16[1024,256]{1,0:T(8,128)(2,1)S(1)} %collective-permute-done.refs_1_.refs_5_), channel_id=1, source_target_pairs={{0,8},{8,0},{16,24},{24,16},{1,9},{9,1},{17,25},{25,17},{2,10},{10... | collective-permute-start | bytes 1572872 | tf_op jit(solution)/shard_map/ppermute | solution.py:22
  27.2 0.8 copy-start.2
  28.0 14.3 %collective-permute-start.4 = (bf16[1024,256]{1,0:T(8,128)(2,1)}, bf16[1024,256]{1,0:T(8,128)(2,1)}, u32[]{:S(2)}, u32[]{:S(2)}) collective-permute-start(bf16[1024,256]{1,0:T(8,128)(2,1)} %get-tuple-element.32.refs_4_.refs_0_), channel_id=1, source_target_pairs={{0,16},{8,24},{16,0},{24,8},{1,17},{9,25},{17,1},{25,9},{2,18},{10... | collective-permute-start | bytes 1572872 | tf_op jit(solution)/shard_map/ppermute | solution.py:27
  35.6 18.0 %all-to-all-start = ((bf16[8,112,256]{2,1,0:T(8,128)(2,1)}), bf16[8,112,256]{2,1,0:T(8,128)(2,1)}, u32[]{:S(2)}, u32[]{:S(2)}) async-start(bf16[8,112,256]{2,1,0:T(8,128)(2,1)} %copy-done.2), calls=%async_computation | async-start | bytes 917504 | tf_op jit(solution)/shard_map/all_to_all | solution.py:380
  42.3 5.7 %collective-permute-start.5 = (bf16[1024,256]{1,0:T(8,128)(2,1)}, bf16[1024,256]{1,0:T(8,128)(2,1)S(1)}, u32[]{:S(2)}, u32[]{:S(2)}) collective-permute-start(bf16[1024,256]{1,0:T(8,128)(2,1)} %collective-permute-done.4.refs_1_), channel_id=1, source_target_pairs={{0,8},{8,0},{16,24},{24,16},{1,9},{9,1},{17,25},{25,17},{2,10},{10... | collective-permute-start | bytes 1572872 | tf_op jit(solution)/shard_map/ppermute | solution.py:22
  44.8 3.2 %copy-start.6 = (f32[4,128,256]{2,1,0:T(8,128)}, f32[4,128,256]{2,1,0:T(8,128)S(1)}, u32[]{:S(2)}) copy-start(f32[4,128,256]{2,1,0:T(8,128)S(1)} %get-tuple-element.37) | copy-start | bytes 1572868
  44.8 16.4 %collective-permute-start.7 = (bf16[8,32,1024]{2,1,0:T(8,128)(2,1)}, bf16[8,32,1024]{2,1,0:T(8,128)(2,1)}, u32[]{:S(2)}, u32[]{:S(2)}) collective-permute-start(bf16[8,32,1024]{2,1,0:T(8,128)(2,1)} %get-tuple-element.46.refs_0_), channel_id=1, source_target_pairs={{0,16},{8,24},{16,0},{24,8},{1,17},{9,25},{17,1},{25,9},{2,18},{10... | collective-permute-start | bytes 1572872 | tf_op jit(solution)/shard_map/ppermute | solution.py:27
  46.3 13.7 %collective-permute-start.8 = (bf16[4,128,256]{2,1,0:T(8,128)(2,1)S(1)}, bf16[4,128,256]{2,1,0:T(8,128)(2,1)}, u32[]{:S(2)}, u32[]{:S(2)}) collective-permute-start(bf16[4,128,256]{2,1,0:T(8,128)(2,1)S(1)} %get-tuple-element.38), channel_id=1, source_target_pairs={{0,1},{1,0},{2,3},{3,2},{4,5},{5,4},{6,7},{7,6},{8,9},{9,8},{10,11... | collective-permute-start | bytes 786440 | tf_op jit(solution)/shard_map/ppermute | solution.py:50
  52.3 0.9 copy-start.3
  53.2 13.4 %copy-start.4 = (f32[4,224,256]{2,1,0:T(8,128)S(1)}, f32[4,224,256]{2,1,0:T(8,128)}, u32[]{:S(2)}) copy-start(f32[4,224,256]{2,1,0:T(8,128)} %copy-done.3) | copy-start | bytes 2752516
  53.2 12.6 %collective-permute-start.6 = (bf16[4,224,256]{2,1,0:T(8,128)(2,1)}, bf16[4,224,256]{2,1,0:T(8,128)(2,1)S(1)}, u32[]{:S(2)}, u32[]{:S(2)}) collective-permute-start(bf16[4,224,256]{2,1,0:T(8,128)(2,1)} %get-tuple-element.34), channel_id=1, source_target_pairs={{0,1},{1,0},{2,3},{3,2},{4,5},{5,4},{6,7},{7,6},{8,9},{9,8},{10,11... | collective-permute-start | bytes 1376264 | tf_op jit(solution)/shard_map/ppermute | solution.py:50
  55.3 13.3 %all-to-all-start.1 = ((bf16[4,96,256]{2,1,0:T(8,128)(2,1)}), bf16[4,96,256]{2,1,0:T(8,128)(2,1)S(1)}, u32[]{:S(2)}, u32[]{:S(2)}) async-start(bf16[4,96,256]{2,1,0:T(8,128)(2,1)} %broadcast_in_dim.6), calls=%async_computation.1 | async-start | bytes 393216 | tf_op jit(solution)/shard_map/all_to_all | solution.py:56
  65.8 0.8 copy-start.12
  68.6 22.5 %all-to-all-start.3 = ((bf16[4,352,256]{2,1,0:T(8,128)(2,1)}), bf16[4,352,256]{2,1,0:T(8,128)(2,1)S(1)}, u32[]{:S(2)}, u32[]{:S(2)}) async-start(bf16[4,352,256]{2,1,0:T(8,128)(2,1)} %pad_maximum_fusion), calls=%async_computation.3 | async-start | bytes 1441792 | tf_op jit(solution)/shard_map/all_to_all | solution.py:56
  73.1 7.8 %collective-permute-start.9 = (bf16[8,32,1024]{2,1,0:T(8,128)(2,1)}, bf16[8,32,1024]{2,1,0:T(8,128)(2,1)}, u32[]{:S(2)}, u32[]{:S(2)}) collective-permute-start(bf16[8,32,1024]{2,1,0:T(8,128)(2,1)} %get-tuple-element.46.refs_0_), channel_id=1, source_target_pairs={{0,8},{8,0},{16,24},{24,16},{1,9},{9,1},{17,25},{25,17},{2,10},{10... | collective-permute-start | bytes 1572872 | tf_op jit(solution)/shard_map/ppermute | solution.py:22
  73.1 7.3 %collective-permute-start.14 = (bf16[4,96,256]{2,1,0:T(8,128)(2,1)S(1)}, bf16[4,96,256]{2,1,0:T(8,128)(2,1)S(1)}, u32[]{:S(2)}, u32[]{:S(2)}) collective-permute-start(bf16[4,96,256]{2,1,0:T(8,128)(2,1)S(1)} %all-to-all-done.1.refs_0_), channel_id=1, source_target_pairs={{0,1},{1,0},{2,3},{3,2},{4,5},{5,4},{6,7},{7,6},{8,9},{9,8},{10,11... | collective-permute-start | bytes 589832 | tf_op jit(solution)/shard_map/ppermute | solution.py:50
  73.9 14.5 %collective-permute-start.10 = (bf16[8,32,1024]{2,1,0:T(8,128)(2,1)}, bf16[8,32,1024]{2,1,0:T(8,128)(2,1)}, u32[]{:S(2)}, u32[]{:S(2)}) collective-permute-start(bf16[8,32,1024]{2,1,0:T(8,128)(2,1)} %collective-permute-done.7.refs_1_), channel_id=1, source_target_pairs={{0,8},{8,0},{16,24},{24,16},{1,9},{9,1},{17,25},{25,17},{2,10},{10... | collective-permute-start | bytes 1572872 | tf_op jit(solution)/shard_map/ppermute | solution.py:22
  74.1 7.3 %collective-permute-start.11 = (bf16[4,96,256]{2,1,0:T(8,128)(2,1)S(1)}, bf16[4,96,256]{2,1,0:T(8,128)(2,1)S(1)}, u32[]{:S(2)}, u32[]{:S(2)}) collective-permute-start(bf16[4,96,256]{2,1,0:T(8,128)(2,1)S(1)} %all-to-all-done.1.refs_0_), channel_id=1, source_target_pairs={{0,16},{8,24},{16,0},{24,8},{1,17},{9,25},{17,1},{25,9},{2,18},{10... | collective-permute-start | bytes 589832 | tf_op jit(solution)/shard_map/ppermute | solution.py:27
  80.4 6.5 %collective-permute-start.15 = (bf16[4,96,256]{2,1,0:T(8,128)(2,1)S(1)}, bf16[4,96,256]{2,1,0:T(8,128)(2,1)S(1)}, u32[]{:S(2)}, u32[]{:S(2)}) collective-permute-start(bf16[4,96,256]{2,1,0:T(8,128)(2,1)S(1)} %collective-permute-done.14.refs_4_), channel_id=1, source_target_pairs={{0,16},{8,24},{16,0},{24,8},{1,17},{9,25},{17,1},{25,9},{2,18},{10... | collective-permute-start | bytes 589832 | tf_op jit(solution)/shard_map/ppermute | solution.py:27
  81.0 10.1 %collective-permute-start.12 = (bf16[4,96,256]{2,1,0:T(8,128)(2,1)S(1)}, bf16[4,96,256]{2,1,0:T(8,128)(2,1)S(1)}, u32[]{:S(2)}, u32[]{:S(2)}) collective-permute-start(bf16[4,96,256]{2,1,0:T(8,128)(2,1)S(1)} %all-to-all-done.1.refs_0_), channel_id=1, source_target_pairs={{0,8},{8,0},{16,24},{24,16},{1,9},{9,1},{17,25},{25,17},{2,10},{10... | collective-permute-start | bytes 589832 | tf_op jit(solution)/shard_map/ppermute | solution.py:22
  81.0 10.1 %collective-permute-start.16 = (bf16[4,96,256]{2,1,0:T(8,128)(2,1)S(1)}, bf16[4,96,256]{2,1,0:T(8,128)(2,1)S(1)}, u32[]{:S(2)}, u32[]{:S(2)}) collective-permute-start(bf16[4,96,256]{2,1,0:T(8,128)(2,1)S(1)} %collective-permute-done.14.refs_4_), channel_id=1, source_target_pairs={{0,8},{8,0},{16,24},{24,16},{1,9},{9,1},{17,25},{25,17},{2,10},{10... | collective-permute-start | bytes 589832 | tf_op jit(solution)/shard_map/ppermute | solution.py:22
  81.5 9.6 %collective-permute-start.13 = (bf16[4,96,256]{2,1,0:T(8,128)(2,1)S(1)}, bf16[4,96,256]{2,1,0:T(8,128)(2,1)}, u32[]{:S(2)}, u32[]{:S(2)}) collective-permute-start(bf16[4,96,256]{2,1,0:T(8,128)(2,1)S(1)} %collective-permute-done.11.refs_1_), channel_id=1, source_target_pairs={{0,8},{8,0},{16,24},{24,16},{1,9},{9,1},{17,25},{25,17},{2,10},{10... | collective-permute-start | bytes 589832 | tf_op jit(solution)/shard_map/ppermute | solution.py:22
  87.0 4.1 %collective-permute-start.17 = (bf16[4,96,256]{2,1,0:T(8,128)(2,1)S(1)}, bf16[4,96,256]{2,1,0:T(8,128)(2,1)}, u32[]{:S(2)}, u32[]{:S(2)}) collective-permute-start(bf16[4,96,256]{2,1,0:T(8,128)(2,1)S(1)} %collective-permute-done.15.refs_5_), channel_id=1, source_target_pairs={{0,8},{8,0},{16,24},{24,16},{1,9},{9,1},{17,25},{25,17},{2,10},{10... | collective-permute-start | bytes 589832 | tf_op jit(solution)/shard_map/ppermute | solution.py:22
  94.6 13.4 %all-to-all-start.4 = ((bf16[4,5,32,256]{3,2,1,0:T(8,128)(2,1)}), bf16[4,5,32,256]{3,2,1,0:T(8,128)(2,1)S(1)}, u32[]{:S(2)}, u32[]{:S(2)}) async-start(bf16[4,5,32,256]{3,2,1,0:T(8,128)(2,1)} %get-tuple-element.50), calls=%async_computation.4 | async-start | bytes 655360 | tf_op jit(solution)/shard_map/all_to_all | solution.py:56
  98.1 4.2 %collective-permute-start.18 = (bf16[2,32,256]{2,1,0:T(8,128)(2,1)}, bf16[2,32,256]{2,1,0:T(8,128)(2,1)S(1)}, u32[]{:S(2)}, u32[]{:S(2)}) collective-permute-start(bf16[2,32,256]{2,1,0:T(8,128)(2,1)} %bitcast.17), channel_id=1, source_target_pairs={{0,16},{8,24},{16,0},{24,8},{1,17},{9,25},{17,1},{25,9},{2,18},{10... | collective-permute-start | bytes 98312 | tf_op jit(solution)/shard_map/ppermute | solution.py:27
  108.0 7.5 %collective-permute-start.23 = (bf16[4,5,32,256]{3,2,1,0:T(8,128)(2,1)S(1)}, bf16[4,5,32,256]{3,2,1,0:T(8,128)(2,1)S(1)}, u32[]{:S(2)}, u32[]{:S(2)}) collective-permute-start(bf16[4,5,32,256]{3,2,1,0:T(8,128)(2,1)S(1)} %all-to-all-done.4.refs_8_), channel_id=1, source_target_pairs={{0,1},{1,0},{2,3},{3,2},{4,5},{5,4},{6,7},{7,6},{8,9},{9,8},{10,11... | collective-permute-start | bytes 983048 | tf_op jit(solution)/shard_map/ppermute | solution.py:50
  109.4 9.2 %all-to-all-start.5 = ((bf16[4,2,32,256]{3,2,1,0:T(8,128)(2,1)}), bf16[4,2,32,256]{3,2,1,0:T(8,128)(2,1)S(1)}, u32[]{:S(2)}, u32[]{:S(2)}) async-start(bf16[4,2,32,256]{3,2,1,0:T(8,128)(2,1)} %broadcast_in_dim.7), calls=%async_computation.5 | async-start | bytes 262144 | tf_op jit(solution)/shard_map/all_to_all | solution.py:56
  113.6 6.7 %collective-permute-start.19 = (bf16[4,3,32,256]{3,2,1,0:T(8,128)(2,1)}, bf16[4,3,32,256]{3,2,1,0:T(8,128)(2,1)S(1)}, u32[]{:S(2)}, u32[]{:S(2)}) collective-permute-start(bf16[4,3,32,256]{3,2,1,0:T(8,128)(2,1)} %slice.14), channel_id=1, source_target_pairs={{0,16},{8,24},{16,0},{24,8},{1,17},{9,25},{17,1},{25,9},{2,18},{10... | collective-permute-start | bytes 589832 | tf_op jit(solution)/shard_map/ppermute | solution.py:27
  116.2 7.5 %collective-permute-start.25 = (bf16[4,3,32,256]{3,2,1,0:T(8,128)(2,1)}, bf16[4,3,32,256]{3,2,1,0:T(8,128)(2,1)S(1)}, u32[]{:S(2)}, u32[]{:S(2)}) collective-permute-start(bf16[4,3,32,256]{3,2,1,0:T(8,128)(2,1)} %slice.18), channel_id=1, source_target_pairs={{0,16},{8,24},{16,0},{24,8},{1,17},{9,25},{17,1},{25,9},{2,18},{10... | collective-permute-start | bytes 589832 | tf_op jit(solution)/shard_map/ppermute | solution.py:27
  116.6 8.9 %collective-permute-start.20 = (bf16[4,5,32,256]{3,2,1,0:T(8,128)(2,1)S(1)}, bf16[4,5,32,256]{3,2,1,0:T(8,128)(2,1)S(1)}, u32[]{:S(2)}, u32[]{:S(2)}) collective-permute-start(bf16[4,5,32,256]{3,2,1,0:T(8,128)(2,1)S(1)} %all-to-all-done.4.refs_8_), channel_id=1, source_target_pairs={{0,8},{8,0},{16,24},{24,16},{1,9},{9,1},{17,25},{25,17},{2,10},{10... | collective-permute-start | bytes 983048 | tf_op jit(solution)/shard_map/ppermute | solution.py:22
  118.6 5.0 %collective-permute-start.24 = (bf16[4,2,32,256]{3,2,1,0:T(8,128)(2,1)S(1)}, bf16[4,2,32,256]{3,2,1,0:T(8,128)(2,1)S(1)}, u32[]{:S(2)}, u32[]{:S(2)}) collective-permute-start(bf16[4,2,32,256]{3,2,1,0:T(8,128)(2,1)S(1)} %all-to-all-done.5.refs_9_), channel_id=1, source_target_pairs={{0,1},{1,0},{2,3},{3,2},{4,5},{5,4},{6,7},{7,6},{8,9},{9,8},{10,11... | collective-permute-start | bytes 393224 | tf_op jit(solution)/shard_map/ppermute | solution.py:50
  119.9 6.4 %collective-permute-start.26 = (bf16[4,5,32,256]{3,2,1,0:T(8,128)(2,1)S(1)}, bf16[4,5,32,256]{3,2,1,0:T(8,128)(2,1)S(1)}, u32[]{:S(2)}, u32[]{:S(2)}) collective-permute-start(bf16[4,5,32,256]{3,2,1,0:T(8,128)(2,1)S(1)} %collective-permute-done.23.refs_14_), channel_id=1, source_target_pairs={{0,8},{8,0},{16,24},{24,16},{1,9},{9,1},{17,25},{25,17},{2,10},{10... | collective-permute-start | bytes 983048 | tf_op jit(solution)/shard_map/ppermute | solution.py:22
  120.3 3.8 %collective-permute-start.21 = (bf16[4,2,32,256]{3,2,1,0:T(8,128)(2,1)S(1)}, bf16[4,2,32,256]{3,2,1,0:T(8,128)(2,1)S(1)}, u32[]{:S(2)}, u32[]{:S(2)}) collective-permute-start(bf16[4,2,32,256]{3,2,1,0:T(8,128)(2,1)S(1)} %all-to-all-done.5.refs_9_), channel_id=1, source_target_pairs={{0,8},{8,0},{16,24},{24,16},{1,9},{9,1},{17,25},{25,17},{2,10},{10... | collective-permute-start | bytes 393224 | tf_op jit(solution)/shard_map/ppermute | solution.py:22
  123.6 1.9 %collective-permute-start.22 = (bf16[4,3,32,256]{3,2,1,0:T(8,128)(2,1)S(1)}, bf16[4,3,32,256]{3,2,1,0:T(8,128)(2,1)}, u32[]{:S(2)}, u32[]{:S(2)}) collective-permute-start(bf16[4,3,32,256]{3,2,1,0:T(8,128)(2,1)S(1)} %collective-permute-done.19.refs_10_), channel_id=1, source_target_pairs={{0,8},{8,0},{16,24},{24,16},{1,9},{9,1},{17,25},{25,17},{2,10},{10... | collective-permute-start | bytes 589832 | tf_op jit(solution)/shard_map/ppermute | solution.py:22
  123.6 2.7 %collective-permute-start.28 = (bf16[4,3,32,256]{3,2,1,0:T(8,128)(2,1)S(1)}, bf16[4,3,32,256]{3,2,1,0:T(8,128)(2,1)}, u32[]{:S(2)}, u32[]{:S(2)}) collective-permute-start(bf16[4,3,32,256]{3,2,1,0:T(8,128)(2,1)S(1)} %collective-permute-done.25.refs_16_), channel_id=1, source_target_pairs={{0,8},{8,0},{16,24},{24,16},{1,9},{9,1},{17,25},{25,17},{2,10},{10... | collective-permute-start | bytes 589832 | tf_op jit(solution)/shard_map/ppermute | solution.py:22
  124.8 1.5 %collective-permute-start.27 = (bf16[4,2,32,256]{3,2,1,0:T(8,128)(2,1)S(1)}, bf16[4,2,32,256]{3,2,1,0:T(8,128)(2,1)}, u32[]{:S(2)}, u32[]{:S(2)}) collective-permute-start(bf16[4,2,32,256]{3,2,1,0:T(8,128)(2,1)S(1)} %collective-permute-done.24.refs_15_), channel_id=1, source_target_pairs={{0,8},{8,0},{16,24},{24,16},{1,9},{9,1},{17,25},{25,17},{2,10},{10... | collective-permute-start | bytes 393224 | tf_op jit(solution)/shard_map/ppermute | solution.py:22
  126.3 0.9 copy-start.8
  (2 other events, 1.3 us)

commit v6 on v5

--- a/solution.py
+++ b/solution.py
@@ -71,19 +71,28 @@
     return listed
 
 
-def prepare_kernel(tokens_ref, cot_ref, rows_ref, sems):
+def prepare_kernel(tokens_ref, cot_ref, rows_ref, held, sems, out_sems):
     peers, rows, block = rows_ref.shape
     t = rows // 2
     start = pl.multiple_of(lax.axis_index("section") * t, t)
-    copies = []
+    pairs = []
     for n in range(peers):
         for k, ref in enumerate((tokens_ref, cot_ref)):
             source = ref.at[pl.ds(start, t), pl.ds(n * block, block)]
-            copies.append(pltpu.make_async_copy(source, rows_ref.at[n, pl.ds(k * t, t)], sems.at[k, n]))
-    for copy in copies:
-        copy.start()
-    for copy in copies:
-        copy.wait()
+            place = (n, pl.ds(k * t, t))
+            pairs.append(
+                (
+                    pltpu.make_async_copy(source, held.at[place], sems.at[k, n]),
+                    pltpu.make_async_copy(held.at[place], rows_ref.at[place], out_sems.at[k, n]),
+                )
+            )
+    for come, _ in pairs:
+        come.start()
+    for come, leave in pairs:
+        come.wait()
+        leave.start()
+    for _, leave in pairs:
+        leave.wait()
 
 
 def weight_kernel(place, rows_ref, down_ref, gain_ref, square_ref, weight_ref):
@@ -155,6 +164,21 @@
     c = paired(lambda p: [rows_ref[2 * z + p, t:] for z in range(peers // 2)], lax.rem(spot[0], 2))
     for i in range(count):
         store_pair(keep_ref, send_ref, order[i], t, dot(c, ups[i][...], 1, 0))
+
+
+def combine_kernel(keep_ref, got_ref, back_keep_ref, back_got_ref, out_ref):
+    cut = keep_ref.shape[1]
+    out_ref[:, :cut] = (keep_ref[...] + got_ref[...].astype(f32)).astype(bf16)
+    out_ref[:, cut:] = (back_keep_ref[...] + back_got_ref[...].astype(f32)).astype(bf16)
+
+
+def collect_kernel(packed_ref, gram_ref, lengths_ref):
+    copies, rows, _ = gram_ref.shape
+    total = jnp.sum(packed_ref[:, :rows].astype(f32), axis=0).astype(bf16)
+    for z in range(copies):
+        gram_ref[z] = total
+    for n in range(packed_ref.shape[0]):
+        lengths_ref[n : n + 1] = packed_ref[n, rows : rows + 16].astype(f32)[:1]
 
 
 def recur_kernel(count, width, order, spot, sums_ref, sq_ref, *refs):
@@ -231,23 +255,16 @@
             out_ref[j - 1, m] = grads[2 * lax.rem(chip + half - j, half) + m]
 
 
-def fisher_kernel(count, seqs, scale, order, place, lengths, *refs):
+def fisher_kernel(count, seqs, scale, order, place, *refs):
     half = count // 2
-    sources = refs[:count]
+    rows = refs[:count]
     ups = refs[count : 2 * count]
-    rest = list(refs[2 * count :])
-    states = []
-    for i in range(2 * count):
-        if i % half:
-            states.append((rest.pop(0), rest.pop(0), 0))
-        else:
-            both = rest.pop(0)
-            states.append((both, both, 2))
-    gain_ref, out_ref, rows, acc, hidden, masks, sems = rest
-    copies = [pltpu.make_async_copy(sources[i], rows.at[i], sems.at[i]) for i in range(count)]
-    for copy in copies:
-        copy.start()
-    _, peers, t, width = rows.shape
+    states = refs[2 * count : 4 * count]
+    far_count = 2 * (half - 1)
+    apart = refs[4 * count : 4 * count + far_count]
+    rest = refs[4 * count + far_count :]
+    lengths_ref, gain_ref, out_ref, acc, hidden, masks = rest
+    peers, t, width = rows[0].shape
     r = out_ref.shape[1]
     chunk = min(r, width)
     span = count * t
@@ -260,14 +277,20 @@
     for i in range(count):
         inside = (spot >= i * t) & (spot < (i + 1) * t)
         position = jnp.where(inside, spot + (order[i] - i) * t, position)
+    position = position.astype(f32)
 
     def grad_rows(n, m):
         found = states[n // line * count :][:count]
-        return jnp.concatenate([grads[n % line, m] for grads, _, _ in found], axis=0)
+        parts = []
+        for i in range(count):
+            core, j = divmod(i, half)
+            parts.append(apart[core * (half - 1) + j - 1][names[n], m] if j else found[i][n % line, m])
+        return jnp.concatenate(parts, axis=0)
 
     def act_rows(n, k):
         found = states[n // line * count :][:count]
-        return jnp.concatenate([acts[n % line, shift + k] for _, acts, shift in found], axis=0)
+        shifts = [0 if i % half else 2 for i in range(count)]
+        return jnp.concatenate([found[i][n % line, shifts[i] + k] for i in range(count)], axis=0)
 
     acts = []
     for i in range(1, count):
@@ -275,9 +298,10 @@
         acts.append(jnp.where(order[i] < me, act, jnp.zeros_like(act)))
     for n in range(peers):
         grad = grad_rows(n, lax.rem(me, 2)).astype(f32).T
-        start = 0
+        lengths = lengths_ref[pl.ds(names[n], 1)]
+        start = jnp.zeros((1, 1), f32)
         for q in range(seqs):
-            stop = start + lengths[names[n], q]
+            stop = start + lengths[:, q : q + 1]
             inside = (position >= start) & (position < stop)
             masks[n, q * r : (q + 1) * r] = jnp.where(inside, grad, 0.0).astype(bf16)
             start = stop
@@ -286,11 +310,8 @@
         update = dot(acts[0], ups[1][cols], 1, 1)
         for i in range(2, count):
             update = update + dot(acts[i - 1], ups[i][cols], 1, 1)
-        if f == 0:
-            for copy in copies:
-                copy.wait()
         for n in range(peers):
-            h = jnp.concatenate([rows[i, names[n], :, cols] for i in range(count)], axis=0).astype(f32)
+            h = jnp.concatenate([rows[i][names[n], :, cols] for i in range(count)], axis=0).astype(f32)
             hidden[n] = (h + update[n * span : (n + 1) * span]).astype(bf16)
         for n in range(peers):
             total = None
@@ -327,10 +348,14 @@
     ups = gather_section(up_weight[0])
     send = pl.pallas_call(
         prepare_kernel,
-        out_shape=jax.ShapeDtypeStruct((peers, 2 * t, block), bf16),
+        out_shape=pltpu.HBM((peers, 2 * t, block), bf16),
         in_specs=[anywhere, anywhere],
-        out_specs=vmem,
-        scratch_shapes=[pltpu.SemaphoreType.DMA((2, peers))],
+        out_specs=anywhere,
+        scratch_shapes=[
+            pltpu.VMEM((peers, 2 * t, block), bf16),
+            pltpu.SemaphoreType.DMA((2, peers)),
+            pltpu.SemaphoreType.DMA((2, peers)),
+        ],
         name="prepare",
     )(tokens, cotangent)
     square, weight = pl.pallas_call(
@@ -375,7 +400,6 @@
     )(order, left, right, lengths, *ups, weight, partner)
     packed, weight = lax.optimization_barrier((packed, weight))
     far = [chip_shift(weight, j) for j in range(1, count // 2)]
-    downs = [weight, *far, partner, *[core_swap(b) for b in far]]
 
     packed = lax.all_to_all(packed, "dp", 0, 0, tiled=True)
 
@@ -383,12 +407,9 @@
 
     def pair_shapes(blocks):
         return (
-            jax.ShapeDtypeStruct((line, blocks * t, r), f32),
-            jax.ShapeDtypeStruct((line, blocks * t, r), bf16),
+            pltpu.HBM((line, blocks * t, r), f32),
+            pltpu.HBM((line, blocks * t, r), bf16),
         )
-
-    def pair_sum(keep, give):
-        return (keep + give.astype(f32)).astype(bf16)
 
     back_keep, back_give, token_rows = pl.pallas_call(
         functools.partial(project_cot_kernel, count),
@@ -398,7 +419,9 @@
         compiler_params=limit(16),
         name="project_cot",
     )(order, spot_ref, rows, *ups)
-    back_part = pair_sum(back_keep, pair_swap(back_give))
+    back_got = pair_swap(back_give)
+    back_keep, *far = lax.optimization_barrier((back_keep, *far))
+    downs = [weight, *far, partner, *[core_swap(b) for b in far]]
     far_rows = [chip_shift(token_rows, j) for j in range(1, count // 2)]
     keep, give = pl.pallas_call(
         functools.partial(project_kernel, count),
@@ -409,10 +432,24 @@
         name="project",
     )(order, spot_ref, rows, *downs, *ups)
     got, *far_rows = lax.optimization_barrier((pair_swap(give), *far_rows))
-    gram_sum = jnp.sum(packed[:, :gram_rows].astype(f32), axis=0).astype(bf16)
-    all_lengths = packed[:, gram_rows, :seqs].astype(jnp.int32)
-    own_grams = line_exchange(repeated(gram_sum, line))
-    part = jnp.concatenate([pair_sum(keep, got), back_part], axis=1)
+    gram_sums, all_lengths = pl.pallas_call(
+        collect_kernel,
+        out_shape=(pltpu.HBM((line, gram_rows, r), bf16), jax.ShapeDtypeStruct((peers, r), f32)),
+        in_specs=[vmem],
+        out_specs=(vmem, vmem),
+        compiler_params=limit(8),
+        name="collect",
+    )(packed)
+    gram_sums, back_got = lax.optimization_barrier((gram_sums, back_got))
+    own_grams = line_exchange(gram_sums)
+    part = pl.pallas_call(
+        combine_kernel,
+        out_shape=pltpu.HBM((line, (3 * count - 1) * t, r), bf16),
+        in_specs=[vmem] * 4,
+        out_specs=vmem,
+        compiler_params=limit(12),
+        name="combine",
+    )(kept(keep, pltpu.HBM), got, kept(back_keep, pltpu.HBM), back_got)
     own_grams, part = lax.optimization_barrier((own_grams, part))
     sums = line_exchange(part)
     all_rows = [token_rows, *far_rows]
@@ -440,38 +477,33 @@
 
     half = count // 2
     own = line_exchange(own_held)
-    held = [chip_shift(held[j - 1], j) for j in range(1, half)]
-    own, *held = lax.optimization_barrier((own, *held))
+    far = [repeated(chip_shift(held[j - 1], j), peers) for j in range(1, half)]
+    acts = own[:, 2:]
+    own, acts, *far = lax.optimization_barrier((own, acts, *far))
     own = [own, pair_swap(own)]
-    acts = [x[:, 2:] for x in own]
-    states = [[None] * count, [None] * count]
-    for j in range(half):
-        if j:
-            grads = line_exchange(repeated(held[j - 1], line))
-            blocks = [[g, chip_shift(a, j)] for g, a in zip([grads, pair_swap(grads)], acts)]
-        else:
-            blocks = [[x] for x in own]
-        for p in range(2):
-            states[p][j] = blocks[p]
-            states[p][half + j] = [core_swap(x) for x in blocks[p]]
-    flat = [x for row in states for parts in row for x in parts]
+    acts = [acts, own[1][:, 2:]]
+    mine = [lax.all_to_all(x, "dp", 0, 0, tiled=True) for x in far]
+    grads = [*mine, *[core_swap(x) for x in mine]]
+    states = []
+    for p in range(2):
+        blocks = [own[p], *[chip_shift(acts[p], j) for j in range(1, half)]]
+        states += [*blocks, *[core_swap(x) for x in blocks]]
+    flat = [*states, *grads]
 
     chunk = min(r, block)
     fisher = pl.pallas_call(
         functools.partial(fisher_kernel, count, seqs, 1.0 / (row_count * peers)),
         out_shape=jax.ShapeDtypeStruct((block, r), f32),
-        in_specs=[smem, smem, smem] + [anywhere] * count + [vmem] * (count + len(flat) + 1),
+        in_specs=[smem, smem] + [vmem] * (2 * count + len(flat) + 2),
         out_specs=vmem,
         scratch_shapes=[
-            pltpu.VMEM((count, peers, t, block), bf16),
             pltpu.VMEM((r, chunk), f32),
             pltpu.VMEM((peers, row_count, chunk), bf16),
             pltpu.VMEM((peers, seqs * r, row_count), bf16),
-            pltpu.SemaphoreType.DMA((count,)),
         ],
         compiler_params=limit(24),
         name="squares",
-    )(order, place, all_lengths, *[kept(x, pltpu.HBM) for x in all_rows], *ups, *flat, gain)
+    )(order, place, *all_rows, *ups, *flat, all_lengths, gain)
     return fisher[None]
 
 

time: 140 us -> 135 us (0.964)
  other arithmetic: 5.12 us -> 0.15 us
  local copies, waits for them, and re-layouts: 9.99 us -> 5.4 us
  starting transfers between devices: 42.9 us -> 47.2 us
  Pallas kernels: 28 us -> 31.5 us
  waiting for transfers between devices: 52.7 us -> 49.4 us
    ppermute x8, starting transfers between devices: 8.4 us -> 13.7 us  [chip_shift(): lax.ppermute(x, 'section', [(i, (i - 2 * by) % count) for i in range(coun...]
    all_to_all x4 -> x3, starting transfers between devices: 16.2 us -> 11.4 us  [line_exchange(): return lax.all_to_all(x, 'dp', 0, 0, axis_index_groups=groups, tiled=True)]
    ppermute x8, waiting for transfers between devices: 19.9 us -> 15.5 us  [chip_shift(): lax.ppermute(x, 'section', [(i, (i - 2 * by) % count) for i in range(coun...]
    pallas_call x1 -> x3, Pallas kernels: 2.35 us -> 6.19 us  [the longest x1 2.3 us: per_device(): pl.pallas_call(combine_kernel, out_shape=pltpu.HBM((line, (3 * count - 1)...]
    all_to_all x0 -> x1, starting transfers between devices: none -> 3.59 us  [per_device(): mine = [lax.all_to_all(x, 'dp', 0, 0, tiled=True) for x in far]]
    unnamed x30 -> x18, local copies, waits for them, and re-layouts: 5.71 us -> 2.43 us
    convert_element_type x3 -> x0, other arithmetic: 3.01 us -> none  [the longest x2 2.29 us: pair_sum(): return (keep + give.astype(f32)).astype(bf16)]
    ppermute x5 -> x4, waiting for transfers between devices: 13.9 us -> 11.1 us  [pair_swap(): return lax.ppermute(x, 'dp', [(i, i ^ 1) for i in range(peers)])]
  transfers between devices with their start and end apart: 35 -> 33, of which waited for: 15 -> 15; matrix products, arithmetic and copies ran while one was open for 7% -> 2% of each run, Pallas kernels for 8% -> 11%
where the time goes in v6:
time: 135 us; the launch traced here: 134 us
  waiting for transfers between devices  49.4 us (37%)
  starting transfers between devices  47.2 us (35%)
  Pallas kernels  31.5 us (23%)
  local copies, waits for them, and re-layouts  5.4 us (4%)
    ppermute x8, waiting for transfers between devices, chip_shift(): lax.ppermute(x, 'section', [(i, (i - 2 * by) % count) for i in range(coun...  15.5 us
    ppermute x8, starting transfers between devices, chip_shift(): lax.ppermute(x, 'section', [(i, (i - 2 * by) % count) for i in range(coun...  13.7 us
    all_to_all x3, starting transfers between devices, line_exchange(): return lax.all_to_all(x, 'dp', 0, 0, axis_index_groups=groups, tiled=True)  11.4 us
    ppermute x4, waiting for transfers between devices, pair_swap(): return lax.ppermute(x, 'dp', [(i, i ^ 1) for i in range(peers)])  11.1 us
    all_to_all x3, waiting for transfers between devices, line_exchange(): return lax.all_to_all(x, 'dp', 0, 0, axis_index_groups=groups, tiled=True)  11 us
    pallas_call x1, Pallas kernels, per_device(): pl.pallas_call(functools.partial(fisher_kernel, count, seqs, 1.0 / (row_c...  10.4 us
    all_to_all x1, starting transfers between devices, per_device(): rows = lax.all_to_all(send, 'dp', 0, 0, tiled=True)  7.4 us
    all_to_all x1, waiting for transfers between devices, per_device(): rows = lax.all_to_all(send, 'dp', 0, 0, tiled=True)  6.07 us
  transfers between devices with their start and end apart: 33, of which 15 were waited for; matrix products, arithmetic and copies ran while one was open for 2% of the time, Pallas kernels for 11%

profile of v6, /device:TPU:0, one launch (start us, length us, event | category | flops | bytes accessed | tf_op | source)
XLA Modules:
  0.0 133.8 jit_solution(7403303061946623752)
XLA Ops:
  0.0 2.2 %prepare.1.rows_ref = bf16[8,64,1024]{2,1,0:T(8,128)(2,1)} custom-call(bf16[128,8192]{1,0:T(8,128)(2,1)} %tokens_ref.1, bf16[128,8192]{1,0:T(8,128)(2,1)} %cot_ref.1), custom_call_target="tpu_custom_call" | custom-call | tf_op jit(solution)/shard_map/prepare/pallas_call | solution.py:349
  2.2 7.4 %all-to-all-start.1 = ((bf16[8,64,1024]{2,1,0:T(8,128)(2,1)}), bf16[8,64,1024]{2,1,0:T(8,128)(2,1)S(1)}, u32[]{:S(2)}, u32[]{:S(2)}) async-start(bf16[8,64,1024]{2,1,0:T(8,128)(2,1)} %prepare.1.rows_ref), calls=%async_computation.1 | async-start | bytes 2097152 | tf_op jit(solution)/shard_map/all_to_all | solution.py:384
  9.6 1.6 %collective-permute-start = (bf16[1024,256]{1,0:T(8,128)(2,1)S(1)}, bf16[1024,256]{1,0:T(8,128)(2,1)S(1)}, u32[]{:S(2)}, u32[]{:S(2)}) collective-permute-start(bf16[1024,256]{1,0:T(8,128)(2,1)S(1)} %bitcast.9), channel_id=1, source_target_pairs={{0,16},{8,24},{16,0},{24,8},{1,17},{9,25},{17,1},{25,9},{2,18},{10... | collective-permute-start | bytes 1572872 | tf_op jit(solution)/shard_map/ppermute | solution.py:27
  11.3 1.0 copy-done.3
  12.4 1.6 %weight.1 = (f32[32,1]{1,0:T(8,128)S(1)}, bf16[1024,256]{1,0:T(8,128)(2,1)}) custom-call(s32[2]{0:T(128)S(1)} %pad_add_fusion.1.place, bf16[8,64,1024]{2,1,0:T(8,128)(2,1)S(1)} %copy-done, bf16[1,1024,256]{2,1,0:T(8,128)(2,1)S(1)} %copy-done.3, f32[1,8192]{1,0:T(1,128)S(1)} %copy-done.4), custom_call_target="tpu_custom_call" | custom-call | tf_op jit(solution)/shard_map/weight/pallas_call | solution.py:361
  14.0 0.6 copy-done.5
  15.1 8.0 %collective-permute-done.refs_1_.refs_5_ = bf16[1024,256]{1,0:T(8,128)(2,1)S(1)} collective-permute-done((bf16[1024,256]{1,0:T(8,128)(2,1)S(1)}, bf16[1024,256]{1,0:T(8,128)(2,1)S(1)}, u32[]{:S(2)}, u32[]{:S(2)}) %collective-permute-start) | collective-permute-done | bytes 524320 | tf_op jit(solution)/shard_map/ppermute | solution.py:27
  23.3 1.7 %collective-permute-done.2.refs_3_.refs_7_ = bf16[1024,256]{1,0:T(8,128)(2,1)S(1)} collective-permute-done((bf16[1024,256]{1,0:T(8,128)(2,1)S(1)}, bf16[1024,256]{1,0:T(8,128)(2,1)S(1)}, u32[]{:S(2)}, u32[]{:S(2)}) %collective-permute-start.2) | collective-permute-done | bytes 524320 | tf_op jit(solution)/shard_map/ppermute | solution.py:22
  25.0 2.0 %gram.1 = bf16[8,112,256]{2,1,0:T(8,128)(2,1)S(1)} custom-call(s32[4]{0:T(128)S(1)} %pad_add_fusion.order, s32[3]{0:T(128)S(1)} %dynamic_slice.9.left, s32[3]{0:T(128)S(1)} %dynamic_slice.10.right, s32[1,4]{1,0:T(1,128)S(1)} %copy-done.6, bf16[1024,256]{1,0:T(8,128)(2,1)S(1)} %bitcast.11, bf16[1024,256]{1,0:T(8,128)(2,1)S(1)} %collective-permute-done.refs_1_.refs_5_, ...), custom_call_target="tpu_custom_call" | custom-call | tf_op jit(solution)/shard_map/gram/pallas_call | solution.py:392
  27.1 0.8 copy-done.2
  27.8 1.5 %collective-permute-start.5 = (bf16[1024,256]{1,0:T(8,128)(2,1)}, bf16[1024,256]{1,0:T(8,128)(2,1)}, u32[]{:S(2)}, u32[]{:S(2)}) collective-permute-start(bf16[1024,256]{1,0:T(8,128)(2,1)} %get-tuple-element.42.refs_4_.refs_0_), channel_id=1, source_target_pairs={{0,16},{8,24},{16,0},{24,8},{1,17},{9,25},{17,1},{25,9},{2,18},{10... | collective-permute-start | bytes 1572872 | tf_op jit(solution)/shard_map/ppermute | solution.py:27
  29.3 6.1 %all-to-all-done.1.rows_ref = bf16[8,64,1024]{2,1,0:T(8,128)(2,1)S(1)} async-done(((bf16[8,64,1024]{2,1,0:T(8,128)(2,1)}), bf16[8,64,1024]{2,1,0:T(8,128)(2,1)S(1)}, u32[]{:S(2)}, u32[]{:S(2)}) %all-to-all-start.1) | async-done | bytes 1048608 | tf_op jit(solution)/shard_map/all_to_all | solution.py:384
  35.4 4.1 %all-to-all-start = ((bf16[8,112,256]{2,1,0:T(8,128)(2,1)}), bf16[8,112,256]{2,1,0:T(8,128)(2,1)}, u32[]{:S(2)}, u32[]{:S(2)}) async-start(bf16[8,112,256]{2,1,0:T(8,128)(2,1)} %copy-done.2), calls=%async_computation | async-start | bytes 917504 | tf_op jit(solution)/shard_map/all_to_all | solution.py:404
  39.5 2.9 %project_cot.1 = (f32[4,128,256]{2,1,0:T(8,128)}, bf16[4,128,256]{2,1,0:T(8,128)(2,1)}, bf16[8,32,1024]{2,1,0:T(8,128)(2,1)}) custom-call(s32[4]{0:T(128)S(1)} %pad_add_fusion.order, s32[1]{0:T(128)} %bitcast.5.spot, bf16[8,64,1024]{2,1,0:T(8,128)(2,1)S(1)} %all-to-all-done.1.rows_ref, bf16[1024,256]{1,0:T(8,128)(2,1)S(1)} %bitcast.12, ...), custom_call_target="tpu_custom_call" | custom-call | tf_op jit(solution)/shard_map/project_cot/pallas_call | solution.py:414
  42.4 2.0 %collective-permute-start.4 = (bf16[4,128,256]{2,1,0:T(8,128)(2,1)}, bf16[4,128,256]{2,1,0:T(8,128)(2,1)S(1)}, u32[]{:S(2)}, u32[]{:S(2)}) collective-permute-start(bf16[4,128,256]{2,1,0:T(8,128)(2,1)} %get-tuple-element.40), channel_id=1, source_target_pairs={{0,1},{1,0},{2,3},{3,2},{4,5},{5,4},{6,7},{7,6},{8,9},{9,8},{10,11... | collective-permute-start | bytes 786440 | tf_op jit(solution)/shard_map/ppermute | solution.py:50
  44.4 1.5 %collective-permute-start.8 = (bf16[8,32,1024]{2,1,0:T(8,128)(2,1)}, bf16[8,32,1024]{2,1,0:T(8,128)(2,1)}, u32[]{:S(2)}, u32[]{:S(2)}) collective-permute-start(bf16[8,32,1024]{2,1,0:T(8,128)(2,1)} %get-tuple-element.53.refs_0_), channel_id=1, source_target_pairs={{0,16},{8,24},{16,0},{24,8},{1,17},{9,25},{17,1},{25,9},{2,18},{10... | collective-permute-start | bytes 1572872 | tf_op jit(solution)/shard_map/ppermute | solution.py:27
  45.9 4.6 %project.1 = (f32[4,224,256]{2,1,0:T(8,128)}, bf16[4,224,256]{2,1,0:T(8,128)(2,1)}) custom-call(s32[4]{0:T(128)S(1)} %pad_add_fusion.order, s32[1]{0:T(128)} %bitcast.5.spot, bf16[8,64,1024]{2,1,0:T(8,128)(2,1)S(1)} %all-to-all-done.1.rows_ref, bf16[1024,256]{1,0:T(8,128)(2,1)} %get-tuple-element.42.refs_4_.refs_0_, ...), custom_call_target="tpu_custom_call" | custom-call | tf_op jit(solution)/shard_map/project/pallas_call | solution.py:426
  50.5 0.5 collective-permute-start.7
  51.0 1.4 %all-to-all-done.packed_ref = bf16[8,112,256]{2,1,0:T(8,128)(2,1)} async-done(((bf16[8,112,256]{2,1,0:T(8,128)(2,1)}), bf16[8,112,256]{2,1,0:T(8,128)(2,1)}, u32[]{:S(2)}, u32[]{:S(2)}) %all-to-all-start) | async-done | bytes 458784 | tf_op jit(solution)/shard_map/all_to_all | solution.py:404
  52.4 1.7 %collect.1 = (bf16[4,96,256]{2,1,0:T(8,128)(2,1)}, f32[8,256]{1,0:T(8,128)S(1)}) custom-call(bf16[8,112,256]{2,1,0:T(8,128)(2,1)} %all-to-all-done.packed_ref), custom_call_target="tpu_custom_call" | custom-call | tf_op jit(solution)/shard_map/collect/pallas_call | solution.py:435
  54.1 3.6 %all-to-all-start.2 = ((bf16[4,96,256]{2,1,0:T(8,128)(2,1)}), bf16[4,96,256]{2,1,0:T(8,128)(2,1)S(1)}, u32[]{:S(2)}, u32[]{:S(2)}) async-start(bf16[4,96,256]{2,1,0:T(8,128)(2,1)} %get-tuple-element.41), calls=%async_computation.2 | async-start | bytes 393216 | tf_op jit(solution)/shard_map/all_to_all | solution.py:56
  57.7 1.0 collective-permute-done.8.refs_1_
  58.7 4.4 %collective-permute-done.7.got_ref = bf16[4,224,256]{2,1,0:T(8,128)(2,1)S(1)} collective-permute-done((bf16[4,224,256]{2,1,0:T(8,128)(2,1)}, bf16[4,224,256]{2,1,0:T(8,128)(2,1)S(1)}, u32[]{:S(2)}, u32[]{:S(2)}) %collective-permute-start.7) | collective-permute-done | bytes 458784 | tf_op jit(solution)/shard_map/ppermute | solution.py:50
  63.1 2.3 %combine.1 = bf16[4,352,256]{2,1,0:T(8,128)(2,1)} custom-call(f32[4,224,256]{2,1,0:T(8,128)} %get-tuple-element.45.keep_ref, bf16[4,224,256]{2,1,0:T(8,128)(2,1)S(1)} %collective-permute-done.7.got_ref, f32[4,128,256]{2,1,0:T(8,128)} %get-tuple-element.49.back_keep_ref, bf16[4,128,256]{2,1,0:T(8,128)(2,1)S(1)} %collective-permute-done.4.back_got_ref), custom_call_target="tpu_custom_call" | custom-call | tf_op jit(solution)/shard_map/combine/pallas_call | solution.py:445
  65.5 4.4 %all-to-all-start.3 = ((bf16[4,352,256]{2,1,0:T(8,128)(2,1)}), bf16[4,352,256]{2,1,0:T(8,128)(2,1)S(1)}, u32[]{:S(2)}, u32[]{:S(2)}) async-start(bf16[4,352,256]{2,1,0:T(8,128)(2,1)} %combine.1), calls=%async_computation.3 | async-start | bytes 1441792 | tf_op jit(solution)/shard_map/all_to_all | solution.py:56
  69.9 1.0 collective-permute-start.14
  71.1 1.5 %collective-permute-start.11 = (bf16[4,96,256]{2,1,0:T(8,128)(2,1)S(1)}, bf16[4,96,256]{2,1,0:T(8,128)(2,1)S(1)}, u32[]{:S(2)}, u32[]{:S(2)}) collective-permute-start(bf16[4,96,256]{2,1,0:T(8,128)(2,1)S(1)} %all-to-all-done.2.refs_0_), channel_id=1, source_target_pairs={{0,16},{8,24},{16,0},{24,8},{1,17},{9,25},{17,1},{25,9},{2,18},{10... | collective-permute-start | bytes 589832 | tf_op jit(solution)/shard_map/ppermute | solution.py:27
  72.6 4.5 %collective-permute-done.14.refs_4_ = bf16[4,96,256]{2,1,0:T(8,128)(2,1)S(1)} collective-permute-done((bf16[4,96,256]{2,1,0:T(8,128)(2,1)S(1)}, bf16[4,96,256]{2,1,0:T(8,128)(2,1)S(1)}, u32[]{:S(2)}, u32[]{:S(2)}) %collective-permute-start.14) | collective-permute-done | bytes 196640 | tf_op jit(solution)/shard_map/ppermute | solution.py:50
  77.2 1.5 %collective-permute-start.15 = (bf16[4,96,256]{2,1,0:T(8,128)(2,1)S(1)}, bf16[4,96,256]{2,1,0:T(8,128)(2,1)}, u32[]{:S(2)}, u32[]{:S(2)}) collective-permute-start(bf16[4,96,256]{2,1,0:T(8,128)(2,1)S(1)} %collective-permute-done.14.refs_4_), channel_id=1, source_target_pairs={{0,16},{8,24},{16,0},{24,8},{1,17},{9,25},{17,1},{25,9},{2,18},{10... | collective-permute-start | bytes 589832 | tf_op jit(solution)/shard_map/ppermute | solution.py:27
  79.3 4.6 %collective-permute-done.15.refs_5_ = bf16[4,96,256]{2,1,0:T(8,128)(2,1)} collective-permute-done((bf16[4,96,256]{2,1,0:T(8,128)(2,1)S(1)}, bf16[4,96,256]{2,1,0:T(8,128)(2,1)}, u32[]{:S(2)}, u32[]{:S(2)}) %collective-permute-start.15) | collective-permute-done | bytes 196640 | tf_op jit(solution)/shard_map/ppermute | solution.py:27
  83.8 0.7 constant_dynamic-slice_fusion.refs_19_
  84.5 3.2 %all-to-all-done.3.sums_ref = bf16[4,352,256]{2,1,0:T(8,128)(2,1)S(1)} async-done(((bf16[4,352,256]{2,1,0:T(8,128)(2,1)}), bf16[4,352,256]{2,1,0:T(8,128)(2,1)S(1)}, u32[]{:S(2)}, u32[]{:S(2)}) %all-to-all-start.3) | async-done | bytes 720928 | tf_op jit(solution)/shard_map/all_to_all | solution.py:56
  87.8 3.7 %recur.1 = (bf16[4,5,32,256]{3,2,1,0:T(8,128)(2,1)}, bf16[1,2,32,256]{3,2,1,0:T(8,128)(2,1)}) custom-call(s32[4]{0:T(128)S(1)} %pad_add_fusion.order, s32[1]{0:T(128)} %bitcast.5.spot, bf16[4,352,256]{2,1,0:T(8,128)(2,1)S(1)} %all-to-all-done.3.sums_ref, f32[32,1]{1,0:T(8,128)} %copy-done.5, bf16[4,96,256]{2,1,0:T(8,128)(2,1)S(1)} %all-to-all-done.2.refs_0_, ...), custom_call_target="tpu_custom_call" | custom-call | tf_op jit(solution)/shard_map/recur/pallas_call | solution.py:460
  91.5 3.5 %all-to-all-start.4 = ((bf16[4,5,32,256]{3,2,1,0:T(8,128)(2,1)}), bf16[4,5,32,256]{3,2,1,0:T(8,128)(2,1)S(1)}, u32[]{:S(2)}, u32[]{:S(2)}) async-start(bf16[4,5,32,256]{3,2,1,0:T(8,128)(2,1)} %get-tuple-element.62), calls=%async_computation.4 | async-start | bytes 655360 | tf_op jit(solution)/shard_map/all_to_all | solution.py:56
  95.0 2.4 %collective-permute-start.18 = (bf16[2,32,256]{2,1,0:T(8,128)(2,1)}, bf16[2,32,256]{2,1,0:T(8,128)(2,1)S(1)}, u32[]{:S(2)}, u32[]{:S(2)}) collective-permute-start(bf16[2,32,256]{2,1,0:T(8,128)(2,1)} %bitcast.15), channel_id=1, source_target_pairs={{0,16},{8,24},{16,0},{24,8},{1,17},{9,25},{17,1},{25,9},{2,18},{10... | collective-permute-start | bytes 98312 | tf_op jit(solution)/shard_map/ppermute | solution.py:27
  97.4 7.7 %all-to-all-done.4.refs_8_ = bf16[4,5,32,256]{3,2,1,0:T(8,128)(2,1)S(1)} async-done(((bf16[4,5,32,256]{3,2,1,0:T(8,128)(2,1)}), bf16[4,5,32,256]{3,2,1,0:T(8,128)(2,1)S(1)}, u32[]{:S(2)}, u32[]{:S(2)}) %all-to-all-start.4) | async-done | bytes 327712 | tf_op jit(solution)/shard_map/all_to_all | solution.py:56
  105.1 0.7 slice.8
  105.8 0.7 broadcast_in_dim.4
  106.5 1.2 collective-permute-start.22
  107.7 3.6 %all-to-all-start.5 = ((bf16[8,2,32,256]{3,2,1,0:T(8,128)(2,1)}), bf16[8,2,32,256]{3,2,1,0:T(8,128)(2,1)S(1)}, u32[]{:S(2)}, u32[]{:S(2)}) async-start(bf16[8,2,32,256]{3,2,1,0:T(8,128)(2,1)} %broadcast_in_dim.4), calls=%async_computation.5 | async-start | bytes 524288 | tf_op jit(solution)/shard_map/all_to_all | solution.py:485
  111.3 1.6 %collective-permute-start.19 = (bf16[4,3,32,256]{3,2,1,0:T(8,128)(2,1)}, bf16[4,3,32,256]{3,2,1,0:T(8,128)(2,1)}, u32[]{:S(2)}, u32[]{:S(2)}) collective-permute-start(bf16[4,3,32,256]{3,2,1,0:T(8,128)(2,1)} %slice.8), channel_id=1, source_target_pairs={{0,16},{8,24},{16,0},{24,8},{1,17},{9,25},{17,1},{25,9},{2,18},{10... | collective-permute-start | bytes 589832 | tf_op jit(solution)/shard_map/ppermute | solution.py:27
  112.9 2.1 %collective-permute-done.22.refs_12_ = bf16[4,5,32,256]{3,2,1,0:T(8,128)(2,1)S(1)} collective-permute-done((bf16[4,5,32,256]{3,2,1,0:T(8,128)(2,1)S(1)}, bf16[4,5,32,256]{3,2,1,0:T(8,128)(2,1)S(1)}, u32[]{:S(2)}, u32[]{:S(2)}) %collective-permute-start.22) | collective-permute-done | bytes 327712 | tf_op jit(solution)/shard_map/ppermute | solution.py:50
  115.0 0.7 slice.9
  115.7 2.0 %collective-permute-start.23 = (bf16[4,3,32,256]{3,2,1,0:T(8,128)(2,1)}, bf16[4,3,32,256]{3,2,1,0:T(8,128)(2,1)}, u32[]{:S(2)}, u32[]{:S(2)}) collective-permute-start(bf16[4,3,32,256]{3,2,1,0:T(8,128)(2,1)} %slice.9), channel_id=1, source_target_pairs={{0,16},{8,24},{16,0},{24,8},{1,17},{9,25},{17,1},{25,9},{2,18},{10... | collective-permute-start | bytes 589832 | tf_op jit(solution)/shard_map/ppermute | solution.py:27
  118.3 1.0 all-to-all-done.5.refs_16_
  119.8 1.9 %collective-permute-done.23.refs_13_ = bf16[4,3,32,256]{3,2,1,0:T(8,128)(2,1)} collective-permute-done((bf16[4,3,32,256]{3,2,1,0:T(8,128)(2,1)}, bf16[4,3,32,256]{3,2,1,0:T(8,128)(2,1)}, u32[]{:S(2)}, u32[]{:S(2)}) %collective-permute-start.23) | collective-permute-done | bytes 196640 | tf_op jit(solution)/shard_map/ppermute | solution.py:27
  121.8 1.6 %collective-permute-done.25.refs_15_ = bf16[4,3,32,256]{3,2,1,0:T(8,128)(2,1)S(1)} collective-permute-done((bf16[4,3,32,256]{3,2,1,0:T(8,128)(2,1)}, bf16[4,3,32,256]{3,2,1,0:T(8,128)(2,1)S(1)}, u32[]{:S(2)}, u32[]{:S(2)}) %collective-permute-start.25) | collective-permute-done | bytes 196640 | tf_op jit(solution)/shard_map/ppermute | solution.py:22
  123.4 10.4 %squares.1 = f32[1024,256]{1,0:T(8,128)} custom-call(s32[4]{0:T(128)S(1)} %pad_add_fusion.order, s32[2]{0:T(128)S(1)} %pad_add_fusion.1.place, bf16[8,32,1024]{2,1,0:T(8,128)(2,1)} %get-tuple-element.53.refs_0_, bf16[8,32,1024]{2,1,0:T(8,128)(2,1)} %collective-permute-done.8.refs_1_, bf16[8,32,1024]{2,1,0:T(8,128)(2,1)S(1)} %collective-permute-done.9.refs_2_, ...), custom_call_target="tpu_custom_call" | custom-call | tf_op jit(solution)/shard_map/squares/pallas_call | solution.py:494
  (53 shorter events, 2.8 us)
Async XLA Ops:
  2.2 7.5 %copy-start.1 = (bf16[1,1024,256]{2,1,0:T(8,128)(2,1)S(1)}, bf16[1,1024,256]{2,1,0:T(8,128)(2,1)}, u32[]{:S(2)}) copy-start(bf16[1,1024,256]{2,1,0:T(8,128)(2,1)} %param.11) | copy-start | bytes 1572868
  2.2 9.1 %copy-start = (bf16[8,64,1024]{2,1,0:T(8,128)(2,1)S(1)}, bf16[8,64,1024]{2,1,0:T(8,128)(2,1)}, u32[]{:S(2)}) copy-start(bf16[8,64,1024]{2,1,0:T(8,128)(2,1)} %prepare.1.rows_ref) | copy-start | bytes 3145732
  2.2 9.1 %copy-start.4 = (f32[1,8192]{1,0:T(1,128)S(1)}, f32[1,8192]{1,0:T(1,128)}, u32[]{:S(2)}) copy-start(f32[1,8192]{1,0:T(1,128)} %gain_ref.1) | copy-start | bytes 98308
  2.2 20.9 %copy-start.8 = (s32[12]{0:T(128)S(1)}, s32[12]{0:T(128)}, u32[]{:S(2)}) copy-start(s32[12]{0:T(128)} %constant.49.clone) | copy-start | bytes 148
  2.2 21.0 %copy-start.7 = (s32[12]{0:T(128)S(1)}, s32[12]{0:T(128)}, u32[]{:S(2)}) copy-start(s32[12]{0:T(128)} %constant.50.clone) | copy-start | bytes 148
  2.2 22.8 %copy-start.6 = (s32[1,4]{1,0:T(1,128)S(1)}, s32[1,4]{1,0:T(1,128)}, u32[]{:S(2)}) copy-start(s32[1,4]{1,0:T(1,128)} %lengths.1) | copy-start | bytes 52
  2.2 33.2 %all-to-all-start.1 = ((bf16[8,64,1024]{2,1,0:T(8,128)(2,1)}), bf16[8,64,1024]{2,1,0:T(8,128)(2,1)S(1)}, u32[]{:S(2)}, u32[]{:S(2)}) async-start(bf16[8,64,1024]{2,1,0:T(8,128)(2,1)} %prepare.1.rows_ref), calls=%async_computation.1 | async-start | bytes 2097152 | tf_op jit(solution)/shard_map/all_to_all | solution.py:384
  9.6 13.4 %collective-permute-start = (bf16[1024,256]{1,0:T(8,128)(2,1)S(1)}, bf16[1024,256]{1,0:T(8,128)(2,1)S(1)}, u32[]{:S(2)}, u32[]{:S(2)}) collective-permute-start(bf16[1024,256]{1,0:T(8,128)(2,1)S(1)} %bitcast.9), channel_id=1, source_target_pairs={{0,16},{8,24},{16,0},{24,8},{1,17},{9,25},{17,1},{25,9},{2,18},{10... | collective-permute-start | bytes 1572872 | tf_op jit(solution)/shard_map/ppermute | solution.py:27
  11.2 12.1 %collective-permute-start.1 = (bf16[1024,256]{1,0:T(8,128)(2,1)S(1)}, bf16[1024,256]{1,0:T(8,128)(2,1)}, u32[]{:S(2)}, u32[]{:S(2)}) collective-permute-start(bf16[1024,256]{1,0:T(8,128)(2,1)S(1)} %bitcast.10), channel_id=1, source_target_pairs={{0,8},{8,0},{16,24},{24,16},{1,9},{9,1},{17,25},{25,17},{2,10},{10... | collective-permute-start | bytes 1572872 | tf_op jit(solution)/shard_map/ppermute | solution.py:22
  11.3 1.0 copy-start.3
  14.0 0.6 copy-start.5
  14.6 8.7 %collective-permute-start.3 = (bf16[1024,256]{1,0:T(8,128)(2,1)}, bf16[1024,256]{1,0:T(8,128)(2,1)S(1)}, u32[]{:S(2)}, u32[]{:S(2)}) collective-permute-start(bf16[1024,256]{1,0:T(8,128)(2,1)} %get-tuple-element.42.refs_4_.refs_0_), channel_id=1, source_target_pairs={{0,8},{8,0},{16,24},{24,16},{1,9},{9,1},{17,25},{25,17},{2,10},{10... | collective-permute-start | bytes 1572872 | tf_op jit(solution)/shard_map/ppermute | solution.py:22
  23.1 1.9 %collective-permute-start.2 = (bf16[1024,256]{1,0:T(8,128)(2,1)S(1)}, bf16[1024,256]{1,0:T(8,128)(2,1)S(1)}, u32[]{:S(2)}, u32[]{:S(2)}) collective-permute-start(bf16[1024,256]{1,0:T(8,128)(2,1)S(1)} %collective-permute-done.refs_1_.refs_5_), channel_id=1, source_target_pairs={{0,8},{8,0},{16,24},{24,16},{1,9},{9,1},{17,25},{25,17},{2,10},{10... | collective-permute-start | bytes 1572872 | tf_op jit(solution)/shard_map/ppermute | solution.py:22
  27.1 0.8 copy-start.2
  27.8 14.6 %collective-permute-start.5 = (bf16[1024,256]{1,0:T(8,128)(2,1)}, bf16[1024,256]{1,0:T(8,128)(2,1)}, u32[]{:S(2)}, u32[]{:S(2)}) collective-permute-start(bf16[1024,256]{1,0:T(8,128)(2,1)} %get-tuple-element.42.refs_4_.refs_0_), channel_id=1, source_target_pairs={{0,16},{8,24},{16,0},{24,8},{1,17},{9,25},{17,1},{25,9},{2,18},{10... | collective-permute-start | bytes 1572872 | tf_op jit(solution)/shard_map/ppermute | solution.py:27
  35.4 17.0 %all-to-all-start = ((bf16[8,112,256]{2,1,0:T(8,128)(2,1)}), bf16[8,112,256]{2,1,0:T(8,128)(2,1)}, u32[]{:S(2)}, u32[]{:S(2)}) async-start(bf16[8,112,256]{2,1,0:T(8,128)(2,1)} %copy-done.2), calls=%async_computation | async-start | bytes 917504 | tf_op jit(solution)/shard_map/all_to_all | solution.py:404
  42.4 3.5 %collective-permute-start.6 = (bf16[1024,256]{1,0:T(8,128)(2,1)}, bf16[1024,256]{1,0:T(8,128)(2,1)S(1)}, u32[]{:S(2)}, u32[]{:S(2)}) collective-permute-start(bf16[1024,256]{1,0:T(8,128)(2,1)} %collective-permute-done.5.refs_1_), channel_id=1, source_target_pairs={{0,8},{8,0},{16,24},{24,16},{1,9},{9,1},{17,25},{25,17},{2,10},{10... | collective-permute-start | bytes 1572872 | tf_op jit(solution)/shard_map/ppermute | solution.py:22
  42.4 11.7 %collective-permute-start.4 = (bf16[4,128,256]{2,1,0:T(8,128)(2,1)}, bf16[4,128,256]{2,1,0:T(8,128)(2,1)S(1)}, u32[]{:S(2)}, u32[]{:S(2)}) collective-permute-start(bf16[4,128,256]{2,1,0:T(8,128)(2,1)} %get-tuple-element.40), channel_id=1, source_target_pairs={{0,1},{1,0},{2,3},{3,2},{4,5},{5,4},{6,7},{7,6},{8,9},{9,8},{10,11... | collective-permute-start | bytes 786440 | tf_op jit(solution)/shard_map/ppermute | solution.py:50
  44.4 14.3 %collective-permute-start.8 = (bf16[8,32,1024]{2,1,0:T(8,128)(2,1)}, bf16[8,32,1024]{2,1,0:T(8,128)(2,1)}, u32[]{:S(2)}, u32[]{:S(2)}) collective-permute-start(bf16[8,32,1024]{2,1,0:T(8,128)(2,1)} %get-tuple-element.53.refs_0_), channel_id=1, source_target_pairs={{0,16},{8,24},{16,0},{24,8},{1,17},{9,25},{17,1},{25,9},{2,18},{10... | collective-permute-start | bytes 1572872 | tf_op jit(solution)/shard_map/ppermute | solution.py:27
  50.5 12.6 %collective-permute-start.7 = (bf16[4,224,256]{2,1,0:T(8,128)(2,1)}, bf16[4,224,256]{2,1,0:T(8,128)(2,1)S(1)}, u32[]{:S(2)}, u32[]{:S(2)}) collective-permute-start(bf16[4,224,256]{2,1,0:T(8,128)(2,1)} %get-tuple-element.46), channel_id=1, source_target_pairs={{0,1},{1,0},{2,3},{3,2},{4,5},{5,4},{6,7},{7,6},{8,9},{9,8},{10,11... | collective-permute-start | bytes 1376264 | tf_op jit(solution)/shard_map/ppermute | solution.py:50
  54.1 11.3 %all-to-all-start.2 = ((bf16[4,96,256]{2,1,0:T(8,128)(2,1)}), bf16[4,96,256]{2,1,0:T(8,128)(2,1)S(1)}, u32[]{:S(2)}, u32[]{:S(2)}) async-start(bf16[4,96,256]{2,1,0:T(8,128)(2,1)} %get-tuple-element.41), calls=%async_computation.2 | async-start | bytes 393216 | tf_op jit(solution)/shard_map/all_to_all | solution.py:56
  65.5 22.3 %all-to-all-start.3 = ((bf16[4,352,256]{2,1,0:T(8,128)(2,1)}), bf16[4,352,256]{2,1,0:T(8,128)(2,1)S(1)}, u32[]{:S(2)}, u32[]{:S(2)}) async-start(bf16[4,352,256]{2,1,0:T(8,128)(2,1)} %combine.1), calls=%async_computation.3 | async-start | bytes 1441792 | tf_op jit(solution)/shard_map/all_to_all | solution.py:56
  69.9 8.8 %collective-permute-start.9 = (bf16[8,32,1024]{2,1,0:T(8,128)(2,1)}, bf16[8,32,1024]{2,1,0:T(8,128)(2,1)S(1)}, u32[]{:S(2)}, u32[]{:S(2)}) collective-permute-start(bf16[8,32,1024]{2,1,0:T(8,128)(2,1)} %get-tuple-element.53.refs_0_), channel_id=1, source_target_pairs={{0,8},{8,0},{16,24},{24,16},{1,9},{9,1},{17,25},{25,17},{2,10},{10... | collective-permute-start | bytes 1572872 | tf_op jit(solution)/shard_map/ppermute | solution.py:22
  69.9 7.3 %collective-permute-start.14 = (bf16[4,96,256]{2,1,0:T(8,128)(2,1)S(1)}, bf16[4,96,256]{2,1,0:T(8,128)(2,1)S(1)}, u32[]{:S(2)}, u32[]{:S(2)}) collective-permute-start(bf16[4,96,256]{2,1,0:T(8,128)(2,1)S(1)} %all-to-all-done.2.refs_0_), channel_id=1, source_target_pairs={{0,1},{1,0},{2,3},{3,2},{4,5},{5,4},{6,7},{7,6},{8,9},{9,8},{10,11... | collective-permute-start | bytes 589832 | tf_op jit(solution)/shard_map/ppermute | solution.py:50
  70.9 13.6 %collective-permute-start.10 = (bf16[8,32,1024]{2,1,0:T(8,128)(2,1)}, bf16[8,32,1024]{2,1,0:T(8,128)(2,1)}, u32[]{:S(2)}, u32[]{:S(2)}) collective-permute-start(bf16[8,32,1024]{2,1,0:T(8,128)(2,1)} %collective-permute-done.8.refs_1_), channel_id=1, source_target_pairs={{0,8},{8,0},{16,24},{24,16},{1,9},{9,1},{17,25},{25,17},{2,10},{10... | collective-permute-start | bytes 1572872 | tf_op jit(solution)/shard_map/ppermute | solution.py:22
  71.1 8.1 %collective-permute-start.11 = (bf16[4,96,256]{2,1,0:T(8,128)(2,1)S(1)}, bf16[4,96,256]{2,1,0:T(8,128)(2,1)S(1)}, u32[]{:S(2)}, u32[]{:S(2)}) collective-permute-start(bf16[4,96,256]{2,1,0:T(8,128)(2,1)S(1)} %all-to-all-done.2.refs_0_), channel_id=1, source_target_pairs={{0,16},{8,24},{16,0},{24,8},{1,17},{9,25},{17,1},{25,9},{2,18},{10... | collective-permute-start | bytes 589832 | tf_op jit(solution)/shard_map/ppermute | solution.py:27
  77.2 6.6 %collective-permute-start.15 = (bf16[4,96,256]{2,1,0:T(8,128)(2,1)S(1)}, bf16[4,96,256]{2,1,0:T(8,128)(2,1)}, u32[]{:S(2)}, u32[]{:S(2)}) collective-permute-start(bf16[4,96,256]{2,1,0:T(8,128)(2,1)S(1)} %collective-permute-done.14.refs_4_), channel_id=1, source_target_pairs={{0,16},{8,24},{16,0},{24,8},{1,17},{9,25},{17,1},{25,9},{2,18},{10... | collective-permute-start | bytes 589832 | tf_op jit(solution)/shard_map/ppermute | solution.py:27
  78.7 9.1 %collective-permute-start.12 = (bf16[4,96,256]{2,1,0:T(8,128)(2,1)S(1)}, bf16[4,96,256]{2,1,0:T(8,128)(2,1)}, u32[]{:S(2)}, u32[]{:S(2)}) collective-permute-start(bf16[4,96,256]{2,1,0:T(8,128)(2,1)S(1)} %all-to-all-done.2.refs_0_), channel_id=1, source_target_pairs={{0,8},{8,0},{16,24},{24,16},{1,9},{9,1},{17,25},{25,17},{2,10},{10... | collective-permute-start | bytes 589832 | tf_op jit(solution)/shard_map/ppermute | solution.py:22
  78.7 9.1 %collective-permute-start.16 = (bf16[4,96,256]{2,1,0:T(8,128)(2,1)S(1)}, bf16[4,96,256]{2,1,0:T(8,128)(2,1)}, u32[]{:S(2)}, u32[]{:S(2)}) collective-permute-start(bf16[4,96,256]{2,1,0:T(8,128)(2,1)S(1)} %collective-permute-done.14.refs_4_), channel_id=1, source_target_pairs={{0,8},{8,0},{16,24},{24,16},{1,9},{9,1},{17,25},{25,17},{2,10},{10... | collective-permute-start | bytes 589832 | tf_op jit(solution)/shard_map/ppermute | solution.py:22
  79.2 8.6 %collective-permute-start.13 = (bf16[4,96,256]{2,1,0:T(8,128)(2,1)S(1)}, bf16[4,96,256]{2,1,0:T(8,128)(2,1)}, u32[]{:S(2)}, u32[]{:S(2)}) collective-permute-start(bf16[4,96,256]{2,1,0:T(8,128)(2,1)S(1)} %collective-permute-done.11.refs_1_), channel_id=1, source_target_pairs={{0,8},{8,0},{16,24},{24,16},{1,9},{9,1},{17,25},{25,17},{2,10},{10... | collective-permute-start | bytes 589832 | tf_op jit(solution)/shard_map/ppermute | solution.py:22
  83.8 3.9 %collective-permute-start.17 = (bf16[4,96,256]{2,1,0:T(8,128)(2,1)}, bf16[4,96,256]{2,1,0:T(8,128)(2,1)}, u32[]{:S(2)}, u32[]{:S(2)}) collective-permute-start(bf16[4,96,256]{2,1,0:T(8,128)(2,1)} %collective-permute-done.15.refs_5_), channel_id=1, source_target_pairs={{0,8},{8,0},{16,24},{24,16},{1,9},{9,1},{17,25},{25,17},{2,10},{10... | collective-permute-start | bytes 589832 | tf_op jit(solution)/shard_map/ppermute | solution.py:22
  91.5 13.5 %all-to-all-start.4 = ((bf16[4,5,32,256]{3,2,1,0:T(8,128)(2,1)}), bf16[4,5,32,256]{3,2,1,0:T(8,128)(2,1)S(1)}, u32[]{:S(2)}, u32[]{:S(2)}) async-start(bf16[4,5,32,256]{3,2,1,0:T(8,128)(2,1)} %get-tuple-element.62), calls=%async_computation.4 | async-start | bytes 655360 | tf_op jit(solution)/shard_map/all_to_all | solution.py:56
  95.0 10.8 %collective-permute-start.18 = (bf16[2,32,256]{2,1,0:T(8,128)(2,1)}, bf16[2,32,256]{2,1,0:T(8,128)(2,1)S(1)}, u32[]{:S(2)}, u32[]{:S(2)}) collective-permute-start(bf16[2,32,256]{2,1,0:T(8,128)(2,1)} %bitcast.15), channel_id=1, source_target_pairs={{0,16},{8,24},{16,0},{24,8},{1,17},{9,25},{17,1},{25,9},{2,18},{10... | collective-permute-start | bytes 98312 | tf_op jit(solution)/shard_map/ppermute | solution.py:27
  106.5 8.5 %collective-permute-start.22 = (bf16[4,5,32,256]{3,2,1,0:T(8,128)(2,1)S(1)}, bf16[4,5,32,256]{3,2,1,0:T(8,128)(2,1)S(1)}, u32[]{:S(2)}, u32[]{:S(2)}) collective-permute-start(bf16[4,5,32,256]{3,2,1,0:T(8,128)(2,1)S(1)} %all-to-all-done.4.refs_8_), channel_id=1, source_target_pairs={{0,1},{1,0},{2,3},{3,2},{4,5},{5,4},{6,7},{7,6},{8,9},{9,8},{10,11... | collective-permute-start | bytes 983048 | tf_op jit(solution)/shard_map/ppermute | solution.py:50
  107.7 11.6 %all-to-all-start.5 = ((bf16[8,2,32,256]{3,2,1,0:T(8,128)(2,1)}), bf16[8,2,32,256]{3,2,1,0:T(8,128)(2,1)S(1)}, u32[]{:S(2)}, u32[]{:S(2)}) async-start(bf16[8,2,32,256]{3,2,1,0:T(8,128)(2,1)} %broadcast_in_dim.4), calls=%async_computation.5 | async-start | bytes 524288 | tf_op jit(solution)/shard_map/all_to_all | solution.py:485
  111.3 8.0 %collective-permute-start.19 = (bf16[4,3,32,256]{3,2,1,0:T(8,128)(2,1)}, bf16[4,3,32,256]{3,2,1,0:T(8,128)(2,1)}, u32[]{:S(2)}, u32[]{:S(2)}) collective-permute-start(bf16[4,3,32,256]{3,2,1,0:T(8,128)(2,1)} %slice.8), channel_id=1, source_target_pairs={{0,16},{8,24},{16,0},{24,8},{1,17},{9,25},{17,1},{25,9},{2,18},{10... | collective-permute-start | bytes 589832 | tf_op jit(solution)/shard_map/ppermute | solution.py:27
  115.7 6.0 %collective-permute-start.23 = (bf16[4,3,32,256]{3,2,1,0:T(8,128)(2,1)}, bf16[4,3,32,256]{3,2,1,0:T(8,128)(2,1)}, u32[]{:S(2)}, u32[]{:S(2)}) collective-permute-start(bf16[4,3,32,256]{3,2,1,0:T(8,128)(2,1)} %slice.9), channel_id=1, source_target_pairs={{0,16},{8,24},{16,0},{24,8},{1,17},{9,25},{17,1},{25,9},{2,18},{10... | collective-permute-start | bytes 589832 | tf_op jit(solution)/shard_map/ppermute | solution.py:27
  117.7 4.0 %collective-permute-start.20 = (bf16[4,5,32,256]{3,2,1,0:T(8,128)(2,1)S(1)}, bf16[4,5,32,256]{3,2,1,0:T(8,128)(2,1)S(1)}, u32[]{:S(2)}, u32[]{:S(2)}) collective-permute-start(bf16[4,5,32,256]{3,2,1,0:T(8,128)(2,1)S(1)} %all-to-all-done.4.refs_8_), channel_id=1, source_target_pairs={{0,8},{8,0},{16,24},{24,16},{1,9},{9,1},{17,25},{25,17},{2,10},{10... | collective-permute-start | bytes 983048 | tf_op jit(solution)/shard_map/ppermute | solution.py:22
  117.7 4.0 %collective-permute-start.24 = (bf16[4,5,32,256]{3,2,1,0:T(8,128)(2,1)S(1)}, bf16[4,5,32,256]{3,2,1,0:T(8,128)(2,1)}, u32[]{:S(2)}, u32[]{:S(2)}) collective-permute-start(bf16[4,5,32,256]{3,2,1,0:T(8,128)(2,1)S(1)} %collective-permute-done.22.refs_12_), channel_id=1, source_target_pairs={{0,8},{8,0},{16,24},{24,16},{1,9},{9,1},{17,25},{25,17},{2,10},{10... | collective-permute-start | bytes 983048 | tf_op jit(solution)/shard_map/ppermute | solution.py:22
  119.3 4.1 %collective-permute-start.26 = (bf16[8,2,32,256]{3,2,1,0:T(8,128)(2,1)S(1)}, bf16[8,2,32,256]{3,2,1,0:T(8,128)(2,1)S(1)}, u32[]{:S(2)}, u32[]{:S(2)}) collective-permute-start(bf16[8,2,32,256]{3,2,1,0:T(8,128)(2,1)S(1)} %all-to-all-done.5.refs_16_), channel_id=1, source_target_pairs={{0,8},{8,0},{16,24},{24,16},{1,9},{9,1},{17,25},{25,17},{2,10},{10... | collective-permute-start | bytes 786440 | tf_op jit(solution)/shard_map/ppermute | solution.py:22
  119.3 2.5 %collective-permute-start.21 = (bf16[4,3,32,256]{3,2,1,0:T(8,128)(2,1)}, bf16[4,3,32,256]{3,2,1,0:T(8,128)(2,1)S(1)}, u32[]{:S(2)}, u32[]{:S(2)}) collective-permute-start(bf16[4,3,32,256]{3,2,1,0:T(8,128)(2,1)} %collective-permute-done.19.refs_9_), channel_id=1, source_target_pairs={{0,8},{8,0},{16,24},{24,16},{1,9},{9,1},{17,25},{25,17},{2,10},{10... | collective-permute-start | bytes 589832 | tf_op jit(solution)/shard_map/ppermute | solution.py:22
  121.7 1.7 %collective-permute-start.25 = (bf16[4,3,32,256]{3,2,1,0:T(8,128)(2,1)}, bf16[4,3,32,256]{3,2,1,0:T(8,128)(2,1)S(1)}, u32[]{:S(2)}, u32[]{:S(2)}) collective-permute-start(bf16[4,3,32,256]{3,2,1,0:T(8,128)(2,1)} %collective-permute-done.23.refs_13_), channel_id=1, source_target_pairs={{0,8},{8,0},{16,24},{24,16},{1,9},{9,1},{17,25},{25,17},{2,10},{10... | collective-permute-start | bytes 589832 | tf_op jit(solution)/shard_map/ppermute | solution.py:22

commit v7 on v6

--- a/solution.py
+++ b/solution.py
@@ -478,10 +478,9 @@
     half = count // 2
     own = line_exchange(own_held)
     far = [repeated(chip_shift(held[j - 1], j), peers) for j in range(1, half)]
-    acts = own[:, 2:]
-    own, acts, *far = lax.optimization_barrier((own, acts, *far))
+    own, *far = lax.optimization_barrier((own, *far))
     own = [own, pair_swap(own)]
-    acts = [acts, own[1][:, 2:]]
+    acts = [x[:, 2:] for x in own]
     mine = [lax.all_to_all(x, "dp", 0, 0, tiled=True) for x in far]
     grads = [*mine, *[core_swap(x) for x in mine]]
     states = []

time: 135 us -> 134 us (level)
    ppermute x8, waiting for transfers between devices: 15.5 us -> 17.6 us  [chip_shift(): lax.ppermute(x, 'section', [(i, (i - 2 * by) % count) for i in range(coun...]
    all_to_all x3, waiting for transfers between devices: 11 us -> 8.89 us  [line_exchange(): return lax.all_to_all(x, 'dp', 0, 0, axis_index_groups=groups, tiled=True)]
  transfers between devices with their start and end apart: 33 -> 33, of which waited for: 15 -> 16; matrix products, arithmetic and copies ran while one was open for 2% -> 2% of each run, Pallas kernels for 11% -> 11%
where the time goes in v7:
time: 134 us; the launch traced here: 133 us
  waiting for transfers between devices  48.8 us (36%)
  starting transfers between devices  47.2 us (35%)
  Pallas kernels  31.5 us (24%)
  local copies, waits for them, and re-layouts  5.4 us (4%)
    ppermute x8, waiting for transfers between devices, chip_shift(): lax.ppermute(x, 'section', [(i, (i - 2 * by) % count) for i in range(coun...  17.6 us
    ppermute x8, starting transfers between devices, chip_shift(): lax.ppermute(x, 'section', [(i, (i - 2 * by) % count) for i in range(coun...  13.6 us
    all_to_all x3, starting transfers between devices, line_exchange(): return lax.all_to_all(x, 'dp', 0, 0, axis_index_groups=groups, tiled=True)  11.4 us
    pallas_call x1, Pallas kernels, per_device(): pl.pallas_call(functools.partial(fisher_kernel, count, seqs, 1.0 / (row_c...  10.4 us
    ppermute x4, waiting for transfers between devices, pair_swap(): return lax.ppermute(x, 'dp', [(i, i ^ 1) for i in range(peers)])  10.4 us
    all_to_all x3, waiting for transfers between devices, line_exchange(): return lax.all_to_all(x, 'dp', 0, 0, axis_index_groups=groups, tiled=True)  8.89 us
    all_to_all x1, starting transfers between devices, per_device(): rows = lax.all_to_all(send, 'dp', 0, 0, tiled=True)  7.4 us
    all_to_all x1, waiting for transfers between devices, per_device(): rows = lax.all_to_all(send, 'dp', 0, 0, tiled=True)  6.07 us
  transfers between devices with their start and end apart: 33, of which 16 were waited for; matrix products, arithmetic and copies ran while one was open for 2% of the time, Pallas kernels for 11%

profile of v7, /device:TPU:0, one launch (start us, length us, event | category | flops | bytes accessed | tf_op | source)
XLA Modules:
  0.0 133.1 jit_solution(17102958044326973015)
XLA Ops:
  0.0 2.2 %prepare.1.rows_ref = bf16[8,64,1024]{2,1,0:T(8,128)(2,1)} custom-call(bf16[128,8192]{1,0:T(8,128)(2,1)} %tokens_ref.1, bf16[128,8192]{1,0:T(8,128)(2,1)} %cot_ref.1), custom_call_target="tpu_custom_call" | custom-call | tf_op jit(solution)/shard_map/prepare/pallas_call | solution.py:349
  2.2 7.4 %all-to-all-start.1 = ((bf16[8,64,1024]{2,1,0:T(8,128)(2,1)}), bf16[8,64,1024]{2,1,0:T(8,128)(2,1)S(1)}, u32[]{:S(2)}, u32[]{:S(2)}) async-start(bf16[8,64,1024]{2,1,0:T(8,128)(2,1)} %prepare.1.rows_ref), calls=%async_computation.1 | async-start | bytes 2097152 | tf_op jit(solution)/shard_map/all_to_all | solution.py:384
  9.6 1.6 %collective-permute-start = (bf16[1024,256]{1,0:T(8,128)(2,1)S(1)}, bf16[1024,256]{1,0:T(8,128)(2,1)S(1)}, u32[]{:S(2)}, u32[]{:S(2)}) collective-permute-start(bf16[1024,256]{1,0:T(8,128)(2,1)S(1)} %bitcast.9), channel_id=1, source_target_pairs={{0,16},{8,24},{16,0},{24,8},{1,17},{9,25},{17,1},{25,9},{2,18},{10... | collective-permute-start | bytes 1572872 | tf_op jit(solution)/shard_map/ppermute | solution.py:27
  11.3 1.0 copy-done.3
  12.4 1.6 %weight.1 = (f32[32,1]{1,0:T(8,128)S(1)}, bf16[1024,256]{1,0:T(8,128)(2,1)}) custom-call(s32[2]{0:T(128)S(1)} %pad_add_fusion.1.place, bf16[8,64,1024]{2,1,0:T(8,128)(2,1)S(1)} %copy-done, bf16[1,1024,256]{2,1,0:T(8,128)(2,1)S(1)} %copy-done.3, f32[1,8192]{1,0:T(1,128)S(1)} %copy-done.4), custom_call_target="tpu_custom_call" | custom-call | tf_op jit(solution)/shard_map/weight/pallas_call | solution.py:361
  14.0 0.6 copy-done.5
  15.1 8.0 %collective-permute-done.refs_1_.refs_5_ = bf16[1024,256]{1,0:T(8,128)(2,1)S(1)} collective-permute-done((bf16[1024,256]{1,0:T(8,128)(2,1)S(1)}, bf16[1024,256]{1,0:T(8,128)(2,1)S(1)}, u32[]{:S(2)}, u32[]{:S(2)}) %collective-permute-start) | collective-permute-done | bytes 524320 | tf_op jit(solution)/shard_map/ppermute | solution.py:27
  23.3 1.7 %collective-permute-done.2.refs_3_.refs_7_ = bf16[1024,256]{1,0:T(8,128)(2,1)S(1)} collective-permute-done((bf16[1024,256]{1,0:T(8,128)(2,1)S(1)}, bf16[1024,256]{1,0:T(8,128)(2,1)S(1)}, u32[]{:S(2)}, u32[]{:S(2)}) %collective-permute-start.2) | collective-permute-done | bytes 524320 | tf_op jit(solution)/shard_map/ppermute | solution.py:22
  25.0 2.0 %gram.1 = bf16[8,112,256]{2,1,0:T(8,128)(2,1)S(1)} custom-call(s32[4]{0:T(128)S(1)} %pad_add_fusion.order, s32[3]{0:T(128)S(1)} %dynamic_slice.9.left, s32[3]{0:T(128)S(1)} %dynamic_slice.10.right, s32[1,4]{1,0:T(1,128)S(1)} %copy-done.6, bf16[1024,256]{1,0:T(8,128)(2,1)S(1)} %bitcast.11, bf16[1024,256]{1,0:T(8,128)(2,1)S(1)} %collective-permute-done.refs_1_.refs_5_, ...), custom_call_target="tpu_custom_call" | custom-call | tf_op jit(solution)/shard_map/gram/pallas_call | solution.py:392
  27.1 0.8 copy-done.2
  27.8 1.5 %collective-permute-start.5 = (bf16[1024,256]{1,0:T(8,128)(2,1)}, bf16[1024,256]{1,0:T(8,128)(2,1)}, u32[]{:S(2)}, u32[]{:S(2)}) collective-permute-start(bf16[1024,256]{1,0:T(8,128)(2,1)} %get-tuple-element.41.refs_4_.refs_0_), channel_id=1, source_target_pairs={{0,16},{8,24},{16,0},{24,8},{1,17},{9,25},{17,1},{25,9},{2,18},{10... | collective-permute-start | bytes 1572872 | tf_op jit(solution)/shard_map/ppermute | solution.py:27
  29.3 6.1 %all-to-all-done.1.rows_ref = bf16[8,64,1024]{2,1,0:T(8,128)(2,1)S(1)} async-done(((bf16[8,64,1024]{2,1,0:T(8,128)(2,1)}), bf16[8,64,1024]{2,1,0:T(8,128)(2,1)S(1)}, u32[]{:S(2)}, u32[]{:S(2)}) %all-to-all-start.1) | async-done | bytes 1048608 | tf_op jit(solution)/shard_map/all_to_all | solution.py:384
  35.4 4.1 %all-to-all-start = ((bf16[8,112,256]{2,1,0:T(8,128)(2,1)}), bf16[8,112,256]{2,1,0:T(8,128)(2,1)}, u32[]{:S(2)}, u32[]{:S(2)}) async-start(bf16[8,112,256]{2,1,0:T(8,128)(2,1)} %copy-done.2), calls=%async_computation | async-start | bytes 917504 | tf_op jit(solution)/shard_map/all_to_all | solution.py:404
  39.5 2.9 %project_cot.1 = (f32[4,128,256]{2,1,0:T(8,128)}, bf16[4,128,256]{2,1,0:T(8,128)(2,1)}, bf16[8,32,1024]{2,1,0:T(8,128)(2,1)}) custom-call(s32[4]{0:T(128)S(1)} %pad_add_fusion.order, s32[1]{0:T(128)} %bitcast.5.spot, bf16[8,64,1024]{2,1,0:T(8,128)(2,1)S(1)} %all-to-all-done.1.rows_ref, bf16[1024,256]{1,0:T(8,128)(2,1)S(1)} %bitcast.12, ...), custom_call_target="tpu_custom_call" | custom-call | tf_op jit(solution)/shard_map/project_cot/pallas_call | solution.py:414
  42.4 2.0 %collective-permute-start.4 = (bf16[4,128,256]{2,1,0:T(8,128)(2,1)}, bf16[4,128,256]{2,1,0:T(8,128)(2,1)S(1)}, u32[]{:S(2)}, u32[]{:S(2)}) collective-permute-start(bf16[4,128,256]{2,1,0:T(8,128)(2,1)} %get-tuple-element.39), channel_id=1, source_target_pairs={{0,1},{1,0},{2,3},{3,2},{4,5},{5,4},{6,7},{7,6},{8,9},{9,8},{10,11... | collective-permute-start | bytes 786440 | tf_op jit(solution)/shard_map/ppermute | solution.py:50
  44.4 1.5 %collective-permute-start.8 = (bf16[8,32,1024]{2,1,0:T(8,128)(2,1)}, bf16[8,32,1024]{2,1,0:T(8,128)(2,1)}, u32[]{:S(2)}, u32[]{:S(2)}) collective-permute-start(bf16[8,32,1024]{2,1,0:T(8,128)(2,1)} %get-tuple-element.52.refs_0_), channel_id=1, source_target_pairs={{0,16},{8,24},{16,0},{24,8},{1,17},{9,25},{17,1},{25,9},{2,18},{10... | collective-permute-start | bytes 1572872 | tf_op jit(solution)/shard_map/ppermute | solution.py:27
  45.9 4.6 %project.1 = (f32[4,224,256]{2,1,0:T(8,128)}, bf16[4,224,256]{2,1,0:T(8,128)(2,1)}) custom-call(s32[4]{0:T(128)S(1)} %pad_add_fusion.order, s32[1]{0:T(128)} %bitcast.5.spot, bf16[8,64,1024]{2,1,0:T(8,128)(2,1)S(1)} %all-to-all-done.1.rows_ref, bf16[1024,256]{1,0:T(8,128)(2,1)} %get-tuple-element.41.refs_4_.refs_0_, ...), custom_call_target="tpu_custom_call" | custom-call | tf_op jit(solution)/shard_map/project/pallas_call | solution.py:426
  51.0 1.4 %all-to-all-done.packed_ref = bf16[8,112,256]{2,1,0:T(8,128)(2,1)} async-done(((bf16[8,112,256]{2,1,0:T(8,128)(2,1)}), bf16[8,112,256]{2,1,0:T(8,128)(2,1)}, u32[]{:S(2)}, u32[]{:S(2)}) %all-to-all-start) | async-done | bytes 458784 | tf_op jit(solution)/shard_map/all_to_all | solution.py:404
  52.4 1.7 %collect.1 = (bf16[4,96,256]{2,1,0:T(8,128)(2,1)}, f32[8,256]{1,0:T(8,128)S(1)}) custom-call(bf16[8,112,256]{2,1,0:T(8,128)(2,1)} %all-to-all-done.packed_ref), custom_call_target="tpu_custom_call" | custom-call | tf_op jit(solution)/shard_map/collect/pallas_call | solution.py:435
  54.1 3.6 %all-to-all-start.2 = ((bf16[4,96,256]{2,1,0:T(8,128)(2,1)}), bf16[4,96,256]{2,1,0:T(8,128)(2,1)S(1)}, u32[]{:S(2)}, u32[]{:S(2)}) async-start(bf16[4,96,256]{2,1,0:T(8,128)(2,1)} %get-tuple-element.40), calls=%async_computation.2 | async-start | bytes 393216 | tf_op jit(solution)/shard_map/all_to_all | solution.py:56
  57.7 1.0 collective-permute-done.8.refs_1_
  58.7 4.4 %collective-permute-done.7.got_ref = bf16[4,224,256]{2,1,0:T(8,128)(2,1)S(1)} collective-permute-done((bf16[4,224,256]{2,1,0:T(8,128)(2,1)}, bf16[4,224,256]{2,1,0:T(8,128)(2,1)S(1)}, u32[]{:S(2)}, u32[]{:S(2)}) %collective-permute-start.7) | collective-permute-done | bytes 458784 | tf_op jit(solution)/shard_map/ppermute | solution.py:50
  63.1 2.3 %combine.1 = bf16[4,352,256]{2,1,0:T(8,128)(2,1)} custom-call(f32[4,224,256]{2,1,0:T(8,128)} %get-tuple-element.44.keep_ref, bf16[4,224,256]{2,1,0:T(8,128)(2,1)S(1)} %collective-permute-done.7.got_ref, f32[4,128,256]{2,1,0:T(8,128)} %get-tuple-element.48.back_keep_ref, bf16[4,128,256]{2,1,0:T(8,128)(2,1)S(1)} %collective-permute-done.4.back_got_ref), custom_call_target="tpu_custom_call" | custom-call | tf_op jit(solution)/shard_map/combine/pallas_call | solution.py:445
  65.5 4.4 %all-to-all-start.3 = ((bf16[4,352,256]{2,1,0:T(8,128)(2,1)}), bf16[4,352,256]{2,1,0:T(8,128)(2,1)S(1)}, u32[]{:S(2)}, u32[]{:S(2)}) async-start(bf16[4,352,256]{2,1,0:T(8,128)(2,1)} %combine.1), calls=%async_computation.3 | async-start | bytes 1441792 | tf_op jit(solution)/shard_map/all_to_all | solution.py:56
  69.9 1.0 collective-permute-start.14
  71.1 1.5 %collective-permute-start.11 = (bf16[4,96,256]{2,1,0:T(8,128)(2,1)S(1)}, bf16[4,96,256]{2,1,0:T(8,128)(2,1)S(1)}, u32[]{:S(2)}, u32[]{:S(2)}) collective-permute-start(bf16[4,96,256]{2,1,0:T(8,128)(2,1)S(1)} %all-to-all-done.2.refs_0_), channel_id=1, source_target_pairs={{0,16},{8,24},{16,0},{24,8},{1,17},{9,25},{17,1},{25,9},{2,18},{10... | collective-permute-start | bytes 589832 | tf_op jit(solution)/shard_map/ppermute | solution.py:27
  72.6 4.5 %collective-permute-done.14.refs_4_ = bf16[4,96,256]{2,1,0:T(8,128)(2,1)S(1)} collective-permute-done((bf16[4,96,256]{2,1,0:T(8,128)(2,1)S(1)}, bf16[4,96,256]{2,1,0:T(8,128)(2,1)S(1)}, u32[]{:S(2)}, u32[]{:S(2)}) %collective-permute-start.14) | collective-permute-done | bytes 196640 | tf_op jit(solution)/shard_map/ppermute | solution.py:50
  77.2 1.5 %collective-permute-start.15 = (bf16[4,96,256]{2,1,0:T(8,128)(2,1)S(1)}, bf16[4,96,256]{2,1,0:T(8,128)(2,1)}, u32[]{:S(2)}, u32[]{:S(2)}) collective-permute-start(bf16[4,96,256]{2,1,0:T(8,128)(2,1)S(1)} %collective-permute-done.14.refs_4_), channel_id=1, source_target_pairs={{0,16},{8,24},{16,0},{24,8},{1,17},{9,25},{17,1},{25,9},{2,18},{10... | collective-permute-start | bytes 589832 | tf_op jit(solution)/shard_map/ppermute | solution.py:27
  79.3 4.6 %collective-permute-done.15.refs_5_ = bf16[4,96,256]{2,1,0:T(8,128)(2,1)} collective-permute-done((bf16[4,96,256]{2,1,0:T(8,128)(2,1)S(1)}, bf16[4,96,256]{2,1,0:T(8,128)(2,1)}, u32[]{:S(2)}, u32[]{:S(2)}) %collective-permute-start.15) | collective-permute-done | bytes 196640 | tf_op jit(solution)/shard_map/ppermute | solution.py:27
  83.8 0.7 constant_dynamic-slice_fusion.refs_19_
  84.5 3.2 %all-to-all-done.3.sums_ref = bf16[4,352,256]{2,1,0:T(8,128)(2,1)S(1)} async-done(((bf16[4,352,256]{2,1,0:T(8,128)(2,1)}), bf16[4,352,256]{2,1,0:T(8,128)(2,1)S(1)}, u32[]{:S(2)}, u32[]{:S(2)}) %all-to-all-start.3) | async-done | bytes 720928 | tf_op jit(solution)/shard_map/all_to_all | solution.py:56
  87.8 3.7 %recur.1 = (bf16[4,5,32,256]{3,2,1,0:T(8,128)(2,1)}, bf16[1,2,32,256]{3,2,1,0:T(8,128)(2,1)}) custom-call(s32[4]{0:T(128)S(1)} %pad_add_fusion.order, s32[1]{0:T(128)} %bitcast.5.spot, bf16[4,352,256]{2,1,0:T(8,128)(2,1)S(1)} %all-to-all-done.3.sums_ref, f32[32,1]{1,0:T(8,128)} %copy-done.5, bf16[4,96,256]{2,1,0:T(8,128)(2,1)S(1)} %all-to-all-done.2.refs_0_, ...), custom_call_target="tpu_custom_call" | custom-call | tf_op jit(solution)/shard_map/recur/pallas_call | solution.py:460
  91.5 3.5 %all-to-all-start.4 = ((bf16[4,5,32,256]{3,2,1,0:T(8,128)(2,1)}), bf16[4,5,32,256]{3,2,1,0:T(8,128)(2,1)S(1)}, u32[]{:S(2)}, u32[]{:S(2)}) async-start(bf16[4,5,32,256]{3,2,1,0:T(8,128)(2,1)} %get-tuple-element.61), calls=%async_computation.4 | async-start | bytes 655360 | tf_op jit(solution)/shard_map/all_to_all | solution.py:56
  95.0 2.4 %collective-permute-start.18 = (bf16[2,32,256]{2,1,0:T(8,128)(2,1)}, bf16[2,32,256]{2,1,0:T(8,128)(2,1)S(1)}, u32[]{:S(2)}, u32[]{:S(2)}) collective-permute-start(bf16[2,32,256]{2,1,0:T(8,128)(2,1)} %bitcast.15), channel_id=1, source_target_pairs={{0,16},{8,24},{16,0},{24,8},{1,17},{9,25},{17,1},{25,9},{2,18},{10... | collective-permute-start | bytes 98312 | tf_op jit(solution)/shard_map/ppermute | solution.py:27
  97.4 2.1 %collective-permute-done.18 = bf16[2,32,256]{2,1,0:T(8,128)(2,1)S(1)} collective-permute-done((bf16[2,32,256]{2,1,0:T(8,128)(2,1)}, bf16[2,32,256]{2,1,0:T(8,128)(2,1)S(1)}, u32[]{:S(2)}, u32[]{:S(2)}) %collective-permute-start.18) | collective-permute-done | bytes 32800 | tf_op jit(solution)/shard_map/ppermute | solution.py:27
  99.5 5.6 %all-to-all-done.4.refs_8_ = bf16[4,5,32,256]{3,2,1,0:T(8,128)(2,1)S(1)} async-done(((bf16[4,5,32,256]{3,2,1,0:T(8,128)(2,1)}), bf16[4,5,32,256]{3,2,1,0:T(8,128)(2,1)S(1)}, u32[]{:S(2)}, u32[]{:S(2)}) %all-to-all-start.4) | async-done | bytes 327712 | tf_op jit(solution)/shard_map/all_to_all | solution.py:56
  105.1 0.7 broadcast_in_dim.4
  105.8 1.2 collective-permute-start.22
  107.0 3.6 %all-to-all-start.5 = ((bf16[8,2,32,256]{3,2,1,0:T(8,128)(2,1)}), bf16[8,2,32,256]{3,2,1,0:T(8,128)(2,1)S(1)}, u32[]{:S(2)}, u32[]{:S(2)}) async-start(bf16[8,2,32,256]{3,2,1,0:T(8,128)(2,1)} %broadcast_in_dim.4), calls=%async_computation.5 | async-start | bytes 524288 | tf_op jit(solution)/shard_map/all_to_all | solution.py:484
  110.6 0.7 slice.6
  111.3 1.5 %collective-permute-start.19 = (bf16[4,3,32,256]{3,2,1,0:T(8,128)(2,1)}, bf16[4,3,32,256]{3,2,1,0:T(8,128)(2,1)}, u32[]{:S(2)}, u32[]{:S(2)}) collective-permute-start(bf16[4,3,32,256]{3,2,1,0:T(8,128)(2,1)} %slice.6), channel_id=1, source_target_pairs={{0,16},{8,24},{16,0},{24,8},{1,17},{9,25},{17,1},{25,9},{2,18},{10... | collective-permute-start | bytes 589832 | tf_op jit(solution)/shard_map/ppermute | solution.py:27
  112.8 1.5 %collective-permute-done.22.refs_12_ = bf16[4,5,32,256]{3,2,1,0:T(8,128)(2,1)S(1)} collective-permute-done((bf16[4,5,32,256]{3,2,1,0:T(8,128)(2,1)S(1)}, bf16[4,5,32,256]{3,2,1,0:T(8,128)(2,1)S(1)}, u32[]{:S(2)}, u32[]{:S(2)}) %collective-permute-start.22) | collective-permute-done | bytes 327712 | tf_op jit(solution)/shard_map/ppermute | solution.py:50
  114.3 0.7 slice.8
  115.1 2.0 %collective-permute-start.23 = (bf16[4,3,32,256]{3,2,1,0:T(8,128)(2,1)}, bf16[4,3,32,256]{3,2,1,0:T(8,128)(2,1)}, u32[]{:S(2)}, u32[]{:S(2)}) collective-permute-start(bf16[4,3,32,256]{3,2,1,0:T(8,128)(2,1)} %slice.8), channel_id=1, source_target_pairs={{0,16},{8,24},{16,0},{24,8},{1,17},{9,25},{17,1},{25,9},{2,18},{10... | collective-permute-start | bytes 589832 | tf_op jit(solution)/shard_map/ppermute | solution.py:27
  117.6 1.0 all-to-all-done.5.refs_16_
  119.1 1.9 %collective-permute-done.23.refs_13_ = bf16[4,3,32,256]{3,2,1,0:T(8,128)(2,1)} collective-permute-done((bf16[4,3,32,256]{3,2,1,0:T(8,128)(2,1)}, bf16[4,3,32,256]{3,2,1,0:T(8,128)(2,1)}, u32[]{:S(2)}, u32[]{:S(2)}) %collective-permute-start.23) | collective-permute-done | bytes 196640 | tf_op jit(solution)/shard_map/ppermute | solution.py:27
  121.1 1.6 %collective-permute-done.25.refs_15_ = bf16[4,3,32,256]{3,2,1,0:T(8,128)(2,1)S(1)} collective-permute-done((bf16[4,3,32,256]{3,2,1,0:T(8,128)(2,1)}, bf16[4,3,32,256]{3,2,1,0:T(8,128)(2,1)S(1)}, u32[]{:S(2)}, u32[]{:S(2)}) %collective-permute-start.25) | collective-permute-done | bytes 196640 | tf_op jit(solution)/shard_map/ppermute | solution.py:22
  122.7 10.4 %squares.1 = f32[1024,256]{1,0:T(8,128)} custom-call(s32[4]{0:T(128)S(1)} %pad_add_fusion.order, s32[2]{0:T(128)S(1)} %pad_add_fusion.1.place, bf16[8,32,1024]{2,1,0:T(8,128)(2,1)} %get-tuple-element.52.refs_0_, bf16[8,32,1024]{2,1,0:T(8,128)(2,1)} %collective-permute-done.8.refs_1_, bf16[8,32,1024]{2,1,0:T(8,128)(2,1)S(1)} %collective-permute-done.9.refs_2_, ...), custom_call_target="tpu_custom_call" | custom-call | tf_op jit(solution)/shard_map/squares/pallas_call | solution.py:493
  (53 shorter events, 3.4 us)
Async XLA Ops:
  2.2 7.5 %copy-start.1 = (bf16[1,1024,256]{2,1,0:T(8,128)(2,1)S(1)}, bf16[1,1024,256]{2,1,0:T(8,128)(2,1)}, u32[]{:S(2)}) copy-start(bf16[1,1024,256]{2,1,0:T(8,128)(2,1)} %param.11) | copy-start | bytes 1572868
  2.2 9.1 %copy-start = (bf16[8,64,1024]{2,1,0:T(8,128)(2,1)S(1)}, bf16[8,64,1024]{2,1,0:T(8,128)(2,1)}, u32[]{:S(2)}) copy-start(bf16[8,64,1024]{2,1,0:T(8,128)(2,1)} %prepare.1.rows_ref) | copy-start | bytes 3145732
  2.2 9.1 %copy-start.4 = (f32[1,8192]{1,0:T(1,128)S(1)}, f32[1,8192]{1,0:T(1,128)}, u32[]{:S(2)}) copy-start(f32[1,8192]{1,0:T(1,128)} %gain_ref.1) | copy-start | bytes 98308
  2.2 20.9 %copy-start.8 = (s32[12]{0:T(128)S(1)}, s32[12]{0:T(128)}, u32[]{:S(2)}) copy-start(s32[12]{0:T(128)} %constant.49.clone) | copy-start | bytes 148
  2.2 21.0 %copy-start.7 = (s32[12]{0:T(128)S(1)}, s32[12]{0:T(128)}, u32[]{:S(2)}) copy-start(s32[12]{0:T(128)} %constant.50.clone) | copy-start | bytes 148
  2.2 22.8 %copy-start.6 = (s32[1,4]{1,0:T(1,128)S(1)}, s32[1,4]{1,0:T(1,128)}, u32[]{:S(2)}) copy-start(s32[1,4]{1,0:T(1,128)} %lengths.1) | copy-start | bytes 52
  2.2 33.2 %all-to-all-start.1 = ((bf16[8,64,1024]{2,1,0:T(8,128)(2,1)}), bf16[8,64,1024]{2,1,0:T(8,128)(2,1)S(1)}, u32[]{:S(2)}, u32[]{:S(2)}) async-start(bf16[8,64,1024]{2,1,0:T(8,128)(2,1)} %prepare.1.rows_ref), calls=%async_computation.1 | async-start | bytes 2097152 | tf_op jit(solution)/shard_map/all_to_all | solution.py:384
  9.6 13.4 %collective-permute-start = (bf16[1024,256]{1,0:T(8,128)(2,1)S(1)}, bf16[1024,256]{1,0:T(8,128)(2,1)S(1)}, u32[]{:S(2)}, u32[]{:S(2)}) collective-permute-start(bf16[1024,256]{1,0:T(8,128)(2,1)S(1)} %bitcast.9), channel_id=1, source_target_pairs={{0,16},{8,24},{16,0},{24,8},{1,17},{9,25},{17,1},{25,9},{2,18},{10... | collective-permute-start | bytes 1572872 | tf_op jit(solution)/shard_map/ppermute | solution.py:27
  11.2 12.1 %collective-permute-start.1 = (bf16[1024,256]{1,0:T(8,128)(2,1)S(1)}, bf16[1024,256]{1,0:T(8,128)(2,1)}, u32[]{:S(2)}, u32[]{:S(2)}) collective-permute-start(bf16[1024,256]{1,0:T(8,128)(2,1)S(1)} %bitcast.10), channel_id=1, source_target_pairs={{0,8},{8,0},{16,24},{24,16},{1,9},{9,1},{17,25},{25,17},{2,10},{10... | collective-permute-start | bytes 1572872 | tf_op jit(solution)/shard_map/ppermute | solution.py:22
  11.3 1.0 copy-start.3
  14.0 0.6 copy-start.5
  14.6 8.7 %collective-permute-start.3 = (bf16[1024,256]{1,0:T(8,128)(2,1)}, bf16[1024,256]{1,0:T(8,128)(2,1)S(1)}, u32[]{:S(2)}, u32[]{:S(2)}) collective-permute-start(bf16[1024,256]{1,0:T(8,128)(2,1)} %get-tuple-element.41.refs_4_.refs_0_), channel_id=1, source_target_pairs={{0,8},{8,0},{16,24},{24,16},{1,9},{9,1},{17,25},{25,17},{2,10},{10... | collective-permute-start | bytes 1572872 | tf_op jit(solution)/shard_map/ppermute | solution.py:22
  23.1 1.9 %collective-permute-start.2 = (bf16[1024,256]{1,0:T(8,128)(2,1)S(1)}, bf16[1024,256]{1,0:T(8,128)(2,1)S(1)}, u32[]{:S(2)}, u32[]{:S(2)}) collective-permute-start(bf16[1024,256]{1,0:T(8,128)(2,1)S(1)} %collective-permute-done.refs_1_.refs_5_), channel_id=1, source_target_pairs={{0,8},{8,0},{16,24},{24,16},{1,9},{9,1},{17,25},{25,17},{2,10},{10... | collective-permute-start | bytes 1572872 | tf_op jit(solution)/shard_map/ppermute | solution.py:22
  27.1 0.8 copy-start.2
  27.8 14.6 %collective-permute-start.5 = (bf16[1024,256]{1,0:T(8,128)(2,1)}, bf16[1024,256]{1,0:T(8,128)(2,1)}, u32[]{:S(2)}, u32[]{:S(2)}) collective-permute-start(bf16[1024,256]{1,0:T(8,128)(2,1)} %get-tuple-element.41.refs_4_.refs_0_), channel_id=1, source_target_pairs={{0,16},{8,24},{16,0},{24,8},{1,17},{9,25},{17,1},{25,9},{2,18},{10... | collective-permute-start | bytes 1572872 | tf_op jit(solution)/shard_map/ppermute | solution.py:27
  35.4 17.0 %all-to-all-start = ((bf16[8,112,256]{2,1,0:T(8,128)(2,1)}), bf16[8,112,256]{2,1,0:T(8,128)(2,1)}, u32[]{:S(2)}, u32[]{:S(2)}) async-start(bf16[8,112,256]{2,1,0:T(8,128)(2,1)} %copy-done.2), calls=%async_computation | async-start | bytes 917504 | tf_op jit(solution)/shard_map/all_to_all | solution.py:404
  42.4 3.5 %collective-permute-start.6 = (bf16[1024,256]{1,0:T(8,128)(2,1)}, bf16[1024,256]{1,0:T(8,128)(2,1)S(1)}, u32[]{:S(2)}, u32[]{:S(2)}) collective-permute-start(bf16[1024,256]{1,0:T(8,128)(2,1)} %collective-permute-done.5.refs_1_), channel_id=1, source_target_pairs={{0,8},{8,0},{16,24},{24,16},{1,9},{9,1},{17,25},{25,17},{2,10},{10... | collective-permute-start | bytes 1572872 | tf_op jit(solution)/shard_map/ppermute | solution.py:22
  42.4 11.7 %collective-permute-start.4 = (bf16[4,128,256]{2,1,0:T(8,128)(2,1)}, bf16[4,128,256]{2,1,0:T(8,128)(2,1)S(1)}, u32[]{:S(2)}, u32[]{:S(2)}) collective-permute-start(bf16[4,128,256]{2,1,0:T(8,128)(2,1)} %get-tuple-element.39), channel_id=1, source_target_pairs={{0,1},{1,0},{2,3},{3,2},{4,5},{5,4},{6,7},{7,6},{8,9},{9,8},{10,11... | collective-permute-start | bytes 786440 | tf_op jit(solution)/shard_map/ppermute | solution.py:50
  44.4 14.3 %collective-permute-start.8 = (bf16[8,32,1024]{2,1,0:T(8,128)(2,1)}, bf16[8,32,1024]{2,1,0:T(8,128)(2,1)}, u32[]{:S(2)}, u32[]{:S(2)}) collective-permute-start(bf16[8,32,1024]{2,1,0:T(8,128)(2,1)} %get-tuple-element.52.refs_0_), channel_id=1, source_target_pairs={{0,16},{8,24},{16,0},{24,8},{1,17},{9,25},{17,1},{25,9},{2,18},{10... | collective-permute-start | bytes 1572872 | tf_op jit(solution)/shard_map/ppermute | solution.py:27
  50.5 12.6 %collective-permute-start.7 = (bf16[4,224,256]{2,1,0:T(8,128)(2,1)}, bf16[4,224,256]{2,1,0:T(8,128)(2,1)S(1)}, u32[]{:S(2)}, u32[]{:S(2)}) collective-permute-start(bf16[4,224,256]{2,1,0:T(8,128)(2,1)} %get-tuple-element.45), channel_id=1, source_target_pairs={{0,1},{1,0},{2,3},{3,2},{4,5},{5,4},{6,7},{7,6},{8,9},{9,8},{10,11... | collective-permute-start | bytes 1376264 | tf_op jit(solution)/shard_map/ppermute | solution.py:50
  54.1 11.3 %all-to-all-start.2 = ((bf16[4,96,256]{2,1,0:T(8,128)(2,1)}), bf16[4,96,256]{2,1,0:T(8,128)(2,1)S(1)}, u32[]{:S(2)}, u32[]{:S(2)}) async-start(bf16[4,96,256]{2,1,0:T(8,128)(2,1)} %get-tuple-element.40), calls=%async_computation.2 | async-start | bytes 393216 | tf_op jit(solution)/shard_map/all_to_all | solution.py:56
  65.5 22.3 %all-to-all-start.3 = ((bf16[4,352,256]{2,1,0:T(8,128)(2,1)}), bf16[4,352,256]{2,1,0:T(8,128)(2,1)S(1)}, u32[]{:S(2)}, u32[]{:S(2)}) async-start(bf16[4,352,256]{2,1,0:T(8,128)(2,1)} %combine.1), calls=%async_computation.3 | async-start | bytes 1441792 | tf_op jit(solution)/shard_map/all_to_all | solution.py:56
  69.9 8.8 %collective-permute-start.9 = (bf16[8,32,1024]{2,1,0:T(8,128)(2,1)}, bf16[8,32,1024]{2,1,0:T(8,128)(2,1)S(1)}, u32[]{:S(2)}, u32[]{:S(2)}) collective-permute-start(bf16[8,32,1024]{2,1,0:T(8,128)(2,1)} %get-tuple-element.52.refs_0_), channel_id=1, source_target_pairs={{0,8},{8,0},{16,24},{24,16},{1,9},{9,1},{17,25},{25,17},{2,10},{10... | collective-permute-start | bytes 1572872 | tf_op jit(solution)/shard_map/ppermute | solution.py:22
  69.9 7.3 %collective-permute-start.14 = (bf16[4,96,256]{2,1,0:T(8,128)(2,1)S(1)}, bf16[4,96,256]{2,1,0:T(8,128)(2,1)S(1)}, u32[]{:S(2)}, u32[]{:S(2)}) collective-permute-start(bf16[4,96,256]{2,1,0:T(8,128)(2,1)S(1)} %all-to-all-done.2.refs_0_), channel_id=1, source_target_pairs={{0,1},{1,0},{2,3},{3,2},{4,5},{5,4},{6,7},{7,6},{8,9},{9,8},{10,11... | collective-permute-start | bytes 589832 | tf_op jit(solution)/shard_map/ppermute | solution.py:50
  70.9 13.6 %collective-permute-start.10 = (bf16[8,32,1024]{2,1,0:T(8,128)(2,1)}, bf16[8,32,1024]{2,1,0:T(8,128)(2,1)}, u32[]{:S(2)}, u32[]{:S(2)}) collective-permute-start(bf16[8,32,1024]{2,1,0:T(8,128)(2,1)} %collective-permute-done.8.refs_1_), channel_id=1, source_target_pairs={{0,8},{8,0},{16,24},{24,16},{1,9},{9,1},{17,25},{25,17},{2,10},{10... | collective-permute-start | bytes 1572872 | tf_op jit(solution)/shard_map/ppermute | solution.py:22
  71.1 8.1 %collective-permute-start.11 = (bf16[4,96,256]{2,1,0:T(8,128)(2,1)S(1)}, bf16[4,96,256]{2,1,0:T(8,128)(2,1)S(1)}, u32[]{:S(2)}, u32[]{:S(2)}) collective-permute-start(bf16[4,96,256]{2,1,0:T(8,128)(2,1)S(1)} %all-to-all-done.2.refs_0_), channel_id=1, source_target_pairs={{0,16},{8,24},{16,0},{24,8},{1,17},{9,25},{17,1},{25,9},{2,18},{10... | collective-permute-start | bytes 589832 | tf_op jit(solution)/shard_map/ppermute | solution.py:27
  77.2 6.6 %collective-permute-start.15 = (bf16[4,96,256]{2,1,0:T(8,128)(2,1)S(1)}, bf16[4,96,256]{2,1,0:T(8,128)(2,1)}, u32[]{:S(2)}, u32[]{:S(2)}) collective-permute-start(bf16[4,96,256]{2,1,0:T(8,128)(2,1)S(1)} %collective-permute-done.14.refs_4_), channel_id=1, source_target_pairs={{0,16},{8,24},{16,0},{24,8},{1,17},{9,25},{17,1},{25,9},{2,18},{10... | collective-permute-start | bytes 589832 | tf_op jit(solution)/shard_map/ppermute | solution.py:27
  78.7 9.1 %collective-permute-start.12 = (bf16[4,96,256]{2,1,0:T(8,128)(2,1)S(1)}, bf16[4,96,256]{2,1,0:T(8,128)(2,1)}, u32[]{:S(2)}, u32[]{:S(2)}) collective-permute-start(bf16[4,96,256]{2,1,0:T(8,128)(2,1)S(1)} %all-to-all-done.2.refs_0_), channel_id=1, source_target_pairs={{0,8},{8,0},{16,24},{24,16},{1,9},{9,1},{17,25},{25,17},{2,10},{10... | collective-permute-start | bytes 589832 | tf_op jit(solution)/shard_map/ppermute | solution.py:22
  78.7 9.1 %collective-permute-start.16 = (bf16[4,96,256]{2,1,0:T(8,128)(2,1)S(1)}, bf16[4,96,256]{2,1,0:T(8,128)(2,1)}, u32[]{:S(2)}, u32[]{:S(2)}) collective-permute-start(bf16[4,96,256]{2,1,0:T(8,128)(2,1)S(1)} %collective-permute-done.14.refs_4_), channel_id=1, source_target_pairs={{0,8},{8,0},{16,24},{24,16},{1,9},{9,1},{17,25},{25,17},{2,10},{10... | collective-permute-start | bytes 589832 | tf_op jit(solution)/shard_map/ppermute | solution.py:22
  79.2 8.6 %collective-permute-start.13 = (bf16[4,96,256]{2,1,0:T(8,128)(2,1)S(1)}, bf16[4,96,256]{2,1,0:T(8,128)(2,1)}, u32[]{:S(2)}, u32[]{:S(2)}) collective-permute-start(bf16[4,96,256]{2,1,0:T(8,128)(2,1)S(1)} %collective-permute-done.11.refs_1_), channel_id=1, source_target_pairs={{0,8},{8,0},{16,24},{24,16},{1,9},{9,1},{17,25},{25,17},{2,10},{10... | collective-permute-start | bytes 589832 | tf_op jit(solution)/shard_map/ppermute | solution.py:22
  83.8 3.9 %collective-permute-start.17 = (bf16[4,96,256]{2,1,0:T(8,128)(2,1)}, bf16[4,96,256]{2,1,0:T(8,128)(2,1)}, u32[]{:S(2)}, u32[]{:S(2)}) collective-permute-start(bf16[4,96,256]{2,1,0:T(8,128)(2,1)} %collective-permute-done.15.refs_5_), channel_id=1, source_target_pairs={{0,8},{8,0},{16,24},{24,16},{1,9},{9,1},{17,25},{25,17},{2,10},{10... | collective-permute-start | bytes 589832 | tf_op jit(solution)/shard_map/ppermute | solution.py:22
  91.5 13.5 %all-to-all-start.4 = ((bf16[4,5,32,256]{3,2,1,0:T(8,128)(2,1)}), bf16[4,5,32,256]{3,2,1,0:T(8,128)(2,1)S(1)}, u32[]{:S(2)}, u32[]{:S(2)}) async-start(bf16[4,5,32,256]{3,2,1,0:T(8,128)(2,1)} %get-tuple-element.61), calls=%async_computation.4 | async-start | bytes 655360 | tf_op jit(solution)/shard_map/all_to_all | solution.py:56
  95.0 4.5 %collective-permute-start.18 = (bf16[2,32,256]{2,1,0:T(8,128)(2,1)}, bf16[2,32,256]{2,1,0:T(8,128)(2,1)S(1)}, u32[]{:S(2)}, u32[]{:S(2)}) collective-permute-start(bf16[2,32,256]{2,1,0:T(8,128)(2,1)} %bitcast.15), channel_id=1, source_target_pairs={{0,16},{8,24},{16,0},{24,8},{1,17},{9,25},{17,1},{25,9},{2,18},{10... | collective-permute-start | bytes 98312 | tf_op jit(solution)/shard_map/ppermute | solution.py:27
  105.8 8.5 %collective-permute-start.22 = (bf16[4,5,32,256]{3,2,1,0:T(8,128)(2,1)S(1)}, bf16[4,5,32,256]{3,2,1,0:T(8,128)(2,1)S(1)}, u32[]{:S(2)}, u32[]{:S(2)}) collective-permute-start(bf16[4,5,32,256]{3,2,1,0:T(8,128)(2,1)S(1)} %all-to-all-done.4.refs_8_), channel_id=1, source_target_pairs={{0,1},{1,0},{2,3},{3,2},{4,5},{5,4},{6,7},{7,6},{8,9},{9,8},{10,11... | collective-permute-start | bytes 983048 | tf_op jit(solution)/shard_map/ppermute | solution.py:50
  107.0 11.6 %all-to-all-start.5 = ((bf16[8,2,32,256]{3,2,1,0:T(8,128)(2,1)}), bf16[8,2,32,256]{3,2,1,0:T(8,128)(2,1)S(1)}, u32[]{:S(2)}, u32[]{:S(2)}) async-start(bf16[8,2,32,256]{3,2,1,0:T(8,128)(2,1)} %broadcast_in_dim.4), calls=%async_computation.5 | async-start | bytes 524288 | tf_op jit(solution)/shard_map/all_to_all | solution.py:484
  111.3 7.3 %collective-permute-start.19 = (bf16[4,3,32,256]{3,2,1,0:T(8,128)(2,1)}, bf16[4,3,32,256]{3,2,1,0:T(8,128)(2,1)}, u32[]{:S(2)}, u32[]{:S(2)}) collective-permute-start(bf16[4,3,32,256]{3,2,1,0:T(8,128)(2,1)} %slice.6), channel_id=1, source_target_pairs={{0,16},{8,24},{16,0},{24,8},{1,17},{9,25},{17,1},{25,9},{2,18},{10... | collective-permute-start | bytes 589832 | tf_op jit(solution)/shard_map/ppermute | solution.py:27
  115.1 6.0 %collective-permute-start.23 = (bf16[4,3,32,256]{3,2,1,0:T(8,128)(2,1)}, bf16[4,3,32,256]{3,2,1,0:T(8,128)(2,1)}, u32[]{:S(2)}, u32[]{:S(2)}) collective-permute-start(bf16[4,3,32,256]{3,2,1,0:T(8,128)(2,1)} %slice.8), channel_id=1, source_target_pairs={{0,16},{8,24},{16,0},{24,8},{1,17},{9,25},{17,1},{25,9},{2,18},{10... | collective-permute-start | bytes 589832 | tf_op jit(solution)/shard_map/ppermute | solution.py:27
  117.1 4.0 %collective-permute-start.20 = (bf16[4,5,32,256]{3,2,1,0:T(8,128)(2,1)S(1)}, bf16[4,5,32,256]{3,2,1,0:T(8,128)(2,1)S(1)}, u32[]{:S(2)}, u32[]{:S(2)}) collective-permute-start(bf16[4,5,32,256]{3,2,1,0:T(8,128)(2,1)S(1)} %all-to-all-done.4.refs_8_), channel_id=1, source_target_pairs={{0,8},{8,0},{16,24},{24,16},{1,9},{9,1},{17,25},{25,17},{2,10},{10... | collective-permute-start | bytes 983048 | tf_op jit(solution)/shard_map/ppermute | solution.py:22
  117.1 4.0 %collective-permute-start.24 = (bf16[4,5,32,256]{3,2,1,0:T(8,128)(2,1)S(1)}, bf16[4,5,32,256]{3,2,1,0:T(8,128)(2,1)}, u32[]{:S(2)}, u32[]{:S(2)}) collective-permute-start(bf16[4,5,32,256]{3,2,1,0:T(8,128)(2,1)S(1)} %collective-permute-done.22.refs_12_), channel_id=1, source_target_pairs={{0,8},{8,0},{16,24},{24,16},{1,9},{9,1},{17,25},{25,17},{2,10},{10... | collective-permute-start | bytes 983048 | tf_op jit(solution)/shard_map/ppermute | solution.py:22
  118.6 4.1 %collective-permute-start.26 = (bf16[8,2,32,256]{3,2,1,0:T(8,128)(2,1)S(1)}, bf16[8,2,32,256]{3,2,1,0:T(8,128)(2,1)S(1)}, u32[]{:S(2)}, u32[]{:S(2)}) collective-permute-start(bf16[8,2,32,256]{3,2,1,0:T(8,128)(2,1)S(1)} %all-to-all-done.5.refs_16_), channel_id=1, source_target_pairs={{0,8},{8,0},{16,24},{24,16},{1,9},{9,1},{17,25},{25,17},{2,10},{10... | collective-permute-start | bytes 786440 | tf_op jit(solution)/shard_map/ppermute | solution.py:22
  118.6 2.4 %collective-permute-start.21 = (bf16[4,3,32,256]{3,2,1,0:T(8,128)(2,1)}, bf16[4,3,32,256]{3,2,1,0:T(8,128)(2,1)S(1)}, u32[]{:S(2)}, u32[]{:S(2)}) collective-permute-start(bf16[4,3,32,256]{3,2,1,0:T(8,128)(2,1)} %collective-permute-done.19.refs_9_), channel_id=1, source_target_pairs={{0,8},{8,0},{16,24},{24,16},{1,9},{9,1},{17,25},{25,17},{2,10},{10... | collective-permute-start | bytes 589832 | tf_op jit(solution)/shard_map/ppermute | solution.py:22
  121.0 1.7 %collective-permute-start.25 = (bf16[4,3,32,256]{3,2,1,0:T(8,128)(2,1)}, bf16[4,3,32,256]{3,2,1,0:T(8,128)(2,1)S(1)}, u32[]{:S(2)}, u32[]{:S(2)}) collective-permute-start(bf16[4,3,32,256]{3,2,1,0:T(8,128)(2,1)} %collective-permute-done.23.refs_13_), channel_id=1, source_target_pairs={{0,8},{8,0},{16,24},{24,16},{1,9},{9,1},{17,25},{25,17},{2,10},{10... | collective-permute-start | bytes 589832 | tf_op jit(solution)/shard_map/ppermute | solution.py:22

commit v8 on v7

--- a/solution.py
+++ b/solution.py
@@ -240,8 +240,8 @@
             hu = [hu[j] + step[j] for j in range(count - 1)]
     for l in reversed(range(count)):
         s = jax.nn.sigmoid(pres[l])
-        grad = (back[l] * s * (1.0 + pres[l] * (1.0 - s))).astype(bf16)
-        wide = grad.astype(f32)
+        wide = back[l] * s * (1.0 + pres[l] * (1.0 - s))
+        grad = wide.astype(bf16)
         grads[l] = (wide * invs[l]).astype(bf16)
         inner = jnp.sum(wide * proj[l], axis=-1, keepdims=True) / width
         for j in range(l):

time: 134 us -> 134 us (level)
  no operation moved by 1% of the time
where the time goes in v8:
time: 134 us; the launch traced here: 133 us
  waiting for transfers between devices  48.7 us (36%)
  starting transfers between devices  47.2 us (35%)
  Pallas kernels  31.5 us (24%)
  local copies, waits for them, and re-layouts  5.4 us (4%)
    ppermute x8, waiting for transfers between devices, chip_shift(): lax.ppermute(x, 'section', [(i, (i - 2 * by) % count) for i in range(coun...  17.6 us
    ppermute x8, starting transfers between devices, chip_shift(): lax.ppermute(x, 'section', [(i, (i - 2 * by) % count) for i in range(coun...  13.6 us
    all_to_all x3, starting transfers between devices, line_exchange(): return lax.all_to_all(x, 'dp', 0, 0, axis_index_groups=groups, tiled=True)  11.4 us
    pallas_call x1, Pallas kernels, per_device(): pl.pallas_call(functools.partial(fisher_kernel, count, seqs, 1.0 / (row_c...  10.4 us
    ppermute x4, waiting for transfers between devices, pair_swap(): return lax.ppermute(x, 'dp', [(i, i ^ 1) for i in range(peers)])  10.4 us
    all_to_all x3, waiting for transfers between devices, line_exchange(): return lax.all_to_all(x, 'dp', 0, 0, axis_index_groups=groups, tiled=True)  8.89 us
    all_to_all x1, starting transfers between devices, per_device(): rows = lax.all_to_all(send, 'dp', 0, 0, tiled=True)  7.4 us
    all_to_all x1, waiting for transfers between devices, per_device(): rows = lax.all_to_all(send, 'dp', 0, 0, tiled=True)  6.07 us
  transfers between devices with their start and end apart: 33, of which 16 were waited for; matrix products, arithmetic and copies ran while one was open for 2% of the time, Pallas kernels for 11%

profile of v8, /device:TPU:0, one launch (start us, length us, event | category | flops | bytes accessed | tf_op | source)
XLA Modules:
  0.0 133.1 jit_solution(15451714708779421611)
XLA Ops:
  0.0 2.2 %prepare.1.rows_ref = bf16[8,64,1024]{2,1,0:T(8,128)(2,1)} custom-call(bf16[128,8192]{1,0:T(8,128)(2,1)} %tokens_ref.1, bf16[128,8192]{1,0:T(8,128)(2,1)} %cot_ref.1), custom_call_target="tpu_custom_call" | custom-call | tf_op jit(solution)/shard_map/prepare/pallas_call | solution.py:349
  2.2 7.4 %all-to-all-start.1 = ((bf16[8,64,1024]{2,1,0:T(8,128)(2,1)}), bf16[8,64,1024]{2,1,0:T(8,128)(2,1)S(1)}, u32[]{:S(2)}, u32[]{:S(2)}) async-start(bf16[8,64,1024]{2,1,0:T(8,128)(2,1)} %prepare.1.rows_ref), calls=%async_computation.1 | async-start | bytes 2097152 | tf_op jit(solution)/shard_map/all_to_all | solution.py:384
  9.6 1.6 %collective-permute-start = (bf16[1024,256]{1,0:T(8,128)(2,1)S(1)}, bf16[1024,256]{1,0:T(8,128)(2,1)S(1)}, u32[]{:S(2)}, u32[]{:S(2)}) collective-permute-start(bf16[1024,256]{1,0:T(8,128)(2,1)S(1)} %bitcast.9), channel_id=1, source_target_pairs={{0,16},{8,24},{16,0},{24,8},{1,17},{9,25},{17,1},{25,9},{2,18},{10... | collective-permute-start | bytes 1572872 | tf_op jit(solution)/shard_map/ppermute | solution.py:27
  11.3 1.0 copy-done.3
  12.4 1.6 %weight.1 = (f32[32,1]{1,0:T(8,128)S(1)}, bf16[1024,256]{1,0:T(8,128)(2,1)}) custom-call(s32[2]{0:T(128)S(1)} %pad_add_fusion.1.place, bf16[8,64,1024]{2,1,0:T(8,128)(2,1)S(1)} %copy-done, bf16[1,1024,256]{2,1,0:T(8,128)(2,1)S(1)} %copy-done.3, f32[1,8192]{1,0:T(1,128)S(1)} %copy-done.4), custom_call_target="tpu_custom_call" | custom-call | tf_op jit(solution)/shard_map/weight/pallas_call | solution.py:361
  14.0 0.6 copy-done.5
  15.1 8.0 %collective-permute-done.refs_1_.refs_5_ = bf16[1024,256]{1,0:T(8,128)(2,1)S(1)} collective-permute-done((bf16[1024,256]{1,0:T(8,128)(2,1)S(1)}, bf16[1024,256]{1,0:T(8,128)(2,1)S(1)}, u32[]{:S(2)}, u32[]{:S(2)}) %collective-permute-start) | collective-permute-done | bytes 524320 | tf_op jit(solution)/shard_map/ppermute | solution.py:27
  23.3 1.7 %collective-permute-done.2.refs_3_.refs_7_ = bf16[1024,256]{1,0:T(8,128)(2,1)S(1)} collective-permute-done((bf16[1024,256]{1,0:T(8,128)(2,1)S(1)}, bf16[1024,256]{1,0:T(8,128)(2,1)S(1)}, u32[]{:S(2)}, u32[]{:S(2)}) %collective-permute-start.2) | collective-permute-done | bytes 524320 | tf_op jit(solution)/shard_map/ppermute | solution.py:22
  25.0 2.0 %gram.1 = bf16[8,112,256]{2,1,0:T(8,128)(2,1)S(1)} custom-call(s32[4]{0:T(128)S(1)} %pad_add_fusion.order, s32[3]{0:T(128)S(1)} %dynamic_slice.9.left, s32[3]{0:T(128)S(1)} %dynamic_slice.10.right, s32[1,4]{1,0:T(1,128)S(1)} %copy-done.6, bf16[1024,256]{1,0:T(8,128)(2,1)S(1)} %bitcast.11, bf16[1024,256]{1,0:T(8,128)(2,1)S(1)} %collective-permute-done.refs_1_.refs_5_, ...), custom_call_target="tpu_custom_call" | custom-call | tf_op jit(solution)/shard_map/gram/pallas_call | solution.py:392
  27.1 0.8 copy-done.2
  27.8 1.5 %collective-permute-start.5 = (bf16[1024,256]{1,0:T(8,128)(2,1)}, bf16[1024,256]{1,0:T(8,128)(2,1)}, u32[]{:S(2)}, u32[]{:S(2)}) collective-permute-start(bf16[1024,256]{1,0:T(8,128)(2,1)} %get-tuple-element.41.refs_4_.refs_0_), channel_id=1, source_target_pairs={{0,16},{8,24},{16,0},{24,8},{1,17},{9,25},{17,1},{25,9},{2,18},{10... | collective-permute-start | bytes 1572872 | tf_op jit(solution)/shard_map/ppermute | solution.py:27
  29.3 6.1 %all-to-all-done.1.rows_ref = bf16[8,64,1024]{2,1,0:T(8,128)(2,1)S(1)} async-done(((bf16[8,64,1024]{2,1,0:T(8,128)(2,1)}), bf16[8,64,1024]{2,1,0:T(8,128)(2,1)S(1)}, u32[]{:S(2)}, u32[]{:S(2)}) %all-to-all-start.1) | async-done | bytes 1048608 | tf_op jit(solution)/shard_map/all_to_all | solution.py:384
  35.4 4.1 %all-to-all-start = ((bf16[8,112,256]{2,1,0:T(8,128)(2,1)}), bf16[8,112,256]{2,1,0:T(8,128)(2,1)}, u32[]{:S(2)}, u32[]{:S(2)}) async-start(bf16[8,112,256]{2,1,0:T(8,128)(2,1)} %copy-done.2), calls=%async_computation | async-start | bytes 917504 | tf_op jit(solution)/shard_map/all_to_all | solution.py:404
  39.5 2.9 %project_cot.1 = (f32[4,128,256]{2,1,0:T(8,128)}, bf16[4,128,256]{2,1,0:T(8,128)(2,1)}, bf16[8,32,1024]{2,1,0:T(8,128)(2,1)}) custom-call(s32[4]{0:T(128)S(1)} %pad_add_fusion.order, s32[1]{0:T(128)} %bitcast.5.spot, bf16[8,64,1024]{2,1,0:T(8,128)(2,1)S(1)} %all-to-all-done.1.rows_ref, bf16[1024,256]{1,0:T(8,128)(2,1)S(1)} %bitcast.12, ...), custom_call_target="tpu_custom_call" | custom-call | tf_op jit(solution)/shard_map/project_cot/pallas_call | solution.py:414
  42.4 2.0 %collective-permute-start.4 = (bf16[4,128,256]{2,1,0:T(8,128)(2,1)}, bf16[4,128,256]{2,1,0:T(8,128)(2,1)S(1)}, u32[]{:S(2)}, u32[]{:S(2)}) collective-permute-start(bf16[4,128,256]{2,1,0:T(8,128)(2,1)} %get-tuple-element.39), channel_id=1, source_target_pairs={{0,1},{1,0},{2,3},{3,2},{4,5},{5,4},{6,7},{7,6},{8,9},{9,8},{10,11... | collective-permute-start | bytes 786440 | tf_op jit(solution)/shard_map/ppermute | solution.py:50
  44.4 1.5 %collective-permute-start.8 = (bf16[8,32,1024]{2,1,0:T(8,128)(2,1)}, bf16[8,32,1024]{2,1,0:T(8,128)(2,1)}, u32[]{:S(2)}, u32[]{:S(2)}) collective-permute-start(bf16[8,32,1024]{2,1,0:T(8,128)(2,1)} %get-tuple-element.52.refs_0_), channel_id=1, source_target_pairs={{0,16},{8,24},{16,0},{24,8},{1,17},{9,25},{17,1},{25,9},{2,18},{10... | collective-permute-start | bytes 1572872 | tf_op jit(solution)/shard_map/ppermute | solution.py:27
  45.9 4.6 %project.1 = (f32[4,224,256]{2,1,0:T(8,128)}, bf16[4,224,256]{2,1,0:T(8,128)(2,1)}) custom-call(s32[4]{0:T(128)S(1)} %pad_add_fusion.order, s32[1]{0:T(128)} %bitcast.5.spot, bf16[8,64,1024]{2,1,0:T(8,128)(2,1)S(1)} %all-to-all-done.1.rows_ref, bf16[1024,256]{1,0:T(8,128)(2,1)} %get-tuple-element.41.refs_4_.refs_0_, ...), custom_call_target="tpu_custom_call" | custom-call | tf_op jit(solution)/shard_map/project/pallas_call | solution.py:426
  51.0 1.4 %all-to-all-done.packed_ref = bf16[8,112,256]{2,1,0:T(8,128)(2,1)} async-done(((bf16[8,112,256]{2,1,0:T(8,128)(2,1)}), bf16[8,112,256]{2,1,0:T(8,128)(2,1)}, u32[]{:S(2)}, u32[]{:S(2)}) %all-to-all-start) | async-done | bytes 458784 | tf_op jit(solution)/shard_map/all_to_all | solution.py:404
  52.4 1.7 %collect.1 = (bf16[4,96,256]{2,1,0:T(8,128)(2,1)}, f32[8,256]{1,0:T(8,128)S(1)}) custom-call(bf16[8,112,256]{2,1,0:T(8,128)(2,1)} %all-to-all-done.packed_ref), custom_call_target="tpu_custom_call" | custom-call | tf_op jit(solution)/shard_map/collect/pallas_call | solution.py:435
  54.1 3.6 %all-to-all-start.2 = ((bf16[4,96,256]{2,1,0:T(8,128)(2,1)}), bf16[4,96,256]{2,1,0:T(8,128)(2,1)S(1)}, u32[]{:S(2)}, u32[]{:S(2)}) async-start(bf16[4,96,256]{2,1,0:T(8,128)(2,1)} %get-tuple-element.40), calls=%async_computation.2 | async-start | bytes 393216 | tf_op jit(solution)/shard_map/all_to_all | solution.py:56
  57.7 1.0 collective-permute-done.8.refs_1_
  58.7 4.4 %collective-permute-done.7.got_ref = bf16[4,224,256]{2,1,0:T(8,128)(2,1)S(1)} collective-permute-done((bf16[4,224,256]{2,1,0:T(8,128)(2,1)}, bf16[4,224,256]{2,1,0:T(8,128)(2,1)S(1)}, u32[]{:S(2)}, u32[]{:S(2)}) %collective-permute-start.7) | collective-permute-done | bytes 458784 | tf_op jit(solution)/shard_map/ppermute | solution.py:50
  63.1 2.3 %combine.1 = bf16[4,352,256]{2,1,0:T(8,128)(2,1)} custom-call(f32[4,224,256]{2,1,0:T(8,128)} %get-tuple-element.44.keep_ref, bf16[4,224,256]{2,1,0:T(8,128)(2,1)S(1)} %collective-permute-done.7.got_ref, f32[4,128,256]{2,1,0:T(8,128)} %get-tuple-element.48.back_keep_ref, bf16[4,128,256]{2,1,0:T(8,128)(2,1)S(1)} %collective-permute-done.4.back_got_ref), custom_call_target="tpu_custom_call" | custom-call | tf_op jit(solution)/shard_map/combine/pallas_call | solution.py:445
  65.5 4.4 %all-to-all-start.3 = ((bf16[4,352,256]{2,1,0:T(8,128)(2,1)}), bf16[4,352,256]{2,1,0:T(8,128)(2,1)S(1)}, u32[]{:S(2)}, u32[]{:S(2)}) async-start(bf16[4,352,256]{2,1,0:T(8,128)(2,1)} %combine.1), calls=%async_computation.3 | async-start | bytes 1441792 | tf_op jit(solution)/shard_map/all_to_all | solution.py:56
  69.9 1.0 collective-permute-start.14
  71.1 1.5 %collective-permute-start.11 = (bf16[4,96,256]{2,1,0:T(8,128)(2,1)S(1)}, bf16[4,96,256]{2,1,0:T(8,128)(2,1)S(1)}, u32[]{:S(2)}, u32[]{:S(2)}) collective-permute-start(bf16[4,96,256]{2,1,0:T(8,128)(2,1)S(1)} %all-to-all-done.2.refs_0_), channel_id=1, source_target_pairs={{0,16},{8,24},{16,0},{24,8},{1,17},{9,25},{17,1},{25,9},{2,18},{10... | collective-permute-start | bytes 589832 | tf_op jit(solution)/shard_map/ppermute | solution.py:27
  72.6 4.5 %collective-permute-done.14.refs_4_ = bf16[4,96,256]{2,1,0:T(8,128)(2,1)S(1)} collective-permute-done((bf16[4,96,256]{2,1,0:T(8,128)(2,1)S(1)}, bf16[4,96,256]{2,1,0:T(8,128)(2,1)S(1)}, u32[]{:S(2)}, u32[]{:S(2)}) %collective-permute-start.14) | collective-permute-done | bytes 196640 | tf_op jit(solution)/shard_map/ppermute | solution.py:50
  77.2 1.5 %collective-permute-start.15 = (bf16[4,96,256]{2,1,0:T(8,128)(2,1)S(1)}, bf16[4,96,256]{2,1,0:T(8,128)(2,1)}, u32[]{:S(2)}, u32[]{:S(2)}) collective-permute-start(bf16[4,96,256]{2,1,0:T(8,128)(2,1)S(1)} %collective-permute-done.14.refs_4_), channel_id=1, source_target_pairs={{0,16},{8,24},{16,0},{24,8},{1,17},{9,25},{17,1},{25,9},{2,18},{10... | collective-permute-start | bytes 589832 | tf_op jit(solution)/shard_map/ppermute | solution.py:27
  79.3 4.6 %collective-permute-done.15.refs_5_ = bf16[4,96,256]{2,1,0:T(8,128)(2,1)} collective-permute-done((bf16[4,96,256]{2,1,0:T(8,128)(2,1)S(1)}, bf16[4,96,256]{2,1,0:T(8,128)(2,1)}, u32[]{:S(2)}, u32[]{:S(2)}) %collective-permute-start.15) | collective-permute-done | bytes 196640 | tf_op jit(solution)/shard_map/ppermute | solution.py:27
  83.8 0.7 constant_dynamic-slice_fusion.refs_19_
  84.5 3.2 %all-to-all-done.3.sums_ref = bf16[4,352,256]{2,1,0:T(8,128)(2,1)S(1)} async-done(((bf16[4,352,256]{2,1,0:T(8,128)(2,1)}), bf16[4,352,256]{2,1,0:T(8,128)(2,1)S(1)}, u32[]{:S(2)}, u32[]{:S(2)}) %all-to-all-start.3) | async-done | bytes 720928 | tf_op jit(solution)/shard_map/all_to_all | solution.py:56
  87.8 3.7 %recur.1 = (bf16[4,5,32,256]{3,2,1,0:T(8,128)(2,1)}, bf16[1,2,32,256]{3,2,1,0:T(8,128)(2,1)}) custom-call(s32[4]{0:T(128)S(1)} %pad_add_fusion.order, s32[1]{0:T(128)} %bitcast.5.spot, bf16[4,352,256]{2,1,0:T(8,128)(2,1)S(1)} %all-to-all-done.3.sums_ref, f32[32,1]{1,0:T(8,128)} %copy-done.5, bf16[4,96,256]{2,1,0:T(8,128)(2,1)S(1)} %all-to-all-done.2.refs_0_, ...), custom_call_target="tpu_custom_call" | custom-call | tf_op jit(solution)/shard_map/recur/pallas_call | solution.py:460
  91.5 3.5 %all-to-all-start.4 = ((bf16[4,5,32,256]{3,2,1,0:T(8,128)(2,1)}), bf16[4,5,32,256]{3,2,1,0:T(8,128)(2,1)S(1)}, u32[]{:S(2)}, u32[]{:S(2)}) async-start(bf16[4,5,32,256]{3,2,1,0:T(8,128)(2,1)} %get-tuple-element.61), calls=%async_computation.4 | async-start | bytes 655360 | tf_op jit(solution)/shard_map/all_to_all | solution.py:56
  95.0 2.4 %collective-permute-start.18 = (bf16[2,32,256]{2,1,0:T(8,128)(2,1)}, bf16[2,32,256]{2,1,0:T(8,128)(2,1)S(1)}, u32[]{:S(2)}, u32[]{:S(2)}) collective-permute-start(bf16[2,32,256]{2,1,0:T(8,128)(2,1)} %bitcast.15), channel_id=1, source_target_pairs={{0,16},{8,24},{16,0},{24,8},{1,17},{9,25},{17,1},{25,9},{2,18},{10... | collective-permute-start | bytes 98312 | tf_op jit(solution)/shard_map/ppermute | solution.py:27
  97.4 2.1 %collective-permute-done.18 = bf16[2,32,256]{2,1,0:T(8,128)(2,1)S(1)} collective-permute-done((bf16[2,32,256]{2,1,0:T(8,128)(2,1)}, bf16[2,32,256]{2,1,0:T(8,128)(2,1)S(1)}, u32[]{:S(2)}, u32[]{:S(2)}) %collective-permute-start.18) | collective-permute-done | bytes 32800 | tf_op jit(solution)/shard_map/ppermute | solution.py:27
  99.5 5.6 %all-to-all-done.4.refs_8_ = bf16[4,5,32,256]{3,2,1,0:T(8,128)(2,1)S(1)} async-done(((bf16[4,5,32,256]{3,2,1,0:T(8,128)(2,1)}), bf16[4,5,32,256]{3,2,1,0:T(8,128)(2,1)S(1)}, u32[]{:S(2)}, u32[]{:S(2)}) %all-to-all-start.4) | async-done | bytes 327712 | tf_op jit(solution)/shard_map/all_to_all | solution.py:56
  105.1 0.7 broadcast_in_dim.4
  105.8 1.2 collective-permute-start.22
  107.0 3.6 %all-to-all-start.5 = ((bf16[8,2,32,256]{3,2,1,0:T(8,128)(2,1)}), bf16[8,2,32,256]{3,2,1,0:T(8,128)(2,1)S(1)}, u32[]{:S(2)}, u32[]{:S(2)}) async-start(bf16[8,2,32,256]{3,2,1,0:T(8,128)(2,1)} %broadcast_in_dim.4), calls=%async_computation.5 | async-start | bytes 524288 | tf_op jit(solution)/shard_map/all_to_all | solution.py:484
  110.6 0.7 slice.6
  111.3 1.5 %collective-permute-start.19 = (bf16[4,3,32,256]{3,2,1,0:T(8,128)(2,1)}, bf16[4,3,32,256]{3,2,1,0:T(8,128)(2,1)}, u32[]{:S(2)}, u32[]{:S(2)}) collective-permute-start(bf16[4,3,32,256]{3,2,1,0:T(8,128)(2,1)} %slice.6), channel_id=1, source_target_pairs={{0,16},{8,24},{16,0},{24,8},{1,17},{9,25},{17,1},{25,9},{2,18},{10... | collective-permute-start | bytes 589832 | tf_op jit(solution)/shard_map/ppermute | solution.py:27
  112.8 1.5 %collective-permute-done.22.refs_12_ = bf16[4,5,32,256]{3,2,1,0:T(8,128)(2,1)S(1)} collective-permute-done((bf16[4,5,32,256]{3,2,1,0:T(8,128)(2,1)S(1)}, bf16[4,5,32,256]{3,2,1,0:T(8,128)(2,1)S(1)}, u32[]{:S(2)}, u32[]{:S(2)}) %collective-permute-start.22) | collective-permute-done | bytes 327712 | tf_op jit(solution)/shard_map/ppermute | solution.py:50
  114.3 0.7 slice.8
  115.0 2.0 %collective-permute-start.23 = (bf16[4,3,32,256]{3,2,1,0:T(8,128)(2,1)}, bf16[4,3,32,256]{3,2,1,0:T(8,128)(2,1)}, u32[]{:S(2)}, u32[]{:S(2)}) collective-permute-start(bf16[4,3,32,256]{3,2,1,0:T(8,128)(2,1)} %slice.8), channel_id=1, source_target_pairs={{0,16},{8,24},{16,0},{24,8},{1,17},{9,25},{17,1},{25,9},{2,18},{10... | collective-permute-start | bytes 589832 | tf_op jit(solution)/shard_map/ppermute | solution.py:27
  117.6 1.0 all-to-all-done.5.refs_16_
  119.1 1.9 %collective-permute-done.23.refs_13_ = bf16[4,3,32,256]{3,2,1,0:T(8,128)(2,1)} collective-permute-done((bf16[4,3,32,256]{3,2,1,0:T(8,128)(2,1)}, bf16[4,3,32,256]{3,2,1,0:T(8,128)(2,1)}, u32[]{:S(2)}, u32[]{:S(2)}) %collective-permute-start.23) | collective-permute-done | bytes 196640 | tf_op jit(solution)/shard_map/ppermute | solution.py:27
  121.1 1.6 %collective-permute-done.25.refs_15_ = bf16[4,3,32,256]{3,2,1,0:T(8,128)(2,1)S(1)} collective-permute-done((bf16[4,3,32,256]{3,2,1,0:T(8,128)(2,1)}, bf16[4,3,32,256]{3,2,1,0:T(8,128)(2,1)S(1)}, u32[]{:S(2)}, u32[]{:S(2)}) %collective-permute-start.25) | collective-permute-done | bytes 196640 | tf_op jit(solution)/shard_map/ppermute | solution.py:22
  122.7 10.4 %squares.1 = f32[1024,256]{1,0:T(8,128)} custom-call(s32[4]{0:T(128)S(1)} %pad_add_fusion.order, s32[2]{0:T(128)S(1)} %pad_add_fusion.1.place, bf16[8,32,1024]{2,1,0:T(8,128)(2,1)} %get-tuple-element.52.refs_0_, bf16[8,32,1024]{2,1,0:T(8,128)(2,1)} %collective-permute-done.8.refs_1_, bf16[8,32,1024]{2,1,0:T(8,128)(2,1)S(1)} %collective-permute-done.9.refs_2_, ...), custom_call_target="tpu_custom_call" | custom-call | tf_op jit(solution)/shard_map/squares/pallas_call | solution.py:493
  (53 shorter events, 3.4 us)
Async XLA Ops:
  2.2 7.5 %copy-start.1 = (bf16[1,1024,256]{2,1,0:T(8,128)(2,1)S(1)}, bf16[1,1024,256]{2,1,0:T(8,128)(2,1)}, u32[]{:S(2)}) copy-start(bf16[1,1024,256]{2,1,0:T(8,128)(2,1)} %param.11) | copy-start | bytes 1572868
  2.2 9.1 %copy-start = (bf16[8,64,1024]{2,1,0:T(8,128)(2,1)S(1)}, bf16[8,64,1024]{2,1,0:T(8,128)(2,1)}, u32[]{:S(2)}) copy-start(bf16[8,64,1024]{2,1,0:T(8,128)(2,1)} %prepare.1.rows_ref) | copy-start | bytes 3145732
  2.2 9.1 %copy-start.4 = (f32[1,8192]{1,0:T(1,128)S(1)}, f32[1,8192]{1,0:T(1,128)}, u32[]{:S(2)}) copy-start(f32[1,8192]{1,0:T(1,128)} %gain_ref.1) | copy-start | bytes 98308
  2.2 20.9 %copy-start.8 = (s32[12]{0:T(128)S(1)}, s32[12]{0:T(128)}, u32[]{:S(2)}) copy-start(s32[12]{0:T(128)} %constant.49.clone) | copy-start | bytes 148
  2.2 21.0 %copy-start.7 = (s32[12]{0:T(128)S(1)}, s32[12]{0:T(128)}, u32[]{:S(2)}) copy-start(s32[12]{0:T(128)} %constant.50.clone) | copy-start | bytes 148
  2.2 22.8 %copy-start.6 = (s32[1,4]{1,0:T(1,128)S(1)}, s32[1,4]{1,0:T(1,128)}, u32[]{:S(2)}) copy-start(s32[1,4]{1,0:T(1,128)} %lengths.1) | copy-start | bytes 52
  2.2 33.2 %all-to-all-start.1 = ((bf16[8,64,1024]{2,1,0:T(8,128)(2,1)}), bf16[8,64,1024]{2,1,0:T(8,128)(2,1)S(1)}, u32[]{:S(2)}, u32[]{:S(2)}) async-start(bf16[8,64,1024]{2,1,0:T(8,128)(2,1)} %prepare.1.rows_ref), calls=%async_computation.1 | async-start | bytes 2097152 | tf_op jit(solution)/shard_map/all_to_all | solution.py:384
  9.6 13.4 %collective-permute-start = (bf16[1024,256]{1,0:T(8,128)(2,1)S(1)}, bf16[1024,256]{1,0:T(8,128)(2,1)S(1)}, u32[]{:S(2)}, u32[]{:S(2)}) collective-permute-start(bf16[1024,256]{1,0:T(8,128)(2,1)S(1)} %bitcast.9), channel_id=1, source_target_pairs={{0,16},{8,24},{16,0},{24,8},{1,17},{9,25},{17,1},{25,9},{2,18},{10... | collective-permute-start | bytes 1572872 | tf_op jit(solution)/shard_map/ppermute | solution.py:27
  11.2 12.1 %collective-permute-start.1 = (bf16[1024,256]{1,0:T(8,128)(2,1)S(1)}, bf16[1024,256]{1,0:T(8,128)(2,1)}, u32[]{:S(2)}, u32[]{:S(2)}) collective-permute-start(bf16[1024,256]{1,0:T(8,128)(2,1)S(1)} %bitcast.10), channel_id=1, source_target_pairs={{0,8},{8,0},{16,24},{24,16},{1,9},{9,1},{17,25},{25,17},{2,10},{10... | collective-permute-start | bytes 1572872 | tf_op jit(solution)/shard_map/ppermute | solution.py:22
  11.3 1.0 copy-start.3
  14.0 0.6 copy-start.5
  14.6 8.7 %collective-permute-start.3 = (bf16[1024,256]{1,0:T(8,128)(2,1)}, bf16[1024,256]{1,0:T(8,128)(2,1)S(1)}, u32[]{:S(2)}, u32[]{:S(2)}) collective-permute-start(bf16[1024,256]{1,0:T(8,128)(2,1)} %get-tuple-element.41.refs_4_.refs_0_), channel_id=1, source_target_pairs={{0,8},{8,0},{16,24},{24,16},{1,9},{9,1},{17,25},{25,17},{2,10},{10... | collective-permute-start | bytes 1572872 | tf_op jit(solution)/shard_map/ppermute | solution.py:22
  23.1 1.9 %collective-permute-start.2 = (bf16[1024,256]{1,0:T(8,128)(2,1)S(1)}, bf16[1024,256]{1,0:T(8,128)(2,1)S(1)}, u32[]{:S(2)}, u32[]{:S(2)}) collective-permute-start(bf16[1024,256]{1,0:T(8,128)(2,1)S(1)} %collective-permute-done.refs_1_.refs_5_), channel_id=1, source_target_pairs={{0,8},{8,0},{16,24},{24,16},{1,9},{9,1},{17,25},{25,17},{2,10},{10... | collective-permute-start | bytes 1572872 | tf_op jit(solution)/shard_map/ppermute | solution.py:22
  27.1 0.8 copy-start.2
  27.8 14.6 %collective-permute-start.5 = (bf16[1024,256]{1,0:T(8,128)(2,1)}, bf16[1024,256]{1,0:T(8,128)(2,1)}, u32[]{:S(2)}, u32[]{:S(2)}) collective-permute-start(bf16[1024,256]{1,0:T(8,128)(2,1)} %get-tuple-element.41.refs_4_.refs_0_), channel_id=1, source_target_pairs={{0,16},{8,24},{16,0},{24,8},{1,17},{9,25},{17,1},{25,9},{2,18},{10... | collective-permute-start | bytes 1572872 | tf_op jit(solution)/shard_map/ppermute | solution.py:27
  35.4 17.0 %all-to-all-start = ((bf16[8,112,256]{2,1,0:T(8,128)(2,1)}), bf16[8,112,256]{2,1,0:T(8,128)(2,1)}, u32[]{:S(2)}, u32[]{:S(2)}) async-start(bf16[8,112,256]{2,1,0:T(8,128)(2,1)} %copy-done.2), calls=%async_computation | async-start | bytes 917504 | tf_op jit(solution)/shard_map/all_to_all | solution.py:404
  42.4 3.5 %collective-permute-start.6 = (bf16[1024,256]{1,0:T(8,128)(2,1)}, bf16[1024,256]{1,0:T(8,128)(2,1)S(1)}, u32[]{:S(2)}, u32[]{:S(2)}) collective-permute-start(bf16[1024,256]{1,0:T(8,128)(2,1)} %collective-permute-done.5.refs_1_), channel_id=1, source_target_pairs={{0,8},{8,0},{16,24},{24,16},{1,9},{9,1},{17,25},{25,17},{2,10},{10... | collective-permute-start | bytes 1572872 | tf_op jit(solution)/shard_map/ppermute | solution.py:22
  42.4 11.7 %collective-permute-start.4 = (bf16[4,128,256]{2,1,0:T(8,128)(2,1)}, bf16[4,128,256]{2,1,0:T(8,128)(2,1)S(1)}, u32[]{:S(2)}, u32[]{:S(2)}) collective-permute-start(bf16[4,128,256]{2,1,0:T(8,128)(2,1)} %get-tuple-element.39), channel_id=1, source_target_pairs={{0,1},{1,0},{2,3},{3,2},{4,5},{5,4},{6,7},{7,6},{8,9},{9,8},{10,11... | collective-permute-start | bytes 786440 | tf_op jit(solution)/shard_map/ppermute | solution.py:50
  44.4 14.3 %collective-permute-start.8 = (bf16[8,32,1024]{2,1,0:T(8,128)(2,1)}, bf16[8,32,1024]{2,1,0:T(8,128)(2,1)}, u32[]{:S(2)}, u32[]{:S(2)}) collective-permute-start(bf16[8,32,1024]{2,1,0:T(8,128)(2,1)} %get-tuple-element.52.refs_0_), channel_id=1, source_target_pairs={{0,16},{8,24},{16,0},{24,8},{1,17},{9,25},{17,1},{25,9},{2,18},{10... | collective-permute-start | bytes 1572872 | tf_op jit(solution)/shard_map/ppermute | solution.py:27
  50.5 12.6 %collective-permute-start.7 = (bf16[4,224,256]{2,1,0:T(8,128)(2,1)}, bf16[4,224,256]{2,1,0:T(8,128)(2,1)S(1)}, u32[]{:S(2)}, u32[]{:S(2)}) collective-permute-start(bf16[4,224,256]{2,1,0:T(8,128)(2,1)} %get-tuple-element.45), channel_id=1, source_target_pairs={{0,1},{1,0},{2,3},{3,2},{4,5},{5,4},{6,7},{7,6},{8,9},{9,8},{10,11... | collective-permute-start | bytes 1376264 | tf_op jit(solution)/shard_map/ppermute | solution.py:50
  54.1 11.3 %all-to-all-start.2 = ((bf16[4,96,256]{2,1,0:T(8,128)(2,1)}), bf16[4,96,256]{2,1,0:T(8,128)(2,1)S(1)}, u32[]{:S(2)}, u32[]{:S(2)}) async-start(bf16[4,96,256]{2,1,0:T(8,128)(2,1)} %get-tuple-element.40), calls=%async_computation.2 | async-start | bytes 393216 | tf_op jit(solution)/shard_map/all_to_all | solution.py:56
  65.5 22.3 %all-to-all-start.3 = ((bf16[4,352,256]{2,1,0:T(8,128)(2,1)}), bf16[4,352,256]{2,1,0:T(8,128)(2,1)S(1)}, u32[]{:S(2)}, u32[]{:S(2)}) async-start(bf16[4,352,256]{2,1,0:T(8,128)(2,1)} %combine.1), calls=%async_computation.3 | async-start | bytes 1441792 | tf_op jit(solution)/shard_map/all_to_all | solution.py:56
  69.9 8.8 %collective-permute-start.9 = (bf16[8,32,1024]{2,1,0:T(8,128)(2,1)}, bf16[8,32,1024]{2,1,0:T(8,128)(2,1)S(1)}, u32[]{:S(2)}, u32[]{:S(2)}) collective-permute-start(bf16[8,32,1024]{2,1,0:T(8,128)(2,1)} %get-tuple-element.52.refs_0_), channel_id=1, source_target_pairs={{0,8},{8,0},{16,24},{24,16},{1,9},{9,1},{17,25},{25,17},{2,10},{10... | collective-permute-start | bytes 1572872 | tf_op jit(solution)/shard_map/ppermute | solution.py:22
  69.9 7.3 %collective-permute-start.14 = (bf16[4,96,256]{2,1,0:T(8,128)(2,1)S(1)}, bf16[4,96,256]{2,1,0:T(8,128)(2,1)S(1)}, u32[]{:S(2)}, u32[]{:S(2)}) collective-permute-start(bf16[4,96,256]{2,1,0:T(8,128)(2,1)S(1)} %all-to-all-done.2.refs_0_), channel_id=1, source_target_pairs={{0,1},{1,0},{2,3},{3,2},{4,5},{5,4},{6,7},{7,6},{8,9},{9,8},{10,11... | collective-permute-start | bytes 589832 | tf_op jit(solution)/shard_map/ppermute | solution.py:50
  70.9 13.6 %collective-permute-start.10 = (bf16[8,32,1024]{2,1,0:T(8,128)(2,1)}, bf16[8,32,1024]{2,1,0:T(8,128)(2,1)}, u32[]{:S(2)}, u32[]{:S(2)}) collective-permute-start(bf16[8,32,1024]{2,1,0:T(8,128)(2,1)} %collective-permute-done.8.refs_1_), channel_id=1, source_target_pairs={{0,8},{8,0},{16,24},{24,16},{1,9},{9,1},{17,25},{25,17},{2,10},{10... | collective-permute-start | bytes 1572872 | tf_op jit(solution)/shard_map/ppermute | solution.py:22
  71.1 8.1 %collective-permute-start.11 = (bf16[4,96,256]{2,1,0:T(8,128)(2,1)S(1)}, bf16[4,96,256]{2,1,0:T(8,128)(2,1)S(1)}, u32[]{:S(2)}, u32[]{:S(2)}) collective-permute-start(bf16[4,96,256]{2,1,0:T(8,128)(2,1)S(1)} %all-to-all-done.2.refs_0_), channel_id=1, source_target_pairs={{0,16},{8,24},{16,0},{24,8},{1,17},{9,25},{17,1},{25,9},{2,18},{10... | collective-permute-start | bytes 589832 | tf_op jit(solution)/shard_map/ppermute | solution.py:27
  77.2 6.6 %collective-permute-start.15 = (bf16[4,96,256]{2,1,0:T(8,128)(2,1)S(1)}, bf16[4,96,256]{2,1,0:T(8,128)(2,1)}, u32[]{:S(2)}, u32[]{:S(2)}) collective-permute-start(bf16[4,96,256]{2,1,0:T(8,128)(2,1)S(1)} %collective-permute-done.14.refs_4_), channel_id=1, source_target_pairs={{0,16},{8,24},{16,0},{24,8},{1,17},{9,25},{17,1},{25,9},{2,18},{10... | collective-permute-start | bytes 589832 | tf_op jit(solution)/shard_map/ppermute | solution.py:27
  78.7 9.1 %collective-permute-start.12 = (bf16[4,96,256]{2,1,0:T(8,128)(2,1)S(1)}, bf16[4,96,256]{2,1,0:T(8,128)(2,1)}, u32[]{:S(2)}, u32[]{:S(2)}) collective-permute-start(bf16[4,96,256]{2,1,0:T(8,128)(2,1)S(1)} %all-to-all-done.2.refs_0_), channel_id=1, source_target_pairs={{0,8},{8,0},{16,24},{24,16},{1,9},{9,1},{17,25},{25,17},{2,10},{10... | collective-permute-start | bytes 589832 | tf_op jit(solution)/shard_map/ppermute | solution.py:22
  78.7 9.1 %collective-permute-start.16 = (bf16[4,96,256]{2,1,0:T(8,128)(2,1)S(1)}, bf16[4,96,256]{2,1,0:T(8,128)(2,1)}, u32[]{:S(2)}, u32[]{:S(2)}) collective-permute-start(bf16[4,96,256]{2,1,0:T(8,128)(2,1)S(1)} %collective-permute-done.14.refs_4_), channel_id=1, source_target_pairs={{0,8},{8,0},{16,24},{24,16},{1,9},{9,1},{17,25},{25,17},{2,10},{10... | collective-permute-start | bytes 589832 | tf_op jit(solution)/shard_map/ppermute | solution.py:22
  79.2 8.6 %collective-permute-start.13 = (bf16[4,96,256]{2,1,0:T(8,128)(2,1)S(1)}, bf16[4,96,256]{2,1,0:T(8,128)(2,1)}, u32[]{:S(2)}, u32[]{:S(2)}) collective-permute-start(bf16[4,96,256]{2,1,0:T(8,128)(2,1)S(1)} %collective-permute-done.11.refs_1_), channel_id=1, source_target_pairs={{0,8},{8,0},{16,24},{24,16},{1,9},{9,1},{17,25},{25,17},{2,10},{10... | collective-permute-start | bytes 589832 | tf_op jit(solution)/shard_map/ppermute | solution.py:22
  83.8 3.9 %collective-permute-start.17 = (bf16[4,96,256]{2,1,0:T(8,128)(2,1)}, bf16[4,96,256]{2,1,0:T(8,128)(2,1)}, u32[]{:S(2)}, u32[]{:S(2)}) collective-permute-start(bf16[4,96,256]{2,1,0:T(8,128)(2,1)} %collective-permute-done.15.refs_5_), channel_id=1, source_target_pairs={{0,8},{8,0},{16,24},{24,16},{1,9},{9,1},{17,25},{25,17},{2,10},{10... | collective-permute-start | bytes 589832 | tf_op jit(solution)/shard_map/ppermute | solution.py:22
  91.5 13.5 %all-to-all-start.4 = ((bf16[4,5,32,256]{3,2,1,0:T(8,128)(2,1)}), bf16[4,5,32,256]{3,2,1,0:T(8,128)(2,1)S(1)}, u32[]{:S(2)}, u32[]{:S(2)}) async-start(bf16[4,5,32,256]{3,2,1,0:T(8,128)(2,1)} %get-tuple-element.61), calls=%async_computation.4 | async-start | bytes 655360 | tf_op jit(solution)/shard_map/all_to_all | solution.py:56
  95.0 4.5 %collective-permute-start.18 = (bf16[2,32,256]{2,1,0:T(8,128)(2,1)}, bf16[2,32,256]{2,1,0:T(8,128)(2,1)S(1)}, u32[]{:S(2)}, u32[]{:S(2)}) collective-permute-start(bf16[2,32,256]{2,1,0:T(8,128)(2,1)} %bitcast.15), channel_id=1, source_target_pairs={{0,16},{8,24},{16,0},{24,8},{1,17},{9,25},{17,1},{25,9},{2,18},{10... | collective-permute-start | bytes 98312 | tf_op jit(solution)/shard_map/ppermute | solution.py:27
  105.8 8.5 %collective-permute-start.22 = (bf16[4,5,32,256]{3,2,1,0:T(8,128)(2,1)S(1)}, bf16[4,5,32,256]{3,2,1,0:T(8,128)(2,1)S(1)}, u32[]{:S(2)}, u32[]{:S(2)}) collective-permute-start(bf16[4,5,32,256]{3,2,1,0:T(8,128)(2,1)S(1)} %all-to-all-done.4.refs_8_), channel_id=1, source_target_pairs={{0,1},{1,0},{2,3},{3,2},{4,5},{5,4},{6,7},{7,6},{8,9},{9,8},{10,11... | collective-permute-start | bytes 983048 | tf_op jit(solution)/shard_map/ppermute | solution.py:50
  107.0 11.6 %all-to-all-start.5 = ((bf16[8,2,32,256]{3,2,1,0:T(8,128)(2,1)}), bf16[8,2,32,256]{3,2,1,0:T(8,128)(2,1)S(1)}, u32[]{:S(2)}, u32[]{:S(2)}) async-start(bf16[8,2,32,256]{3,2,1,0:T(8,128)(2,1)} %broadcast_in_dim.4), calls=%async_computation.5 | async-start | bytes 524288 | tf_op jit(solution)/shard_map/all_to_all | solution.py:484
  111.3 7.3 %collective-permute-start.19 = (bf16[4,3,32,256]{3,2,1,0:T(8,128)(2,1)}, bf16[4,3,32,256]{3,2,1,0:T(8,128)(2,1)}, u32[]{:S(2)}, u32[]{:S(2)}) collective-permute-start(bf16[4,3,32,256]{3,2,1,0:T(8,128)(2,1)} %slice.6), channel_id=1, source_target_pairs={{0,16},{8,24},{16,0},{24,8},{1,17},{9,25},{17,1},{25,9},{2,18},{10... | collective-permute-start | bytes 589832 | tf_op jit(solution)/shard_map/ppermute | solution.py:27
  115.0 6.0 %collective-permute-start.23 = (bf16[4,3,32,256]{3,2,1,0:T(8,128)(2,1)}, bf16[4,3,32,256]{3,2,1,0:T(8,128)(2,1)}, u32[]{:S(2)}, u32[]{:S(2)}) collective-permute-start(bf16[4,3,32,256]{3,2,1,0:T(8,128)(2,1)} %slice.8), channel_id=1, source_target_pairs={{0,16},{8,24},{16,0},{24,8},{1,17},{9,25},{17,1},{25,9},{2,18},{10... | collective-permute-start | bytes 589832 | tf_op jit(solution)/shard_map/ppermute | solution.py:27
  117.0 4.0 %collective-permute-start.20 = (bf16[4,5,32,256]{3,2,1,0:T(8,128)(2,1)S(1)}, bf16[4,5,32,256]{3,2,1,0:T(8,128)(2,1)S(1)}, u32[]{:S(2)}, u32[]{:S(2)}) collective-permute-start(bf16[4,5,32,256]{3,2,1,0:T(8,128)(2,1)S(1)} %all-to-all-done.4.refs_8_), channel_id=1, source_target_pairs={{0,8},{8,0},{16,24},{24,16},{1,9},{9,1},{17,25},{25,17},{2,10},{10... | collective-permute-start | bytes 983048 | tf_op jit(solution)/shard_map/ppermute | solution.py:22
  117.0 4.0 %collective-permute-start.24 = (bf16[4,5,32,256]{3,2,1,0:T(8,128)(2,1)S(1)}, bf16[4,5,32,256]{3,2,1,0:T(8,128)(2,1)}, u32[]{:S(2)}, u32[]{:S(2)}) collective-permute-start(bf16[4,5,32,256]{3,2,1,0:T(8,128)(2,1)S(1)} %collective-permute-done.22.refs_12_), channel_id=1, source_target_pairs={{0,8},{8,0},{16,24},{24,16},{1,9},{9,1},{17,25},{25,17},{2,10},{10... | collective-permute-start | bytes 983048 | tf_op jit(solution)/shard_map/ppermute | solution.py:22
  118.6 4.1 %collective-permute-start.26 = (bf16[8,2,32,256]{3,2,1,0:T(8,128)(2,1)S(1)}, bf16[8,2,32,256]{3,2,1,0:T(8,128)(2,1)S(1)}, u32[]{:S(2)}, u32[]{:S(2)}) collective-permute-start(bf16[8,2,32,256]{3,2,1,0:T(8,128)(2,1)S(1)} %all-to-all-done.5.refs_16_), channel_id=1, source_target_pairs={{0,8},{8,0},{16,24},{24,16},{1,9},{9,1},{17,25},{25,17},{2,10},{10... | collective-permute-start | bytes 786440 | tf_op jit(solution)/shard_map/ppermute | solution.py:22
  118.6 2.4 %collective-permute-start.21 = (bf16[4,3,32,256]{3,2,1,0:T(8,128)(2,1)}, bf16[4,3,32,256]{3,2,1,0:T(8,128)(2,1)S(1)}, u32[]{:S(2)}, u32[]{:S(2)}) collective-permute-start(bf16[4,3,32,256]{3,2,1,0:T(8,128)(2,1)} %collective-permute-done.19.refs_9_), channel_id=1, source_target_pairs={{0,8},{8,0},{16,24},{24,16},{1,9},{9,1},{17,25},{25,17},{2,10},{10... | collective-permute-start | bytes 589832 | tf_op jit(solution)/shard_map/ppermute | solution.py:22
  121.0 1.7 %collective-permute-start.25 = (bf16[4,3,32,256]{3,2,1,0:T(8,128)(2,1)}, bf16[4,3,32,256]{3,2,1,0:T(8,128)(2,1)S(1)}, u32[]{:S(2)}, u32[]{:S(2)}) collective-permute-start(bf16[4,3,32,256]{3,2,1,0:T(8,128)(2,1)} %collective-permute-done.23.refs_13_), channel_id=1, source_target_pairs={{0,8},{8,0},{16,24},{24,16},{1,9},{9,1},{17,25},{25,17},{2,10},{10... | collective-permute-start | bytes 589832 | tf_op jit(solution)/shard_map/ppermute | solution.py:22

commit v9 on v8

--- a/solution.py
+++ b/solution.py
@@ -252,7 +252,8 @@
     for m in range(2):
         put(m, grads[2 * chip + m])
         for j in range(1, half):
-            out_ref[j - 1, m] = grads[2 * lax.rem(chip + half - j, half) + m]
+            for n in range(out_ref.shape[1]):
+                out_ref[j - 1, n, m] = grads[2 * lax.rem(chip + half - j, half) + m]
 
 
 def fisher_kernel(count, seqs, scale, order, place, *refs):
@@ -461,7 +462,7 @@
         functools.partial(recur_kernel, count, width),
         out_shape=(
             pltpu.HBM((line, count + 1, t, r), bf16),
-            pltpu.HBM((count // 2 - 1, 2, t, r), bf16),
+            pltpu.HBM((count // 2 - 1, peers, 2, t, r), bf16),
         ),
         in_specs=[smem, smem] + [vmem] * (2 + 2 * count),
         out_specs=(vmem, vmem),
@@ -477,7 +478,7 @@
 
     half = count // 2
     own = line_exchange(own_held)
-    far = [repeated(chip_shift(held[j - 1], j), peers) for j in range(1, half)]
+    far = [chip_shift(held[j - 1], j) for j in range(1, half)]
     own, *far = lax.optimization_barrier((own, *far))
     own = [own, pair_swap(own)]
     acts = [x[:, 2:] for x in own]

time: 134 us -> 133 us (level)
    ppermute x8, waiting for transfers between devices: 17.6 us -> 21.4 us  [chip_shift(): lax.ppermute(x, 'section', [(i, (i - 2 * by) % count) for i in range(coun...]
    all_to_all x3, waiting for transfers between devices: 8.89 us -> 5.14 us  [line_exchange(): return lax.all_to_all(x, 'dp', 0, 0, axis_index_groups=groups, tiled=True)]
where the time goes in v9:
time: 133 us; the launch traced here: 132 us
  waiting for transfers between devices  48.8 us (37%)
  starting transfers between devices  47.1 us (35%)
  Pallas kernels  31.6 us (24%)
  local copies, waits for them, and re-layouts  4.67 us (4%)
    ppermute x8, waiting for transfers between devices, chip_shift(): lax.ppermute(x, 'section', [(i, (i - 2 * by) % count) for i in range(coun...  21.4 us
    ppermute x8, starting transfers between devices, chip_shift(): lax.ppermute(x, 'section', [(i, (i - 2 * by) % count) for i in range(coun...  13.6 us
    all_to_all x3, starting transfers between devices, line_exchange(): return lax.all_to_all(x, 'dp', 0, 0, axis_index_groups=groups, tiled=True)  11.4 us
    pallas_call x1, Pallas kernels, per_device(): pl.pallas_call(functools.partial(fisher_kernel, count, seqs, 1.0 / (row_c...  10.4 us
    ppermute x4, waiting for transfers between devices, pair_swap(): return lax.ppermute(x, 'dp', [(i, i ^ 1) for i in range(peers)])  10.4 us
    all_to_all x1, starting transfers between devices, per_device(): rows = lax.all_to_all(send, 'dp', 0, 0, tiled=True)  7.4 us
    all_to_all x1, waiting for transfers between devices, per_device(): rows = lax.all_to_all(send, 'dp', 0, 0, tiled=True)  6.07 us
    all_to_all x3, waiting for transfers between devices, line_exchange(): return lax.all_to_all(x, 'dp', 0, 0, axis_index_groups=groups, tiled=True)  5.14 us
  transfers between devices with their start and end apart: 33, of which 16 were waited for; matrix products, arithmetic and copies ran while one was open for 2% of the time, Pallas kernels for 11%

profile of v9, /device:TPU:0, one launch (start us, length us, event | category | flops | bytes accessed | tf_op | source)
XLA Modules:
  0.0 132.5 jit_solution(2653567619214981255)
XLA Ops:
  0.0 2.2 %prepare.1.rows_ref = bf16[8,64,1024]{2,1,0:T(8,128)(2,1)} custom-call(bf16[128,8192]{1,0:T(8,128)(2,1)} %tokens_ref.1, bf16[128,8192]{1,0:T(8,128)(2,1)} %cot_ref.1), custom_call_target="tpu_custom_call" | custom-call | tf_op jit(solution)/shard_map/prepare/pallas_call | solution.py:350
  2.2 7.4 %all-to-all-start.1 = ((bf16[8,64,1024]{2,1,0:T(8,128)(2,1)}), bf16[8,64,1024]{2,1,0:T(8,128)(2,1)S(1)}, u32[]{:S(2)}, u32[]{:S(2)}) async-start(bf16[8,64,1024]{2,1,0:T(8,128)(2,1)} %prepare.1.rows_ref), calls=%async_computation.1 | async-start | bytes 2097152 | tf_op jit(solution)/shard_map/all_to_all | solution.py:385
  9.6 1.6 %collective-permute-start = (bf16[1024,256]{1,0:T(8,128)(2,1)S(1)}, bf16[1024,256]{1,0:T(8,128)(2,1)S(1)}, u32[]{:S(2)}, u32[]{:S(2)}) collective-permute-start(bf16[1024,256]{1,0:T(8,128)(2,1)S(1)} %bitcast.9), channel_id=1, source_target_pairs={{0,16},{8,24},{16,0},{24,8},{1,17},{9,25},{17,1},{25,9},{2,18},{10... | collective-permute-start | bytes 1572872 | tf_op jit(solution)/shard_map/ppermute | solution.py:27
  11.3 1.0 copy-done.3
  12.4 1.6 %weight.1 = (f32[32,1]{1,0:T(8,128)S(1)}, bf16[1024,256]{1,0:T(8,128)(2,1)}) custom-call(s32[2]{0:T(128)S(1)} %pad_add_fusion.1.place, bf16[8,64,1024]{2,1,0:T(8,128)(2,1)S(1)} %copy-done, bf16[1,1024,256]{2,1,0:T(8,128)(2,1)S(1)} %copy-done.3, f32[1,8192]{1,0:T(1,128)S(1)} %copy-done.4), custom_call_target="tpu_custom_call" | custom-call | tf_op jit(solution)/shard_map/weight/pallas_call | solution.py:362
  14.0 0.6 copy-done.5
  15.1 8.0 %collective-permute-done.refs_1_.refs_5_ = bf16[1024,256]{1,0:T(8,128)(2,1)S(1)} collective-permute-done((bf16[1024,256]{1,0:T(8,128)(2,1)S(1)}, bf16[1024,256]{1,0:T(8,128)(2,1)S(1)}, u32[]{:S(2)}, u32[]{:S(2)}) %collective-permute-start) | collective-permute-done | bytes 524320 | tf_op jit(solution)/shard_map/ppermute | solution.py:27
  23.3 1.7 %collective-permute-done.2.refs_3_.refs_7_ = bf16[1024,256]{1,0:T(8,128)(2,1)S(1)} collective-permute-done((bf16[1024,256]{1,0:T(8,128)(2,1)S(1)}, bf16[1024,256]{1,0:T(8,128)(2,1)S(1)}, u32[]{:S(2)}, u32[]{:S(2)}) %collective-permute-start.2) | collective-permute-done | bytes 524320 | tf_op jit(solution)/shard_map/ppermute | solution.py:22
  25.0 2.0 %gram.1 = bf16[8,112,256]{2,1,0:T(8,128)(2,1)S(1)} custom-call(s32[4]{0:T(128)S(1)} %pad_add_fusion.order, s32[3]{0:T(128)S(1)} %dynamic_slice.9.left, s32[3]{0:T(128)S(1)} %dynamic_slice.10.right, s32[1,4]{1,0:T(1,128)S(1)} %copy-done.6, bf16[1024,256]{1,0:T(8,128)(2,1)S(1)} %bitcast.11, bf16[1024,256]{1,0:T(8,128)(2,1)S(1)} %collective-permute-done.refs_1_.refs_5_, ...), custom_call_target="tpu_custom_call" | custom-call | tf_op jit(solution)/shard_map/gram/pallas_call | solution.py:393
  27.1 0.8 copy-done.2
  27.8 1.5 %collective-permute-start.5 = (bf16[1024,256]{1,0:T(8,128)(2,1)}, bf16[1024,256]{1,0:T(8,128)(2,1)}, u32[]{:S(2)}, u32[]{:S(2)}) collective-permute-start(bf16[1024,256]{1,0:T(8,128)(2,1)} %get-tuple-element.41.refs_4_.refs_0_), channel_id=1, source_target_pairs={{0,16},{8,24},{16,0},{24,8},{1,17},{9,25},{17,1},{25,9},{2,18},{10... | collective-permute-start | bytes 1572872 | tf_op jit(solution)/shard_map/ppermute | solution.py:27
  29.3 6.1 %all-to-all-done.1.rows_ref = bf16[8,64,1024]{2,1,0:T(8,128)(2,1)S(1)} async-done(((bf16[8,64,1024]{2,1,0:T(8,128)(2,1)}), bf16[8,64,1024]{2,1,0:T(8,128)(2,1)S(1)}, u32[]{:S(2)}, u32[]{:S(2)}) %all-to-all-start.1) | async-done | bytes 1048608 | tf_op jit(solution)/shard_map/all_to_all | solution.py:385
  35.4 4.1 %all-to-all-start = ((bf16[8,112,256]{2,1,0:T(8,128)(2,1)}), bf16[8,112,256]{2,1,0:T(8,128)(2,1)}, u32[]{:S(2)}, u32[]{:S(2)}) async-start(bf16[8,112,256]{2,1,0:T(8,128)(2,1)} %copy-done.2), calls=%async_computation | async-start | bytes 917504 | tf_op jit(solution)/shard_map/all_to_all | solution.py:405
  39.5 2.9 %project_cot.1 = (f32[4,128,256]{2,1,0:T(8,128)}, bf16[4,128,256]{2,1,0:T(8,128)(2,1)}, bf16[8,32,1024]{2,1,0:T(8,128)(2,1)}) custom-call(s32[4]{0:T(128)S(1)} %pad_add_fusion.order, s32[1]{0:T(128)} %bitcast.5.spot, bf16[8,64,1024]{2,1,0:T(8,128)(2,1)S(1)} %all-to-all-done.1.rows_ref, bf16[1024,256]{1,0:T(8,128)(2,1)S(1)} %bitcast.12, ...), custom_call_target="tpu_custom_call" | custom-call | tf_op jit(solution)/shard_map/project_cot/pallas_call | solution.py:415
  42.4 2.0 %collective-permute-start.4 = (bf16[4,128,256]{2,1,0:T(8,128)(2,1)}, bf16[4,128,256]{2,1,0:T(8,128)(2,1)S(1)}, u32[]{:S(2)}, u32[]{:S(2)}) collective-permute-start(bf16[4,128,256]{2,1,0:T(8,128)(2,1)} %get-tuple-element.39), channel_id=1, source_target_pairs={{0,1},{1,0},{2,3},{3,2},{4,5},{5,4},{6,7},{7,6},{8,9},{9,8},{10,11... | collective-permute-start | bytes 786440 | tf_op jit(solution)/shard_map/ppermute | solution.py:50
  44.4 1.5 %collective-permute-start.8 = (bf16[8,32,1024]{2,1,0:T(8,128)(2,1)}, bf16[8,32,1024]{2,1,0:T(8,128)(2,1)}, u32[]{:S(2)}, u32[]{:S(2)}) collective-permute-start(bf16[8,32,1024]{2,1,0:T(8,128)(2,1)} %get-tuple-element.52.refs_0_), channel_id=1, source_target_pairs={{0,16},{8,24},{16,0},{24,8},{1,17},{9,25},{17,1},{25,9},{2,18},{10... | collective-permute-start | bytes 1572872 | tf_op jit(solution)/shard_map/ppermute | solution.py:27
  45.9 4.6 %project.1 = (f32[4,224,256]{2,1,0:T(8,128)}, bf16[4,224,256]{2,1,0:T(8,128)(2,1)}) custom-call(s32[4]{0:T(128)S(1)} %pad_add_fusion.order, s32[1]{0:T(128)} %bitcast.5.spot, bf16[8,64,1024]{2,1,0:T(8,128)(2,1)S(1)} %all-to-all-done.1.rows_ref, bf16[1024,256]{1,0:T(8,128)(2,1)} %get-tuple-element.41.refs_4_.refs_0_, ...), custom_call_target="tpu_custom_call" | custom-call | tf_op jit(solution)/shard_map/project/pallas_call | solution.py:427
  50.5 0.5 collective-permute-start.7
  51.0 1.4 %all-to-all-done.packed_ref = bf16[8,112,256]{2,1,0:T(8,128)(2,1)} async-done(((bf16[8,112,256]{2,1,0:T(8,128)(2,1)}), bf16[8,112,256]{2,1,0:T(8,128)(2,1)}, u32[]{:S(2)}, u32[]{:S(2)}) %all-to-all-start) | async-done | bytes 458784 | tf_op jit(solution)/shard_map/all_to_all | solution.py:405
  52.4 1.7 %collect.1 = (bf16[4,96,256]{2,1,0:T(8,128)(2,1)}, f32[8,256]{1,0:T(8,128)S(1)}) custom-call(bf16[8,112,256]{2,1,0:T(8,128)(2,1)} %all-to-all-done.packed_ref), custom_call_target="tpu_custom_call" | custom-call | tf_op jit(solution)/shard_map/collect/pallas_call | solution.py:436
  54.1 3.6 %all-to-all-start.2 = ((bf16[4,96,256]{2,1,0:T(8,128)(2,1)}), bf16[4,96,256]{2,1,0:T(8,128)(2,1)S(1)}, u32[]{:S(2)}, u32[]{:S(2)}) async-start(bf16[4,96,256]{2,1,0:T(8,128)(2,1)} %get-tuple-element.40), calls=%async_computation.2 | async-start | bytes 393216 | tf_op jit(solution)/shard_map/all_to_all | solution.py:56
  57.7 1.0 collective-permute-done.8.refs_1_
  58.7 4.4 %collective-permute-done.7.got_ref = bf16[4,224,256]{2,1,0:T(8,128)(2,1)S(1)} collective-permute-done((bf16[4,224,256]{2,1,0:T(8,128)(2,1)}, bf16[4,224,256]{2,1,0:T(8,128)(2,1)S(1)}, u32[]{:S(2)}, u32[]{:S(2)}) %collective-permute-start.7) | collective-permute-done | bytes 458784 | tf_op jit(solution)/shard_map/ppermute | solution.py:50
  63.1 2.3 %combine.1 = bf16[4,352,256]{2,1,0:T(8,128)(2,1)} custom-call(f32[4,224,256]{2,1,0:T(8,128)} %get-tuple-element.44.keep_ref, bf16[4,224,256]{2,1,0:T(8,128)(2,1)S(1)} %collective-permute-done.7.got_ref, f32[4,128,256]{2,1,0:T(8,128)} %get-tuple-element.48.back_keep_ref, bf16[4,128,256]{2,1,0:T(8,128)(2,1)S(1)} %collective-permute-done.4.back_got_ref), custom_call_target="tpu_custom_call" | custom-call | tf_op jit(solution)/shard_map/combine/pallas_call | solution.py:446
  65.5 4.4 %all-to-all-start.3 = ((bf16[4,352,256]{2,1,0:T(8,128)(2,1)}), bf16[4,352,256]{2,1,0:T(8,128)(2,1)S(1)}, u32[]{:S(2)}, u32[]{:S(2)}) async-start(bf16[4,352,256]{2,1,0:T(8,128)(2,1)} %combine.1), calls=%async_computation.3 | async-start | bytes 1441792 | tf_op jit(solution)/shard_map/all_to_all | solution.py:56
  69.9 1.0 collective-permute-start.14
  71.1 1.5 %collective-permute-start.11 = (bf16[4,96,256]{2,1,0:T(8,128)(2,1)S(1)}, bf16[4,96,256]{2,1,0:T(8,128)(2,1)S(1)}, u32[]{:S(2)}, u32[]{:S(2)}) collective-permute-start(bf16[4,96,256]{2,1,0:T(8,128)(2,1)S(1)} %all-to-all-done.2.refs_0_), channel_id=1, source_target_pairs={{0,16},{8,24},{16,0},{24,8},{1,17},{9,25},{17,1},{25,9},{2,18},{10... | collective-permute-start | bytes 589832 | tf_op jit(solution)/shard_map/ppermute | solution.py:27
  72.6 4.5 %collective-permute-done.14.refs_4_ = bf16[4,96,256]{2,1,0:T(8,128)(2,1)S(1)} collective-permute-done((bf16[4,96,256]{2,1,0:T(8,128)(2,1)S(1)}, bf16[4,96,256]{2,1,0:T(8,128)(2,1)S(1)}, u32[]{:S(2)}, u32[]{:S(2)}) %collective-permute-start.14) | collective-permute-done | bytes 196640 | tf_op jit(solution)/shard_map/ppermute | solution.py:50
  77.2 1.5 %collective-permute-start.15 = (bf16[4,96,256]{2,1,0:T(8,128)(2,1)S(1)}, bf16[4,96,256]{2,1,0:T(8,128)(2,1)}, u32[]{:S(2)}, u32[]{:S(2)}) collective-permute-start(bf16[4,96,256]{2,1,0:T(8,128)(2,1)S(1)} %collective-permute-done.14.refs_4_), channel_id=1, source_target_pairs={{0,16},{8,24},{16,0},{24,8},{1,17},{9,25},{17,1},{25,9},{2,18},{10... | collective-permute-start | bytes 589832 | tf_op jit(solution)/shard_map/ppermute | solution.py:27
  79.3 4.6 %collective-permute-done.15.refs_5_ = bf16[4,96,256]{2,1,0:T(8,128)(2,1)} collective-permute-done((bf16[4,96,256]{2,1,0:T(8,128)(2,1)S(1)}, bf16[4,96,256]{2,1,0:T(8,128)(2,1)}, u32[]{:S(2)}, u32[]{:S(2)}) %collective-permute-start.15) | collective-permute-done | bytes 196640 | tf_op jit(solution)/shard_map/ppermute | solution.py:27
  83.8 0.7 constant_dynamic-slice_fusion.refs_19_
  84.5 3.2 %all-to-all-done.3.sums_ref = bf16[4,352,256]{2,1,0:T(8,128)(2,1)S(1)} async-done(((bf16[4,352,256]{2,1,0:T(8,128)(2,1)}), bf16[4,352,256]{2,1,0:T(8,128)(2,1)S(1)}, u32[]{:S(2)}, u32[]{:S(2)}) %all-to-all-start.3) | async-done | bytes 720928 | tf_op jit(solution)/shard_map/all_to_all | solution.py:56
  87.8 3.8 %recur.1 = (bf16[4,5,32,256]{3,2,1,0:T(8,128)(2,1)}, bf16[1,8,2,32,256]{4,3,2,1,0:T(8,128)(2,1)}) custom-call(s32[4]{0:T(128)S(1)} %pad_add_fusion.order, s32[1]{0:T(128)} %bitcast.5.spot, bf16[4,352,256]{2,1,0:T(8,128)(2,1)S(1)} %all-to-all-done.3.sums_ref, f32[32,1]{1,0:T(8,128)} %copy-done.5, bf16[4,96,256]{2,1,0:T(8,128)(2,1)S(1)} %all-to-all-done.2.refs_0_, ...), custom_call_target="tpu_custom_call" | custom-call | tf_op jit(solution)/shard_map/recur/pallas_call | solution.py:461
  91.6 3.5 %all-to-all-start.4 = ((bf16[4,5,32,256]{3,2,1,0:T(8,128)(2,1)}), bf16[4,5,32,256]{3,2,1,0:T(8,128)(2,1)S(1)}, u32[]{:S(2)}, u32[]{:S(2)}) async-start(bf16[4,5,32,256]{3,2,1,0:T(8,128)(2,1)} %get-tuple-element.61), calls=%async_computation.4 | async-start | bytes 655360 | tf_op jit(solution)/shard_map/all_to_all | solution.py:56
  95.1 2.4 %collective-permute-start.18 = (bf16[8,2,32,256]{3,2,1,0:T(8,128)(2,1)}, bf16[8,2,32,256]{3,2,1,0:T(8,128)(2,1)}, u32[]{:S(2)}, u32[]{:S(2)}) collective-permute-start(bf16[8,2,32,256]{3,2,1,0:T(8,128)(2,1)} %bitcast.15), channel_id=1, source_target_pairs={{0,16},{8,24},{16,0},{24,8},{1,17},{9,25},{17,1},{25,9},{2,18},{10... | collective-permute-start | bytes 786440 | tf_op jit(solution)/shard_map/ppermute | solution.py:27
  97.5 5.9 %collective-permute-done.18 = bf16[8,2,32,256]{3,2,1,0:T(8,128)(2,1)} collective-permute-done((bf16[8,2,32,256]{3,2,1,0:T(8,128)(2,1)}, bf16[8,2,32,256]{3,2,1,0:T(8,128)(2,1)}, u32[]{:S(2)}, u32[]{:S(2)}) %collective-permute-start.18) | collective-permute-done | bytes 262176 | tf_op jit(solution)/shard_map/ppermute | solution.py:27
  103.3 1.8 %all-to-all-done.4.refs_8_ = bf16[4,5,32,256]{3,2,1,0:T(8,128)(2,1)S(1)} async-done(((bf16[4,5,32,256]{3,2,1,0:T(8,128)(2,1)}), bf16[4,5,32,256]{3,2,1,0:T(8,128)(2,1)S(1)}, u32[]{:S(2)}, u32[]{:S(2)}) %all-to-all-start.4) | async-done | bytes 327712 | tf_op jit(solution)/shard_map/all_to_all | solution.py:56
  105.1 1.2 collective-permute-start.22
  106.3 3.6 %all-to-all-start.5 = ((bf16[8,2,32,256]{3,2,1,0:T(8,128)(2,1)}), bf16[8,2,32,256]{3,2,1,0:T(8,128)(2,1)S(1)}, u32[]{:S(2)}, u32[]{:S(2)}) async-start(bf16[8,2,32,256]{3,2,1,0:T(8,128)(2,1)} %collective-permute-done.18), calls=%async_computation.5 | async-start | bytes 524288 | tf_op jit(solution)/shard_map/all_to_all | solution.py:485
  109.9 0.7 slice.6
  110.6 1.5 %collective-permute-start.19 = (bf16[4,3,32,256]{3,2,1,0:T(8,128)(2,1)}, bf16[4,3,32,256]{3,2,1,0:T(8,128)(2,1)}, u32[]{:S(2)}, u32[]{:S(2)}) collective-permute-start(bf16[4,3,32,256]{3,2,1,0:T(8,128)(2,1)} %slice.6), channel_id=1, source_target_pairs={{0,16},{8,24},{16,0},{24,8},{1,17},{9,25},{17,1},{25,9},{2,18},{10... | collective-permute-start | bytes 589832 | tf_op jit(solution)/shard_map/ppermute | solution.py:27
  112.2 1.5 %collective-permute-done.22.refs_12_ = bf16[4,5,32,256]{3,2,1,0:T(8,128)(2,1)S(1)} collective-permute-done((bf16[4,5,32,256]{3,2,1,0:T(8,128)(2,1)S(1)}, bf16[4,5,32,256]{3,2,1,0:T(8,128)(2,1)S(1)}, u32[]{:S(2)}, u32[]{:S(2)}) %collective-permute-start.22) | collective-permute-done | bytes 327712 | tf_op jit(solution)/shard_map/ppermute | solution.py:50
  113.7 0.7 slice.8
  114.4 2.0 %collective-permute-start.23 = (bf16[4,3,32,256]{3,2,1,0:T(8,128)(2,1)}, bf16[4,3,32,256]{3,2,1,0:T(8,128)(2,1)}, u32[]{:S(2)}, u32[]{:S(2)}) collective-permute-start(bf16[4,3,32,256]{3,2,1,0:T(8,128)(2,1)} %slice.8), channel_id=1, source_target_pairs={{0,16},{8,24},{16,0},{24,8},{1,17},{9,25},{17,1},{25,9},{2,18},{10... | collective-permute-start | bytes 589832 | tf_op jit(solution)/shard_map/ppermute | solution.py:27
  116.9 1.0 all-to-all-done.5.refs_16_
  118.4 2.0 %collective-permute-done.23.refs_13_ = bf16[4,3,32,256]{3,2,1,0:T(8,128)(2,1)} collective-permute-done((bf16[4,3,32,256]{3,2,1,0:T(8,128)(2,1)}, bf16[4,3,32,256]{3,2,1,0:T(8,128)(2,1)}, u32[]{:S(2)}, u32[]{:S(2)}) %collective-permute-start.23) | collective-permute-done | bytes 196640 | tf_op jit(solution)/shard_map/ppermute | solution.py:27
  120.4 1.6 %collective-permute-done.25.refs_15_ = bf16[4,3,32,256]{3,2,1,0:T(8,128)(2,1)S(1)} collective-permute-done((bf16[4,3,32,256]{3,2,1,0:T(8,128)(2,1)}, bf16[4,3,32,256]{3,2,1,0:T(8,128)(2,1)S(1)}, u32[]{:S(2)}, u32[]{:S(2)}) %collective-permute-start.25) | collective-permute-done | bytes 196640 | tf_op jit(solution)/shard_map/ppermute | solution.py:22
  122.0 10.4 %squares.1 = f32[1024,256]{1,0:T(8,128)} custom-call(s32[4]{0:T(128)S(1)} %pad_add_fusion.order, s32[2]{0:T(128)S(1)} %pad_add_fusion.1.place, bf16[8,32,1024]{2,1,0:T(8,128)(2,1)} %get-tuple-element.52.refs_0_, bf16[8,32,1024]{2,1,0:T(8,128)(2,1)} %collective-permute-done.8.refs_1_, bf16[8,32,1024]{2,1,0:T(8,128)(2,1)S(1)} %collective-permute-done.9.refs_2_, ...), custom_call_target="tpu_custom_call" | custom-call | tf_op jit(solution)/shard_map/squares/pallas_call | solution.py:494
  (52 shorter events, 2.8 us)
Async XLA Ops:
  2.2 7.5 %copy-start.1 = (bf16[1,1024,256]{2,1,0:T(8,128)(2,1)S(1)}, bf16[1,1024,256]{2,1,0:T(8,128)(2,1)}, u32[]{:S(2)}) copy-start(bf16[1,1024,256]{2,1,0:T(8,128)(2,1)} %param.11) | copy-start | bytes 1572868
  2.2 9.1 %copy-start = (bf16[8,64,1024]{2,1,0:T(8,128)(2,1)S(1)}, bf16[8,64,1024]{2,1,0:T(8,128)(2,1)}, u32[]{:S(2)}) copy-start(bf16[8,64,1024]{2,1,0:T(8,128)(2,1)} %prepare.1.rows_ref) | copy-start | bytes 3145732
  2.2 9.1 %copy-start.4 = (f32[1,8192]{1,0:T(1,128)S(1)}, f32[1,8192]{1,0:T(1,128)}, u32[]{:S(2)}) copy-start(f32[1,8192]{1,0:T(1,128)} %gain_ref.1) | copy-start | bytes 98308
  2.2 20.9 %copy-start.8 = (s32[12]{0:T(128)S(1)}, s32[12]{0:T(128)}, u32[]{:S(2)}) copy-start(s32[12]{0:T(128)} %constant.49.clone) | copy-start | bytes 148
  2.2 21.0 %copy-start.7 = (s32[12]{0:T(128)S(1)}, s32[12]{0:T(128)}, u32[]{:S(2)}) copy-start(s32[12]{0:T(128)} %constant.50.clone) | copy-start | bytes 148
  2.2 22.8 %copy-start.6 = (s32[1,4]{1,0:T(1,128)S(1)}, s32[1,4]{1,0:T(1,128)}, u32[]{:S(2)}) copy-start(s32[1,4]{1,0:T(1,128)} %lengths.1) | copy-start | bytes 52
  2.2 33.2 %all-to-all-start.1 = ((bf16[8,64,1024]{2,1,0:T(8,128)(2,1)}), bf16[8,64,1024]{2,1,0:T(8,128)(2,1)S(1)}, u32[]{:S(2)}, u32[]{:S(2)}) async-start(bf16[8,64,1024]{2,1,0:T(8,128)(2,1)} %prepare.1.rows_ref), calls=%async_computation.1 | async-start | bytes 2097152 | tf_op jit(solution)/shard_map/all_to_all | solution.py:385
  9.6 13.4 %collective-permute-start = (bf16[1024,256]{1,0:T(8,128)(2,1)S(1)}, bf16[1024,256]{1,0:T(8,128)(2,1)S(1)}, u32[]{:S(2)}, u32[]{:S(2)}) collective-permute-start(bf16[1024,256]{1,0:T(8,128)(2,1)S(1)} %bitcast.9), channel_id=1, source_target_pairs={{0,16},{8,24},{16,0},{24,8},{1,17},{9,25},{17,1},{25,9},{2,18},{10... | collective-permute-start | bytes 1572872 | tf_op jit(solution)/shard_map/ppermute | solution.py:27
  11.2 12.1 %collective-permute-start.1 = (bf16[1024,256]{1,0:T(8,128)(2,1)S(1)}, bf16[1024,256]{1,0:T(8,128)(2,1)}, u32[]{:S(2)}, u32[]{:S(2)}) collective-permute-start(bf16[1024,256]{1,0:T(8,128)(2,1)S(1)} %bitcast.10), channel_id=1, source_target_pairs={{0,8},{8,0},{16,24},{24,16},{1,9},{9,1},{17,25},{25,17},{2,10},{10... | collective-permute-start | bytes 1572872 | tf_op jit(solution)/shard_map/ppermute | solution.py:22
  11.3 1.0 copy-start.3
  14.0 0.6 copy-start.5
  14.6 8.7 %collective-permute-start.3 = (bf16[1024,256]{1,0:T(8,128)(2,1)}, bf16[1024,256]{1,0:T(8,128)(2,1)S(1)}, u32[]{:S(2)}, u32[]{:S(2)}) collective-permute-start(bf16[1024,256]{1,0:T(8,128)(2,1)} %get-tuple-element.41.refs_4_.refs_0_), channel_id=1, source_target_pairs={{0,8},{8,0},{16,24},{24,16},{1,9},{9,1},{17,25},{25,17},{2,10},{10... | collective-permute-start | bytes 1572872 | tf_op jit(solution)/shard_map/ppermute | solution.py:22
  23.1 1.9 %collective-permute-start.2 = (bf16[1024,256]{1,0:T(8,128)(2,1)S(1)}, bf16[1024,256]{1,0:T(8,128)(2,1)S(1)}, u32[]{:S(2)}, u32[]{:S(2)}) collective-permute-start(bf16[1024,256]{1,0:T(8,128)(2,1)S(1)} %collective-permute-done.refs_1_.refs_5_), channel_id=1, source_target_pairs={{0,8},{8,0},{16,24},{24,16},{1,9},{9,1},{17,25},{25,17},{2,10},{10... | collective-permute-start | bytes 1572872 | tf_op jit(solution)/shard_map/ppermute | solution.py:22
  27.1 0.8 copy-start.2
  27.8 14.6 %collective-permute-start.5 = (bf16[1024,256]{1,0:T(8,128)(2,1)}, bf16[1024,256]{1,0:T(8,128)(2,1)}, u32[]{:S(2)}, u32[]{:S(2)}) collective-permute-start(bf16[1024,256]{1,0:T(8,128)(2,1)} %get-tuple-element.41.refs_4_.refs_0_), channel_id=1, source_target_pairs={{0,16},{8,24},{16,0},{24,8},{1,17},{9,25},{17,1},{25,9},{2,18},{10... | collective-permute-start | bytes 1572872 | tf_op jit(solution)/shard_map/ppermute | solution.py:27
  35.4 17.0 %all-to-all-start = ((bf16[8,112,256]{2,1,0:T(8,128)(2,1)}), bf16[8,112,256]{2,1,0:T(8,128)(2,1)}, u32[]{:S(2)}, u32[]{:S(2)}) async-start(bf16[8,112,256]{2,1,0:T(8,128)(2,1)} %copy-done.2), calls=%async_computation | async-start | bytes 917504 | tf_op jit(solution)/shard_map/all_to_all | solution.py:405
  42.4 3.5 %collective-permute-start.6 = (bf16[1024,256]{1,0:T(8,128)(2,1)}, bf16[1024,256]{1,0:T(8,128)(2,1)S(1)}, u32[]{:S(2)}, u32[]{:S(2)}) collective-permute-start(bf16[1024,256]{1,0:T(8,128)(2,1)} %collective-permute-done.5.refs_1_), channel_id=1, source_target_pairs={{0,8},{8,0},{16,24},{24,16},{1,9},{9,1},{17,25},{25,17},{2,10},{10... | collective-permute-start | bytes 1572872 | tf_op jit(solution)/shard_map/ppermute | solution.py:22
  42.4 11.7 %collective-permute-start.4 = (bf16[4,128,256]{2,1,0:T(8,128)(2,1)}, bf16[4,128,256]{2,1,0:T(8,128)(2,1)S(1)}, u32[]{:S(2)}, u32[]{:S(2)}) collective-permute-start(bf16[4,128,256]{2,1,0:T(8,128)(2,1)} %get-tuple-element.39), channel_id=1, source_target_pairs={{0,1},{1,0},{2,3},{3,2},{4,5},{5,4},{6,7},{7,6},{8,9},{9,8},{10,11... | collective-permute-start | bytes 786440 | tf_op jit(solution)/shard_map/ppermute | solution.py:50
  44.4 14.3 %collective-permute-start.8 = (bf16[8,32,1024]{2,1,0:T(8,128)(2,1)}, bf16[8,32,1024]{2,1,0:T(8,128)(2,1)}, u32[]{:S(2)}, u32[]{:S(2)}) collective-permute-start(bf16[8,32,1024]{2,1,0:T(8,128)(2,1)} %get-tuple-element.52.refs_0_), channel_id=1, source_target_pairs={{0,16},{8,24},{16,0},{24,8},{1,17},{9,25},{17,1},{25,9},{2,18},{10... | collective-permute-start | bytes 1572872 | tf_op jit(solution)/shard_map/ppermute | solution.py:27
  50.5 12.6 %collective-permute-start.7 = (bf16[4,224,256]{2,1,0:T(8,128)(2,1)}, bf16[4,224,256]{2,1,0:T(8,128)(2,1)S(1)}, u32[]{:S(2)}, u32[]{:S(2)}) collective-permute-start(bf16[4,224,256]{2,1,0:T(8,128)(2,1)} %get-tuple-element.45), channel_id=1, source_target_pairs={{0,1},{1,0},{2,3},{3,2},{4,5},{5,4},{6,7},{7,6},{8,9},{9,8},{10,11... | collective-permute-start | bytes 1376264 | tf_op jit(solution)/shard_map/ppermute | solution.py:50
  54.1 11.3 %all-to-all-start.2 = ((bf16[4,96,256]{2,1,0:T(8,128)(2,1)}), bf16[4,96,256]{2,1,0:T(8,128)(2,1)S(1)}, u32[]{:S(2)}, u32[]{:S(2)}) async-start(bf16[4,96,256]{2,1,0:T(8,128)(2,1)} %get-tuple-element.40), calls=%async_computation.2 | async-start | bytes 393216 | tf_op jit(solution)/shard_map/all_to_all | solution.py:56
  65.5 22.3 %all-to-all-start.3 = ((bf16[4,352,256]{2,1,0:T(8,128)(2,1)}), bf16[4,352,256]{2,1,0:T(8,128)(2,1)S(1)}, u32[]{:S(2)}, u32[]{:S(2)}) async-start(bf16[4,352,256]{2,1,0:T(8,128)(2,1)} %combine.1), calls=%async_computation.3 | async-start | bytes 1441792 | tf_op jit(solution)/shard_map/all_to_all | solution.py:56
  69.9 8.8 %collective-permute-start.9 = (bf16[8,32,1024]{2,1,0:T(8,128)(2,1)}, bf16[8,32,1024]{2,1,0:T(8,128)(2,1)S(1)}, u32[]{:S(2)}, u32[]{:S(2)}) collective-permute-start(bf16[8,32,1024]{2,1,0:T(8,128)(2,1)} %get-tuple-element.52.refs_0_), channel_id=1, source_target_pairs={{0,8},{8,0},{16,24},{24,16},{1,9},{9,1},{17,25},{25,17},{2,10},{10... | collective-permute-start | bytes 1572872 | tf_op jit(solution)/shard_map/ppermute | solution.py:22
  69.9 7.3 %collective-permute-start.14 = (bf16[4,96,256]{2,1,0:T(8,128)(2,1)S(1)}, bf16[4,96,256]{2,1,0:T(8,128)(2,1)S(1)}, u32[]{:S(2)}, u32[]{:S(2)}) collective-permute-start(bf16[4,96,256]{2,1,0:T(8,128)(2,1)S(1)} %all-to-all-done.2.refs_0_), channel_id=1, source_target_pairs={{0,1},{1,0},{2,3},{3,2},{4,5},{5,4},{6,7},{7,6},{8,9},{9,8},{10,11... | collective-permute-start | bytes 589832 | tf_op jit(solution)/shard_map/ppermute | solution.py:50
  70.9 13.6 %collective-permute-start.10 = (bf16[8,32,1024]{2,1,0:T(8,128)(2,1)}, bf16[8,32,1024]{2,1,0:T(8,128)(2,1)}, u32[]{:S(2)}, u32[]{:S(2)}) collective-permute-start(bf16[8,32,1024]{2,1,0:T(8,128)(2,1)} %collective-permute-done.8.refs_1_), channel_id=1, source_target_pairs={{0,8},{8,0},{16,24},{24,16},{1,9},{9,1},{17,25},{25,17},{2,10},{10... | collective-permute-start | bytes 1572872 | tf_op jit(solution)/shard_map/ppermute | solution.py:22
  71.1 8.1 %collective-permute-start.11 = (bf16[4,96,256]{2,1,0:T(8,128)(2,1)S(1)}, bf16[4,96,256]{2,1,0:T(8,128)(2,1)S(1)}, u32[]{:S(2)}, u32[]{:S(2)}) collective-permute-start(bf16[4,96,256]{2,1,0:T(8,128)(2,1)S(1)} %all-to-all-done.2.refs_0_), channel_id=1, source_target_pairs={{0,16},{8,24},{16,0},{24,8},{1,17},{9,25},{17,1},{25,9},{2,18},{10... | collective-permute-start | bytes 589832 | tf_op jit(solution)/shard_map/ppermute | solution.py:27
  77.2 6.6 %collective-permute-start.15 = (bf16[4,96,256]{2,1,0:T(8,128)(2,1)S(1)}, bf16[4,96,256]{2,1,0:T(8,128)(2,1)}, u32[]{:S(2)}, u32[]{:S(2)}) collective-permute-start(bf16[4,96,256]{2,1,0:T(8,128)(2,1)S(1)} %collective-permute-done.14.refs_4_), channel_id=1, source_target_pairs={{0,16},{8,24},{16,0},{24,8},{1,17},{9,25},{17,1},{25,9},{2,18},{10... | collective-permute-start | bytes 589832 | tf_op jit(solution)/shard_map/ppermute | solution.py:27
  78.7 9.1 %collective-permute-start.12 = (bf16[4,96,256]{2,1,0:T(8,128)(2,1)S(1)}, bf16[4,96,256]{2,1,0:T(8,128)(2,1)}, u32[]{:S(2)}, u32[]{:S(2)}) collective-permute-start(bf16[4,96,256]{2,1,0:T(8,128)(2,1)S(1)} %all-to-all-done.2.refs_0_), channel_id=1, source_target_pairs={{0,8},{8,0},{16,24},{24,16},{1,9},{9,1},{17,25},{25,17},{2,10},{10... | collective-permute-start | bytes 589832 | tf_op jit(solution)/shard_map/ppermute | solution.py:22
  78.7 9.1 %collective-permute-start.16 = (bf16[4,96,256]{2,1,0:T(8,128)(2,1)S(1)}, bf16[4,96,256]{2,1,0:T(8,128)(2,1)}, u32[]{:S(2)}, u32[]{:S(2)}) collective-permute-start(bf16[4,96,256]{2,1,0:T(8,128)(2,1)S(1)} %collective-permute-done.14.refs_4_), channel_id=1, source_target_pairs={{0,8},{8,0},{16,24},{24,16},{1,9},{9,1},{17,25},{25,17},{2,10},{10... | collective-permute-start | bytes 589832 | tf_op jit(solution)/shard_map/ppermute | solution.py:22
  79.2 8.6 %collective-permute-start.13 = (bf16[4,96,256]{2,1,0:T(8,128)(2,1)S(1)}, bf16[4,96,256]{2,1,0:T(8,128)(2,1)}, u32[]{:S(2)}, u32[]{:S(2)}) collective-permute-start(bf16[4,96,256]{2,1,0:T(8,128)(2,1)S(1)} %collective-permute-done.11.refs_1_), channel_id=1, source_target_pairs={{0,8},{8,0},{16,24},{24,16},{1,9},{9,1},{17,25},{25,17},{2,10},{10... | collective-permute-start | bytes 589832 | tf_op jit(solution)/shard_map/ppermute | solution.py:22
  83.8 3.9 %collective-permute-start.17 = (bf16[4,96,256]{2,1,0:T(8,128)(2,1)}, bf16[4,96,256]{2,1,0:T(8,128)(2,1)}, u32[]{:S(2)}, u32[]{:S(2)}) collective-permute-start(bf16[4,96,256]{2,1,0:T(8,128)(2,1)} %collective-permute-done.15.refs_5_), channel_id=1, source_target_pairs={{0,8},{8,0},{16,24},{24,16},{1,9},{9,1},{17,25},{25,17},{2,10},{10... | collective-permute-start | bytes 589832 | tf_op jit(solution)/shard_map/ppermute | solution.py:22
  91.6 13.5 %all-to-all-start.4 = ((bf16[4,5,32,256]{3,2,1,0:T(8,128)(2,1)}), bf16[4,5,32,256]{3,2,1,0:T(8,128)(2,1)S(1)}, u32[]{:S(2)}, u32[]{:S(2)}) async-start(bf16[4,5,32,256]{3,2,1,0:T(8,128)(2,1)} %get-tuple-element.61), calls=%async_computation.4 | async-start | bytes 655360 | tf_op jit(solution)/shard_map/all_to_all | solution.py:56
  95.1 8.3 %collective-permute-start.18 = (bf16[8,2,32,256]{3,2,1,0:T(8,128)(2,1)}, bf16[8,2,32,256]{3,2,1,0:T(8,128)(2,1)}, u32[]{:S(2)}, u32[]{:S(2)}) collective-permute-start(bf16[8,2,32,256]{3,2,1,0:T(8,128)(2,1)} %bitcast.15), channel_id=1, source_target_pairs={{0,16},{8,24},{16,0},{24,8},{1,17},{9,25},{17,1},{25,9},{2,18},{10... | collective-permute-start | bytes 786440 | tf_op jit(solution)/shard_map/ppermute | solution.py:27
  105.1 8.5 %collective-permute-start.22 = (bf16[4,5,32,256]{3,2,1,0:T(8,128)(2,1)S(1)}, bf16[4,5,32,256]{3,2,1,0:T(8,128)(2,1)S(1)}, u32[]{:S(2)}, u32[]{:S(2)}) collective-permute-start(bf16[4,5,32,256]{3,2,1,0:T(8,128)(2,1)S(1)} %all-to-all-done.4.refs_8_), channel_id=1, source_target_pairs={{0,1},{1,0},{2,3},{3,2},{4,5},{5,4},{6,7},{7,6},{8,9},{9,8},{10,11... | collective-permute-start | bytes 983048 | tf_op jit(solution)/shard_map/ppermute | solution.py:50
  106.3 11.6 %all-to-all-start.5 = ((bf16[8,2,32,256]{3,2,1,0:T(8,128)(2,1)}), bf16[8,2,32,256]{3,2,1,0:T(8,128)(2,1)S(1)}, u32[]{:S(2)}, u32[]{:S(2)}) async-start(bf16[8,2,32,256]{3,2,1,0:T(8,128)(2,1)} %collective-permute-done.18), calls=%async_computation.5 | async-start | bytes 524288 | tf_op jit(solution)/shard_map/all_to_all | solution.py:485
  110.6 7.3 %collective-permute-start.19 = (bf16[4,3,32,256]{3,2,1,0:T(8,128)(2,1)}, bf16[4,3,32,256]{3,2,1,0:T(8,128)(2,1)}, u32[]{:S(2)}, u32[]{:S(2)}) collective-permute-start(bf16[4,3,32,256]{3,2,1,0:T(8,128)(2,1)} %slice.6), channel_id=1, source_target_pairs={{0,16},{8,24},{16,0},{24,8},{1,17},{9,25},{17,1},{25,9},{2,18},{10... | collective-permute-start | bytes 589832 | tf_op jit(solution)/shard_map/ppermute | solution.py:27
  114.4 6.0 %collective-permute-start.23 = (bf16[4,3,32,256]{3,2,1,0:T(8,128)(2,1)}, bf16[4,3,32,256]{3,2,1,0:T(8,128)(2,1)}, u32[]{:S(2)}, u32[]{:S(2)}) collective-permute-start(bf16[4,3,32,256]{3,2,1,0:T(8,128)(2,1)} %slice.8), channel_id=1, source_target_pairs={{0,16},{8,24},{16,0},{24,8},{1,17},{9,25},{17,1},{25,9},{2,18},{10... | collective-permute-start | bytes 589832 | tf_op jit(solution)/shard_map/ppermute | solution.py:27
  116.4 4.0 %collective-permute-start.20 = (bf16[4,5,32,256]{3,2,1,0:T(8,128)(2,1)S(1)}, bf16[4,5,32,256]{3,2,1,0:T(8,128)(2,1)S(1)}, u32[]{:S(2)}, u32[]{:S(2)}) collective-permute-start(bf16[4,5,32,256]{3,2,1,0:T(8,128)(2,1)S(1)} %all-to-all-done.4.refs_8_), channel_id=1, source_target_pairs={{0,8},{8,0},{16,24},{24,16},{1,9},{9,1},{17,25},{25,17},{2,10},{10... | collective-permute-start | bytes 983048 | tf_op jit(solution)/shard_map/ppermute | solution.py:22
  116.4 4.0 %collective-permute-start.24 = (bf16[4,5,32,256]{3,2,1,0:T(8,128)(2,1)S(1)}, bf16[4,5,32,256]{3,2,1,0:T(8,128)(2,1)}, u32[]{:S(2)}, u32[]{:S(2)}) collective-permute-start(bf16[4,5,32,256]{3,2,1,0:T(8,128)(2,1)S(1)} %collective-permute-done.22.refs_12_), channel_id=1, source_target_pairs={{0,8},{8,0},{16,24},{24,16},{1,9},{9,1},{17,25},{25,17},{2,10},{10... | collective-permute-start | bytes 983048 | tf_op jit(solution)/shard_map/ppermute | solution.py:22
  117.9 4.1 %collective-permute-start.26 = (bf16[8,2,32,256]{3,2,1,0:T(8,128)(2,1)S(1)}, bf16[8,2,32,256]{3,2,1,0:T(8,128)(2,1)S(1)}, u32[]{:S(2)}, u32[]{:S(2)}) collective-permute-start(bf16[8,2,32,256]{3,2,1,0:T(8,128)(2,1)S(1)} %all-to-all-done.5.refs_16_), channel_id=1, source_target_pairs={{0,8},{8,0},{16,24},{24,16},{1,9},{9,1},{17,25},{25,17},{2,10},{10... | collective-permute-start | bytes 786440 | tf_op jit(solution)/shard_map/ppermute | solution.py:22
  118.0 2.4 %collective-permute-start.21 = (bf16[4,3,32,256]{3,2,1,0:T(8,128)(2,1)}, bf16[4,3,32,256]{3,2,1,0:T(8,128)(2,1)S(1)}, u32[]{:S(2)}, u32[]{:S(2)}) collective-permute-start(bf16[4,3,32,256]{3,2,1,0:T(8,128)(2,1)} %collective-permute-done.19.refs_9_), channel_id=1, source_target_pairs={{0,8},{8,0},{16,24},{24,16},{1,9},{9,1},{17,25},{25,17},{2,10},{10... | collective-permute-start | bytes 589832 | tf_op jit(solution)/shard_map/ppermute | solution.py:22
  120.4 1.7 %collective-permute-start.25 = (bf16[4,3,32,256]{3,2,1,0:T(8,128)(2,1)}, bf16[4,3,32,256]{3,2,1,0:T(8,128)(2,1)S(1)}, u32[]{:S(2)}, u32[]{:S(2)}) collective-permute-start(bf16[4,3,32,256]{3,2,1,0:T(8,128)(2,1)} %collective-permute-done.23.refs_13_), channel_id=1, source_target_pairs={{0,8},{8,0},{16,24},{24,16},{1,9},{9,1},{17,25},{25,17},{2,10},{10... | collective-permute-start | bytes 589832 | tf_op jit(solution)/shard_map/ppermute | solution.py:22

commit v10 on v9

--- a/solution.py
+++ b/solution.py
@@ -166,10 +166,14 @@
         store_pair(keep_ref, send_ref, order[i], t, dot(c, ups[i][...], 1, 0))
 
 
-def combine_kernel(keep_ref, got_ref, back_keep_ref, back_got_ref, out_ref):
+def pair_kernel(keep_ref, got_ref, out_ref):
+    out_ref[...] = (keep_ref[...] + got_ref[...].astype(f32)).astype(bf16)
+
+
+def combine_kernel(keep_ref, got_ref, back_ref, out_ref):
     cut = keep_ref.shape[1]
     out_ref[:, :cut] = (keep_ref[...] + got_ref[...].astype(f32)).astype(bf16)
-    out_ref[:, cut:] = (back_keep_ref[...] + back_got_ref[...].astype(f32)).astype(bf16)
+    out_ref[:, cut:] = back_ref[...]
 
 
 def collect_kernel(packed_ref, gram_ref, lengths_ref):
@@ -178,7 +182,7 @@
     for z in range(copies):
         gram_ref[z] = total
     for n in range(packed_ref.shape[0]):
-        lengths_ref[n : n + 1] = packed_ref[n, rows : rows + 16].astype(f32)[:1]
+        lengths_ref[n : n + 1] = packed_ref[n, rows : rows + 8].astype(f32)[:1]
 
 
 def recur_kernel(count, width, order, spot, sums_ref, sq_ref, *refs):
@@ -264,7 +268,7 @@
     far_count = 2 * (half - 1)
     apart = refs[4 * count : 4 * count + far_count]
     rest = refs[4 * count + far_count :]
-    lengths_ref, gain_ref, out_ref, acc, hidden, masks = rest
+    lengths_ref, gain_ref, out_ref, acc, hidden, masks, held, sems = rest
     peers, t, width = rows[0].shape
     r = out_ref.shape[1]
     chunk = min(r, width)
@@ -306,6 +310,7 @@
             inside = (position >= start) & (position < stop)
             masks[n, q * r : (q + 1) * r] = jnp.where(inside, grad, 0.0).astype(bf16)
             start = stop
+    copies = []
     for f in range(width // chunk):
         cols = slice(f * chunk, (f + 1) * chunk)
         update = dot(acts[0], ups[1][cols], 1, 1)
@@ -324,7 +329,11 @@
             else:
                 acc[...] = acc[...] + total
         gain = gain_ref[:, cols]
-        out_ref[cols] = (acc[...] * (gain * gain * scale)).T
+        held[cols] = (acc[...] * (gain * gain * scale)).T
+        copies.append(pltpu.make_async_copy(held.at[cols], out_ref.at[cols], sems.at[f]))
+        copies[-1].start()
+    for copy in copies:
+        copy.wait()
 
 
 def per_device(tokens, cotangent, down_weight, up_weight, norm_gain, lengths):
@@ -392,7 +401,7 @@
     gram_rows = (count - 1) * (r // peers)
     packed = pl.pallas_call(
         functools.partial(gram_kernel, count, seqs),
-        out_shape=jax.ShapeDtypeStruct((peers, gram_rows + 16, r), bf16),
+        out_shape=jax.ShapeDtypeStruct((peers, gram_rows + 8, r), bf16),
         in_specs=[smem] * 4 + [vmem] * (count + 2),
         out_specs=vmem,
         scratch_shapes=[pltpu.VMEM((2 + count, block, r), bf16)],
@@ -443,14 +452,22 @@
     )(packed)
     gram_sums, back_got = lax.optimization_barrier((gram_sums, back_got))
     own_grams = line_exchange(gram_sums)
+    back_part = pl.pallas_call(
+        pair_kernel,
+        out_shape=jax.ShapeDtypeStruct((line, count * t, r), bf16),
+        in_specs=[vmem] * 2,
+        out_specs=vmem,
+        compiler_params=limit(8),
+        name="pair",
+    )(kept(back_keep, pltpu.HBM), back_got)
     part = pl.pallas_call(
         combine_kernel,
         out_shape=pltpu.HBM((line, (3 * count - 1) * t, r), bf16),
-        in_specs=[vmem] * 4,
+        in_specs=[vmem] * 3,
         out_specs=vmem,
         compiler_params=limit(12),
         name="combine",
-    )(kept(keep, pltpu.HBM), got, kept(back_keep, pltpu.HBM), back_got)
+    )(kept(keep, pltpu.HBM), got, back_part)
     own_grams, part = lax.optimization_barrier((own_grams, part))
     sums = line_exchange(part)
     all_rows = [token_rows, *far_rows]
@@ -493,13 +510,15 @@
     chunk = min(r, block)
     fisher = pl.pallas_call(
         functools.partial(fisher_kernel, count, seqs, 1.0 / (row_count * peers)),
-        out_shape=jax.ShapeDtypeStruct((block, r), f32),
+        out_shape=pltpu.HBM((block, r), f32),
         in_specs=[smem, smem] + [vmem] * (2 * count + len(flat) + 2),
-        out_specs=vmem,
+        out_specs=anywhere,
         scratch_shapes=[
             pltpu.VMEM((r, chunk), f32),
             pltpu.VMEM((peers, row_count, chunk), bf16),
             pltpu.VMEM((peers, seqs * r, row_count), bf16),
+            pltpu.VMEM((block, r), f32),
+            pltpu.SemaphoreType.DMA((block // chunk,)),
         ],
         compiler_params=limit(24),
         name="squares",

time: 133 us -> 133 us (level)
  starting transfers between devices: 47.1 us -> 45.6 us
    ppermute x8, starting transfers between devices: 13.6 us -> 12.2 us  [chip_shift(): lax.ppermute(x, 'section', [(i, (i - 2 * by) % count) for i in range(coun...]
  transfers between devices with their start and end apart: 33 -> 33, of which waited for: 16 -> 16; matrix products, arithmetic and copies ran while one was open for 2% -> 2% of each run, Pallas kernels for 11% -> 12%
where the time goes in v10:
time: 133 us; the launch traced here: 132 us
  waiting for transfers between devices  49.2 us (37%)
  starting transfers between devices  45.6 us (34%)
  Pallas kernels  32.4 us (24%)
  local copies, waits for them, and re-layouts  4.67 us (4%)
    ppermute x8, waiting for transfers between devices, chip_shift(): lax.ppermute(x, 'section', [(i, (i - 2 * by) % count) for i in range(coun...  21.3 us
    ppermute x8, starting transfers between devices, chip_shift(): lax.ppermute(x, 'section', [(i, (i - 2 * by) % count) for i in range(coun...  12.2 us
    all_to_all x3, starting transfers between devices, line_exchange(): return lax.all_to_all(x, 'dp', 0, 0, axis_index_groups=groups, tiled=True)  11.8 us
    ppermute x4, waiting for transfers between devices, pair_swap(): return lax.ppermute(x, 'dp', [(i, i ^ 1) for i in range(peers)])  10.9 us
    pallas_call x1, Pallas kernels, per_device(): pl.pallas_call(functools.partial(fisher_kernel, count, seqs, 1.0 / (row_c...  10.3 us
    all_to_all x1, starting transfers between devices, per_device(): rows = lax.all_to_all(send, 'dp', 0, 0, tiled=True)  7.4 us
    all_to_all x1, waiting for transfers between devices, per_device(): rows = lax.all_to_all(send, 'dp', 0, 0, tiled=True)  6.07 us
    all_to_all x3, waiting for transfers between devices, line_exchange(): return lax.all_to_all(x, 'dp', 0, 0, axis_index_groups=groups, tiled=True)  5.64 us
  transfers between devices with their start and end apart: 33, of which 16 were waited for; matrix products, arithmetic and copies ran while one was open for 2% of the time, Pallas kernels for 12%

profile of v10, /device:TPU:0, one launch (start us, length us, event | category | flops | bytes accessed | tf_op | source)
XLA Modules:
  0.0 132.3 jit_solution(1506175584706040249)
XLA Ops:
  0.0 2.2 %prepare.1.rows_ref = bf16[8,64,1024]{2,1,0:T(8,128)(2,1)} custom-call(bf16[128,8192]{1,0:T(8,128)(2,1)} %tokens_ref.1, bf16[128,8192]{1,0:T(8,128)(2,1)} %cot_ref.1), custom_call_target="tpu_custom_call" | custom-call | tf_op jit(solution)/shard_map/prepare/pallas_call | solution.py:359
  2.2 7.4 %all-to-all-start.1 = ((bf16[8,64,1024]{2,1,0:T(8,128)(2,1)}), bf16[8,64,1024]{2,1,0:T(8,128)(2,1)S(1)}, u32[]{:S(2)}, u32[]{:S(2)}) async-start(bf16[8,64,1024]{2,1,0:T(8,128)(2,1)} %prepare.1.rows_ref), calls=%async_computation.1 | async-start | bytes 2097152 | tf_op jit(solution)/shard_map/all_to_all | solution.py:394
  9.6 1.6 %collective-permute-start = (bf16[1024,256]{1,0:T(8,128)(2,1)S(1)}, bf16[1024,256]{1,0:T(8,128)(2,1)S(1)}, u32[]{:S(2)}, u32[]{:S(2)}) collective-permute-start(bf16[1024,256]{1,0:T(8,128)(2,1)S(1)} %bitcast.9), channel_id=1, source_target_pairs={{0,16},{8,24},{16,0},{24,8},{1,17},{9,25},{17,1},{25,9},{2,18},{10... | collective-permute-start | bytes 1572872 | tf_op jit(solution)/shard_map/ppermute | solution.py:27
  11.3 1.0 copy-done.3
  12.4 1.6 %weight.1 = (f32[32,1]{1,0:T(8,128)S(1)}, bf16[1024,256]{1,0:T(8,128)(2,1)}) custom-call(s32[2]{0:T(128)S(1)} %pad_add_fusion.1.place, bf16[8,64,1024]{2,1,0:T(8,128)(2,1)S(1)} %copy-done, bf16[1,1024,256]{2,1,0:T(8,128)(2,1)S(1)} %copy-done.3, f32[1,8192]{1,0:T(1,128)S(1)} %copy-done.4), custom_call_target="tpu_custom_call" | custom-call | tf_op jit(solution)/shard_map/weight/pallas_call | solution.py:371
  14.0 0.6 copy-done.5
  15.1 8.0 %collective-permute-done.refs_1_.refs_5_ = bf16[1024,256]{1,0:T(8,128)(2,1)S(1)} collective-permute-done((bf16[1024,256]{1,0:T(8,128)(2,1)S(1)}, bf16[1024,256]{1,0:T(8,128)(2,1)S(1)}, u32[]{:S(2)}, u32[]{:S(2)}) %collective-permute-start) | collective-permute-done | bytes 524320 | tf_op jit(solution)/shard_map/ppermute | solution.py:27
  23.3 1.7 %collective-permute-done.2.refs_3_.refs_7_ = bf16[1024,256]{1,0:T(8,128)(2,1)S(1)} collective-permute-done((bf16[1024,256]{1,0:T(8,128)(2,1)S(1)}, bf16[1024,256]{1,0:T(8,128)(2,1)S(1)}, u32[]{:S(2)}, u32[]{:S(2)}) %collective-permute-start.2) | collective-permute-done | bytes 524320 | tf_op jit(solution)/shard_map/ppermute | solution.py:22
  25.0 2.0 %gram.1 = bf16[8,104,256]{2,1,0:T(8,128)(2,1)S(1)} custom-call(s32[4]{0:T(128)S(1)} %pad_add_fusion.order, s32[3]{0:T(128)S(1)} %dynamic_slice.9.left, s32[3]{0:T(128)S(1)} %dynamic_slice.10.right, s32[1,4]{1,0:T(1,128)S(1)} %copy-done.6, bf16[1024,256]{1,0:T(8,128)(2,1)S(1)} %bitcast.11, bf16[1024,256]{1,0:T(8,128)(2,1)S(1)} %collective-permute-done.refs_1_.refs_5_, ...), custom_call_target="tpu_custom_call" | custom-call | tf_op jit(solution)/shard_map/gram/pallas_call | solution.py:402
  27.1 0.7 copy-done.2
  27.8 1.5 %collective-permute-start.5 = (bf16[1024,256]{1,0:T(8,128)(2,1)}, bf16[1024,256]{1,0:T(8,128)(2,1)}, u32[]{:S(2)}, u32[]{:S(2)}) collective-permute-start(bf16[1024,256]{1,0:T(8,128)(2,1)} %get-tuple-element.41.refs_4_.refs_0_), channel_id=1, source_target_pairs={{0,16},{8,24},{16,0},{24,8},{1,17},{9,25},{17,1},{25,9},{2,18},{10... | collective-permute-start | bytes 1572872 | tf_op jit(solution)/shard_map/ppermute | solution.py:27
  29.3 6.1 %all-to-all-done.1.rows_ref = bf16[8,64,1024]{2,1,0:T(8,128)(2,1)S(1)} async-done(((bf16[8,64,1024]{2,1,0:T(8,128)(2,1)}), bf16[8,64,1024]{2,1,0:T(8,128)(2,1)S(1)}, u32[]{:S(2)}, u32[]{:S(2)}) %all-to-all-start.1) | async-done | bytes 1048608 | tf_op jit(solution)/shard_map/all_to_all | solution.py:394
  35.4 4.1 %all-to-all-start = ((bf16[8,104,256]{2,1,0:T(8,128)(2,1)}), bf16[8,104,256]{2,1,0:T(8,128)(2,1)}, u32[]{:S(2)}, u32[]{:S(2)}) async-start(bf16[8,104,256]{2,1,0:T(8,128)(2,1)} %copy-done.2), calls=%async_computation | async-start | bytes 851968 | tf_op jit(solution)/shard_map/all_to_all | solution.py:414
  39.5 2.9 %project_cot.1 = (f32[4,128,256]{2,1,0:T(8,128)}, bf16[4,128,256]{2,1,0:T(8,128)(2,1)}, bf16[8,32,1024]{2,1,0:T(8,128)(2,1)}) custom-call(s32[4]{0:T(128)S(1)} %pad_add_fusion.order, s32[1]{0:T(128)} %bitcast.5.spot, bf16[8,64,1024]{2,1,0:T(8,128)(2,1)S(1)} %all-to-all-done.1.rows_ref, bf16[1024,256]{1,0:T(8,128)(2,1)S(1)} %bitcast.12, ...), custom_call_target="tpu_custom_call" | custom-call | tf_op jit(solution)/shard_map/project_cot/pallas_call | solution.py:424
  42.4 2.0 %collective-permute-start.4 = (bf16[4,128,256]{2,1,0:T(8,128)(2,1)}, bf16[4,128,256]{2,1,0:T(8,128)(2,1)S(1)}, u32[]{:S(2)}, u32[]{:S(2)}) collective-permute-start(bf16[4,128,256]{2,1,0:T(8,128)(2,1)} %get-tuple-element.39), channel_id=1, source_target_pairs={{0,1},{1,0},{2,3},{3,2},{4,5},{5,4},{6,7},{7,6},{8,9},{9,8},{10,11... | collective-permute-start | bytes 786440 | tf_op jit(solution)/shard_map/ppermute | solution.py:50
  44.3 1.5 %collective-permute-start.8 = (bf16[8,32,1024]{2,1,0:T(8,128)(2,1)}, bf16[8,32,1024]{2,1,0:T(8,128)(2,1)}, u32[]{:S(2)}, u32[]{:S(2)}) collective-permute-start(bf16[8,32,1024]{2,1,0:T(8,128)(2,1)} %get-tuple-element.52.refs_0_), channel_id=1, source_target_pairs={{0,16},{8,24},{16,0},{24,8},{1,17},{9,25},{17,1},{25,9},{2,18},{10... | collective-permute-start | bytes 1572872 | tf_op jit(solution)/shard_map/ppermute | solution.py:27
  45.9 4.6 %project.1 = (f32[4,224,256]{2,1,0:T(8,128)}, bf16[4,224,256]{2,1,0:T(8,128)(2,1)}) custom-call(s32[4]{0:T(128)S(1)} %pad_add_fusion.order, s32[1]{0:T(128)} %bitcast.5.spot, bf16[8,64,1024]{2,1,0:T(8,128)(2,1)S(1)} %all-to-all-done.1.rows_ref, bf16[1024,256]{1,0:T(8,128)(2,1)} %get-tuple-element.41.refs_4_.refs_0_, ...), custom_call_target="tpu_custom_call" | custom-call | tf_op jit(solution)/shard_map/project/pallas_call | solution.py:436
  50.4 0.5 collective-permute-start.7
  51.0 0.8 all-to-all-done.packed_ref
  51.7 1.8 %collect.1 = (bf16[4,96,256]{2,1,0:T(8,128)(2,1)}, f32[8,256]{1,0:T(8,128)S(1)}) custom-call(bf16[8,104,256]{2,1,0:T(8,128)(2,1)} %all-to-all-done.packed_ref), custom_call_target="tpu_custom_call" | custom-call | tf_op jit(solution)/shard_map/collect/pallas_call | solution.py:445
  53.5 3.9 %all-to-all-start.2 = ((bf16[4,96,256]{2,1,0:T(8,128)(2,1)}), bf16[4,96,256]{2,1,0:T(8,128)(2,1)S(1)}, u32[]{:S(2)}, u32[]{:S(2)}) async-start(bf16[4,96,256]{2,1,0:T(8,128)(2,1)} %get-tuple-element.40), calls=%async_computation.2 | async-start | bytes 393216 | tf_op jit(solution)/shard_map/all_to_all | solution.py:56
  57.4 1.1 pair.1.back_ref
  58.7 4.3 %collective-permute-done.7.got_ref = bf16[4,224,256]{2,1,0:T(8,128)(2,1)S(1)} collective-permute-done((bf16[4,224,256]{2,1,0:T(8,128)(2,1)}, bf16[4,224,256]{2,1,0:T(8,128)(2,1)S(1)}, u32[]{:S(2)}, u32[]{:S(2)}) %collective-permute-start.7) | collective-permute-done | bytes 458784 | tf_op jit(solution)/shard_map/ppermute | solution.py:50
  62.9 2.1 %combine.1 = bf16[4,352,256]{2,1,0:T(8,128)(2,1)} custom-call(f32[4,224,256]{2,1,0:T(8,128)} %get-tuple-element.44.keep_ref, bf16[4,224,256]{2,1,0:T(8,128)(2,1)S(1)} %collective-permute-done.7.got_ref, bf16[4,128,256]{2,1,0:T(8,128)(2,1)S(1)} %pair.1.back_ref), custom_call_target="tpu_custom_call" | custom-call | tf_op jit(solution)/shard_map/combine/pallas_call | solution.py:463
  65.2 4.4 %all-to-all-start.3 = ((bf16[4,352,256]{2,1,0:T(8,128)(2,1)}), bf16[4,352,256]{2,1,0:T(8,128)(2,1)S(1)}, u32[]{:S(2)}, u32[]{:S(2)}) async-start(bf16[4,352,256]{2,1,0:T(8,128)(2,1)} %combine.1), calls=%async_computation.3 | async-start | bytes 1441792 | tf_op jit(solution)/shard_map/all_to_all | solution.py:56
  69.7 0.8 collective-permute-start.14
  70.7 1.5 %collective-permute-start.11 = (bf16[4,96,256]{2,1,0:T(8,128)(2,1)S(1)}, bf16[4,96,256]{2,1,0:T(8,128)(2,1)S(1)}, u32[]{:S(2)}, u32[]{:S(2)}) collective-permute-start(bf16[4,96,256]{2,1,0:T(8,128)(2,1)S(1)} %all-to-all-done.2.refs_0_), channel_id=1, source_target_pairs={{0,16},{8,24},{16,0},{24,8},{1,17},{9,25},{17,1},{25,9},{2,18},{10... | collective-permute-start | bytes 589832 | tf_op jit(solution)/shard_map/ppermute | solution.py:27
  72.2 4.7 %collective-permute-done.14.refs_4_ = bf16[4,96,256]{2,1,0:T(8,128)(2,1)S(1)} collective-permute-done((bf16[4,96,256]{2,1,0:T(8,128)(2,1)S(1)}, bf16[4,96,256]{2,1,0:T(8,128)(2,1)S(1)}, u32[]{:S(2)}, u32[]{:S(2)}) %collective-permute-start.14) | collective-permute-done | bytes 196640 | tf_op jit(solution)/shard_map/ppermute | solution.py:50
  77.0 1.2 collective-permute-start.15
  78.8 4.8 %collective-permute-done.15.refs_5_ = bf16[4,96,256]{2,1,0:T(8,128)(2,1)} collective-permute-done((bf16[4,96,256]{2,1,0:T(8,128)(2,1)S(1)}, bf16[4,96,256]{2,1,0:T(8,128)(2,1)}, u32[]{:S(2)}, u32[]{:S(2)}) %collective-permute-start.15) | collective-permute-done | bytes 196640 | tf_op jit(solution)/shard_map/ppermute | solution.py:27
  83.6 0.7 constant_dynamic-slice_fusion.refs_19_
  84.3 3.2 %all-to-all-done.3.sums_ref = bf16[4,352,256]{2,1,0:T(8,128)(2,1)S(1)} async-done(((bf16[4,352,256]{2,1,0:T(8,128)(2,1)}), bf16[4,352,256]{2,1,0:T(8,128)(2,1)S(1)}, u32[]{:S(2)}, u32[]{:S(2)}) %all-to-all-start.3) | async-done | bytes 720928 | tf_op jit(solution)/shard_map/all_to_all | solution.py:56
  87.6 3.8 %recur.1 = (bf16[4,5,32,256]{3,2,1,0:T(8,128)(2,1)}, bf16[1,8,2,32,256]{4,3,2,1,0:T(8,128)(2,1)}) custom-call(s32[4]{0:T(128)S(1)} %pad_add_fusion.order, s32[1]{0:T(128)} %bitcast.5.spot, bf16[4,352,256]{2,1,0:T(8,128)(2,1)S(1)} %all-to-all-done.3.sums_ref, f32[32,1]{1,0:T(8,128)} %copy-done.5, bf16[4,96,256]{2,1,0:T(8,128)(2,1)S(1)} %all-to-all-done.2.refs_0_, ...), custom_call_target="tpu_custom_call" | custom-call | tf_op jit(solution)/shard_map/recur/pallas_call | solution.py:478
  91.4 3.5 %all-to-all-start.4 = ((bf16[4,5,32,256]{3,2,1,0:T(8,128)(2,1)}), bf16[4,5,32,256]{3,2,1,0:T(8,128)(2,1)S(1)}, u32[]{:S(2)}, u32[]{:S(2)}) async-start(bf16[4,5,32,256]{3,2,1,0:T(8,128)(2,1)} %get-tuple-element.61), calls=%async_computation.4 | async-start | bytes 655360 | tf_op jit(solution)/shard_map/all_to_all | solution.py:56
  94.8 1.9 %collective-permute-start.18 = (bf16[8,2,32,256]{3,2,1,0:T(8,128)(2,1)}, bf16[8,2,32,256]{3,2,1,0:T(8,128)(2,1)}, u32[]{:S(2)}, u32[]{:S(2)}) collective-permute-start(bf16[8,2,32,256]{3,2,1,0:T(8,128)(2,1)} %bitcast.15), channel_id=1, source_target_pairs={{0,16},{8,24},{16,0},{24,8},{1,17},{9,25},{17,1},{25,9},{2,18},{10... | collective-permute-start | bytes 786440 | tf_op jit(solution)/shard_map/ppermute | solution.py:27
  96.7 6.0 %collective-permute-done.18 = bf16[8,2,32,256]{3,2,1,0:T(8,128)(2,1)} collective-permute-done((bf16[8,2,32,256]{3,2,1,0:T(8,128)(2,1)}, bf16[8,2,32,256]{3,2,1,0:T(8,128)(2,1)}, u32[]{:S(2)}, u32[]{:S(2)}) %collective-permute-start.18) | collective-permute-done | bytes 262176 | tf_op jit(solution)/shard_map/ppermute | solution.py:27
  102.7 2.2 %all-to-all-done.4.refs_8_ = bf16[4,5,32,256]{3,2,1,0:T(8,128)(2,1)S(1)} async-done(((bf16[4,5,32,256]{3,2,1,0:T(8,128)(2,1)}), bf16[4,5,32,256]{3,2,1,0:T(8,128)(2,1)S(1)}, u32[]{:S(2)}, u32[]{:S(2)}) %all-to-all-start.4) | async-done | bytes 327712 | tf_op jit(solution)/shard_map/all_to_all | solution.py:56
  104.9 0.8 collective-permute-start.22
  105.8 3.6 %all-to-all-start.5 = ((bf16[8,2,32,256]{3,2,1,0:T(8,128)(2,1)}), bf16[8,2,32,256]{3,2,1,0:T(8,128)(2,1)S(1)}, u32[]{:S(2)}, u32[]{:S(2)}) async-start(bf16[8,2,32,256]{3,2,1,0:T(8,128)(2,1)} %collective-permute-done.18), calls=%async_computation.5 | async-start | bytes 524288 | tf_op jit(solution)/shard_map/all_to_all | solution.py:502
  109.4 0.7 slice.6
  110.0 1.5 %collective-permute-start.19 = (bf16[4,3,32,256]{3,2,1,0:T(8,128)(2,1)}, bf16[4,3,32,256]{3,2,1,0:T(8,128)(2,1)}, u32[]{:S(2)}, u32[]{:S(2)}) collective-permute-start(bf16[4,3,32,256]{3,2,1,0:T(8,128)(2,1)} %slice.6), channel_id=1, source_target_pairs={{0,16},{8,24},{16,0},{24,8},{1,17},{9,25},{17,1},{25,9},{2,18},{10... | collective-permute-start | bytes 589832 | tf_op jit(solution)/shard_map/ppermute | solution.py:27
  111.6 1.9 %collective-permute-done.22.refs_12_ = bf16[4,5,32,256]{3,2,1,0:T(8,128)(2,1)S(1)} collective-permute-done((bf16[4,5,32,256]{3,2,1,0:T(8,128)(2,1)S(1)}, bf16[4,5,32,256]{3,2,1,0:T(8,128)(2,1)S(1)}, u32[]{:S(2)}, u32[]{:S(2)}) %collective-permute-start.22) | collective-permute-done | bytes 327712 | tf_op jit(solution)/shard_map/ppermute | solution.py:50
  113.5 0.7 slice.8
  114.2 1.4 %collective-permute-start.23 = (bf16[4,3,32,256]{3,2,1,0:T(8,128)(2,1)}, bf16[4,3,32,256]{3,2,1,0:T(8,128)(2,1)}, u32[]{:S(2)}, u32[]{:S(2)}) collective-permute-start(bf16[4,3,32,256]{3,2,1,0:T(8,128)(2,1)} %slice.8), channel_id=1, source_target_pairs={{0,16},{8,24},{16,0},{24,8},{1,17},{9,25},{17,1},{25,9},{2,18},{10... | collective-permute-start | bytes 589832 | tf_op jit(solution)/shard_map/ppermute | solution.py:27
  116.1 1.2 all-to-all-done.5.refs_16_
  117.9 2.3 %collective-permute-done.23.refs_13_ = bf16[4,3,32,256]{3,2,1,0:T(8,128)(2,1)} collective-permute-done((bf16[4,3,32,256]{3,2,1,0:T(8,128)(2,1)}, bf16[4,3,32,256]{3,2,1,0:T(8,128)(2,1)}, u32[]{:S(2)}, u32[]{:S(2)}) %collective-permute-start.23) | collective-permute-done | bytes 196640 | tf_op jit(solution)/shard_map/ppermute | solution.py:27
  120.2 1.6 %collective-permute-done.25.refs_15_ = bf16[4,3,32,256]{3,2,1,0:T(8,128)(2,1)S(1)} collective-permute-done((bf16[4,3,32,256]{3,2,1,0:T(8,128)(2,1)}, bf16[4,3,32,256]{3,2,1,0:T(8,128)(2,1)S(1)}, u32[]{:S(2)}, u32[]{:S(2)}) %collective-permute-start.25) | collective-permute-done | bytes 196640 | tf_op jit(solution)/shard_map/ppermute | solution.py:22
  121.8 10.3 %squares.1 = f32[1024,256]{1,0:T(8,128)} custom-call(s32[4]{0:T(128)S(1)} %pad_add_fusion.order, s32[2]{0:T(128)S(1)} %pad_add_fusion.1.place, bf16[8,32,1024]{2,1,0:T(8,128)(2,1)} %get-tuple-element.52.refs_0_, bf16[8,32,1024]{2,1,0:T(8,128)(2,1)} %collective-permute-done.8.refs_1_, bf16[8,32,1024]{2,1,0:T(8,128)(2,1)S(1)} %collective-permute-done.9.refs_2_, ...), custom_call_target="tpu_custom_call" | custom-call | tf_op jit(solution)/shard_map/squares/pallas_call | solution.py:511
  (53 shorter events, 3.1 us)
Async XLA Ops:
  2.2 7.5 %copy-start.1 = (bf16[1,1024,256]{2,1,0:T(8,128)(2,1)S(1)}, bf16[1,1024,256]{2,1,0:T(8,128)(2,1)}, u32[]{:S(2)}) copy-start(bf16[1,1024,256]{2,1,0:T(8,128)(2,1)} %param.11) | copy-start | bytes 1572868
  2.2 9.1 %copy-start = (bf16[8,64,1024]{2,1,0:T(8,128)(2,1)S(1)}, bf16[8,64,1024]{2,1,0:T(8,128)(2,1)}, u32[]{:S(2)}) copy-start(bf16[8,64,1024]{2,1,0:T(8,128)(2,1)} %prepare.1.rows_ref) | copy-start | bytes 3145732
  2.2 9.1 %copy-start.4 = (f32[1,8192]{1,0:T(1,128)S(1)}, f32[1,8192]{1,0:T(1,128)}, u32[]{:S(2)}) copy-start(f32[1,8192]{1,0:T(1,128)} %gain_ref.1) | copy-start | bytes 98308
  2.2 20.9 %copy-start.8 = (s32[12]{0:T(128)S(1)}, s32[12]{0:T(128)}, u32[]{:S(2)}) copy-start(s32[12]{0:T(128)} %constant.49.clone) | copy-start | bytes 148
  2.2 21.0 %copy-start.7 = (s32[12]{0:T(128)S(1)}, s32[12]{0:T(128)}, u32[]{:S(2)}) copy-start(s32[12]{0:T(128)} %constant.50.clone) | copy-start | bytes 148
  2.2 22.8 %copy-start.6 = (s32[1,4]{1,0:T(1,128)S(1)}, s32[1,4]{1,0:T(1,128)}, u32[]{:S(2)}) copy-start(s32[1,4]{1,0:T(1,128)} %lengths.1) | copy-start | bytes 52
  2.2 33.2 %all-to-all-start.1 = ((bf16[8,64,1024]{2,1,0:T(8,128)(2,1)}), bf16[8,64,1024]{2,1,0:T(8,128)(2,1)S(1)}, u32[]{:S(2)}, u32[]{:S(2)}) async-start(bf16[8,64,1024]{2,1,0:T(8,128)(2,1)} %prepare.1.rows_ref), calls=%async_computation.1 | async-start | bytes 2097152 | tf_op jit(solution)/shard_map/all_to_all | solution.py:394
  9.6 13.4 %collective-permute-start = (bf16[1024,256]{1,0:T(8,128)(2,1)S(1)}, bf16[1024,256]{1,0:T(8,128)(2,1)S(1)}, u32[]{:S(2)}, u32[]{:S(2)}) collective-permute-start(bf16[1024,256]{1,0:T(8,128)(2,1)S(1)} %bitcast.9), channel_id=1, source_target_pairs={{0,16},{8,24},{16,0},{24,8},{1,17},{9,25},{17,1},{25,9},{2,18},{10... | collective-permute-start | bytes 1572872 | tf_op jit(solution)/shard_map/ppermute | solution.py:27
  11.2 12.1 %collective-permute-start.1 = (bf16[1024,256]{1,0:T(8,128)(2,1)S(1)}, bf16[1024,256]{1,0:T(8,128)(2,1)}, u32[]{:S(2)}, u32[]{:S(2)}) collective-permute-start(bf16[1024,256]{1,0:T(8,128)(2,1)S(1)} %bitcast.10), channel_id=1, source_target_pairs={{0,8},{8,0},{16,24},{24,16},{1,9},{9,1},{17,25},{25,17},{2,10},{10... | collective-permute-start | bytes 1572872 | tf_op jit(solution)/shard_map/ppermute | solution.py:22
  11.3 1.0 copy-start.3
  14.0 0.6 copy-start.5
  14.6 8.7 %collective-permute-start.3 = (bf16[1024,256]{1,0:T(8,128)(2,1)}, bf16[1024,256]{1,0:T(8,128)(2,1)S(1)}, u32[]{:S(2)}, u32[]{:S(2)}) collective-permute-start(bf16[1024,256]{1,0:T(8,128)(2,1)} %get-tuple-element.41.refs_4_.refs_0_), channel_id=1, source_target_pairs={{0,8},{8,0},{16,24},{24,16},{1,9},{9,1},{17,25},{25,17},{2,10},{10... | collective-permute-start | bytes 1572872 | tf_op jit(solution)/shard_map/ppermute | solution.py:22
  23.1 1.9 %collective-permute-start.2 = (bf16[1024,256]{1,0:T(8,128)(2,1)S(1)}, bf16[1024,256]{1,0:T(8,128)(2,1)S(1)}, u32[]{:S(2)}, u32[]{:S(2)}) collective-permute-start(bf16[1024,256]{1,0:T(8,128)(2,1)S(1)} %collective-permute-done.refs_1_.refs_5_), channel_id=1, source_target_pairs={{0,8},{8,0},{16,24},{24,16},{1,9},{9,1},{17,25},{25,17},{2,10},{10... | collective-permute-start | bytes 1572872 | tf_op jit(solution)/shard_map/ppermute | solution.py:22
  27.1 0.8 copy-start.2
  27.8 14.6 %collective-permute-start.5 = (bf16[1024,256]{1,0:T(8,128)(2,1)}, bf16[1024,256]{1,0:T(8,128)(2,1)}, u32[]{:S(2)}, u32[]{:S(2)}) collective-permute-start(bf16[1024,256]{1,0:T(8,128)(2,1)} %get-tuple-element.41.refs_4_.refs_0_), channel_id=1, source_target_pairs={{0,16},{8,24},{16,0},{24,8},{1,17},{9,25},{17,1},{25,9},{2,18},{10... | collective-permute-start | bytes 1572872 | tf_op jit(solution)/shard_map/ppermute | solution.py:27
  35.4 16.3 %all-to-all-start = ((bf16[8,104,256]{2,1,0:T(8,128)(2,1)}), bf16[8,104,256]{2,1,0:T(8,128)(2,1)}, u32[]{:S(2)}, u32[]{:S(2)}) async-start(bf16[8,104,256]{2,1,0:T(8,128)(2,1)} %copy-done.2), calls=%async_computation | async-start | bytes 851968 | tf_op jit(solution)/shard_map/all_to_all | solution.py:414
  42.4 3.5 %collective-permute-start.6 = (bf16[1024,256]{1,0:T(8,128)(2,1)}, bf16[1024,256]{1,0:T(8,128)(2,1)S(1)}, u32[]{:S(2)}, u32[]{:S(2)}) collective-permute-start(bf16[1024,256]{1,0:T(8,128)(2,1)} %collective-permute-done.5.refs_1_), channel_id=1, source_target_pairs={{0,8},{8,0},{16,24},{24,16},{1,9},{9,1},{17,25},{25,17},{2,10},{10... | collective-permute-start | bytes 1572872 | tf_op jit(solution)/shard_map/ppermute | solution.py:22
  42.4 11.1 %collective-permute-start.4 = (bf16[4,128,256]{2,1,0:T(8,128)(2,1)}, bf16[4,128,256]{2,1,0:T(8,128)(2,1)S(1)}, u32[]{:S(2)}, u32[]{:S(2)}) collective-permute-start(bf16[4,128,256]{2,1,0:T(8,128)(2,1)} %get-tuple-element.39), channel_id=1, source_target_pairs={{0,1},{1,0},{2,3},{3,2},{4,5},{5,4},{6,7},{7,6},{8,9},{9,8},{10,11... | collective-permute-start | bytes 786440 | tf_op jit(solution)/shard_map/ppermute | solution.py:50
  44.3 14.3 %collective-permute-start.8 = (bf16[8,32,1024]{2,1,0:T(8,128)(2,1)}, bf16[8,32,1024]{2,1,0:T(8,128)(2,1)}, u32[]{:S(2)}, u32[]{:S(2)}) collective-permute-start(bf16[8,32,1024]{2,1,0:T(8,128)(2,1)} %get-tuple-element.52.refs_0_), channel_id=1, source_target_pairs={{0,16},{8,24},{16,0},{24,8},{1,17},{9,25},{17,1},{25,9},{2,18},{10... | collective-permute-start | bytes 1572872 | tf_op jit(solution)/shard_map/ppermute | solution.py:27
  50.4 12.5 %collective-permute-start.7 = (bf16[4,224,256]{2,1,0:T(8,128)(2,1)}, bf16[4,224,256]{2,1,0:T(8,128)(2,1)S(1)}, u32[]{:S(2)}, u32[]{:S(2)}) collective-permute-start(bf16[4,224,256]{2,1,0:T(8,128)(2,1)} %get-tuple-element.45), channel_id=1, source_target_pairs={{0,1},{1,0},{2,3},{3,2},{4,5},{5,4},{6,7},{7,6},{8,9},{9,8},{10,11... | collective-permute-start | bytes 1376264 | tf_op jit(solution)/shard_map/ppermute | solution.py:50
  53.5 11.8 %all-to-all-start.2 = ((bf16[4,96,256]{2,1,0:T(8,128)(2,1)}), bf16[4,96,256]{2,1,0:T(8,128)(2,1)S(1)}, u32[]{:S(2)}, u32[]{:S(2)}) async-start(bf16[4,96,256]{2,1,0:T(8,128)(2,1)} %get-tuple-element.40), calls=%async_computation.2 | async-start | bytes 393216 | tf_op jit(solution)/shard_map/all_to_all | solution.py:56
  65.2 22.3 %all-to-all-start.3 = ((bf16[4,352,256]{2,1,0:T(8,128)(2,1)}), bf16[4,352,256]{2,1,0:T(8,128)(2,1)S(1)}, u32[]{:S(2)}, u32[]{:S(2)}) async-start(bf16[4,352,256]{2,1,0:T(8,128)(2,1)} %combine.1), calls=%async_computation.3 | async-start | bytes 1441792 | tf_op jit(solution)/shard_map/all_to_all | solution.py:56
  69.6 8.5 %collective-permute-start.9 = (bf16[8,32,1024]{2,1,0:T(8,128)(2,1)}, bf16[8,32,1024]{2,1,0:T(8,128)(2,1)S(1)}, u32[]{:S(2)}, u32[]{:S(2)}) collective-permute-start(bf16[8,32,1024]{2,1,0:T(8,128)(2,1)} %get-tuple-element.52.refs_0_), channel_id=1, source_target_pairs={{0,8},{8,0},{16,24},{24,16},{1,9},{9,1},{17,25},{25,17},{2,10},{10... | collective-permute-start | bytes 1572872 | tf_op jit(solution)/shard_map/ppermute | solution.py:22
  69.7 7.3 %collective-permute-start.14 = (bf16[4,96,256]{2,1,0:T(8,128)(2,1)S(1)}, bf16[4,96,256]{2,1,0:T(8,128)(2,1)S(1)}, u32[]{:S(2)}, u32[]{:S(2)}) collective-permute-start(bf16[4,96,256]{2,1,0:T(8,128)(2,1)S(1)} %all-to-all-done.2.refs_0_), channel_id=1, source_target_pairs={{0,1},{1,0},{2,3},{3,2},{4,5},{5,4},{6,7},{7,6},{8,9},{9,8},{10,11... | collective-permute-start | bytes 589832 | tf_op jit(solution)/shard_map/ppermute | solution.py:50
  70.5 13.8 %collective-permute-start.10 = (bf16[8,32,1024]{2,1,0:T(8,128)(2,1)}, bf16[8,32,1024]{2,1,0:T(8,128)(2,1)}, u32[]{:S(2)}, u32[]{:S(2)}) collective-permute-start(bf16[8,32,1024]{2,1,0:T(8,128)(2,1)} %collective-permute-done.8.refs_1_), channel_id=1, source_target_pairs={{0,8},{8,0},{16,24},{24,16},{1,9},{9,1},{17,25},{25,17},{2,10},{10... | collective-permute-start | bytes 1572872 | tf_op jit(solution)/shard_map/ppermute | solution.py:22
  70.7 8.0 %collective-permute-start.11 = (bf16[4,96,256]{2,1,0:T(8,128)(2,1)S(1)}, bf16[4,96,256]{2,1,0:T(8,128)(2,1)S(1)}, u32[]{:S(2)}, u32[]{:S(2)}) collective-permute-start(bf16[4,96,256]{2,1,0:T(8,128)(2,1)S(1)} %all-to-all-done.2.refs_0_), channel_id=1, source_target_pairs={{0,16},{8,24},{16,0},{24,8},{1,17},{9,25},{17,1},{25,9},{2,18},{10... | collective-permute-start | bytes 589832 | tf_op jit(solution)/shard_map/ppermute | solution.py:27
  77.0 6.6 %collective-permute-start.15 = (bf16[4,96,256]{2,1,0:T(8,128)(2,1)S(1)}, bf16[4,96,256]{2,1,0:T(8,128)(2,1)}, u32[]{:S(2)}, u32[]{:S(2)}) collective-permute-start(bf16[4,96,256]{2,1,0:T(8,128)(2,1)S(1)} %collective-permute-done.14.refs_4_), channel_id=1, source_target_pairs={{0,16},{8,24},{16,0},{24,8},{1,17},{9,25},{17,1},{25,9},{2,18},{10... | collective-permute-start | bytes 589832 | tf_op jit(solution)/shard_map/ppermute | solution.py:27
  78.2 9.4 %collective-permute-start.12 = (bf16[4,96,256]{2,1,0:T(8,128)(2,1)S(1)}, bf16[4,96,256]{2,1,0:T(8,128)(2,1)}, u32[]{:S(2)}, u32[]{:S(2)}) collective-permute-start(bf16[4,96,256]{2,1,0:T(8,128)(2,1)S(1)} %all-to-all-done.2.refs_0_), channel_id=1, source_target_pairs={{0,8},{8,0},{16,24},{24,16},{1,9},{9,1},{17,25},{25,17},{2,10},{10... | collective-permute-start | bytes 589832 | tf_op jit(solution)/shard_map/ppermute | solution.py:22
  78.2 9.4 %collective-permute-start.16 = (bf16[4,96,256]{2,1,0:T(8,128)(2,1)S(1)}, bf16[4,96,256]{2,1,0:T(8,128)(2,1)}, u32[]{:S(2)}, u32[]{:S(2)}) collective-permute-start(bf16[4,96,256]{2,1,0:T(8,128)(2,1)S(1)} %collective-permute-done.14.refs_4_), channel_id=1, source_target_pairs={{0,8},{8,0},{16,24},{24,16},{1,9},{9,1},{17,25},{25,17},{2,10},{10... | collective-permute-start | bytes 589832 | tf_op jit(solution)/shard_map/ppermute | solution.py:22
  78.7 8.8 %collective-permute-start.13 = (bf16[4,96,256]{2,1,0:T(8,128)(2,1)S(1)}, bf16[4,96,256]{2,1,0:T(8,128)(2,1)}, u32[]{:S(2)}, u32[]{:S(2)}) collective-permute-start(bf16[4,96,256]{2,1,0:T(8,128)(2,1)S(1)} %collective-permute-done.11.refs_1_), channel_id=1, source_target_pairs={{0,8},{8,0},{16,24},{24,16},{1,9},{9,1},{17,25},{25,17},{2,10},{10... | collective-permute-start | bytes 589832 | tf_op jit(solution)/shard_map/ppermute | solution.py:22
  83.6 4.0 %collective-permute-start.17 = (bf16[4,96,256]{2,1,0:T(8,128)(2,1)}, bf16[4,96,256]{2,1,0:T(8,128)(2,1)}, u32[]{:S(2)}, u32[]{:S(2)}) collective-permute-start(bf16[4,96,256]{2,1,0:T(8,128)(2,1)} %collective-permute-done.15.refs_5_), channel_id=1, source_target_pairs={{0,8},{8,0},{16,24},{24,16},{1,9},{9,1},{17,25},{25,17},{2,10},{10... | collective-permute-start | bytes 589832 | tf_op jit(solution)/shard_map/ppermute | solution.py:22
  91.4 13.5 %all-to-all-start.4 = ((bf16[4,5,32,256]{3,2,1,0:T(8,128)(2,1)}), bf16[4,5,32,256]{3,2,1,0:T(8,128)(2,1)S(1)}, u32[]{:S(2)}, u32[]{:S(2)}) async-start(bf16[4,5,32,256]{3,2,1,0:T(8,128)(2,1)} %get-tuple-element.61), calls=%async_computation.4 | async-start | bytes 655360 | tf_op jit(solution)/shard_map/all_to_all | solution.py:56
  94.8 7.8 %collective-permute-start.18 = (bf16[8,2,32,256]{3,2,1,0:T(8,128)(2,1)}, bf16[8,2,32,256]{3,2,1,0:T(8,128)(2,1)}, u32[]{:S(2)}, u32[]{:S(2)}) collective-permute-start(bf16[8,2,32,256]{3,2,1,0:T(8,128)(2,1)} %bitcast.15), channel_id=1, source_target_pairs={{0,16},{8,24},{16,0},{24,8},{1,17},{9,25},{17,1},{25,9},{2,18},{10... | collective-permute-start | bytes 786440 | tf_op jit(solution)/shard_map/ppermute | solution.py:27
  104.9 8.5 %collective-permute-start.22 = (bf16[4,5,32,256]{3,2,1,0:T(8,128)(2,1)S(1)}, bf16[4,5,32,256]{3,2,1,0:T(8,128)(2,1)S(1)}, u32[]{:S(2)}, u32[]{:S(2)}) collective-permute-start(bf16[4,5,32,256]{3,2,1,0:T(8,128)(2,1)S(1)} %all-to-all-done.4.refs_8_), channel_id=1, source_target_pairs={{0,1},{1,0},{2,3},{3,2},{4,5},{5,4},{6,7},{7,6},{8,9},{9,8},{10,11... | collective-permute-start | bytes 983048 | tf_op jit(solution)/shard_map/ppermute | solution.py:50
  105.8 11.6 %all-to-all-start.5 = ((bf16[8,2,32,256]{3,2,1,0:T(8,128)(2,1)}), bf16[8,2,32,256]{3,2,1,0:T(8,128)(2,1)S(1)}, u32[]{:S(2)}, u32[]{:S(2)}) async-start(bf16[8,2,32,256]{3,2,1,0:T(8,128)(2,1)} %collective-permute-done.18), calls=%async_computation.5 | async-start | bytes 524288 | tf_op jit(solution)/shard_map/all_to_all | solution.py:502
  110.0 7.3 %collective-permute-start.19 = (bf16[4,3,32,256]{3,2,1,0:T(8,128)(2,1)}, bf16[4,3,32,256]{3,2,1,0:T(8,128)(2,1)}, u32[]{:S(2)}, u32[]{:S(2)}) collective-permute-start(bf16[4,3,32,256]{3,2,1,0:T(8,128)(2,1)} %slice.6), channel_id=1, source_target_pairs={{0,16},{8,24},{16,0},{24,8},{1,17},{9,25},{17,1},{25,9},{2,18},{10... | collective-permute-start | bytes 589832 | tf_op jit(solution)/shard_map/ppermute | solution.py:27
  114.2 6.0 %collective-permute-start.23 = (bf16[4,3,32,256]{3,2,1,0:T(8,128)(2,1)}, bf16[4,3,32,256]{3,2,1,0:T(8,128)(2,1)}, u32[]{:S(2)}, u32[]{:S(2)}) collective-permute-start(bf16[4,3,32,256]{3,2,1,0:T(8,128)(2,1)} %slice.8), channel_id=1, source_target_pairs={{0,16},{8,24},{16,0},{24,8},{1,17},{9,25},{17,1},{25,9},{2,18},{10... | collective-permute-start | bytes 589832 | tf_op jit(solution)/shard_map/ppermute | solution.py:27
  115.6 4.6 %collective-permute-start.20 = (bf16[4,5,32,256]{3,2,1,0:T(8,128)(2,1)S(1)}, bf16[4,5,32,256]{3,2,1,0:T(8,128)(2,1)S(1)}, u32[]{:S(2)}, u32[]{:S(2)}) collective-permute-start(bf16[4,5,32,256]{3,2,1,0:T(8,128)(2,1)S(1)} %all-to-all-done.4.refs_8_), channel_id=1, source_target_pairs={{0,8},{8,0},{16,24},{24,16},{1,9},{9,1},{17,25},{25,17},{2,10},{10... | collective-permute-start | bytes 983048 | tf_op jit(solution)/shard_map/ppermute | solution.py:22
  115.6 4.6 %collective-permute-start.24 = (bf16[4,5,32,256]{3,2,1,0:T(8,128)(2,1)S(1)}, bf16[4,5,32,256]{3,2,1,0:T(8,128)(2,1)}, u32[]{:S(2)}, u32[]{:S(2)}) collective-permute-start(bf16[4,5,32,256]{3,2,1,0:T(8,128)(2,1)S(1)} %collective-permute-done.22.refs_12_), channel_id=1, source_target_pairs={{0,8},{8,0},{16,24},{24,16},{1,9},{9,1},{17,25},{25,17},{2,10},{10... | collective-permute-start | bytes 983048 | tf_op jit(solution)/shard_map/ppermute | solution.py:22
  117.3 2.9 %collective-permute-start.26 = (bf16[8,2,32,256]{3,2,1,0:T(8,128)(2,1)S(1)}, bf16[8,2,32,256]{3,2,1,0:T(8,128)(2,1)S(1)}, u32[]{:S(2)}, u32[]{:S(2)}) collective-permute-start(bf16[8,2,32,256]{3,2,1,0:T(8,128)(2,1)S(1)} %all-to-all-done.5.refs_16_), channel_id=1, source_target_pairs={{0,8},{8,0},{16,24},{24,16},{1,9},{9,1},{17,25},{25,17},{2,10},{10... | collective-permute-start | bytes 786440 | tf_op jit(solution)/shard_map/ppermute | solution.py:22
  117.3 2.8 %collective-permute-start.21 = (bf16[4,3,32,256]{3,2,1,0:T(8,128)(2,1)}, bf16[4,3,32,256]{3,2,1,0:T(8,128)(2,1)S(1)}, u32[]{:S(2)}, u32[]{:S(2)}) collective-permute-start(bf16[4,3,32,256]{3,2,1,0:T(8,128)(2,1)} %collective-permute-done.19.refs_9_), channel_id=1, source_target_pairs={{0,8},{8,0},{16,24},{24,16},{1,9},{9,1},{17,25},{25,17},{2,10},{10... | collective-permute-start | bytes 589832 | tf_op jit(solution)/shard_map/ppermute | solution.py:22
  120.2 1.7 %collective-permute-start.25 = (bf16[4,3,32,256]{3,2,1,0:T(8,128)(2,1)}, bf16[4,3,32,256]{3,2,1,0:T(8,128)(2,1)S(1)}, u32[]{:S(2)}, u32[]{:S(2)}) collective-permute-start(bf16[4,3,32,256]{3,2,1,0:T(8,128)(2,1)} %collective-permute-done.23.refs_13_), channel_id=1, source_target_pairs={{0,8},{8,0},{16,24},{24,16},{1,9},{9,1},{17,25},{25,17},{2,10},{10... | collective-permute-start | bytes 589832 | tf_op jit(solution)/shard_map/ppermute | solution.py:22
